TPU v7x, 32 devices: a whole 2x2x4 slice. The times are simulated.
32 devices in a mesh: group: 2 (over x), hst: 8 (over z, y), cores: 2 (over core).
Axes of the slice: x: 2, y: 2, z: 4, core: 2. Of those that a mesh axis runs over, the one named last changes fastest.
Arguments:
- observations: bfloat16 [512, 16, 512], P(('group', 'hst', 'cores')), parts along dimension 0, may hold values from -20 to 20
- lengths: int32 [512], P(('group', 'hst', 'cores')), parts along dimension 0, may hold values from 1 to 16, as said below
- actions: int32 [512, 16], P(('group', 'hst', 'cores')), parts along dimension 0, may hold values from 0 to 127
- rewards: float32 [512, 16], P(('group', 'hst', 'cores')), parts along dimension 0, may hold values from -6 to 6
- assign: int32 [512], P(('group', 'hst', 'cores')), parts along dimension 0, may hold values from 0 to 15, as said below
- actor_embed: bfloat16 [1024, 1024], P('group'), parts along dimension 0, may hold values from -0.25 to 0.25
- actor_policy: bfloat16 [2048, 128], P('group'), parts along dimension 0, may hold values from -1 to 1
- master_embed: float32 [1024, 1024], P('group'), parts along dimension 0, may hold values from -0.25 to 0.25
- master_policy: float32 [2048, 128], P('group'), parts along dimension 0, may hold values from -1 to 1
- master_value: float32 [2048], P('group'), parts along dimension 0, may hold values from -0.1875 to 0.1875
- embed_moment: float32 [1024, 1024], P('group'), parts along dimension 0, may hold values from -0.15625 to 0.15625
- policy_moment: float32 [2048, 128], P('group'), parts along dimension 0, may hold values from -0.15625 to 0.15625
- value_moment: float32 [2048], P('group'), parts along dimension 0, may hold values from -0.15625 to 0.15625
- next_obs: bfloat16 [8192, 512], P(('group', 'hst', 'cores')), parts along dimension 0, may hold values from -6 to 6
Outputs:
- next_logits: bfloat16 [8192, 128], P(('group', 'hst', 'cores')), parts along dimension 0
- new_embed: float32 [1024, 1024], P('group'), parts along dimension 0
- new_policy: float32 [2048, 128], P('group'), parts along dimension 0
- new_value: float32 [2048], P('group'), parts along dimension 0
- new_embed_moment: float32 [1024, 1024], P('group'), parts along dimension 0
- new_policy_moment: float32 [2048, 128], P('group'), parts along dimension 0
- new_value_moment: float32 [2048], P('group'), parts along dimension 0
There are 2 independent parts, one for each index of `group`. A program takes and returns all parts, laid end to end along the dimension named above; each array names one. Nothing has to cross between parts.
Inputs may be any that keep to these rules, and one draw needn't show every extreme that they name: `lengths`: valid steps of a trajectory; 16 is reached in every draw. `assign`: within each aligned block of 16 trajectories (one actor device), every learner index is named exactly 1 times.
All inputs are finite; a program needn't handle non-finite values.
Results may differ from a plain program's by a relative error of at most 0.006.
The roundings to bfloat16 on the way count: a program that leaves them out, or rounds other values in their place, can miss the bound.
Values may be sent and summed in bfloat16 or wider, within the bound.
No kernel may reach another device: no remote copies, remote signals or barrier semaphores. Data moves between devices by JAX's collectives and lax.ppermute only.
A program may use at most 64 MiB of HBM per device.

v0:
```python
import jax
import jax.numpy as jnp
from jax import lax
from jax.sharding import PartitionSpec as P

GAMMA = 0.99
ENTROPY_COEF = 0.1
MOMENTUM = 0.9
LEARN_RATE = 0.05


def torso(frames, embed, policy):
    preact = jnp.dot(frames, embed, preferred_element_type=jnp.float32)
    hidden = jnp.maximum(preact, 0.0).astype(jnp.bfloat16)
    logits = jnp.dot(hidden, policy, preferred_element_type=jnp.float32)
    return (preact, hidden, logits)


def chosen(logprob, actions):
    labels = jnp.arange(logprob.shape[-1]).astype(actions.dtype)
    onehot = labels[None, :] == actions[:, None]
    return (onehot, jnp.sum(jnp.where(onehot, logprob, 0.0), axis=-1))


def behaviour(observations, actions, embed, policy):
    traj_count, slot_count, feat_count = observations.shape
    preact, hidden, logits = torso(
        observations.reshape(traj_count * slot_count, feat_count), embed, policy
    )
    logprob = jax.nn.log_softmax(logits, axis=-1)
    onehot, taken = chosen(logprob, actions.reshape(-1))
    return taken.reshape(traj_count, slot_count)


def learner_grads(
    observations, actions, rewards, lengths, behave, weight, embed, policy, value_head
):
    traj_count, slot_count, feat_count = observations.shape
    frames = observations.reshape(traj_count * slot_count, feat_count)
    preact, hidden, logits = torso(frames, embed, policy)
    values = jnp.dot(hidden, value_head, preferred_element_type=jnp.float32).reshape(
        traj_count, slot_count
    )
    logprob = jax.nn.log_softmax(logits, axis=-1)
    onehot, taken = chosen(logprob, actions.reshape(-1))
    probs = jnp.exp(logprob)
    entropy = -jnp.sum(probs * logprob, axis=-1)
    positions = jnp.arange(slot_count).astype(lengths.dtype)
    inside = (positions[None, :] < lengths[:, None]).astype(jnp.float32)
    beyond = (positions[None, :] + 1 < lengths[:, None]).astype(jnp.float32)
    ratios = jnp.minimum(1.0, jnp.exp(taken.reshape(traj_count, slot_count) - behave))

    def shifted(series):
        return (
            jnp.concatenate([series[:, 1:], jnp.zeros((traj_count, 1), jnp.float32)], axis=1)
            * beyond
        )

    deltas = inside * ratios * (rewards + GAMMA * shifted(values) - values)

    def backward_step(carry_sum, inputs):
        delta_now, ratio_now, inside_now = inputs
        carry_sum = inside_now * (delta_now + GAMMA * ratio_now * carry_sum)
        return (carry_sum, carry_sum)

    last_sum, corrections = lax.scan(
        backward_step,
        jnp.zeros((traj_count,), jnp.float32),
        (deltas.T, ratios.T, inside.T),
        reverse=True,
    )
    targets = values + corrections.T
    advantage = ratios * (rewards + GAMMA * shifted(targets) - values)
    scale = (weight[:, None] * inside).reshape(-1)
    grad_logits = (
        scale[:, None]
        * (
            -advantage.reshape(-1)[:, None] * (onehot.astype(jnp.float32) - probs)
            + ENTROPY_COEF * probs * (logprob + entropy[:, None])
        )
    ).astype(jnp.bfloat16)
    grad_values = (scale * (values - targets).reshape(-1)).astype(jnp.bfloat16)
    grad_policy = jnp.dot(hidden.T, grad_logits, preferred_element_type=jnp.float32)
    grad_value = jnp.dot(grad_values, hidden, preferred_element_type=jnp.float32)
    grad_hidden = (
        jnp.dot(grad_logits, policy.T, preferred_element_type=jnp.float32)
        + grad_values.astype(jnp.float32)[:, None] * value_head.astype(jnp.float32)[None, :]
    )
    grad_preact = jnp.where(preact > 0.0, grad_hidden, 0.0).astype(jnp.bfloat16)
    grad_embed = jnp.dot(frames.T, grad_preact, preferred_element_type=jnp.float32)
    return (grad_embed, grad_policy, grad_value)


def body(
    observations,
    lengths,
    actions,
    rewards,
    assign,
    actor_embed,
    actor_policy,
    master_embed,
    master_policy,
    master_value,
    embed_moment,
    policy_moment,
    value_moment,
    next_obs,
):
    learners = lax.axis_size("hst") * lax.axis_size("cores")
    embed = master_embed.astype(jnp.bfloat16)
    policy = master_policy.astype(jnp.bfloat16)
    value_head = master_value.astype(jnp.bfloat16)
    behave = behaviour(observations, actions, actor_embed, actor_policy)
    traj_count = observations.shape[0]
    order = jnp.argsort(assign, stable=True)
    per_peer = traj_count // learners

    def grouped(series):
        return jnp.take(series, order, axis=0).reshape((learners, per_peer) + series.shape[1:])

    frames = lax.all_to_all(
        grouped(observations), ("hst", "cores"), split_axis=0, concat_axis=0, tiled=True
    )
    got_rewards, got_behave, got_actions, got_lengths = (
        lax.all_to_all(grouped(rewards), ("hst", "cores"), split_axis=0, concat_axis=0, tiled=True),
        lax.all_to_all(grouped(behave), ("hst", "cores"), split_axis=0, concat_axis=0, tiled=True),
        lax.all_to_all(
            grouped(actions).astype(jnp.float32),
            ("hst", "cores"),
            split_axis=0,
            concat_axis=0,
            tiled=True,
        ),
        lax.all_to_all(
            grouped(lengths).astype(jnp.float32),
            ("hst", "cores"),
            split_axis=0,
            concat_axis=0,
            tiled=True,
        ),
    )
    flat_lengths = got_lengths.reshape(lengths.shape)
    total = jnp.sum(flat_lengths)
    weight = jnp.ones((traj_count,), jnp.float32) * (1.0 / (learners * total))
    grads = learner_grads(
        frames.reshape(observations.shape),
        got_actions.reshape(actions.shape),
        got_rewards.reshape(rewards.shape),
        flat_lengths,
        got_behave.reshape(behave.shape),
        weight,
        embed,
        policy,
        value_head,
    )
    grad_embed, grad_policy, grad_value = lax.psum((grads[0], grads[1], grads[2]), ("hst", "cores"))
    new_embed_moment = MOMENTUM * embed_moment + grad_embed
    new_policy_moment = MOMENTUM * policy_moment + grad_policy
    new_value_moment = MOMENTUM * value_moment + grad_value
    new_embed = master_embed - LEARN_RATE * new_embed_moment
    new_policy = master_policy - LEARN_RATE * new_policy_moment
    new_value = master_value - LEARN_RATE * new_value_moment
    preact, hidden, logits = torso(
        next_obs, new_embed.astype(jnp.bfloat16), new_policy.astype(jnp.bfloat16)
    )
    next_logits = logits.astype(jnp.bfloat16)
    return (
        next_logits,
        new_embed,
        new_policy,
        new_value,
        new_embed_moment,
        new_policy_moment,
        new_value_moment,
    )


def solution(mesh):
    return jax.shard_map(
        body,
        mesh=mesh,
        in_specs=(
            P(("group", "hst", "cores"), None, None),
            P(("group", "hst", "cores")),
            P(("group", "hst", "cores"), None),
            P(("group", "hst", "cores"), None),
            P(("group", "hst", "cores")),
            P("group", None),
            P("group", None),
            P("group", None),
            P("group", None),
            P("group"),
            P("group", None),
            P("group", None),
            P("group"),
            P(("group", "hst", "cores"), None),
        ),
        out_specs=(
            P(("group", "hst", "cores"), None),
            P("group", None),
            P("group", None),
            P("group"),
            P("group", None),
            P("group", None),
            P("group"),
        ),
        check_vma=False,
    )
```

profile of v0, /device:TPU:0, one launch (start us, length us, event | category | flops | bytes accessed | tf_op | source)
XLA Modules:
  0.0 248.6 jit_solution(6340541724222596881)
XLA Ops:
  7.2 2.0 sort.17
  9.2 1.3 gather_fusion.1
  11.2 7.4 %all-to-all-start.1 = ((f32[16,1,1]{2,1,0:T(1,128)}), f32[16,1,1]{2,1,0:T(1,128)S(1)}, u32[]{:S(2)}, u32[]{:S(2)}) async-start(f32[16,1,1]{2,1,0:T(1,128)} %copy.34), calls=%async_computation.1 | async-start | bytes 16384 | tf_op jit(solution)/shard_map/all_to_all | solution.py:135
  20.7 1.5 gather_fusion
  23.7 1.7 fusion.63
  28.0 6.0 %all-to-all-start.2 = ((f32[16,1,16]{2,1,0:T(1,128)}), f32[16,1,16]{2,1,0:T(1,128)S(1)}, u32[]{:S(2)}, u32[]{:S(2)}) async-start(f32[16,1,16]{2,1,0:T(1,128)} %bitcast.4), calls=%async_computation.2 | async-start | bytes 16384 | tf_op jit(solution)/shard_map/all_to_all | solution.py:128
  34.6 5.7 %all-to-all-done.2 = f32[16,1,16]{2,1,0:T(1,128)S(1)} async-done(((f32[16,1,16]{2,1,0:T(1,128)}), f32[16,1,16]{2,1,0:T(1,128)S(1)}, u32[]{:S(2)}, u32[]{:S(2)}) %all-to-all-start.2) | async-done | bytes 1056 | tf_op jit(solution)/shard_map/all_to_all | solution.py:128
  40.3 3.5 %all-to-all-start = ((bf16[16,1,16,512]{3,2,1,0:T(8,128)(2,1)}), bf16[16,1,16,512]{3,2,1,0:T(8,128)(2,1)S(1)}, u32[]{:S(2)}, u32[]{:S(2)}) async-start(bf16[16,1,16,512]{3,2,1,0:T(8,128)(2,1)} %bitcast_select_fusion), calls=%async_computation | async-start | bytes 524288 | tf_op jit(solution)/shard_map/all_to_all | solution.py:122
  48.3 5.6 %all-to-all-done = bf16[16,1,16,512]{3,2,1,0:T(8,128)(2,1)S(1)} async-done(((bf16[16,1,16,512]{3,2,1,0:T(8,128)(2,1)}), bf16[16,1,16,512]{3,2,1,0:T(8,128)(2,1)S(1)}, u32[]{:S(2)}, u32[]{:S(2)}) %all-to-all-start) | async-done | bytes 262176 | tf_op jit(solution)/shard_map/all_to_all | solution.py:122
  53.9 3.5 %all-to-all-start.4 = ((f32[16,1,16]{2,1,0:T(1,128)}), f32[16,1,16]{2,1,0:T(1,128)S(1)}, u32[]{:S(2)}, u32[]{:S(2)}) async-start(f32[16,1,16]{2,1,0:T(1,128)} %bitcast.10), calls=%async_computation.4 | async-start | bytes 16384 | tf_op jit(solution)/shard_map/all_to_all | solution.py:126
  57.4 2.0 maximum_convert_fusion
  60.6 3.0 %all-to-all-done.4 = f32[16,1,16]{2,1,0:T(1,128)S(1)} async-done(((f32[16,1,16]{2,1,0:T(1,128)}), f32[16,1,16]{2,1,0:T(1,128)S(1)}, u32[]{:S(2)}, u32[]{:S(2)}) %all-to-all-start.4) | async-done | bytes 1056 | tf_op jit(solution)/shard_map/all_to_all | solution.py:126
  63.7 4.1 %all-to-all-start.3 = ((f32[16,1,16]{2,1,0:T(1,128)}), f32[16,1,16]{2,1,0:T(1,128)}, u32[]{:S(2)}, u32[]{:S(2)}) async-start(f32[16,1,16]{2,1,0:T(1,128)} %bitcast.7), calls=%async_computation.3 | async-start | bytes 16384 | tf_op jit(solution)/shard_map/all_to_all | solution.py:127
  67.8 1.4 fusion.33
  69.2 1.4 reshape.168
  72.0 2.1 all-to-all-done.3
  74.1 1.4 fusion.54
  75.5 1.4 copy.38
  76.9 1.4 copy.39
  78.9 40.5 %while.17 = (s32[]{:T(128)}, f32[16]{0:T(128)}, f32[16,16]{1,0:T(8,128)}, f32[16,16]{1,0:T(8,128)}, f32[16,16]{1,0:T(8,128)}, /*index=5*/f32[16,16]{1,0:T(8,128)}, s32[]{:T(128)}, s32[]{:T(128)}, s32[]{:T(128)}) while((s32[]{:T(128)}, f32[16]{0:T(128)}, f32[16,16]{1,0:T(8,128)}, f32[16,16]{1,0:T(8,128)}, f32[16,16]{1,0:T(8,128)}, ...), condition=%wide.region_7.10_spmd.clone, body=%wide.region_6.9_spmd.clone.sunk | while | flops 84 | bytes 571 | solution.py:66
  80.1 1.3 dynamic_update_slice.12
  82.6 1.3 dynamic_update_slice.12
  119.4 1.4 copy.40
  120.7 1.3 bitcast_add_fusion
  122.1 1.4 fusion.48
  125.7 1.3 reshape.176
  128.3 1.9 fusion.55
  130.1 2.8 %fusion.13 = f32[512,1024]{1,0:T(8,128)} fusion(bf16[256,512]{1,0:T(8,128)(2,1)S(1)} %bitcast.67, f32[256,1024]{1,0:T(8,128)S(1)} %get-tuple-element.217, f32[1024]{0:T(1024)} %get-tuple-element.207, f32[256]{0:T(256)S(1)} %get-tuple-element.203, f32[1024,128]{1,0:T(8,128)S(1)} %copy-done.2, f32[256,128]{0,1:T(8,128)S(1)} %get-tuple-element.219, ...), kind=kOutput, calls=%fused_computation.27 | convolution fusion | flops 337379328 | bytes 4075008 | tf_op jit(solution)/shard_map/dot_general | solution.py:90
  133.8 32.1 %psum.23 = f32[1024]{0:T(1024)S(1)} all-reduce(f32[1024]{0:T(1024)S(1)} %bitcast.72), channel_id=1, replica_groups=mesh['group'=2,'hst'=8,'cores'=2] {'hst','cores'}, use_global_device_ids=true, to_apply=%region_11.14 | all-reduce | flops 1024 | bytes 8192 | tf_op jit(solution)/shard_map/psum | solution.py:157
  166.5 66.3 %all-reduce.5.cloned.1.call-done = (f32[512,1024]{1,0:T(8,128)}, f32[1024,128]{1,0:T(8,128)}) async-done(((f32[512,1024]{1,0:T(8,128)}, f32[1024,128]{1,0:T(8,128)}), (f32[512,1024]{1,0:T(8,128)}, f32[1024,128]{1,0:T(8,128)})) %all-reduce.5.cloned.1.call-update) | async-done | bytes 2621456 | tf_op jit(solution)/shard_map/psum | solution.py:157
  232.8 5.2 %multiply_subtract_fusion = (f32[512,1024]{1,0:T(8,128)S(1)}, f32[512,1024]{1,0:T(8,128)}) fusion(f32[512,1024]{1,0:T(8,128)} %param.26, f32[512,1024]{1,0:T(8,128)} %get-tuple-element.195, f32[512,1024]{1,0:T(8,128)} %param.29), kind=kLoop, calls=%fused_computation.16 | loop fusion | flops 2097152 | bytes 10485760 | tf_op jit(solution)/shard_map/sub | solution.py:161
  239.2 2.5 %fusion.14 = bf16[256,128]{1,0:T(8,128)(2,1)} fusion(bf16[256,512]{1,0:T(8,128)(2,1)S(1)} %copy-done.7, f32[512,1024]{1,0:T(8,128)S(1)} %get-tuple-element.201, f32[1024,128]{1,0:T(8,128)} %get-tuple-element.199), kind=kOutput, calls=%fused_computation.28 | convolution fusion | flops 336756736 | bytes 2949120 | tf_op jit(solution)/shard_map/dot_general | solution.py:15
  (108 shorter events, 58.3 us)
Async XLA Ops:
  7.2 16.5 %copy-start = (bf16[512,1024]{1,0:T(8,128)(2,1)S(1)}, bf16[512,1024]{1,0:T(8,128)(2,1)}, u32[]{:S(2)}) copy-start(bf16[512,1024]{1,0:T(8,128)(2,1)} %param.24) | copy-start | bytes 3145732
  7.2 19.0 %copy-start.6 = (f32[16,16]{1,0:T(8,128)S(1)}, f32[16,16]{1,0:T(8,128)}, u32[]{:S(2)}) copy-start(f32[16,16]{1,0:T(8,128)} %param.22) | copy-start | bytes 3076
  9.2 18.2 %copy-start.9 = (f32[1024]{0:T(1024)S(1)}, f32[1024]{0:T(1024)}, u32[]{:S(2)}) copy-start(f32[1024]{0:T(1024)} %param.28) | copy-start | bytes 12292
  11.2 16.8 %all-to-all-start.1 = ((f32[16,1,1]{2,1,0:T(1,128)}), f32[16,1,1]{2,1,0:T(1,128)S(1)}, u32[]{:S(2)}, u32[]{:S(2)}) async-start(f32[16,1,1]{2,1,0:T(1,128)} %copy.34), calls=%async_computation.1 | async-start | bytes 16384 | tf_op jit(solution)/shard_map/all_to_all | solution.py:135
  28.0 12.4 %all-to-all-start.2 = ((f32[16,1,16]{2,1,0:T(1,128)}), f32[16,1,16]{2,1,0:T(1,128)S(1)}, u32[]{:S(2)}, u32[]{:S(2)}) async-start(f32[16,1,16]{2,1,0:T(1,128)} %bitcast.4), calls=%async_computation.2 | async-start | bytes 16384 | tf_op jit(solution)/shard_map/all_to_all | solution.py:128
  40.3 13.5 %all-to-all-start = ((bf16[16,1,16,512]{3,2,1,0:T(8,128)(2,1)}), bf16[16,1,16,512]{3,2,1,0:T(8,128)(2,1)S(1)}, u32[]{:S(2)}, u32[]{:S(2)}) async-start(bf16[16,1,16,512]{3,2,1,0:T(8,128)(2,1)} %bitcast_select_fusion), calls=%async_computation | async-start | bytes 524288 | tf_op jit(solution)/shard_map/all_to_all | solution.py:122
  43.9 15.5 %copy-start.2 = (f32[1024,128]{1,0:T(8,128)S(1)}, f32[1024,128]{1,0:T(8,128)}, u32[]{:S(2)}) copy-start(f32[1024,128]{1,0:T(8,128)} %param.27) | copy-start | bytes 1572868
  44.5 2.0 copy-start.14
  45.1 14.3 %copy-start.12 = (f32[16]{0:T(128)}, f32[16]{0:T(128)S(1)}, u32[]{:S(2)}) copy-start(f32[16]{0:T(128)S(1)} %get-tuple-element.181) | copy-start | bytes 196
  53.9 9.8 %all-to-all-start.4 = ((f32[16,1,16]{2,1,0:T(1,128)}), f32[16,1,16]{2,1,0:T(1,128)S(1)}, u32[]{:S(2)}, u32[]{:S(2)}) async-start(f32[16,1,16]{2,1,0:T(1,128)} %bitcast.10), calls=%async_computation.4 | async-start | bytes 16384 | tf_op jit(solution)/shard_map/all_to_all | solution.py:126
  59.8 10.8 %copy-start.8 = (f32[256]{0:T(256)}, f32[256]{0:T(256)S(1)}, u32[]{:S(2)}) copy-start(f32[256]{0:T(256)S(1)} %get-tuple-element.218) | copy-start | bytes 3076
  60.6 9.9 %copy-start.11 = (f32[256]{0:T(256)}, f32[256]{0:T(256)S(1)}, u32[]{:S(2)}) copy-start(f32[256]{0:T(256)S(1)} %log.9) | copy-start | bytes 3076
  63.7 10.5 %all-to-all-start.3 = ((f32[16,1,16]{2,1,0:T(1,128)}), f32[16,1,16]{2,1,0:T(1,128)}, u32[]{:S(2)}, u32[]{:S(2)}) async-start(f32[16,1,16]{2,1,0:T(1,128)} %bitcast.7), calls=%async_computation.3 | async-start | bytes 16384 | tf_op jit(solution)/shard_map/all_to_all | solution.py:127
  67.8 165.0 %all-reduce.5.cloned.1.call-start = ((), (), s32[]{:S(2)}) async-start(), calls=%async_computation.5 | async-start | bytes 5242880 | tf_op jit(solution)/shard_map/psum | solution.py:157
  132.9 0.7 copy-start.15
  132.9 33.0 %copy-start.10 = (f32[1024]{0:T(1024)S(1)}, f32[1024]{0:T(1024)}, u32[]{:S(2)}) copy-start(f32[1024]{0:T(1024)} %param.28) | copy-start | bytes 12292
  132.9 33.0 %copy-start.13 = (f32[1024]{0:T(1024)S(1)}, f32[1024]{0:T(1024)}, u32[]{:S(2)}) copy-start(f32[1024]{0:T(1024)} %param.31) | copy-start | bytes 12292
  232.8 5.3 %copy-start.3 = (f32[1024,128]{1,0:T(8,128)S(1)}, f32[1024,128]{1,0:T(8,128)}, u32[]{:S(2)}) copy-start(f32[1024,128]{1,0:T(8,128)} %param.27) | copy-start | bytes 1572868
  232.8 5.3 %copy-start.4 = (f32[1024,128]{1,0:T(8,128)S(1)}, f32[1024,128]{1,0:T(8,128)}, u32[]{:S(2)}) copy-start(f32[1024,128]{1,0:T(8,128)} %param.30) | copy-start | bytes 1572868
  232.8 5.3 %copy-start.5 = (f32[1024,128]{1,0:T(8,128)S(1)}, f32[1024,128]{1,0:T(8,128)}, u32[]{:S(2)}) copy-start(f32[1024,128]{1,0:T(8,128)} %get-tuple-element.196) | copy-start | bytes 1572868
  238.0 3.7 %copy-start.1 = (f32[512,1024]{1,0:T(8,128)}, f32[512,1024]{1,0:T(8,128)S(1)}, u32[]{:S(2)}) copy-start(f32[512,1024]{1,0:T(8,128)S(1)} %get-tuple-element.201) | copy-start | bytes 6291460
  238.0 1.1 copy-start.7
Sparse Core Ops, SparseCore 0:
  133.1 99.6 all-reduce.4
where the time goes:
time: 251 us; the launch traced here: 249 us
  waiting for transfers between devices  82.8 us (33%)
  other arithmetic  42.1 us (17%)
  local copies, waits for them, and re-layouts  39.8 us (16%)
  blocking collectives  32.1 us (13%)
  starting transfers between devices  24.5 us (10%)
  between operations  14.9 us (6%)
  matrix products  12.3 us (5%)
    psum x1, waiting for transfers between devices, body(): lax.psum((grads[0], grads[1], grads[2]), ('hst', 'cores'))  66.3 us
    psum x1, blocking collectives, body(): lax.psum((grads[0], grads[1], grads[2]), ('hst', 'cores'))  32.1 us
    dynamic_update_slice x16, local copies, waits for them, and re-layouts, learner_grads(): lax.scan(backward_step, jnp.zeros((traj_count,), jnp.float32), (deltas.T,...  20.6 us
    mul x16, other arithmetic, backward_step(): carry_sum = inside_now * (delta_now + GAMMA * ratio_now * carry_sum)  19.9 us
    all_to_all x1, starting transfers between devices, body(): lax.all_to_all(grouped(lengths).astype(jnp.float32), ('hst', 'cores'), sp...  7.39 us
    all_to_all x1, starting transfers between devices, body(): lax.all_to_all(grouped(actions).astype(jnp.float32), ('hst', 'cores'), sp...  6.01 us
    all_to_all x1, waiting for transfers between devices, body(): lax.all_to_all(grouped(actions).astype(jnp.float32), ('hst', 'cores'), sp...  5.75 us
    all_to_all x1, waiting for transfers between devices, body(): lax.all_to_all(grouped(observations), ('hst', 'cores'), split_axis=0, con...  5.58 us
  transfers between devices with their start and end apart: 6, of which 5 were waited for; matrix products, arithmetic and copies ran while one was open for 9% of the time, Pallas kernels for 0%

commit v1 on v0

v1 whole, which is shorter than its diff:
```python
import functools

import jax
import jax.numpy as jnp
from jax import lax
from jax.experimental import pallas as pl
from jax.experimental.pallas import tpu as pltpu
from jax.sharding import PartitionSpec as P

GAMMA = 0.99
ENTROPY_COEF = 0.1
MOMENTUM = 0.9
LEARN_RATE = 0.05
AXES = ("hst", "cores")
F32 = jnp.float32
BF16 = jnp.bfloat16
VMEM = pl.BlockSpec(memory_space=pltpu.VMEM)
PARAMS = pltpu.CompilerParams(vmem_limit_bytes=56 * 2**20)
BEHAVE, ACTION, REWARD, LENGTH, ASSIGN = range(5)


def iota(shape, dim):
    return lax.broadcasted_iota(jnp.int32, shape, dim)


def mm(a, b):
    return jnp.dot(a, b, preferred_element_type=F32)


def actor_kernel(
    obs, lengths, assign, actions, rewards, actor_embed, actor_policy,
    master_embed, master_policy, master_value, side, embed, head, head_t,
):
    rows = obs.shape[0]
    traj, slots = actions.shape
    spread = (lax.rem(iota((slots, rows), 1), slots) == iota((slots, rows), 0)).astype(F32)
    owner = lax.div(iota((traj, rows), 1), slots) == iota((traj, rows), 0)

    def flat(series):
        wide = jnp.dot(series, spread, precision=lax.Precision.HIGHEST, preferred_element_type=F32)
        return jnp.sum(jnp.where(owner, wide, 0.0), axis=0, keepdims=True)

    def repeat(series):
        return jnp.dot(
            series.astype(F32), owner.astype(F32),
            precision=lax.Precision.HIGHEST, preferred_element_type=F32,
        )

    action = flat(actions[...].astype(F32))
    hidden = jnp.maximum(mm(obs[...], actor_embed[...]), 0.0).astype(BF16)
    logits = mm(hidden, actor_policy[...]).T
    top = jnp.max(logits, axis=0, keepdims=True)
    shifted = logits - top
    norm = jnp.log(jnp.sum(jnp.exp(shifted), axis=0, keepdims=True))
    onehot = iota(logits.shape, 0) == action.astype(jnp.int32)
    side[...] = jnp.zeros_like(side)
    side[BEHAVE : BEHAVE + 1, :] = (
        jnp.sum(jnp.where(onehot, shifted, 0.0), axis=0, keepdims=True) - norm
    )
    side[ACTION : ACTION + 1, :] = action
    side[REWARD : REWARD + 1, :] = flat(rewards[...])
    side[LENGTH : LENGTH + 1, :] = repeat(lengths[...])
    side[ASSIGN : ASSIGN + 1, :] = repeat(assign[...])
    embed[...] = master_embed[...].astype(BF16)
    nact = master_policy.shape[1]
    wide = jnp.concatenate(
        [
            master_policy[...].T,
            master_value[...],
            jnp.zeros((head_t.shape[0] - nact - 1, head_t.shape[1]), F32),
        ],
        axis=0,
    )
    head_t[...] = wide.astype(BF16)
    head[...] = wide.T.astype(BF16)


def actor(slots, obs, lengths, assign, actions, rewards, *weights):
    feats, width = weights[0].shape
    nact = weights[1].shape[1]
    return pl.pallas_call(
        actor_kernel,
        out_shape=(
            jax.ShapeDtypeStruct((8, obs.shape[0]), F32),
            jax.ShapeDtypeStruct((feats, width), BF16),
            jax.ShapeDtypeStruct((width, 2 * nact), BF16),
            jax.ShapeDtypeStruct((2 * nact, width), BF16),
        ),
        in_specs=[VMEM] * 10,
        out_specs=(VMEM,) * 4,
        compiler_params=PARAMS,
        name="actor",
    )(obs, lengths, assign, actions, rewards, *weights)


def weight_kernel(slots, sides, out):
    learners = out.shape[0]
    rows = sides.shape[2]
    total = jnp.zeros((learners, rows), F32)
    first = lax.rem(iota((1, rows), 1), slots) == 0
    for index in range(sides.shape[0]):
        assign = sides[index, ASSIGN : ASSIGN + 1, :].astype(jnp.int32)
        length = jnp.where(first, sides[index, LENGTH : LENGTH + 1, :], 0.0)
        total = total + jnp.where(iota((learners, rows), 0) == assign, length, 0.0)
    summed = jnp.sum(total, axis=1, keepdims=True)
    out[...] = jnp.broadcast_to(1.0 / (learners * summed), out.shape)


def weights_of(slots, learners, sides):
    return pl.pallas_call(
        functools.partial(weight_kernel, slots),
        out_shape=jax.ShapeDtypeStruct((learners, 128), F32),
        in_specs=[VMEM],
        out_specs=VMEM,
        compiler_params=PARAMS,
        name="weights",
    )(sides)


def learner_kernel(slots, nact, frames, sides, weights, embed, head, head_t, grads, hidden, logits_t, grad_t):
    blocks, rows = frames.shape[0], frames.shape[1]
    feats, width = embed.shape
    total = blocks * rows

    def forward(index, carry):
        here = pl.ds(pl.multiple_of(index * rows, rows), rows)
        hid = jnp.maximum(mm(frames[index], embed[...]), 0.0).astype(BF16)
        hidden[here, :] = hid
        logits_t[index] = mm(hid, head[...]).T
        return carry

    lax.fori_loop(0, blocks, forward, 0)

    def vtrace(index, carry):
        side = sides[index]
        logits = logits_t[index, 0:nact, :]
        values = logits_t[index, nact : nact + 1, :]
        behave = side[BEHAVE : BEHAVE + 1, :]
        reward = side[REWARD : REWARD + 1, :]
        length = side[LENGTH : LENGTH + 1, :].astype(jnp.int32)
        assign = side[ASSIGN : ASSIGN + 1, :].astype(jnp.int32)
        action = side[ACTION : ACTION + 1, :].astype(jnp.int32)
        learners = weights.shape[0]
        weight = jnp.sum(
            jnp.where(iota((learners, rows), 0) == assign, weights[:, 0:1], 0.0),
            axis=0, keepdims=True,
        )
        top = jnp.max(logits, axis=0, keepdims=True)
        exps = jnp.exp(logits - top)
        norm = jnp.sum(exps, axis=0, keepdims=True)
        logprob = logits - (top + jnp.log(norm))
        probs = exps * (1.0 / norm)
        onehot = iota(logits.shape, 0) == action
        taken = jnp.sum(jnp.where(onehot, logprob, 0.0), axis=0, keepdims=True)
        entropy = -jnp.sum(probs * logprob, axis=0, keepdims=True)
        step = lax.rem(iota((1, rows), 1), slots)
        inside = (step < length).astype(F32)
        beyond = (step + 1 < length).astype(F32)
        ratios = jnp.minimum(1.0, jnp.exp(taken - behave))

        def later(series, by):
            return pltpu.roll(series, rows - by, 1)

        deltas = inside * ratios * (reward + GAMMA * later(values, 1) * beyond - values)
        decay = GAMMA * ratios * inside
        corrections = deltas
        reach = 1
        while reach < slots:
            within = step + reach < slots
            corrections = corrections + decay * jnp.where(within, later(corrections, reach), 0.0)
            decay = decay * jnp.where(within, later(decay, reach), 0.0)
            reach *= 2
        targets = values + corrections
        advantage = ratios * (reward + GAMMA * later(targets, 1) * beyond - values)
        scale = weight * inside
        grad = scale * (
            -advantage * (onehot.astype(F32) - probs) + ENTROPY_COEF * probs * (logprob + entropy)
        )
        pad = jnp.zeros((head_t.shape[0] - nact - 1, rows), F32)
        grad_t[index] = jnp.concatenate([grad, scale * (values - targets), pad], axis=0)
        return carry

    lax.fori_loop(0, blocks, vtrace, 0)
    grads[...] = jnp.zeros_like(grads)

    def backward(index, carry):
        here = pl.ds(pl.multiple_of(index * rows, rows), rows)
        hid = hidden[here, :]
        wide_t = grad_t[index]
        back = mm(wide_t.T.astype(BF16), head_t[...])
        grad_preact = jnp.where(hid.astype(F32) > 0.0, back, 0.0).astype(BF16)
        grads[0:feats, :] += lax.dot_general(
            frames[index], grad_preact, (((0,), (0,)), ((), ())), preferred_element_type=F32
        )
        tail = grads.shape[0] - feats
        grads[feats:, :] += mm(wide_t[0:tail, :].astype(BF16), hid)
        return carry

    lax.fori_loop(0, blocks, backward, 0)


def learner(slots, nact, frames, sides, weights, embed, head, head_t):
    blocks, rows = frames.shape[0], frames.shape[1]
    feats, width = embed.shape
    wide = head.shape[1]
    return pl.pallas_call(
        functools.partial(learner_kernel, slots, nact),
        out_shape=jax.ShapeDtypeStruct((feats + nact + 16, width), F32),
        in_specs=[VMEM] * 6,
        out_specs=VMEM,
        scratch_shapes=[
            pltpu.VMEM((blocks * rows, width), BF16),
            pltpu.VMEM((blocks, wide, rows), F32),
            pltpu.VMEM((blocks, wide, rows), F32),
        ],
        compiler_params=PARAMS,
        name="learner",
    )(frames, sides, weights, embed, head, head_t)


def update_kernel(
    feats, nact, mine, theirs, master_embed, master_policy, master_value,
    embed_moment, policy_moment, value_moment, next_obs,
    next_logits, new_embed, new_policy, new_value, new_em, new_pm, new_vm,
):
    def step(grad, moment, master, new_moment, new_master):
        held = MOMENTUM * moment[...] + grad
        new_moment[...] = held
        fresh = master[...] - LEARN_RATE * held
        new_master[...] = fresh
        return fresh

    def grad(start, size):
        return mine[start : start + size, :].astype(F32) + theirs[start : start + size, :].astype(F32)

    embed = step(grad(0, feats), embed_moment, master_embed, new_em, new_embed)
    hidden = jnp.maximum(mm(next_obs[...], embed.astype(BF16)), 0.0).astype(BF16)
    policy = step(grad(feats, nact).T, policy_moment, master_policy, new_pm, new_policy)
    step(grad(feats + nact, 16)[0:1, :], value_moment, master_value, new_vm, new_value)
    next_logits[...] = mm(hidden, policy.astype(BF16)).astype(BF16)


def update(mine, theirs, *args):
    embed, policy, value = args[0], args[1], args[2]
    next_obs = args[6]
    feats, nact = embed.shape[0], policy.shape[1]
    shapes = [jax.ShapeDtypeStruct(array.shape, F32) for array in (embed, policy, value)]
    return pl.pallas_call(
        functools.partial(update_kernel, feats, nact),
        out_shape=(jax.ShapeDtypeStruct((next_obs.shape[0], nact), BF16), *shapes, *shapes),
        in_specs=[VMEM] * 9,
        out_specs=(VMEM,) * 7,
        compiler_params=PARAMS,
        name="update",
    )(mine, theirs, *args)


def body(
    n_hst, n_cores, observations, lengths, actions, rewards, assign, actor_embed, actor_policy,
    master_embed, master_policy, master_value, embed_moment, policy_moment, value_moment, next_obs,
):
    traj, slots, feats = observations.shape
    nact = master_policy.shape[1]
    learners = n_hst * n_cores
    rows = traj * slots
    own = observations.reshape(rows, feats)
    value_row = master_value.reshape(1, -1)
    gather = n_hst <= 8
    if gather:
        frames = lax.all_gather(own, "hst")
    else:
        frames = own[None]
    side, embed, head, head_t = actor(
        slots, own, lengths.reshape(1, -1), assign.reshape(1, -1), actions, rewards,
        actor_embed, actor_policy, master_embed, master_policy, value_row,
    )
    if gather:
        sides = lax.all_gather(side, AXES)
        weights = weights_of(slots, learners, sides)
        core = lax.axis_index("cores")
        ours = lax.dynamic_index_in_dim(
            sides.reshape(n_hst, n_cores, *side.shape), core, axis=1, keepdims=False
        )
    else:
        named = (assign[:, None] == jnp.arange(learners)[None, :]).astype(F32)
        totals = lax.psum(jnp.sum(named * lengths[:, None].astype(F32), axis=0), AXES)
        weights = jnp.broadcast_to((1.0 / (learners * totals))[:, None], (learners, 128))
        ours = side[None]
    grads = learner(slots, nact, frames, ours, weights, embed, head, head_t)
    if gather:
        mine = grads.astype(BF16)
        theirs = lax.ppermute(mine, "cores", [(i, i ^ 1) for i in range(n_cores)])
    else:
        mine = lax.psum(grads, AXES)
        theirs = jnp.zeros_like(mine)
    outs = update(
        mine, theirs, master_embed, master_policy, value_row, embed_moment, policy_moment,
        value_moment.reshape(1, -1), next_obs,
    )
    logits, new_embed, new_policy, new_value, new_em, new_pm, new_vm = outs
    return logits, new_embed, new_policy, new_value.reshape(-1), new_em, new_pm, new_vm.reshape(-1)


def solution(mesh):
    split = P(("group", "hst", "cores"))
    whole = P("group")
    return jax.shard_map(
        functools.partial(body, mesh.shape["hst"], mesh.shape["cores"]),
        mesh=mesh,
        in_specs=(split,) * 5 + (whole,) * 8 + (split,),
        out_specs=(split,) + (whole,) * 6,
        check_vma=False,
    )
```

time: 251 us -> 102 us (0.41); the launches traced: 249 us -> 102 us
  waiting for transfers between devices: 82.8 us -> 25.6 us
  other arithmetic: 42.1 us -> 1.96 us
  local copies, waits for them, and re-layouts: 39.8 us -> 2.58 us
  Pallas kernels: 0 us -> 32.9 us
  starting transfers between devices: 24.5 us -> 0.11 us
  matrix products: 12.3 us -> 0 us
  blocking collectives: 32.1 us -> 25.1 us
    psum x1 -> x0, waiting for transfers between devices: 66.3 us -> none  [body(): lax.psum((grads[0], grads[1], grads[2]), ('hst', 'cores'))]
    pallas_call x0 -> x4, Pallas kernels: none -> 32.9 us  [the longest x1 20.5 us: learner(): pl.pallas_call(functools.partial(learner_kernel, slots, nact), out_shape=...]
    psum x1 -> x0, blocking collectives: 32.1 us -> none  [body(): lax.psum((grads[0], grads[1], grads[2]), ('hst', 'cores'))]
    all_gather x0 -> x1, blocking collectives: none -> 25.1 us  [body(): sides = lax.all_gather(side, AXES)]
    all_to_all x5 -> x0, starting transfers between devices: 24.5 us -> none  [the longest x1 7.39 us: body(): lax.all_to_all(grouped(lengths).astype(jnp.float32), ('hst', 'cores'), sp...]
    all_gather x0 -> x1, waiting for transfers between devices: none -> 21.8 us  [body(): frames = lax.all_gather(own, 'hst')]
    dynamic_update_slice x16 -> x0, local copies, waits for them, and re-layouts: 20.6 us -> none  [learner_grads(): lax.scan(backward_step, jnp.zeros((traj_count,), jnp.float32), (deltas.T,...]
    mul x16 -> x0, other arithmetic: 19.9 us -> none  [backward_step(): carry_sum = inside_now * (delta_now + GAMMA * ratio_now * carry_sum)]
  transfers between devices with their start and end apart: 6 -> 2, of which waited for: 5 -> 2; matrix products, arithmetic and copies ran while one was open for 9% -> 1% of each run, Pallas kernels for 0% -> 6%
where the time goes in v1:
time: 102 us
  Pallas kernels  32.9 us (32%)
  waiting for transfers between devices  25.6 us (25%)
  blocking collectives  25.1 us (25%)
  between operations  14.1 us (14%)
  local copies, waits for them, and re-layouts  2.58 us (3%)
  other arithmetic  1.96 us (2%)
    all_gather x1, blocking collectives, body(): sides = lax.all_gather(side, AXES)  25.1 us
    all_gather x1, waiting for transfers between devices, body(): frames = lax.all_gather(own, 'hst')  21.8 us
    pallas_call x1, Pallas kernels, learner(): pl.pallas_call(functools.partial(learner_kernel, slots, nact), out_shape=...  20.5 us
    pallas_call x1, Pallas kernels, update(): pl.pallas_call(functools.partial(update_kernel, feats, nact), out_shape=(...  6.35 us
    pallas_call x1, Pallas kernels, actor(): pl.pallas_call(actor_kernel, out_shape=(jax.ShapeDtypeStruct((8, obs.shap...  4.39 us
    ppermute x1, waiting for transfers between devices, body(): theirs = lax.ppermute(mine, 'cores', [(i, i ^ 1) for i in range(n_cores)])  3.07 us
  transfers between devices with their start and end apart: 2, of which 2 were waited for; matrix products, arithmetic and copies ran while one was open for 1% of the time, Pallas kernels for 6%

profile of v1, /device:TPU:0, one launch (start us, length us, event | category | flops | bytes accessed | tf_op | source)
XLA Modules:
  0.0 102.3 jit_solution(10247131220880175296)
XLA Ops:
  7.2 0.0 all-gather.3.cloned.1.call-start
  7.2 0.7 all-gather.3.cloned.1.call-update
  7.9 4.4 %actor.1 = (f32[8,256]{1,0:T(8,128)}, bf16[512,1024]{1,0:T(8,128)(2,1)}, bf16[1024,256]{1,0:T(8,128)(2,1)}, bf16[256,1024]{1,0:T(8,128)(2,1)}) custom-call(bf16[256,512]{1,0:T(8,128)(2,1)} %bitcast.15, s32[1,16]{1,0:T(1,128)} %bitcast.21, s32[1,16]{1,0:T(1,128)} %bitcast.22, s32[16,16]{1,0:T(8,128)} %actions.1, f32[16,16]{1,0:T(8,128)} %rewards.1, ...), custom_call_target="tpu_custom_call" | custom-call | tf_op jit(solution)/shard_map/actor/pallas_call | solution.py:81
  12.3 25.1 %all-gather = f32[128,256]{1,0:T(8,128)} all-gather(f32[8,256]{1,0:T(8,128)} %get-tuple-element.18), channel_id=2, replica_groups=mesh['group'=2,'hst'=8,'cores'=2] {'hst','cores'}, dimensions={0}, use_global_device_ids=true | all-gather | bytes 139264 | tf_op jit(solution)/shard_map/all_gather | solution.py:278
  37.4 1.6 %weights.1 = f32[16,128]{1,0:T(8,128)} custom-call(f32[16,8,256]{2,1,0:T(8,128)} %bitcast.16), custom_call_target="tpu_custom_call" | custom-call | tf_op jit(solution)/shard_map/weights/pallas_call | solution.py:110
  39.0 1.5 %dynamic-slice_bitcast_fusion.sides = f32[8,8,256]{2,1,0:T(8,128)} fusion(f32[8,2,8,256]{3,2,1,0:T(8,128)} %bitcast.17, s32[]{:T(128)S(6)} %select_n.4), kind=kLoop, calls=%fused_computation | loop fusion | bytes 131076 | tf_op jit(solution)/shard_map/jit(dynamic_index_in_dim)/squeeze | solution.py:281
  40.5 21.8 %all-gather.3.cloned.1.call-done.frames = bf16[8,256,512]{2,1,0:T(8,128)(2,1)} async-done(((bf16[1,256,512]{2,1,0:T(8,128)(2,1)}), bf16[8,256,512]{2,1,0:T(8,128)(2,1)}) %all-gather.3.cloned.1.call-update) | async-done | bytes 2097168 | tf_op jit(solution)/shard_map/all_gather | solution.py:270
  62.4 20.5 %learner.1 = f32[656,1024]{1,0:T(8,128)} custom-call(bf16[8,256,512]{2,1,0:T(8,128)(2,1)} %all-gather.3.cloned.1.call-done.frames, f32[8,8,256]{2,1,0:T(8,128)} %dynamic-slice_bitcast_fusion.sides, f32[16,128]{1,0:T(8,128)} %weights.1, bf16[512,1024]{1,0:T(8,128)(2,1)} %get-tuple-element.19.embed, bf16[1024,256]{1,0:T(8,128)(2,1)} %get-tuple-element.20.head, ...), custom_call_target="tpu_custom_call" | custom-call | tf_op jit(solution)/shard_map/learner/pallas_call | solution.py:206
  82.9 2.0 %convert_element_type.3.mine = bf16[656,1024]{1,0:T(8,128)(2,1)S(1)} convert(f32[656,1024]{1,0:T(8,128)} %learner.1) | non-fusion elementwise | flops 671744 | bytes 4030464 | tf_op jit(solution)/shard_map/convert_element_type | solution.py:291
  84.8 0.0 copy-start
  84.8 0.1 collective-permute-start
  84.9 3.1 %collective-permute-done.theirs = bf16[656,1024]{1,0:T(8,128)(2,1)S(1)} collective-permute-done((bf16[656,1024]{1,0:T(8,128)(2,1)S(1)}, bf16[656,1024]{1,0:T(8,128)(2,1)S(1)}, u32[]{:S(2)}, u32[]{:S(2)}) %collective-permute-start) | collective-permute-done | bytes 1343520 | tf_op jit(solution)/shard_map/ppermute | solution.py:292
  88.0 0.0 copy-start.1
  88.0 0.0 copy-done
  88.0 1.1 %copy-done.1 = bf16[656,1024]{1,0:T(8,128)(2,1)} copy-done((bf16[656,1024]{1,0:T(8,128)(2,1)}, bf16[656,1024]{1,0:T(8,128)(2,1)S(1)}, u32[]{:S(2)}) %copy-start.1) | copy-done | bytes 1343512
  89.1 6.4 %update.1 = (bf16[256,128]{1,0:T(8,128)(2,1)}, f32[512,1024]{1,0:T(8,128)}, f32[1024,128]{1,0:T(8,128)}, f32[1,1024]{1,0:T(1,128)}, f32[512,1024]{1,0:T(8,128)}, /*index=5*/f32[1024,128]{1,0:T(8,128)}, f32[1,1024]{1,0:T(1,128)}) custom-call(bf16[656,1024]{1,0:T(8,128)(2,1)} %copy-done, bf16[656,1024]{1,0:T(8,128)(2,1)} %copy-done.1, ...), custom_call_target="tpu_custom_call" | custom-call | tf_op jit(solution)/shard_map/update/pallas_call | solution.py:248
Async XLA Ops:
  7.2 55.2 %all-gather.3.cloned.1.call-start = ((), (), s32[]{:S(2)}) async-start(), calls=%async_computation | async-start | bytes 2359296 | tf_op jit(solution)/shard_map/all_gather | solution.py:270
  84.8 3.2 %copy-start = (bf16[656,1024]{1,0:T(8,128)(2,1)}, bf16[656,1024]{1,0:T(8,128)(2,1)S(1)}, u32[]{:S(2)}) copy-start(bf16[656,1024]{1,0:T(8,128)(2,1)S(1)} %convert_element_type.3.mine) | copy-start | bytes 4030468
  84.8 3.1 %collective-permute-start = (bf16[656,1024]{1,0:T(8,128)(2,1)S(1)}, bf16[656,1024]{1,0:T(8,128)(2,1)S(1)}, u32[]{:S(2)}, u32[]{:S(2)}) collective-permute-start(bf16[656,1024]{1,0:T(8,128)(2,1)S(1)} %convert_element_type.3.mine), channel_id=1, source_target_pairs={{0,1},{1,0},{2,3},{3,2},{4,5},{5,4},{6,7},{7,6},{8,9},{9,8},{10,11... | collective-permute-start | bytes 4030472 | tf_op jit(solution)/shard_map/ppermute | solution.py:292
  88.0 1.1 %copy-start.1 = (bf16[656,1024]{1,0:T(8,128)(2,1)}, bf16[656,1024]{1,0:T(8,128)(2,1)S(1)}, u32[]{:S(2)}) copy-start(bf16[656,1024]{1,0:T(8,128)(2,1)S(1)} %collective-permute-done.theirs) | copy-start | bytes 4030468
Sparse Core Ops, SparseCore 0:
  10.1 52.2 all-gather.2

commit v2 on v1

v2 whole, which is shorter than its diff:
```python
import functools

import jax
import jax.numpy as jnp
from jax import lax
from jax.experimental import pallas as pl
from jax.experimental.pallas import tpu as pltpu
from jax.sharding import PartitionSpec as P

GAMMA = 0.99
ENTROPY_COEF = 0.1
MOMENTUM = 0.9
LEARN_RATE = 0.05
AXES = ("hst", "cores")
F32 = jnp.float32
BF16 = jnp.bfloat16
VMEM = pl.BlockSpec(memory_space=pltpu.VMEM)
MIB = 2**20
BLOCK = 256
PAD = 16
BEHAVE, ACTION, REWARD, LENGTH, ASSIGN = range(5)


def iota(shape, dim):
    return lax.broadcasted_iota(jnp.int32, shape, dim)


def mm(a, b):
    return jnp.dot(a, b, preferred_element_type=F32)


def mm_nt(a, b):
    return lax.dot_general(a, b, (((1,), (1,)), ((), ())), preferred_element_type=F32)


def params(mib):
    return pltpu.CompilerParams(vmem_limit_bytes=mib * MIB)


def actor_kernel(obs, lengths, assign, actions, rewards, actor_embed, actor_policy, side):
    rows = obs.shape[0]
    traj, slots = actions.shape
    spread = (lax.rem(iota((slots, rows), 1), slots) == iota((slots, rows), 0)).astype(F32)
    owner = lax.div(iota((traj, rows), 1), slots) == iota((traj, rows), 0)

    def flat(series):
        wide = jnp.dot(series, spread, precision=lax.Precision.HIGHEST, preferred_element_type=F32)
        return jnp.sum(jnp.where(owner, wide, 0.0), axis=0, keepdims=True)

    def repeat(series):
        return jnp.dot(
            series.astype(F32), owner.astype(F32),
            precision=lax.Precision.HIGHEST, preferred_element_type=F32,
        )

    action = flat(actions[...].astype(F32))
    hidden = jnp.maximum(mm(obs[...], actor_embed[...]), 0.0).astype(BF16)
    logits = mm(hidden, actor_policy[...]).T
    top = jnp.max(logits, axis=0, keepdims=True)
    shifted = logits - top
    norm = jnp.log(jnp.sum(jnp.exp(shifted), axis=0, keepdims=True))
    onehot = iota(logits.shape, 0) == action.astype(jnp.int32)
    side[...] = jnp.zeros_like(side)
    side[BEHAVE : BEHAVE + 1, :] = (
        jnp.sum(jnp.where(onehot, shifted, 0.0), axis=0, keepdims=True) - norm
    )
    side[ACTION : ACTION + 1, :] = action
    side[REWARD : REWARD + 1, :] = flat(rewards[...])
    side[LENGTH : LENGTH + 1, :] = repeat(lengths[...])
    side[ASSIGN : ASSIGN + 1, :] = repeat(assign[...])


def actor(obs, *args):
    return pl.pallas_call(
        actor_kernel,
        out_shape=jax.ShapeDtypeStruct((8, obs.shape[0]), F32),
        in_specs=[VMEM] * 7,
        out_specs=VMEM,
        compiler_params=params(12),
        name="actor",
    )(obs, *args)


def prepare_kernel(master_embed, master_policy, master_value, embed_t, head, head_t):
    embed_t[...] = master_embed[...].T.astype(BF16)
    nact = master_policy.shape[1]
    wide = jnp.concatenate(
        [
            master_policy[...].T,
            master_value[...],
            jnp.zeros((PAD - 1, head_t.shape[1]), F32),
        ],
        axis=0,
    )
    head_t[...] = wide.astype(BF16)
    head[:, 0:nact] = master_policy[...].astype(BF16)
    head[:, nact:] = wide[nact:, :].T.astype(BF16)


def prepare(master_embed, master_policy, master_value):
    feats, width = master_embed.shape
    nact = master_policy.shape[1]
    return pl.pallas_call(
        prepare_kernel,
        out_shape=(
            jax.ShapeDtypeStruct((width, feats), BF16),
            jax.ShapeDtypeStruct((width, nact + PAD), BF16),
            jax.ShapeDtypeStruct((nact + PAD, width), BF16),
        ),
        in_specs=[VMEM] * 3,
        out_specs=(VMEM,) * 3,
        compiler_params=params(12),
        name="prepare",
    )(master_embed, master_policy, master_value)


def learner_weights(slots, sides, out):
    learners, rows = out.shape[0], sides[0].shape[1]
    total = jnp.zeros((learners, rows), F32)
    first = lax.rem(iota((1, rows), 1), slots) == 0
    for side in sides:
        assign = side[ASSIGN : ASSIGN + 1, :].astype(jnp.int32)
        length = jnp.where(first, side[LENGTH : LENGTH + 1, :], 0.0)
        total = total + jnp.where(iota((learners, rows), 0) == assign, length, 0.0)
    summed = jnp.sum(total, axis=1, keepdims=True)
    out[...] = jnp.broadcast_to(1.0 / (learners * summed), out.shape)


def vtrace(slots, nact, side, weights, logits, values):
    rows = logits.shape[1]
    learners = weights.shape[0]
    behave = side[BEHAVE : BEHAVE + 1, :]
    reward = side[REWARD : REWARD + 1, :]
    length = side[LENGTH : LENGTH + 1, :].astype(jnp.int32)
    assign = side[ASSIGN : ASSIGN + 1, :].astype(jnp.int32)
    action = side[ACTION : ACTION + 1, :].astype(jnp.int32)
    weight = jnp.sum(
        jnp.where(iota((learners, rows), 0) == assign, weights[:, 0:1], 0.0), axis=0, keepdims=True
    )
    top = jnp.max(logits, axis=0, keepdims=True)
    exps = jnp.exp(logits - top)
    norm = jnp.sum(exps, axis=0, keepdims=True)
    logprob = logits - (top + jnp.log(norm))
    probs = exps * (1.0 / norm)
    onehot = iota(logits.shape, 0) == action
    taken = jnp.sum(jnp.where(onehot, logprob, 0.0), axis=0, keepdims=True)
    entropy = -jnp.sum(probs * logprob, axis=0, keepdims=True)
    step = lax.rem(iota((1, rows), 1), slots)
    inside = (step < length).astype(F32)
    beyond = (step + 1 < length).astype(F32)
    ratios = jnp.minimum(1.0, jnp.exp(taken - behave))

    def later(series, by):
        return pltpu.roll(series, rows - by, 1)

    deltas = inside * ratios * (reward + GAMMA * later(values, 1) * beyond - values)
    decay = GAMMA * ratios * inside
    corrections = deltas
    reach = 1
    while reach < slots:
        within = step + reach < slots
        corrections = corrections + decay * jnp.where(within, later(corrections, reach), 0.0)
        decay = decay * jnp.where(within, later(decay, reach), 0.0)
        reach *= 2
    targets = values + corrections
    advantage = ratios * (reward + GAMMA * later(targets, 1) * beyond - values)
    scale = weight * inside
    grad = scale * (
        -advantage * (onehot.astype(F32) - probs) + ENTROPY_COEF * probs * (logprob + entropy)
    )
    return grad, scale * (values - targets)


def work(slots, frames, side, weights, embed_t, head, head_t, frames_t, hidden_t, preact_t, add):
    width, feats = embed_t.shape
    nact = head_t.shape[0] - PAD
    tile = 256
    for index, block in enumerate(frames):
        frames_t[:, index * BLOCK : (index + 1) * BLOCK] = block.T
    for start in range(0, width, tile):
        here = slice(start, start + tile)
        hidden_t[here, :] = jnp.maximum(mm(embed_t[here, :], frames_t[...]), 0.0).astype(BF16)
    logits = mm(head_t[...], hidden_t[...])
    grad, grad_values = vtrace(
        slots, nact, side, weights, logits[0:nact, :], logits[nact : nact + 1, :]
    )
    pad = jnp.zeros((PAD - 1, grad.shape[1]), F32)
    grad_t = jnp.concatenate([grad, grad_values, pad], axis=0).astype(BF16)
    for start in range(0, width, tile):
        here = slice(start, start + tile)
        back = mm(head[here, :], grad_t)
        alive = hidden_t[here, :].astype(F32) > 0.0
        preact_t[here, :] = jnp.where(alive, back, 0.0).astype(BF16)
    for index in range(len(frames)):
        lanes = slice(index * BLOCK, (index + 1) * BLOCK)
        add(index, slice(0, feats), mm_nt(frames_t[:, lanes], preact_t[:, lanes]))
        add(index, slice(feats, feats + nact + PAD), mm_nt(grad_t[:, lanes], hidden_t[:, lanes]))


def on_mid():
    line = lax.div(lax.axis_index("hst"), 2)
    return jnp.logical_or(line == 1, line == 2)


def choose(mid, end):
    return jnp.where(on_mid(), mid[...], end[...])


def first_kernel(slots, *refs):
    (own, pair, near, *sides), (embed_t, head, head_t), (out, other, weights), scratch = (
        refs[0:19], refs[19:22], refs[22:25], refs[25:28])
    learner_weights(slots, sides, weights)
    outs = (out, out, other)

    def add(index, rows, value):
        if index == 1:
            outs[index][rows, :] += value
        else:
            outs[index][rows, :] = value

    side = jnp.concatenate([sides[0][...], sides[2][...], sides[4][...]], axis=1)
    work(slots, (own[...], pair[...], near[...]), side, weights, embed_t, head, head_t, *scratch, add)


def second_kernel(slots, *refs):
    (cross, mid, end, side_cross, side_mid, side_end, weights, partial, other) = refs[0:9]
    (embed_t, head, head_t), (out, far), scratch = refs[9:12], refs[12:14], refs[14:17]

    def add(index, rows, value):
        if index == 0:
            out[rows, :] = partial[rows, :] + (other[rows, :] + value)
        else:
            far[rows, :] = value

    side = jnp.concatenate([side_cross[...], choose(side_mid, side_end)], axis=1)
    work(
        slots, (cross[...], mid[...] + end[...]), side, weights, embed_t, head, head_t, *scratch, add
    )


def third_kernel(slots, *refs):
    (mid_a, end_a, mid_b, end_b, smid_a, send_a, smid_b, send_b, weights, far) = refs[0:10]
    (embed_t, head, head_t), (out, last), scratch = refs[10:13], refs[13:15], refs[15:18]

    def add(index, rows, value):
        if index == 0:
            out[rows, :] = far[rows, :] + value
        else:
            last[rows, :] = value

    side = jnp.concatenate([choose(smid_a, send_a), choose(smid_b, send_b)], axis=1)
    work(
        slots, (mid_a[...] + end_a[...], mid_b[...] + end_b[...]), side, weights,
        embed_t, head, head_t, *scratch, add,
    )


def fourth_kernel(slots, *refs):
    (mid, end, side_mid, side_end, weights, half, far, last) = refs[0:8]
    (embed_t, head, head_t), out, scratch = refs[8:11], refs[11], refs[12:15]

    def add(index, rows, value):
        out[rows, :] = (half[rows, :] + (far[rows, :] + (last[rows, :] + value))).astype(BF16)

    work(
        slots, (mid[...] + end[...],), choose(side_mid, side_end), weights,
        embed_t, head, head_t, *scratch, add,
    )


def local_kernel(slots, frames, side, weights, embed_t, head, head_t, out, *scratch):
    def add(index, rows, value):
        if index == 0:
            out[rows, :] = value
        else:
            out[rows, :] += value

    blocks = [frames[index] for index in range(frames.shape[0])]
    work(slots, blocks, side, weights, embed_t, head, head_t, *scratch, add)


def call(kernel, name, slots, blocks, args, mats, outs):
    width, feats = mats[0].shape
    rows = blocks * BLOCK
    return pl.pallas_call(
        functools.partial(kernel, slots),
        out_shape=outs,
        in_specs=[VMEM] * (len(args) + 3),
        out_specs=jax.tree.map(lambda leaf: VMEM, outs),
        scratch_shapes=[
            pltpu.VMEM((feats, rows), BF16),
            pltpu.VMEM((width, rows), BF16),
            pltpu.VMEM((width, rows), BF16),
        ],
        compiler_params=params(32),
        name=name,
    )(*args, *mats)


def update_kernel(
    feats, nact, mine, theirs, master_embed, master_policy, master_value,
    embed_moment, policy_moment, value_moment, next_obs,
    next_logits, new_embed, new_policy, new_value, new_em, new_pm, new_vm,
):
    def step(grad, moment, master, new_moment, new_master):
        held = MOMENTUM * moment[...] + grad
        new_moment[...] = held
        fresh = master[...] - LEARN_RATE * held
        new_master[...] = fresh
        return fresh

    def grad(start, size):
        return mine[start : start + size, :].astype(F32) + theirs[start : start + size, :].astype(F32)

    embed = step(grad(0, feats), embed_moment, master_embed, new_em, new_embed)
    hidden = jnp.maximum(mm(next_obs[...], embed.astype(BF16)), 0.0).astype(BF16)
    policy = step(grad(feats, nact).T, policy_moment, master_policy, new_pm, new_policy)
    step(grad(feats + nact, PAD)[0:1, :], value_moment, master_value, new_vm, new_value)
    next_logits[...] = mm(hidden, policy.astype(BF16)).astype(BF16)


def update(mine, theirs, *args):
    embed, policy, value = args[0], args[1], args[2]
    next_obs = args[6]
    feats, nact = embed.shape[0], policy.shape[1]
    shapes = [jax.ShapeDtypeStruct(array.shape, F32) for array in (embed, policy, value)]
    return pl.pallas_call(
        functools.partial(update_kernel, feats, nact),
        out_shape=(jax.ShapeDtypeStruct((next_obs.shape[0], nact), BF16), *shapes, *shapes),
        in_specs=[VMEM] * 9,
        out_specs=(VMEM,) * 7,
        compiler_params=params(32),
        name="update",
    )(mine, theirs, *args)


def gathered_grads(slots, n_cores, own, side, mats):
    flip = [(place, place ^ 1) for place in range(8)]
    ends = [pair for pair in flip if pair[0] in (0, 1, 6, 7)]
    mids = [pair for pair in flip if pair[0] in (2, 3, 4, 5)]
    near = [(place, place ^ 2) for place in range(8)]
    inner = [(2, 4), (3, 5), (4, 2), (5, 3)]
    outer = [(2, 0), (3, 1), (4, 6), (5, 7)]

    def send(array, pairs):
        return lax.ppermute(array, "hst", pairs)

    pair = send(own, flip)
    close = send(own, near)
    second_mid = send(own, inner)
    sides = [side] + [
        lax.ppermute(side, AXES, [(place, place ^ mask) for place in range(8 * n_cores)])
        for mask in range(1, 8 * n_cores)
    ]
    cross = send(close, flip)
    second_end = send(second_mid, outer)
    third_mid = send(close, inner)
    second_mid_y = send(second_mid, mids)
    second_end_y = send(second_end, ends)
    third_end = send(third_mid, outer)
    third_mid_y = send(third_mid, mids)
    third_end_y = send(third_end, ends)

    width, feats = mats[0].shape
    grads = jax.ShapeDtypeStruct((feats + mats[2].shape[0], width), F32)
    weights = jax.ShapeDtypeStruct((8 * n_cores, 128), F32)
    by = [sides[n_cores * mask] for mask in range(8)]
    partial, other, weights = call(
        first_kernel, "first", slots, 3, (own, pair, close, *sides), mats, (grads, grads, weights)
    )
    half, far = call(
        second_kernel, "second", slots, 2,
        (cross, second_mid, second_end, by[3], by[6], by[4], weights, partial, other), mats,
        (grads, grads),
    )
    far, last = call(
        third_kernel, "third", slots, 2,
        (second_mid_y, second_end_y, third_mid, third_end, by[7], by[5], by[4], by[6], weights, far),
        mats, (grads, grads),
    )
    return call(
        fourth_kernel, "fourth", slots, 1,
        (third_mid_y, third_end_y, by[5], by[7], weights, half, far, last), mats,
        jax.ShapeDtypeStruct(grads.shape, BF16),
    )


def body(
    n_hst, n_cores, observations, lengths, actions, rewards, assign, actor_embed, actor_policy,
    master_embed, master_policy, master_value, embed_moment, policy_moment, value_moment, next_obs,
):
    traj, slots, feats = observations.shape
    learners = n_hst * n_cores
    rows = traj * slots
    own = observations.reshape(rows, feats)
    value_row = master_value.reshape(1, -1)
    side = actor(
        own, lengths.reshape(1, -1), assign.reshape(1, -1), actions, rewards,
        actor_embed, actor_policy,
    )
    mats = prepare(master_embed, master_policy, value_row)
    if n_hst == 8 and n_cores == 2 and rows == BLOCK:
        mine = gathered_grads(slots, n_cores, own, side, mats)
        theirs = lax.ppermute(mine, "cores", [(0, 1), (1, 0)])
    else:
        named = (assign[:, None] == jnp.arange(learners)[None, :]).astype(F32)
        totals = lax.psum(jnp.sum(named * lengths[:, None].astype(F32), axis=0), AXES)
        weights = jnp.broadcast_to((1.0 / (learners * totals))[:, None], (learners, 128))
        grads = call(
            local_kernel, "local", slots, rows // BLOCK,
            (own.reshape(-1, BLOCK, feats), side, weights), mats,
            jax.ShapeDtypeStruct((feats + mats[2].shape[0], mats[0].shape[0]), F32),
        )
        mine = lax.psum(grads, AXES)
        theirs = jnp.zeros_like(mine)
    outs = update(
        mine, theirs, master_embed, master_policy, value_row, embed_moment, policy_moment,
        value_moment.reshape(1, -1), next_obs,
    )
    logits, new_embed, new_policy, new_value, new_em, new_pm, new_vm = outs
    return logits, new_embed, new_policy, new_value.reshape(-1), new_em, new_pm, new_vm.reshape(-1)


def solution(mesh):
    split = P(("group", "hst", "cores"))
    whole = P("group")
    return jax.shard_map(
        functools.partial(body, mesh.shape["hst"], mesh.shape["cores"]),
        mesh=mesh,
        in_specs=(split,) * 5 + (whole,) * 8 + (split,),
        out_specs=(split,) + (whole,) * 6,
        check_vma=False,
    )
```

time: 102 us -> 94.7 us (0.928)
  starting transfers between devices: 0.11 us -> 46.4 us
  blocking collectives: 25.1 us -> 0 us
  Pallas kernels: 32.9 us -> 16.5 us
  between operations: 14.1 us -> 0.93 us
  local copies, waits for them, and re-layouts: 2.58 us -> 9.18 us
  waiting for transfers between devices: 25.6 us -> 21.1 us
  other arithmetic: 1.96 us -> 0 us
    ppermute x1 -> x27, starting transfers between devices: 0.07 us -> 46.4 us  [the longest x15 29.2 us: gathered_grads(): lax.ppermute(side, AXES, [(place, place ^ mask) for place in range(8 * n_...]
    all_gather x1 -> x0, blocking collectives: 25.1 us -> none  [body(): sides = lax.all_gather(side, AXES)]
    all_gather x1 -> x0, waiting for transfers between devices: 21.8 us -> none  [body(): frames = lax.all_gather(own, 'hst')]
    ppermute x1 -> x27, waiting for transfers between devices: 3.07 us -> 21.1 us  [the longest x15 12.2 us: gathered_grads(): lax.ppermute(side, AXES, [(place, place ^ mask) for place in range(8 * n_...]
    pallas_call x3 -> x6, Pallas kernels: 26.5 us -> 13.1 us  [the longest x4 11.9 us: call(): pl.pallas_call(functools.partial(kernel, slots), out_shape=outs, in_specs...]
    unnamed x4 -> x36, local copies, waits for them, and re-layouts: 1.07 us -> 9.18 us
    pallas_call x1, Pallas kernels: 6.35 us -> 3.41 us  [update(): pl.pallas_call(functools.partial(update_kernel, feats, nact), out_shape=(...]
    convert_element_type x1 -> x0, other arithmetic: 1.96 us -> none  [body(): mine = grads.astype(BF16)]
  transfers between devices with their start and end apart: 2 -> 27, of which waited for: 2 -> 14; matrix products, arithmetic and copies ran while one was open for 1% -> 0% of each run, Pallas kernels for 6% -> 12%
where the time goes in v2:
time: 94.7 us; the launch traced here: 94.2 us
  starting transfers between devices  46.4 us (49%)
  waiting for transfers between devices  21.1 us (22%)
  Pallas kernels  16.5 us (17%)
  local copies, waits for them, and re-layouts  9.18 us (10%)
    ppermute x15, starting transfers between devices, gathered_grads(): lax.ppermute(side, AXES, [(place, place ^ mask) for place in range(8 * n_...  29.2 us
    ppermute x11, starting transfers between devices, send(): return lax.ppermute(array, 'hst', pairs)  17.1 us
    ppermute x15, waiting for transfers between devices, gathered_grads(): lax.ppermute(side, AXES, [(place, place ^ mask) for place in range(8 * n_...  12.2 us
    pallas_call x4, Pallas kernels, call(): pl.pallas_call(functools.partial(kernel, slots), out_shape=outs, in_specs...  11.9 us
    unnamed x36, local copies, waits for them, and re-layouts  9.18 us
    ppermute x11, waiting for transfers between devices, send(): return lax.ppermute(array, 'hst', pairs)  5.87 us
    pallas_call x1, Pallas kernels, update(): pl.pallas_call(functools.partial(update_kernel, feats, nact), out_shape=(...  3.41 us
    ppermute x1, waiting for transfers between devices, body(): theirs = lax.ppermute(mine, 'cores', [(0, 1), (1, 0)])  3.07 us
  transfers between devices with their start and end apart: 27, of which 14 were waited for; matrix products, arithmetic and copies ran while one was open for 0% of the time, Pallas kernels for 12%

profile of v2, /device:TPU:0, one launch (start us, length us, event | category | flops | bytes accessed | tf_op | source)
XLA Modules:
  0.0 94.2 jit_solution(5235304510053040023)
XLA Ops:
  0.6 3.1 %collective-permute-start = (bf16[256,512]{1,0:T(8,128)(2,1)}, bf16[256,512]{1,0:T(8,128)(2,1)S(1)}, u32[]{:S(2)}, u32[]{:S(2)}) collective-permute-start(bf16[256,512]{1,0:T(8,128)(2,1)} %bitcast.7), channel_id=1, source_target_pairs={{0,4},{2,6},{4,0},{6,2},{8,12},{10,14},{12,8},{14,10},{1,5},{3,7},... | collective-permute-start | bytes 786440 | tf_op jit(solution)/shard_map/ppermute | solution.py:346
  4.4 5.8 %collective-permute-done.refs_2_ = bf16[256,512]{1,0:T(8,128)(2,1)S(1)} collective-permute-done((bf16[256,512]{1,0:T(8,128)(2,1)}, bf16[256,512]{1,0:T(8,128)(2,1)S(1)}, u32[]{:S(2)}, u32[]{:S(2)}) %collective-permute-start) | collective-permute-done | bytes 262176 | tf_op jit(solution)/shard_map/ppermute | solution.py:346
  10.9 1.3 %collective-permute-start.23 = (bf16[256,512]{1,0:T(8,128)(2,1)S(1)}, bf16[256,512]{1,0:T(8,128)(2,1)S(1)}, u32[]{:S(2)}, u32[]{:S(2)}) collective-permute-start(bf16[256,512]{1,0:T(8,128)(2,1)S(1)} %collective-permute-done.22.refs_1_), channel_id=1, source_target_pairs={{4,0},{6,2},{8,12},{10,14},{5,1},{7,3},{9,13},{11,15},{20,16},{22,... | collective-permute-start | bytes 786440 | tf_op jit(solution)/shard_map/ppermute | solution.py:346
  12.2 1.7 %collective-permute-start.7 = (bf16[256,512]{1,0:T(8,128)(2,1)}, bf16[256,512]{1,0:T(8,128)(2,1)S(1)}, u32[]{:S(2)}, u32[]{:S(2)}) collective-permute-start(bf16[256,512]{1,0:T(8,128)(2,1)} %bitcast.9), channel_id=1, source_target_pairs={{0,2},{2,0},{4,6},{6,4},{8,10},{10,8},{12,14},{14,12},{1,3},{3,1},... | collective-permute-start | bytes 786440 | tf_op jit(solution)/shard_map/ppermute | solution.py:346
  14.0 1.3 %collective-permute-start.3 = (bf16[256,512]{1,0:T(8,128)(2,1)S(1)}, bf16[256,512]{1,0:T(8,128)(2,1)S(1)}, u32[]{:S(2)}, u32[]{:S(2)}) collective-permute-start(bf16[256,512]{1,0:T(8,128)(2,1)S(1)} %collective-permute-done.1.refs_2_), channel_id=1, source_target_pairs={{4,0},{6,2},{8,12},{10,14},{5,1},{7,3},{9,13},{11,15},{20,16},{22,... | collective-permute-start | bytes 786440 | tf_op jit(solution)/shard_map/ppermute | solution.py:346
  15.3 1.2 %copy-done.5 = bf16[512,1024]{1,0:T(8,128)(2,1)S(1)} copy-done((bf16[512,1024]{1,0:T(8,128)(2,1)S(1)}, bf16[512,1024]{1,0:T(8,128)(2,1)}, u32[]{:S(2)}) %copy-start.5) | copy-done | bytes 1048600
  21.8 8.2 %collective-permute-start.15 = (f32[8,256]{1,0:T(8,128)S(1)}, f32[8,256]{1,0:T(8,128)S(1)}, u32[]{:S(2)}, u32[]{:S(2)}) collective-permute-start(f32[8,256]{1,0:T(8,128)S(1)} %actor.1.refs_3_), channel_id=1, source_target_pairs={{0,8},{1,9},{2,10},{3,11},{4,12},{5,13},{6,14},{7,15},{8,0},{9,1},... | collective-permute-start | bytes 24584 | tf_op jit(solution)/shard_map/ppermute | solution.py:352
  30.0 1.3 %collective-permute-start.18 = (f32[8,256]{1,0:T(8,128)S(1)}, f32[8,256]{1,0:T(8,128)S(1)}, u32[]{:S(2)}, u32[]{:S(2)}) collective-permute-start(f32[8,256]{1,0:T(8,128)S(1)} %actor.1.refs_3_), channel_id=1, source_target_pairs={{0,12},{1,13},{2,14},{3,15},{4,8},{5,9},{6,10},{7,11},{8,4},{9,5},... | collective-permute-start | bytes 24584 | tf_op jit(solution)/shard_map/ppermute | solution.py:352
  31.6 3.9 %collective-permute-start.5 = (f32[8,256]{1,0:T(8,128)S(1)}, f32[8,256]{1,0:T(8,128)S(1)}, u32[]{:S(2)}, u32[]{:S(2)}) collective-permute-start(f32[8,256]{1,0:T(8,128)S(1)} %actor.1.refs_3_), channel_id=1, source_target_pairs={{0,10},{1,11},{2,8},{3,9},{4,14},{5,15},{6,12},{7,13},{8,2},{9,3},... | collective-permute-start | bytes 24584 | tf_op jit(solution)/shard_map/ppermute | solution.py:352
  35.5 2.2 %collective-permute-start.6 = (f32[8,256]{1,0:T(8,128)S(1)}, f32[8,256]{1,0:T(8,128)S(1)}, u32[]{:S(2)}, u32[]{:S(2)}) collective-permute-start(f32[8,256]{1,0:T(8,128)S(1)} %actor.1.refs_3_), channel_id=1, source_target_pairs={{0,14},{1,15},{2,12},{3,13},{4,10},{5,11},{6,8},{7,9},{8,6},{9,7},... | collective-permute-start | bytes 24584 | tf_op jit(solution)/shard_map/ppermute | solution.py:352
  37.7 2.2 %collective-permute-start.13 = (f32[8,256]{1,0:T(8,128)S(1)}, f32[8,256]{1,0:T(8,128)S(1)}, u32[]{:S(2)}, u32[]{:S(2)}) collective-permute-start(f32[8,256]{1,0:T(8,128)S(1)} %actor.1.refs_3_), channel_id=1, source_target_pairs={{0,6},{1,7},{2,4},{3,5},{4,2},{5,3},{6,0},{7,1},{8,14},{9,15},{10,... | collective-permute-start | bytes 24584 | tf_op jit(solution)/shard_map/ppermute | solution.py:352
  39.9 1.9 %collective-permute-done.6.refs_17_.refs_4_.refs_3_ = f32[8,256]{1,0:T(8,128)S(1)} collective-permute-done((f32[8,256]{1,0:T(8,128)S(1)}, f32[8,256]{1,0:T(8,128)S(1)}, u32[]{:S(2)}, u32[]{:S(2)}) %collective-permute-start.6) | collective-permute-done | bytes 8224 | tf_op jit(solution)/shard_map/ppermute | solution.py:352
  42.3 1.2 %collective-permute-start.11 = (f32[8,256]{1,0:T(8,128)S(1)}, f32[8,256]{1,0:T(8,128)S(1)}, u32[]{:S(2)}, u32[]{:S(2)}) collective-permute-start(f32[8,256]{1,0:T(8,128)S(1)} %actor.1.refs_3_), channel_id=1, source_target_pairs={{0,4},{1,5},{2,6},{3,7},{4,0},{5,1},{6,2},{7,3},{8,12},{9,13},{10,... | collective-permute-start | bytes 24584 | tf_op jit(solution)/shard_map/ppermute | solution.py:352
  43.5 1.5 %collective-permute-done.10.refs_6_ = f32[8,256]{1,0:T(8,128)S(1)} collective-permute-done((f32[8,256]{1,0:T(8,128)S(1)}, f32[8,256]{1,0:T(8,128)S(1)}, u32[]{:S(2)}, u32[]{:S(2)}) %collective-permute-start.10) | collective-permute-done | bytes 8224 | tf_op jit(solution)/shard_map/ppermute | solution.py:352
  46.0 1.6 %collective-permute-start.14 = (f32[8,256]{1,0:T(8,128)S(1)}, f32[8,256]{1,0:T(8,128)S(1)}, u32[]{:S(2)}, u32[]{:S(2)}) collective-permute-start(f32[8,256]{1,0:T(8,128)S(1)} %actor.1.refs_3_), channel_id=1, source_target_pairs={{0,7},{1,6},{2,5},{3,4},{4,3},{5,2},{6,1},{7,0},{8,15},{9,14},{10,... | collective-permute-start | bytes 24584 | tf_op jit(solution)/shard_map/ppermute | solution.py:352
  48.9 1.1 %collective-permute-done.14.refs_10_ = f32[8,256]{1,0:T(8,128)S(1)} collective-permute-done((f32[8,256]{1,0:T(8,128)S(1)}, f32[8,256]{1,0:T(8,128)S(1)}, u32[]{:S(2)}, u32[]{:S(2)}) %collective-permute-start.14) | collective-permute-done | bytes 8224 | tf_op jit(solution)/shard_map/ppermute | solution.py:352
  49.9 1.6 %collective-permute-start.17 = (f32[8,256]{1,0:T(8,128)S(1)}, f32[8,256]{1,0:T(8,128)S(1)}, u32[]{:S(2)}, u32[]{:S(2)}) collective-permute-start(f32[8,256]{1,0:T(8,128)S(1)} %actor.1.refs_3_), channel_id=1, source_target_pairs={{0,11},{1,10},{2,9},{3,8},{4,15},{5,14},{6,13},{7,12},{8,3},{9,2},... | collective-permute-start | bytes 24584 | tf_op jit(solution)/shard_map/ppermute | solution.py:352
  52.0 2.3 %collective-permute-start.19 = (f32[8,256]{1,0:T(8,128)S(1)}, f32[8,256]{1,0:T(8,128)S(1)}, u32[]{:S(2)}, u32[]{:S(2)}) collective-permute-start(f32[8,256]{1,0:T(8,128)S(1)} %actor.1.refs_3_), channel_id=1, source_target_pairs={{0,13},{1,12},{2,15},{3,14},{4,9},{5,8},{6,11},{7,10},{8,5},{9,4},... | collective-permute-start | bytes 24584 | tf_op jit(solution)/shard_map/ppermute | solution.py:352
  54.8 1.7 %collective-permute-start.20 = (f32[8,256]{1,0:T(8,128)S(1)}, f32[8,256]{1,0:T(8,128)S(1)}, u32[]{:S(2)}, u32[]{:S(2)}) collective-permute-start(f32[8,256]{1,0:T(8,128)S(1)} %actor.1.refs_3_), channel_id=1, source_target_pairs={{0,15},{1,14},{2,13},{3,12},{4,11},{5,10},{6,9},{7,8},{8,7},{9,6},... | collective-permute-start | bytes 24584 | tf_op jit(solution)/shard_map/ppermute | solution.py:352
  56.9 1.2 %collective-permute-start.8 = (f32[8,256]{1,0:T(8,128)S(1)}, f32[8,256]{1,0:T(8,128)S(1)}, u32[]{:S(2)}, u32[]{:S(2)}) collective-permute-start(f32[8,256]{1,0:T(8,128)S(1)} %actor.1.refs_3_), channel_id=1, source_target_pairs={{0,1},{1,0},{2,3},{3,2},{4,5},{5,4},{6,7},{7,6},{8,9},{9,8},{10,11... | collective-permute-start | bytes 24584 | tf_op jit(solution)/shard_map/ppermute | solution.py:352
  58.1 2.5 %collective-permute-done.20.refs_18_ = f32[8,256]{1,0:T(8,128)S(1)} collective-permute-done((f32[8,256]{1,0:T(8,128)S(1)}, f32[8,256]{1,0:T(8,128)S(1)}, u32[]{:S(2)}, u32[]{:S(2)}) %collective-permute-start.20) | collective-permute-done | bytes 8224 | tf_op jit(solution)/shard_map/ppermute | solution.py:352
  62.6 1.7 %collective-permute-done.9.refs_5_ = f32[8,256]{1,0:T(8,128)S(1)} collective-permute-done((f32[8,256]{1,0:T(8,128)S(1)}, f32[8,256]{1,0:T(8,128)S(1)}, u32[]{:S(2)}, u32[]{:S(2)}) %collective-permute-start.9) | collective-permute-done | bytes 8224 | tf_op jit(solution)/shard_map/ppermute | solution.py:352
  64.9 3.0 %collective-permute-start.25 = (bf16[256,512]{1,0:T(8,128)(2,1)S(1)}, bf16[256,512]{1,0:T(8,128)(2,1)S(1)}, u32[]{:S(2)}, u32[]{:S(2)}) collective-permute-start(bf16[256,512]{1,0:T(8,128)(2,1)S(1)} %collective-permute-done.23.refs_2_), channel_id=1, source_target_pairs={{0,2},{2,0},{12,14},{14,12},{1,3},{3,1},{13,15},{15,13},{16,18},{1... | collective-permute-start | bytes 786440 | tf_op jit(solution)/shard_map/ppermute | solution.py:346
  68.6 3.1 %collective-permute-start.4 = (bf16[256,512]{1,0:T(8,128)(2,1)S(1)}, bf16[256,512]{1,0:T(8,128)(2,1)S(1)}, u32[]{:S(2)}, u32[]{:S(2)}) collective-permute-start(bf16[256,512]{1,0:T(8,128)(2,1)S(1)} %collective-permute-done.3.refs_3_), channel_id=1, source_target_pairs={{0,2},{2,0},{12,14},{14,12},{1,3},{3,1},{13,15},{15,13},{16,18},{1... | collective-permute-start | bytes 786440 | tf_op jit(solution)/shard_map/ppermute | solution.py:346
  71.7 1.6 %copy-done = f32[512,1024]{1,0:T(8,128)S(1)} copy-done((f32[512,1024]{1,0:T(8,128)S(1)}, f32[512,1024]{1,0:T(8,128)}, u32[]{:S(2)}) %copy-start) | copy-done | bytes 2097176
  73.3 1.0 %copy-done.3 = f32[1024,128]{1,0:T(8,128)S(1)} copy-done((f32[1024,128]{1,0:T(8,128)S(1)}, f32[1024,128]{1,0:T(8,128)}, u32[]{:S(2)}) %copy-start.3) | copy-done | bytes 524312
  75.5 3.9 %first.1 = (f32[656,1024]{1,0:T(8,128)S(1)}, f32[656,1024]{1,0:T(8,128)S(1)}, f32[16,128]{1,0:T(8,128)S(1)}) custom-call(bf16[256,512]{1,0:T(8,128)(2,1)S(1)} %bitcast.11, bf16[256,512]{1,0:T(8,128)(2,1)S(1)} %collective-permute-done.7.refs_1_, bf16[256,512]{1,0:T(8,128)(2,1)S(1)} %collective-permute-done.refs_2_, f32[8,256]{1,0:T(8,128)S(1)} %actor.1.refs_3_, ...), custom_call_target="tpu_custom_call" | custom-call | tf_op jit(solution)/shard_map/first/pallas_call | solution.py:285
  79.4 2.9 %second.1 = (f32[656,1024]{1,0:T(8,128)S(1)}, f32[656,1024]{1,0:T(8,128)S(1)}) custom-call(bf16[256,512]{1,0:T(8,128)(2,1)S(1)} %collective-permute-done.21.refs_0_, bf16[256,512]{1,0:T(8,128)(2,1)S(1)} %collective-permute-done.22.refs_1_, bf16[256,512]{1,0:T(8,128)(2,1)S(1)} %collective-permute-done.23.refs_2_, ...), custom_call_target="tpu_custom_call" | custom-call | tf_op jit(solution)/shard_map/second/pallas_call | solution.py:285
  82.4 2.9 %third.1 = (f32[656,1024]{1,0:T(8,128)S(1)}, f32[656,1024]{1,0:T(8,128)S(1)}) custom-call(bf16[256,512]{1,0:T(8,128)(2,1)S(1)} %collective-permute-done.24.refs_0_, bf16[256,512]{1,0:T(8,128)(2,1)S(1)} %collective-permute-done.25.refs_1_, bf16[256,512]{1,0:T(8,128)(2,1)S(1)} %collective-permute-done.1.refs_2_, ...), custom_call_target="tpu_custom_call" | custom-call | tf_op jit(solution)/shard_map/third/pallas_call | solution.py:285
  85.4 2.2 %fourth.1.mine = bf16[656,1024]{1,0:T(8,128)(2,1)S(1)} custom-call(bf16[256,512]{1,0:T(8,128)(2,1)S(1)} %collective-permute-done.2.refs_0_, bf16[256,512]{1,0:T(8,128)(2,1)S(1)} %collective-permute-done.4.refs_1_, f32[8,256]{1,0:T(8,128)S(1)} %collective-permute-done.5.refs_13_.refs_5_.refs_2_, f32[8,256]{1,0:T(8,128)S(1)} %collective-permute-done.6.refs_17_.refs_4_.refs_3_, ...), custom_call_target="tpu_custom_call" | custom-call | tf_op jit(solution)/shard_map/fourth/pallas_call | solution.py:285
  87.7 3.1 %collective-permute-done.26.theirs = bf16[656,1024]{1,0:T(8,128)(2,1)S(1)} collective-permute-done((bf16[656,1024]{1,0:T(8,128)(2,1)S(1)}, bf16[656,1024]{1,0:T(8,128)(2,1)S(1)}, u32[]{:S(2)}, u32[]{:S(2)}) %collective-permute-start.26) | collective-permute-done | bytes 1343520 | tf_op jit(solution)/shard_map/ppermute | solution.py:404
  90.8 3.4 %update.1 = (bf16[256,128]{1,0:T(8,128)(2,1)}, f32[512,1024]{1,0:T(8,128)}, f32[1024,128]{1,0:T(8,128)}, f32[1,1024]{1,0:T(1,128)}, f32[512,1024]{1,0:T(8,128)}, /*index=5*/f32[1024,128]{1,0:T(8,128)}, f32[1,1024]{1,0:T(1,128)}) custom-call(bf16[656,1024]{1,0:T(8,128)(2,1)S(1)} %fourth.1.mine, bf16[656,1024]{1,0:T(8,128)(2,1)S(1)} %collective-permute-done.26.theirs, ...), custom_call_target="tpu_custom_call" | custom-call | tf_op jit(solution)/shard_map/update/pallas_call | solution.py:327
  (65 shorter events, 15.8 us)
Async XLA Ops:
  0.6 9.6 %collective-permute-start = (bf16[256,512]{1,0:T(8,128)(2,1)}, bf16[256,512]{1,0:T(8,128)(2,1)S(1)}, u32[]{:S(2)}, u32[]{:S(2)}) collective-permute-start(bf16[256,512]{1,0:T(8,128)(2,1)} %bitcast.7), channel_id=1, source_target_pairs={{0,4},{2,6},{4,0},{6,2},{8,12},{10,14},{12,8},{14,10},{1,5},{3,7},... | collective-permute-start | bytes 786440 | tf_op jit(solution)/shard_map/ppermute | solution.py:346
  3.7 7.2 %collective-permute-start.22 = (bf16[256,512]{1,0:T(8,128)(2,1)}, bf16[256,512]{1,0:T(8,128)(2,1)S(1)}, u32[]{:S(2)}, u32[]{:S(2)}) collective-permute-start(bf16[256,512]{1,0:T(8,128)(2,1)} %bitcast.8), channel_id=1, source_target_pairs={{4,8},{6,10},{8,4},{10,6},{5,9},{7,11},{9,5},{11,7},{20,24},{22,26... | collective-permute-start | bytes 786440 | tf_op jit(solution)/shard_map/ppermute | solution.py:346
  10.2 3.7 %collective-permute-start.1 = (bf16[256,512]{1,0:T(8,128)(2,1)S(1)}, bf16[256,512]{1,0:T(8,128)(2,1)S(1)}, u32[]{:S(2)}, u32[]{:S(2)}) collective-permute-start(bf16[256,512]{1,0:T(8,128)(2,1)S(1)} %collective-permute-done.refs_2_), channel_id=1, source_target_pairs={{4,8},{6,10},{8,4},{10,6},{5,9},{7,11},{9,5},{11,7},{20,24},{22,26... | collective-permute-start | bytes 786440 | tf_op jit(solution)/shard_map/ppermute | solution.py:346
  10.9 54.0 %collective-permute-start.23 = (bf16[256,512]{1,0:T(8,128)(2,1)S(1)}, bf16[256,512]{1,0:T(8,128)(2,1)S(1)}, u32[]{:S(2)}, u32[]{:S(2)}) collective-permute-start(bf16[256,512]{1,0:T(8,128)(2,1)S(1)} %collective-permute-done.22.refs_1_), channel_id=1, source_target_pairs={{4,0},{6,2},{8,12},{10,14},{5,1},{7,3},{9,13},{11,15},{20,16},{22,... | collective-permute-start | bytes 786440 | tf_op jit(solution)/shard_map/ppermute | solution.py:346
  12.2 55.7 %collective-permute-start.7 = (bf16[256,512]{1,0:T(8,128)(2,1)}, bf16[256,512]{1,0:T(8,128)(2,1)S(1)}, u32[]{:S(2)}, u32[]{:S(2)}) collective-permute-start(bf16[256,512]{1,0:T(8,128)(2,1)} %bitcast.9), channel_id=1, source_target_pairs={{0,2},{2,0},{4,6},{6,4},{8,10},{10,8},{12,14},{14,12},{1,3},{3,1},... | collective-permute-start | bytes 786440 | tf_op jit(solution)/shard_map/ppermute | solution.py:346
  14.0 54.7 %collective-permute-start.3 = (bf16[256,512]{1,0:T(8,128)(2,1)S(1)}, bf16[256,512]{1,0:T(8,128)(2,1)S(1)}, u32[]{:S(2)}, u32[]{:S(2)}) collective-permute-start(bf16[256,512]{1,0:T(8,128)(2,1)S(1)} %collective-permute-done.1.refs_2_), channel_id=1, source_target_pairs={{4,0},{6,2},{8,12},{10,14},{5,1},{7,3},{9,13},{11,15},{20,16},{22,... | collective-permute-start | bytes 786440 | tf_op jit(solution)/shard_map/ppermute | solution.py:346
  21.1 54.4 %copy-start.7 = (bf16[16,16,512]{2,1,0:T(8,128)(2,1)S(1)}, bf16[16,16,512]{2,1,0:T(8,128)(2,1)}, u32[]{:S(2)}) copy-start(bf16[16,16,512]{2,1,0:T(8,128)(2,1)} %param.14) | copy-start | bytes 786436
  21.8 9.8 %collective-permute-start.15 = (f32[8,256]{1,0:T(8,128)S(1)}, f32[8,256]{1,0:T(8,128)S(1)}, u32[]{:S(2)}, u32[]{:S(2)}) collective-permute-start(f32[8,256]{1,0:T(8,128)S(1)} %actor.1.refs_3_), channel_id=1, source_target_pairs={{0,8},{1,9},{2,10},{3,11},{4,12},{5,13},{6,14},{7,15},{8,0},{9,1},... | collective-permute-start | bytes 24584 | tf_op jit(solution)/shard_map/ppermute | solution.py:352
  30.0 5.5 %collective-permute-start.18 = (f32[8,256]{1,0:T(8,128)S(1)}, f32[8,256]{1,0:T(8,128)S(1)}, u32[]{:S(2)}, u32[]{:S(2)}) collective-permute-start(f32[8,256]{1,0:T(8,128)S(1)} %actor.1.refs_3_), channel_id=1, source_target_pairs={{0,12},{1,13},{2,14},{3,15},{4,8},{5,9},{6,10},{7,11},{8,4},{9,5},... | collective-permute-start | bytes 24584 | tf_op jit(solution)/shard_map/ppermute | solution.py:352
  31.6 6.1 %collective-permute-start.5 = (f32[8,256]{1,0:T(8,128)S(1)}, f32[8,256]{1,0:T(8,128)S(1)}, u32[]{:S(2)}, u32[]{:S(2)}) collective-permute-start(f32[8,256]{1,0:T(8,128)S(1)} %actor.1.refs_3_), channel_id=1, source_target_pairs={{0,10},{1,11},{2,8},{3,9},{4,14},{5,15},{6,12},{7,13},{8,2},{9,3},... | collective-permute-start | bytes 24584 | tf_op jit(solution)/shard_map/ppermute | solution.py:352
  35.5 6.3 %collective-permute-start.6 = (f32[8,256]{1,0:T(8,128)S(1)}, f32[8,256]{1,0:T(8,128)S(1)}, u32[]{:S(2)}, u32[]{:S(2)}) collective-permute-start(f32[8,256]{1,0:T(8,128)S(1)} %actor.1.refs_3_), channel_id=1, source_target_pairs={{0,14},{1,15},{2,12},{3,13},{4,10},{5,11},{6,8},{7,9},{8,6},{9,7},... | collective-permute-start | bytes 24584 | tf_op jit(solution)/shard_map/ppermute | solution.py:352
  37.7 4.6 %collective-permute-start.13 = (f32[8,256]{1,0:T(8,128)S(1)}, f32[8,256]{1,0:T(8,128)S(1)}, u32[]{:S(2)}, u32[]{:S(2)}) collective-permute-start(f32[8,256]{1,0:T(8,128)S(1)} %actor.1.refs_3_), channel_id=1, source_target_pairs={{0,6},{1,7},{2,4},{3,5},{4,2},{5,3},{6,0},{7,1},{8,14},{9,15},{10,... | collective-permute-start | bytes 24584 | tf_op jit(solution)/shard_map/ppermute | solution.py:352
  41.8 3.1 %collective-permute-start.10 = (f32[8,256]{1,0:T(8,128)S(1)}, f32[8,256]{1,0:T(8,128)S(1)}, u32[]{:S(2)}, u32[]{:S(2)}) collective-permute-start(f32[8,256]{1,0:T(8,128)S(1)} %actor.1.refs_3_), channel_id=1, source_target_pairs={{0,3},{1,2},{2,1},{3,0},{4,7},{5,6},{6,5},{7,4},{8,11},{9,10},{10,... | collective-permute-start | bytes 24584 | tf_op jit(solution)/shard_map/ppermute | solution.py:352
  42.3 3.7 %collective-permute-start.11 = (f32[8,256]{1,0:T(8,128)S(1)}, f32[8,256]{1,0:T(8,128)S(1)}, u32[]{:S(2)}, u32[]{:S(2)}) collective-permute-start(f32[8,256]{1,0:T(8,128)S(1)} %actor.1.refs_3_), channel_id=1, source_target_pairs={{0,4},{1,5},{2,6},{3,7},{4,0},{5,1},{6,2},{7,3},{8,12},{9,13},{10,... | collective-permute-start | bytes 24584 | tf_op jit(solution)/shard_map/ppermute | solution.py:352
  45.0 3.1 %collective-permute-start.12 = (f32[8,256]{1,0:T(8,128)S(1)}, f32[8,256]{1,0:T(8,128)S(1)}, u32[]{:S(2)}, u32[]{:S(2)}) collective-permute-start(f32[8,256]{1,0:T(8,128)S(1)} %actor.1.refs_3_), channel_id=1, source_target_pairs={{0,5},{1,4},{2,7},{3,6},{4,1},{5,0},{6,3},{7,2},{8,13},{9,12},{10,... | collective-permute-start | bytes 24584 | tf_op jit(solution)/shard_map/ppermute | solution.py:352
  46.0 4.0 %collective-permute-start.14 = (f32[8,256]{1,0:T(8,128)S(1)}, f32[8,256]{1,0:T(8,128)S(1)}, u32[]{:S(2)}, u32[]{:S(2)}) collective-permute-start(f32[8,256]{1,0:T(8,128)S(1)} %actor.1.refs_3_), channel_id=1, source_target_pairs={{0,7},{1,6},{2,5},{3,4},{4,3},{5,2},{6,1},{7,0},{8,15},{9,14},{10,... | collective-permute-start | bytes 24584 | tf_op jit(solution)/shard_map/ppermute | solution.py:352
  48.1 4.0 %collective-permute-start.16 = (f32[8,256]{1,0:T(8,128)S(1)}, f32[8,256]{1,0:T(8,128)S(1)}, u32[]{:S(2)}, u32[]{:S(2)}) collective-permute-start(f32[8,256]{1,0:T(8,128)S(1)} %actor.1.refs_3_), channel_id=1, source_target_pairs={{0,9},{1,8},{2,11},{3,10},{4,13},{5,12},{6,15},{7,14},{8,1},{9,0},... | collective-permute-start | bytes 24584 | tf_op jit(solution)/shard_map/ppermute | solution.py:352
  49.9 4.9 %collective-permute-start.17 = (f32[8,256]{1,0:T(8,128)S(1)}, f32[8,256]{1,0:T(8,128)S(1)}, u32[]{:S(2)}, u32[]{:S(2)}) collective-permute-start(f32[8,256]{1,0:T(8,128)S(1)} %actor.1.refs_3_), channel_id=1, source_target_pairs={{0,11},{1,10},{2,9},{3,8},{4,15},{5,14},{6,13},{7,12},{8,3},{9,2},... | collective-permute-start | bytes 24584 | tf_op jit(solution)/shard_map/ppermute | solution.py:352
  52.0 4.9 %collective-permute-start.19 = (f32[8,256]{1,0:T(8,128)S(1)}, f32[8,256]{1,0:T(8,128)S(1)}, u32[]{:S(2)}, u32[]{:S(2)}) collective-permute-start(f32[8,256]{1,0:T(8,128)S(1)} %actor.1.refs_3_), channel_id=1, source_target_pairs={{0,13},{1,12},{2,15},{3,14},{4,9},{5,8},{6,11},{7,10},{8,5},{9,4},... | collective-permute-start | bytes 24584 | tf_op jit(solution)/shard_map/ppermute | solution.py:352
  54.8 5.8 %collective-permute-start.20 = (f32[8,256]{1,0:T(8,128)S(1)}, f32[8,256]{1,0:T(8,128)S(1)}, u32[]{:S(2)}, u32[]{:S(2)}) collective-permute-start(f32[8,256]{1,0:T(8,128)S(1)} %actor.1.refs_3_), channel_id=1, source_target_pairs={{0,15},{1,14},{2,13},{3,12},{4,11},{5,10},{6,9},{7,8},{8,7},{9,6},... | collective-permute-start | bytes 24584 | tf_op jit(solution)/shard_map/ppermute | solution.py:352
  56.9 4.7 %collective-permute-start.8 = (f32[8,256]{1,0:T(8,128)S(1)}, f32[8,256]{1,0:T(8,128)S(1)}, u32[]{:S(2)}, u32[]{:S(2)}) collective-permute-start(f32[8,256]{1,0:T(8,128)S(1)} %actor.1.refs_3_), channel_id=1, source_target_pairs={{0,1},{1,0},{2,3},{3,2},{4,5},{5,4},{6,7},{7,6},{8,9},{9,8},{10,11... | collective-permute-start | bytes 24584 | tf_op jit(solution)/shard_map/ppermute | solution.py:352
  60.6 3.7 %collective-permute-start.9 = (f32[8,256]{1,0:T(8,128)S(1)}, f32[8,256]{1,0:T(8,128)S(1)}, u32[]{:S(2)}, u32[]{:S(2)}) collective-permute-start(f32[8,256]{1,0:T(8,128)S(1)} %actor.1.refs_3_), channel_id=1, source_target_pairs={{0,2},{1,3},{2,0},{3,1},{4,6},{5,7},{6,4},{7,5},{8,10},{9,11},{10,... | collective-permute-start | bytes 24584 | tf_op jit(solution)/shard_map/ppermute | solution.py:352
  61.6 17.8 %collective-permute-start.21 = (bf16[256,512]{1,0:T(8,128)(2,1)S(1)}, bf16[256,512]{1,0:T(8,128)(2,1)S(1)}, u32[]{:S(2)}, u32[]{:S(2)}) collective-permute-start(bf16[256,512]{1,0:T(8,128)(2,1)S(1)} %collective-permute-done.refs_2_), channel_id=1, source_target_pairs={{0,2},{2,0},{4,6},{6,4},{8,10},{10,8},{12,14},{14,12},{1,3},{3,1},... | collective-permute-start | bytes 786440 | tf_op jit(solution)/shard_map/ppermute | solution.py:346
  64.3 18.1 %collective-permute-start.24 = (bf16[256,512]{1,0:T(8,128)(2,1)S(1)}, bf16[256,512]{1,0:T(8,128)(2,1)S(1)}, u32[]{:S(2)}, u32[]{:S(2)}) collective-permute-start(bf16[256,512]{1,0:T(8,128)(2,1)S(1)} %collective-permute-done.22.refs_1_), channel_id=1, source_target_pairs={{4,6},{6,4},{8,10},{10,8},{5,7},{7,5},{9,11},{11,9},{20,22},{22,20... | collective-permute-start | bytes 786440 | tf_op jit(solution)/shard_map/ppermute | solution.py:346
  64.9 17.4 %collective-permute-start.25 = (bf16[256,512]{1,0:T(8,128)(2,1)S(1)}, bf16[256,512]{1,0:T(8,128)(2,1)S(1)}, u32[]{:S(2)}, u32[]{:S(2)}) collective-permute-start(bf16[256,512]{1,0:T(8,128)(2,1)S(1)} %collective-permute-done.23.refs_2_), channel_id=1, source_target_pairs={{0,2},{2,0},{12,14},{14,12},{1,3},{3,1},{13,15},{15,13},{16,18},{1... | collective-permute-start | bytes 786440 | tf_op jit(solution)/shard_map/ppermute | solution.py:346
  67.9 17.3 %collective-permute-start.2 = (bf16[256,512]{1,0:T(8,128)(2,1)S(1)}, bf16[256,512]{1,0:T(8,128)(2,1)S(1)}, u32[]{:S(2)}, u32[]{:S(2)}) collective-permute-start(bf16[256,512]{1,0:T(8,128)(2,1)S(1)} %collective-permute-done.1.refs_2_), channel_id=1, source_target_pairs={{4,6},{6,4},{8,10},{10,8},{5,7},{7,5},{9,11},{11,9},{20,22},{22,20... | collective-permute-start | bytes 786440 | tf_op jit(solution)/shard_map/ppermute | solution.py:346
  68.6 16.6 %collective-permute-start.4 = (bf16[256,512]{1,0:T(8,128)(2,1)S(1)}, bf16[256,512]{1,0:T(8,128)(2,1)S(1)}, u32[]{:S(2)}, u32[]{:S(2)}) collective-permute-start(bf16[256,512]{1,0:T(8,128)(2,1)S(1)} %collective-permute-done.3.refs_3_), channel_id=1, source_target_pairs={{0,2},{2,0},{12,14},{14,12},{1,3},{3,1},{13,15},{15,13},{16,18},{1... | collective-permute-start | bytes 786440 | tf_op jit(solution)/shard_map/ppermute | solution.py:346
  85.3 5.4 %copy-start.1 = (f32[512,1024]{1,0:T(8,128)S(1)}, f32[512,1024]{1,0:T(8,128)}, u32[]{:S(2)}) copy-start(f32[512,1024]{1,0:T(8,128)} %master_embed.3) | copy-start | bytes 6291460
  85.3 5.4 %copy-start.2 = (f32[512,1024]{1,0:T(8,128)S(1)}, f32[512,1024]{1,0:T(8,128)}, u32[]{:S(2)}) copy-start(f32[512,1024]{1,0:T(8,128)} %embed_moment.1) | copy-start | bytes 6291460
  85.3 5.4 %copy-start.4 = (f32[1024,128]{1,0:T(8,128)S(1)}, f32[1024,128]{1,0:T(8,128)}, u32[]{:S(2)}) copy-start(f32[1024,128]{1,0:T(8,128)} %master_policy.3) | copy-start | bytes 1572868
  85.3 5.4 %copy-start.8 = (f32[1024,128]{1,0:T(8,128)S(1)}, f32[1024,128]{1,0:T(8,128)}, u32[]{:S(2)}) copy-start(f32[1024,128]{1,0:T(8,128)} %policy_moment.1) | copy-start | bytes 1572868
  87.6 3.1 %collective-permute-start.26 = (bf16[656,1024]{1,0:T(8,128)(2,1)S(1)}, bf16[656,1024]{1,0:T(8,128)(2,1)S(1)}, u32[]{:S(2)}, u32[]{:S(2)}) collective-permute-start(bf16[656,1024]{1,0:T(8,128)(2,1)S(1)} %fourth.1.mine), channel_id=1, source_target_pairs={{0,1},{1,0},{2,3},{3,2},{4,5},{5,4},{6,7},{7,6},{8,9},{9,8},{10,11... | collective-permute-start | bytes 4030472 | tf_op jit(solution)/shard_map/ppermute | solution.py:404
  (13 other events, 25.4 us)

commit v3 on v2

--- a/solution.py
+++ b/solution.py
@@ -37,19 +37,58 @@
     return pltpu.CompilerParams(vmem_limit_bytes=mib * MIB)
 
 
-def actor_kernel(obs, lengths, assign, actions, rewards, actor_embed, actor_policy, side):
-    rows = obs.shape[0]
-    traj, slots = actions.shape
-    spread = (lax.rem(iota((slots, rows), 1), slots) == iota((slots, rows), 0)).astype(F32)
-    owner = lax.div(iota((traj, rows), 1), slots) == iota((traj, rows), 0)
+def cost(micros):
+    return pl.CostEstimate(flops=int(micros * 1.1e9), bytes_accessed=0, transcendentals=0)
+
+
+def select_kernel(spread, owner):
+    traj, rows = owner.shape
+    slots = spread.shape[0]
+    spread[...] = (lax.rem(iota((slots, rows), 1), slots) == iota((slots, rows), 0)).astype(F32)
+    owner[...] = (lax.div(iota((traj, rows), 1), slots) == iota((traj, rows), 0)).astype(F32)
+
+
+def select(traj, slots):
+    rows = traj * slots
+    return pl.pallas_call(
+        select_kernel,
+        out_shape=(jax.ShapeDtypeStruct((slots, rows), F32), jax.ShapeDtypeStruct((traj, rows), F32)),
+        out_specs=(VMEM, VMEM),
+        cost_estimate=cost(6),
+        name="select",
+    )()
+
+
+def prepare_kernel(
+    lengths_at, assign_at, actions_at, rewards_at, obs_at, actor_embed_at, actor_policy_at,
+    master_embed_at, master_policy_at, master_value_at, spread, owner,
+    side, embed_t, head, head_t, *scratch,
+):
+    sources = (
+        lengths_at, assign_at, actions_at, rewards_at, obs_at, actor_embed_at, actor_policy_at,
+        master_embed_at, master_policy_at, master_value_at,
+    )
+    held, sems = scratch[:-1], scratch[-1]
+    copies = [
+        pltpu.make_async_copy(source, target, sems.at[index])
+        for index, (source, target) in enumerate(zip(sources, held))
+    ]
+    for copy in copies:
+        copy.start()
+    (lengths, assign, actions, rewards, obs, actor_embed, actor_policy,
+     master_embed, master_policy, master_value) = held
+    for copy in copies[:7]:
+        copy.wait()
 
     def flat(series):
-        wide = jnp.dot(series, spread, precision=lax.Precision.HIGHEST, preferred_element_type=F32)
-        return jnp.sum(jnp.where(owner, wide, 0.0), axis=0, keepdims=True)
+        wide = jnp.dot(
+            series, spread[...], precision=lax.Precision.HIGHEST, preferred_element_type=F32
+        )
+        return jnp.sum(wide * owner[...], axis=0, keepdims=True)
 
     def repeat(series):
         return jnp.dot(
-            series.astype(F32), owner.astype(F32),
+            series.astype(F32), owner[...],
             precision=lax.Precision.HIGHEST, preferred_element_type=F32,
         )
 
@@ -69,19 +108,8 @@
     side[LENGTH : LENGTH + 1, :] = repeat(lengths[...])
     side[ASSIGN : ASSIGN + 1, :] = repeat(assign[...])
 
-
-def actor(obs, *args):
-    return pl.pallas_call(
-        actor_kernel,
-        out_shape=jax.ShapeDtypeStruct((8, obs.shape[0]), F32),
-        in_specs=[VMEM] * 7,
-        out_specs=VMEM,
-        compiler_params=params(12),
-        name="actor",
-    )(obs, *args)
-
-
-def prepare_kernel(master_embed, master_policy, master_value, embed_t, head, head_t):
+    for copy in copies[7:]:
+        copy.wait()
     embed_t[...] = master_embed[...].T.astype(BF16)
     nact = master_policy.shape[1]
     wide = jnp.concatenate(
@@ -97,30 +125,36 @@
     head[:, nact:] = wide[nact:, :].T.astype(BF16)
 
 
-def prepare(master_embed, master_policy, master_value):
-    feats, width = master_embed.shape
-    nact = master_policy.shape[1]
+def prepare(*args):
+    masks = select(*args[2].shape)
+    rows = args[4].shape[0]
+    feats, width = args[7].shape
+    nact = args[8].shape[1]
     return pl.pallas_call(
         prepare_kernel,
         out_shape=(
+            jax.ShapeDtypeStruct((8, rows), F32),
             jax.ShapeDtypeStruct((width, feats), BF16),
             jax.ShapeDtypeStruct((width, nact + PAD), BF16),
             jax.ShapeDtypeStruct((nact + PAD, width), BF16),
         ),
-        in_specs=[VMEM] * 3,
-        out_specs=(VMEM,) * 3,
-        compiler_params=params(12),
+        in_specs=[pl.BlockSpec(memory_space=pl.ANY)] * len(args) + [VMEM] * 2,
+        out_specs=(VMEM,) * 4,
+        scratch_shapes=[pltpu.VMEM(arg.shape, arg.dtype) for arg in args]
+        + [pltpu.SemaphoreType.DMA((len(args),))],
+        compiler_params=params(16),
+        cost_estimate=cost(3),
         name="prepare",
-    )(master_embed, master_policy, master_value)
+    )(*args, *masks)
 
 
 def learner_weights(slots, sides, out):
-    learners, rows = out.shape[0], sides[0].shape[1]
+    learners, rows = out.shape[0], sides.shape[1]
     total = jnp.zeros((learners, rows), F32)
     first = lax.rem(iota((1, rows), 1), slots) == 0
-    for side in sides:
-        assign = side[ASSIGN : ASSIGN + 1, :].astype(jnp.int32)
-        length = jnp.where(first, side[LENGTH : LENGTH + 1, :], 0.0)
+    for place in range(0, sides.shape[0], 8):
+        assign = sides[place + ASSIGN : place + ASSIGN + 1, :].astype(jnp.int32)
+        length = jnp.where(first, sides[place + LENGTH : place + LENGTH + 1, :], 0.0)
         total = total + jnp.where(iota((learners, rows), 0) == assign, length, 0.0)
     summed = jnp.sum(total, axis=1, keepdims=True)
     out[...] = jnp.broadcast_to(1.0 / (learners * summed), out.shape)
@@ -197,75 +231,103 @@
         add(index, slice(feats, feats + nact + PAD), mm_nt(grad_t[:, lanes], hidden_t[:, lanes]))
 
 
+def work(slots, frames, side, weights, embed_t, head, head_t, frames_t, hidden_t, preact_t, add):
+    width, feats = embed_t.shape
+    nact = head_t.shape[0] - PAD
+    tile = 256
+    for index, block in enumerate(frames):
+        frames_t[:, index * BLOCK : (index + 1) * BLOCK] = block.T
+    for start in range(0, width, tile):
+        here = slice(start, start + tile)
+        hidden_t[here, :] = jnp.maximum(mm(embed_t[here, :], frames_t[...]), 0.0).astype(BF16)
+    logits = mm(head_t[...], hidden_t[...])
+    grad, grad_values = vtrace(
+        slots, nact, side, weights, logits[0:nact, :], logits[nact : nact + 1, :]
+    )
+    pad = jnp.zeros((PAD - 1, grad.shape[1]), F32)
+    grad_t = jnp.concatenate([grad, grad_values, pad], axis=0).astype(BF16)
+    for start in range(0, width, tile):
+        here = slice(start, start + tile)
+        back = mm(head[here, :], grad_t)
+        alive = hidden_t[here, :].astype(F32) > 0.0
+        preact_t[here, :] = jnp.where(alive, back, 0.0).astype(BF16)
+    for index in range(len(frames)):
+        lanes = slice(index * BLOCK, (index + 1) * BLOCK)
+        add(index, slice(0, feats), mm_nt(frames_t[:, lanes], preact_t[:, lanes]))
+        add(index, slice(feats, feats + nact + PAD), mm_nt(grad_t[:, lanes], hidden_t[:, lanes]))
+
+
 def on_mid():
     line = lax.div(lax.axis_index("hst"), 2)
     return jnp.logical_or(line == 1, line == 2)
 
 
-def choose(mid, end):
-    return jnp.where(on_mid(), mid[...], end[...])
+def side_of(sides, back, flip):
+    line = lax.div(lax.axis_index("hst"), 2)
+    there = lax.bitwise_and(line + 4 - back, 3)
+    mask = 2 * lax.bitwise_xor(line, there) + flip
+    return sides[pl.ds(pl.multiple_of(16 * mask, 8), 8), :]
 
 
 def first_kernel(slots, *refs):
-    (own, pair, near, *sides), (embed_t, head, head_t), (out, other, weights), scratch = (
-        refs[0:19], refs[19:22], refs[22:25], refs[25:28])
+    (own, own_y, one, *pieces), mats, (out, other, weights, sides), scratch = (
+        refs[0:7], refs[7:10], refs[10:14], refs[14:17])
+    start = 0
+    for piece in pieces:
+        sides[start : start + piece.shape[0], :] = piece[...]
+        start += piece.shape[0]
     learner_weights(slots, sides, weights)
-    outs = (out, out, other)
-
-    def add(index, rows, value):
-        if index == 1:
-            outs[index][rows, :] += value
-        else:
-            outs[index][rows, :] = value
-
-    side = jnp.concatenate([sides[0][...], sides[2][...], sides[4][...]], axis=1)
-    work(slots, (own[...], pair[...], near[...]), side, weights, embed_t, head, head_t, *scratch, add)
-
-
-def second_kernel(slots, *refs):
-    (cross, mid, end, side_cross, side_mid, side_end, weights, partial, other) = refs[0:9]
-    (embed_t, head, head_t), (out, far), scratch = refs[9:12], refs[12:14], refs[14:17]
 
     def add(index, rows, value):
         if index == 0:
-            out[rows, :] = partial[rows, :] + (other[rows, :] + value)
+            out[rows, :] = value
+        elif index == 1:
+            out[rows, :] += value
         else:
-            far[rows, :] = value
-
-    side = jnp.concatenate([side_cross[...], choose(side_mid, side_end)], axis=1)
-    work(
-        slots, (cross[...], mid[...] + end[...]), side, weights, embed_t, head, head_t, *scratch, add
-    )
-
-
-def third_kernel(slots, *refs):
-    (mid_a, end_a, mid_b, end_b, smid_a, send_a, smid_b, send_b, weights, far) = refs[0:10]
-    (embed_t, head, head_t), (out, last), scratch = refs[10:13], refs[13:15], refs[15:18]
+            other[rows, :] = value
+
+    side = jnp.concatenate([side_of(sides, *at) for at in ((0, 0), (0, 1), (1, 0))], axis=1)
+    work(slots, (own[...], own_y[...], one[...]), side, weights, *mats, *scratch, add)
+
+
+def second_kernel(slots, *refs):
+    (one_y, two, sides, weights, one_sum), mats, (out, other), scratch = (
+        refs[0:5], refs[5:8], refs[8:10], refs[10:13])
 
     def add(index, rows, value):
         if index == 0:
-            out[rows, :] = far[rows, :] + value
+            out[rows, :] = one_sum[rows, :] + value
         else:
-            last[rows, :] = value
-
-    side = jnp.concatenate([choose(smid_a, send_a), choose(smid_b, send_b)], axis=1)
-    work(
-        slots, (mid_a[...] + end_a[...], mid_b[...] + end_b[...]), side, weights,
-        embed_t, head, head_t, *scratch, add,
-    )
+            other[rows, :] = value
+
+    side = jnp.concatenate([side_of(sides, 1, 1), side_of(sides, 2, 0)], axis=1)
+    work(slots, (one_y[...], two[...]), side, weights, *mats, *scratch, add)
+
+
+def third_kernel(slots, *refs):
+    (two_y, three, sides, weights, own_sum, two_sum), mats, (out, other), scratch = (
+        refs[0:6], refs[6:9], refs[9:11], refs[11:14])
+
+    def add(index, rows, value):
+        if index == 0:
+            out[rows, :] = own_sum[rows, :] + (two_sum[rows, :] + value)
+        else:
+            other[rows, :] = value
+
+    side = jnp.concatenate([side_of(sides, 2, 1), side_of(sides, 3, 0)], axis=1)
+    work(slots, (two_y[...], three[...]), side, weights, *mats, *scratch, add)
 
 
 def fourth_kernel(slots, *refs):
-    (mid, end, side_mid, side_end, weights, half, far, last) = refs[0:8]
-    (embed_t, head, head_t), out, scratch = refs[8:11], refs[11], refs[12:15]
+    (three_y, sides, weights, even_sum, one_sum, three_sum), mats, out, scratch = (
+        refs[0:6], refs[6:9], refs[9], refs[10:13])
 
     def add(index, rows, value):
-        out[rows, :] = (half[rows, :] + (far[rows, :] + (last[rows, :] + value))).astype(BF16)
-
-    work(
-        slots, (mid[...] + end[...],), choose(side_mid, side_end), weights,
-        embed_t, head, head_t, *scratch, add,
-    )
+        out[rows, :] = (
+            even_sum[rows, :] + (one_sum[rows, :] + (three_sum[rows, :] + value))
+        ).astype(BF16)
+
+    work(slots, (three_y[...],), side_of(sides, 3, 1), weights, *mats, *scratch, add)
 
 
 def local_kernel(slots, frames, side, weights, embed_t, head, head_t, out, *scratch):
@@ -293,6 +355,7 @@
             pltpu.VMEM((width, rows), BF16),
         ],
         compiler_params=params(32),
+        cost_estimate=cost(1.2 * blocks + 0.4),
         name=name,
     )(*args, *mats)
 
@@ -330,57 +393,54 @@
         in_specs=[VMEM] * 9,
         out_specs=(VMEM,) * 7,
         compiler_params=params(32),
+        cost_estimate=cost(3.4),
         name="update",
     )(mine, theirs, *args)
 
 
 def gathered_grads(slots, n_cores, own, side, mats):
-    flip = [(place, place ^ 1) for place in range(8)]
-    ends = [pair for pair in flip if pair[0] in (0, 1, 6, 7)]
-    mids = [pair for pair in flip if pair[0] in (2, 3, 4, 5)]
-    near = [(place, place ^ 2) for place in range(8)]
-    inner = [(2, 4), (3, 5), (4, 2), (5, 3)]
-    outer = [(2, 0), (3, 1), (4, 6), (5, 7)]
+    across = [(place, place ^ 1) for place in range(8)]
+    along = [(place, (place + 2) % 8) for place in range(8)]
 
     def send(array, pairs):
         return lax.ppermute(array, "hst", pairs)
 
-    pair = send(own, flip)
-    close = send(own, near)
-    second_mid = send(own, inner)
-    sides = [side] + [
-        lax.ppermute(side, AXES, [(place, place ^ mask) for place in range(8 * n_cores)])
-        for mask in range(1, 8 * n_cores)
-    ]
-    cross = send(close, flip)
-    second_end = send(second_mid, outer)
-    third_mid = send(close, inner)
-    second_mid_y = send(second_mid, mids)
-    second_end_y = send(second_end, ends)
-    third_end = send(third_mid, outer)
-    third_mid_y = send(third_mid, mids)
-    third_end_y = send(third_end, ends)
+    one = send(own, along)
+    own_y = send(own, across)
+    pieces = [side]
+    for scale in (1, 4):
+        held = pieces[0] if scale == 1 else jnp.concatenate(pieces, axis=0)
+        if scale == 4:
+            held, one, own_y = lax.optimization_barrier((held, one, own_y))
+        pieces = [held] + [
+            lax.ppermute(held, AXES, [(at, at ^ (scale * step)) for at in range(8 * n_cores)])
+            for step in (1, 2, 3)
+        ]
+    two = send(one, along)
+    one_y = send(one, across)
+    three = send(two, along)
+    two_y = send(two, across)
+    three_y = send(three, across)
 
     width, feats = mats[0].shape
     grads = jax.ShapeDtypeStruct((feats + mats[2].shape[0], width), F32)
     weights = jax.ShapeDtypeStruct((8 * n_cores, 128), F32)
-    by = [sides[n_cores * mask] for mask in range(8)]
-    partial, other, weights = call(
-        first_kernel, "first", slots, 3, (own, pair, close, *sides), mats, (grads, grads, weights)
-    )
-    half, far = call(
-        second_kernel, "second", slots, 2,
-        (cross, second_mid, second_end, by[3], by[6], by[4], weights, partial, other), mats,
+    sides = jax.ShapeDtypeStruct((64 * n_cores, side.shape[1]), F32)
+    own_sum, one_sum, weights, sides = call(
+        first_kernel, "first", slots, 3, (own, own_y, one, *pieces), mats,
+        (grads, grads, weights, sides),
+    )
+    one_sum, two_sum = call(
+        second_kernel, "second", slots, 2, (one_y, two, sides, weights, one_sum), mats,
         (grads, grads),
     )
-    far, last = call(
-        third_kernel, "third", slots, 2,
-        (second_mid_y, second_end_y, third_mid, third_end, by[7], by[5], by[4], by[6], weights, far),
-        mats, (grads, grads),
+    even_sum, three_sum = call(
+        third_kernel, "third", slots, 2, (two_y, three, sides, weights, own_sum, two_sum), mats,
+        (grads, grads),
     )
     return call(
         fourth_kernel, "fourth", slots, 1,
-        (third_mid_y, third_end_y, by[5], by[7], weights, half, far, last), mats,
+        (three_y, sides, weights, even_sum, one_sum, three_sum), mats,
         jax.ShapeDtypeStruct(grads.shape, BF16),
     )
 
@@ -394,11 +454,10 @@
     rows = traj * slots
     own = observations.reshape(rows, feats)
     value_row = master_value.reshape(1, -1)
-    side = actor(
-        own, lengths.reshape(1, -1), assign.reshape(1, -1), actions, rewards,
-        actor_embed, actor_policy,
-    )
-    mats = prepare(master_embed, master_policy, value_row)
+    side, *mats = prepare(
+        lengths.reshape(1, -1), assign.reshape(1, -1), actions, rewards, own,
+        actor_embed, actor_policy, master_embed, master_policy, value_row,
+    )
     if n_hst == 8 and n_cores == 2 and rows == BLOCK:
         mine = gathered_grads(slots, n_cores, own, side, mats)
         theirs = lax.ppermute(mine, "cores", [(0, 1), (1, 0)])

time: 94.7 us -> 53.4 us (0.56)
  starting transfers between devices: 46.4 us -> 16 us
  waiting for transfers between devices: 21.1 us -> 14.2 us
  local copies, waits for them, and re-layouts: 9.18 us -> 3.48 us
  Pallas kernels: 16.5 us -> 18.5 us
    ppermute x15 -> x6, starting transfers between devices: 29.2 us -> 6.39 us  [gathered_grads(): lax.ppermute(held, AXES, [(at, at ^ scale * step) for at in range(8 * n_c...]
    ppermute x15 -> x6, waiting for transfers between devices: 12.2 us -> 3.35 us  [gathered_grads(): lax.ppermute(held, AXES, [(at, at ^ scale * step) for at in range(8 * n_c...]
    ppermute x11 -> x7, starting transfers between devices: 17.1 us -> 9.58 us  [send(): return lax.ppermute(array, 'hst', pairs)]
    unnamed x36, local copies, waits for them, and re-layouts: 9.18 us -> 3.48 us
    ppermute x11 -> x7, waiting for transfers between devices: 5.87 us -> 7.74 us  [send(): return lax.ppermute(array, 'hst', pairs)]
    pallas_call x2, Pallas kernels: 1.22 us -> 2.27 us  [the longest x1 1.66 us: prepare(): pl.pallas_call(prepare_kernel, out_shape=(jax.ShapeDtypeStruct((8, rows),...]
  transfers between devices with their start and end apart: 27 -> 14, of which waited for: 14 -> 7; matrix products, arithmetic and copies ran while one was open for 0% -> 0% of each run, Pallas kernels for 12% -> 24%
where the time goes in v3:
time: 53.4 us; the launch traced here: 53.1 us
  Pallas kernels  18.5 us (35%)
  starting transfers between devices  16 us (30%)
  waiting for transfers between devices  14.2 us (27%)
  local copies, waits for them, and re-layouts  3.48 us (7%)
  between operations  0.85 us (2%)
    pallas_call x4, Pallas kernels, call(): pl.pallas_call(functools.partial(kernel, slots), out_shape=outs, in_specs...  12.8 us
    ppermute x7, starting transfers between devices, send(): return lax.ppermute(array, 'hst', pairs)  9.58 us
    ppermute x7, waiting for transfers between devices, send(): return lax.ppermute(array, 'hst', pairs)  7.74 us
    ppermute x6, starting transfers between devices, gathered_grads(): lax.ppermute(held, AXES, [(at, at ^ scale * step) for at in range(8 * n_c...  6.39 us
    unnamed x36, local copies, waits for them, and re-layouts  3.48 us
    pallas_call x1, Pallas kernels, update(): pl.pallas_call(functools.partial(update_kernel, feats, nact), out_shape=(...  3.47 us
    ppermute x6, waiting for transfers between devices, gathered_grads(): lax.ppermute(held, AXES, [(at, at ^ scale * step) for at in range(8 * n_c...  3.35 us
    ppermute x1, waiting for transfers between devices, body(): theirs = lax.ppermute(mine, 'cores', [(0, 1), (1, 0)])  3.07 us
  transfers between devices with their start and end apart: 14, of which 7 were waited for; matrix products, arithmetic and copies ran while one was open for 0% of the time, Pallas kernels for 24%

profile of v3, /device:TPU:0, one launch (start us, length us, event | category | flops | bytes accessed | tf_op | source)
XLA Modules:
  0.0 53.1 jit_solution(17602265356773371018)
XLA Ops:
  0.7 3.1 %collective-permute-start.3 = (bf16[256,512]{1,0:T(8,128)(2,1)}, bf16[256,512]{1,0:T(8,128)(2,1)}, u32[]{:S(2)}, u32[]{:S(2)}) collective-permute-start(bf16[256,512]{1,0:T(8,128)(2,1)} %bitcast.7), channel_id=1, source_target_pairs={{0,4},{2,6},{4,8},{6,10},{8,12},{10,14},{12,0},{14,2},{1,5},{3,7},... | collective-permute-start | bytes 786440 | tf_op jit(solution)/shard_map/ppermute | solution.py:406
  3.8 1.5 %collective-permute-start.4 = (bf16[256,512]{1,0:T(8,128)(2,1)}, bf16[256,512]{1,0:T(8,128)(2,1)}, u32[]{:S(2)}, u32[]{:S(2)}) collective-permute-start(bf16[256,512]{1,0:T(8,128)(2,1)} %bitcast.8), channel_id=1, source_target_pairs={{0,2},{2,0},{4,6},{6,4},{8,10},{10,8},{12,14},{14,12},{1,3},{3,1},... | collective-permute-start | bytes 786440 | tf_op jit(solution)/shard_map/ppermute | solution.py:406
  5.3 0.6 %select.1 = (f32[16,256]{1,0:T(8,128)}, f32[16,256]{1,0:T(8,128)}) custom-call(), custom_call_target="tpu_custom_call" | custom-call | flops 6600000000 | tf_op jit(solution)/shard_map/select/pallas_call | solution.py:53
  6.0 1.0 %copy-done.3 = f32[1024,128]{1,0:T(8,128)S(1)} copy-done((f32[1024,128]{1,0:T(8,128)S(1)}, f32[1024,128]{1,0:T(8,128)}, u32[]{:S(2)}) %copy-start.3) | copy-done | bytes 524312
  7.0 0.9 %copy-done.7 = bf16[16,16,512]{2,1,0:T(8,128)(2,1)S(1)} copy-done((bf16[16,16,512]{2,1,0:T(8,128)(2,1)S(1)}, bf16[16,16,512]{2,1,0:T(8,128)(2,1)}, u32[]{:S(2)}) %copy-start.7) | copy-done | bytes 262168
  8.0 0.7 %copy-done.16 = f32[16,256]{1,0:T(8,128)S(1)} copy-done((f32[16,256]{1,0:T(8,128)S(1)}, f32[16,256]{1,0:T(8,128)}, u32[]{:S(2)}) %copy-start.16) | copy-done | bytes 16408
  8.7 0.7 %copy-done.17 = f32[16,256]{1,0:T(8,128)S(1)} copy-done((f32[16,256]{1,0:T(8,128)S(1)}, f32[16,256]{1,0:T(8,128)}, u32[]{:S(2)}) %copy-start.17) | copy-done | bytes 16408
  9.4 1.7 %prepare.1 = (f32[8,256]{1,0:T(8,128)S(1)}, bf16[1024,512]{1,0:T(8,128)(2,1)S(1)}, bf16[1024,144]{1,0:T(8,128)(2,1)S(1)}, bf16[144,1024]{1,0:T(8,128)(2,1)S(1)}) custom-call(s32[1,16]{1,0:T(1,128)S(1)} %bitcast.14, s32[1,16]{1,0:T(1,128)S(1)} %bitcast.15, s32[16,16]{1,0:T(8,128)S(1)} %copy-done.10, f32[16,16]{1,0:T(8,128)S(1)} %copy-done.11, ...), custom_call_target="tpu_custom_call" | custom-call | flops 3300000000 | tf_op jit(solution)/shard_map/prepare/pallas_call | solution.py:133
  11.1 0.1 collective-permute-start
  11.2 0.6 %collective-permute-start.1 = (f32[8,256]{1,0:T(8,128)S(1)}, f32[8,256]{1,0:T(8,128)S(1)}, u32[]{:S(2)}, u32[]{:S(2)}) collective-permute-start(f32[8,256]{1,0:T(8,128)S(1)} %get-tuple-element.33), channel_id=1, source_target_pairs={{0,2},{1,3},{2,0},{3,1},{4,6},{5,7},{6,4},{7,5},{8,10},{9,11},{10,... | collective-permute-start | bytes 24584 | tf_op jit(solution)/shard_map/ppermute | solution.py:416
  11.7 1.3 %collective-permute-start.2 = (f32[8,256]{1,0:T(8,128)S(1)}, f32[8,256]{1,0:T(8,128)S(1)}, u32[]{:S(2)}, u32[]{:S(2)}) collective-permute-start(f32[8,256]{1,0:T(8,128)S(1)} %get-tuple-element.33), channel_id=1, source_target_pairs={{0,3},{1,2},{2,1},{3,0},{4,7},{5,6},{6,5},{7,4},{8,11},{9,10},{10,... | collective-permute-start | bytes 24584 | tf_op jit(solution)/shard_map/ppermute | solution.py:416
  13.0 1.9 %collective-permute-done.1 = f32[8,256]{1,0:T(8,128)S(1)} collective-permute-done((f32[8,256]{1,0:T(8,128)S(1)}, f32[8,256]{1,0:T(8,128)S(1)}, u32[]{:S(2)}, u32[]{:S(2)}) %collective-permute-start.1) | collective-permute-done | bytes 8224 | tf_op jit(solution)/shard_map/ppermute | solution.py:416
  14.9 2.7 %collective-permute-start.10 = (f32[32,256]{1,0:T(8,128)S(1)}, f32[32,256]{1,0:T(8,128)S(1)}, u32[]{:S(2)}, u32[]{:S(2)}) collective-permute-start(f32[32,256]{1,0:T(8,128)S(1)} %pad_maximum_fusion.refs_3_), channel_id=1, source_target_pairs={{0,12},{1,13},{2,14},{3,15},{4,8},{5,9},{6,10},{7,11},{8,4},{9,5},... | collective-permute-start | bytes 98312 | tf_op jit(solution)/shard_map/ppermute | solution.py:416
  17.6 0.5 %collective-permute-start.8 = (f32[32,256]{1,0:T(8,128)S(1)}, f32[32,256]{1,0:T(8,128)S(1)}, u32[]{:S(2)}, u32[]{:S(2)}) collective-permute-start(f32[32,256]{1,0:T(8,128)S(1)} %pad_maximum_fusion.refs_3_), channel_id=1, source_target_pairs={{0,4},{1,5},{2,6},{3,7},{4,0},{5,1},{6,2},{7,3},{8,12},{9,13},{10,... | collective-permute-start | bytes 98312 | tf_op jit(solution)/shard_map/ppermute | solution.py:416
  18.1 1.2 %collective-permute-start.9 = (f32[32,256]{1,0:T(8,128)S(1)}, f32[32,256]{1,0:T(8,128)S(1)}, u32[]{:S(2)}, u32[]{:S(2)}) collective-permute-start(f32[32,256]{1,0:T(8,128)S(1)} %pad_maximum_fusion.refs_3_), channel_id=1, source_target_pairs={{0,8},{1,9},{2,10},{3,11},{4,12},{5,13},{6,14},{7,15},{8,0},{9,1},... | collective-permute-start | bytes 98312 | tf_op jit(solution)/shard_map/ppermute | solution.py:416
  19.4 0.7 %collective-permute-start.5 = (bf16[256,512]{1,0:T(8,128)(2,1)}, bf16[256,512]{1,0:T(8,128)(2,1)S(1)}, u32[]{:S(2)}, u32[]{:S(2)}) collective-permute-start(bf16[256,512]{1,0:T(8,128)(2,1)} %collective-permute-done.3.refs_2_), channel_id=1, source_target_pairs={{0,4},{2,6},{4,8},{6,10},{8,12},{10,14},{12,0},{14,2},{1,5},{3,7},... | collective-permute-start | bytes 786440 | tf_op jit(solution)/shard_map/ppermute | solution.py:406
  20.1 1.4 %collective-permute-start.12 = (bf16[256,512]{1,0:T(8,128)(2,1)}, bf16[256,512]{1,0:T(8,128)(2,1)S(1)}, u32[]{:S(2)}, u32[]{:S(2)}) collective-permute-start(bf16[256,512]{1,0:T(8,128)(2,1)} %collective-permute-done.3.refs_2_), channel_id=1, source_target_pairs={{0,2},{2,0},{4,6},{6,4},{8,10},{10,8},{12,14},{14,12},{1,3},{3,1},... | collective-permute-start | bytes 786440 | tf_op jit(solution)/shard_map/ppermute | solution.py:406
  21.5 0.4 collective-permute-done.8.refs_4_
  21.9 1.1 %collective-permute-done.9.refs_5_ = f32[32,256]{1,0:T(8,128)S(1)} collective-permute-done((f32[32,256]{1,0:T(8,128)S(1)}, f32[32,256]{1,0:T(8,128)S(1)}, u32[]{:S(2)}, u32[]{:S(2)}) %collective-permute-start.9) | collective-permute-done | bytes 32800 | tf_op jit(solution)/shard_map/ppermute | solution.py:416
  23.0 4.9 %first.1 = (f32[656,1024]{1,0:T(8,128)S(1)}, f32[656,1024]{1,0:T(8,128)S(1)}, f32[16,128]{1,0:T(8,128)S(1)}, f32[128,256]{1,0:T(8,128)S(1)}) custom-call(bf16[256,512]{1,0:T(8,128)(2,1)S(1)} %bitcast.10, bf16[256,512]{1,0:T(8,128)(2,1)} %collective-permute-done.4.refs_1_, bf16[256,512]{1,0:T(8,128)(2,1)} %collective-permute-done.3.refs_2_, ...), custom_call_target="tpu_custom_call" | custom-call | flops 4400000000 | tf_op jit(solution)/shard_map/first/pallas_call | solution.py:347
  27.9 1.4 %collective-permute-done.5.refs_1_ = bf16[256,512]{1,0:T(8,128)(2,1)S(1)} collective-permute-done((bf16[256,512]{1,0:T(8,128)(2,1)}, bf16[256,512]{1,0:T(8,128)(2,1)S(1)}, u32[]{:S(2)}, u32[]{:S(2)}) %collective-permute-start.5) | collective-permute-done | bytes 262176 | tf_op jit(solution)/shard_map/ppermute | solution.py:406
  29.2 0.7 %collective-permute-start.6 = (bf16[256,512]{1,0:T(8,128)(2,1)S(1)}, bf16[256,512]{1,0:T(8,128)(2,1)S(1)}, u32[]{:S(2)}, u32[]{:S(2)}) collective-permute-start(bf16[256,512]{1,0:T(8,128)(2,1)S(1)} %collective-permute-done.5.refs_1_), channel_id=1, source_target_pairs={{0,4},{2,6},{4,8},{6,10},{8,12},{10,14},{12,0},{14,2},{1,5},{3,7},... | collective-permute-start | bytes 786440 | tf_op jit(solution)/shard_map/ppermute | solution.py:406
  29.9 0.9 %collective-permute-start.11 = (bf16[256,512]{1,0:T(8,128)(2,1)S(1)}, bf16[256,512]{1,0:T(8,128)(2,1)S(1)}, u32[]{:S(2)}, u32[]{:S(2)}) collective-permute-start(bf16[256,512]{1,0:T(8,128)(2,1)S(1)} %collective-permute-done.5.refs_1_), channel_id=1, source_target_pairs={{0,2},{2,0},{4,6},{6,4},{8,10},{10,8},{12,14},{14,12},{1,3},{3,1},... | collective-permute-start | bytes 786440 | tf_op jit(solution)/shard_map/ppermute | solution.py:406
  30.9 2.9 %second.1 = (f32[656,1024]{1,0:T(8,128)S(1)}, f32[656,1024]{1,0:T(8,128)S(1)}) custom-call(bf16[256,512]{1,0:T(8,128)(2,1)S(1)} %collective-permute-done.12.refs_0_, bf16[256,512]{1,0:T(8,128)(2,1)S(1)} %collective-permute-done.5.refs_1_, f32[128,256]{1,0:T(8,128)S(1)} %get-tuple-element.40.refs_2_.refs_1_, f32[16,128]{1,0:T(8,128)S(1)} %get-tuple-element.41.refs_3_.refs_2_, ...), custom_call_target="tpu_custom_call" | custom-call | flops 3080000000 | tf_op jit(solution)/shard_map/second/pallas_call | solution.py:347
  33.7 4.2 %collective-permute-done.6.refs_1_ = bf16[256,512]{1,0:T(8,128)(2,1)S(1)} collective-permute-done((bf16[256,512]{1,0:T(8,128)(2,1)S(1)}, bf16[256,512]{1,0:T(8,128)(2,1)S(1)}, u32[]{:S(2)}, u32[]{:S(2)}) %collective-permute-start.6) | collective-permute-done | bytes 262176 | tf_op jit(solution)/shard_map/ppermute | solution.py:406
  37.9 1.3 %collective-permute-start.7 = (bf16[256,512]{1,0:T(8,128)(2,1)S(1)}, bf16[256,512]{1,0:T(8,128)(2,1)S(1)}, u32[]{:S(2)}, u32[]{:S(2)}) collective-permute-start(bf16[256,512]{1,0:T(8,128)(2,1)S(1)} %collective-permute-done.6.refs_1_), channel_id=1, source_target_pairs={{0,2},{2,0},{4,6},{6,4},{8,10},{10,8},{12,14},{14,12},{1,3},{3,1},... | collective-permute-start | bytes 786440 | tf_op jit(solution)/shard_map/ppermute | solution.py:406
  39.2 3.0 %third.1 = (f32[656,1024]{1,0:T(8,128)S(1)}, f32[656,1024]{1,0:T(8,128)S(1)}) custom-call(bf16[256,512]{1,0:T(8,128)(2,1)S(1)} %collective-permute-done.11.refs_0_, bf16[256,512]{1,0:T(8,128)(2,1)S(1)} %collective-permute-done.6.refs_1_, f32[128,256]{1,0:T(8,128)S(1)} %get-tuple-element.40.refs_2_.refs_1_, f32[16,128]{1,0:T(8,128)S(1)} %get-tuple-element.41.refs_3_.refs_2_, ...), custom_call_target="tpu_custom_call" | custom-call | flops 3080000000 | tf_op jit(solution)/shard_map/third/pallas_call | solution.py:347
  42.1 2.2 %collective-permute-done.7.refs_0_ = bf16[256,512]{1,0:T(8,128)(2,1)S(1)} collective-permute-done((bf16[256,512]{1,0:T(8,128)(2,1)S(1)}, bf16[256,512]{1,0:T(8,128)(2,1)S(1)}, u32[]{:S(2)}, u32[]{:S(2)}) %collective-permute-start.7) | collective-permute-done | bytes 262176 | tf_op jit(solution)/shard_map/ppermute | solution.py:406
  44.3 2.1 %fourth.1.mine = bf16[656,1024]{1,0:T(8,128)(2,1)S(1)} custom-call(bf16[256,512]{1,0:T(8,128)(2,1)S(1)} %collective-permute-done.7.refs_0_, f32[128,256]{1,0:T(8,128)S(1)} %get-tuple-element.40.refs_2_.refs_1_, f32[16,128]{1,0:T(8,128)S(1)} %get-tuple-element.41.refs_3_.refs_2_, f32[656,1024]{1,0:T(8,128)S(1)} %get-tuple-element.45.refs_3_, ...), custom_call_target="tpu_custom_call" | custom-call | flops 1760000000 | tf_op jit(solution)/shard_map/fourth/pallas_call | solution.py:347
  46.4 0.1 collective-permute-start.13
  46.5 3.1 %collective-permute-done.13.theirs = bf16[656,1024]{1,0:T(8,128)(2,1)S(1)} collective-permute-done((bf16[656,1024]{1,0:T(8,128)(2,1)S(1)}, bf16[656,1024]{1,0:T(8,128)(2,1)S(1)}, u32[]{:S(2)}, u32[]{:S(2)}) %collective-permute-start.13) | collective-permute-done | bytes 1343520 | tf_op jit(solution)/shard_map/ppermute | solution.py:463
  49.6 3.5 %update.1 = (bf16[256,128]{1,0:T(8,128)(2,1)}, f32[512,1024]{1,0:T(8,128)}, f32[1024,128]{1,0:T(8,128)}, f32[1,1024]{1,0:T(1,128)}, f32[512,1024]{1,0:T(8,128)}, /*index=5*/f32[1024,128]{1,0:T(8,128)}, f32[1,1024]{1,0:T(1,128)}) custom-call(bf16[656,1024]{1,0:T(8,128)(2,1)S(1)} %fourth.1.mine, bf16[656,1024]{1,0:T(8,128)(2,1)S(1)} %collective-permute-done.13.theirs, ...), custom_call_target="tpu_custom_call" | custom-call | flops 3740000000 | tf_op jit(solution)/shard_map/update/pallas_call | solution.py:390
  (40 shorter events, 0.1 us)
Async XLA Ops:
  0.6 5.3 %copy-start = (f32[512,1024]{1,0:T(8,128)S(1)}, f32[512,1024]{1,0:T(8,128)}, u32[]{:S(2)}) copy-start(f32[512,1024]{1,0:T(8,128)} %master_embed.1) | copy-start | bytes 6291460
  0.6 5.3 %copy-start.2 = (bf16[512,1024]{1,0:T(8,128)(2,1)S(1)}, bf16[512,1024]{1,0:T(8,128)(2,1)}, u32[]{:S(2)}) copy-start(bf16[512,1024]{1,0:T(8,128)(2,1)} %actor_embed_at.1) | copy-start | bytes 3145732
  0.7 5.3 %copy-start.6 = (bf16[1024,128]{1,0:T(8,128)(2,1)S(1)}, bf16[1024,128]{1,0:T(8,128)(2,1)}, u32[]{:S(2)}) copy-start(bf16[1024,128]{1,0:T(8,128)(2,1)} %actor_policy_at.1) | copy-start | bytes 786436
  0.7 5.3 %copy-start.10 = (s32[16,16]{1,0:T(8,128)S(1)}, s32[16,16]{1,0:T(8,128)}, u32[]{:S(2)}) copy-start(s32[16,16]{1,0:T(8,128)} %actions_at.1) | copy-start | bytes 3076
  0.7 5.3 %copy-start.11 = (f32[16,16]{1,0:T(8,128)S(1)}, f32[16,16]{1,0:T(8,128)}, u32[]{:S(2)}) copy-start(f32[16,16]{1,0:T(8,128)} %rewards_at.1) | copy-start | bytes 3076
  0.7 5.3 %copy-start.12 = (f32[1024]{0:T(1024)S(1)}, f32[1024]{0:T(1024)}, u32[]{:S(2)}) copy-start(f32[1024]{0:T(1024)} %param.23) | copy-start | bytes 12292
  0.7 5.3 %copy-start.14 = (s32[16]{0:T(128)S(1)}, s32[16]{0:T(128)}, u32[]{:S(2)}) copy-start(s32[16]{0:T(128)} %param.15) | copy-start | bytes 196
  0.7 5.3 %copy-start.15 = (s32[16]{0:T(128)S(1)}, s32[16]{0:T(128)}, u32[]{:S(2)}) copy-start(s32[16]{0:T(128)} %param.18) | copy-start | bytes 196
  0.7 14.2 %collective-permute-start.3 = (bf16[256,512]{1,0:T(8,128)(2,1)}, bf16[256,512]{1,0:T(8,128)(2,1)}, u32[]{:S(2)}, u32[]{:S(2)}) collective-permute-start(bf16[256,512]{1,0:T(8,128)(2,1)} %bitcast.7), channel_id=1, source_target_pairs={{0,4},{2,6},{4,8},{6,10},{8,12},{10,14},{12,0},{14,2},{1,5},{3,7},... | collective-permute-start | bytes 786440 | tf_op jit(solution)/shard_map/ppermute | solution.py:406
  3.8 11.1 %collective-permute-start.4 = (bf16[256,512]{1,0:T(8,128)(2,1)}, bf16[256,512]{1,0:T(8,128)(2,1)}, u32[]{:S(2)}, u32[]{:S(2)}) collective-permute-start(bf16[256,512]{1,0:T(8,128)(2,1)} %bitcast.8), channel_id=1, source_target_pairs={{0,2},{2,0},{4,6},{6,4},{8,10},{10,8},{12,14},{14,12},{1,3},{3,1},... | collective-permute-start | bytes 786440 | tf_op jit(solution)/shard_map/ppermute | solution.py:406
  6.0 1.0 %copy-start.3 = (f32[1024,128]{1,0:T(8,128)S(1)}, f32[1024,128]{1,0:T(8,128)}, u32[]{:S(2)}) copy-start(f32[1024,128]{1,0:T(8,128)} %master_policy.1) | copy-start | bytes 1572868
  7.0 0.9 %copy-start.7 = (bf16[16,16,512]{2,1,0:T(8,128)(2,1)S(1)}, bf16[16,16,512]{2,1,0:T(8,128)(2,1)}, u32[]{:S(2)}) copy-start(bf16[16,16,512]{2,1,0:T(8,128)(2,1)} %param.14) | copy-start | bytes 786436
  8.0 0.7 %copy-start.16 = (f32[16,256]{1,0:T(8,128)S(1)}, f32[16,256]{1,0:T(8,128)}, u32[]{:S(2)}) copy-start(f32[16,256]{1,0:T(8,128)} %get-tuple-element.31.spread) | copy-start | bytes 49156
  8.7 0.7 %copy-start.17 = (f32[16,256]{1,0:T(8,128)S(1)}, f32[16,256]{1,0:T(8,128)}, u32[]{:S(2)}) copy-start(f32[16,256]{1,0:T(8,128)} %get-tuple-element.32.owner) | copy-start | bytes 49156
  9.4 13.5 %copy-start.8 = (bf16[16,16,512]{2,1,0:T(8,128)(2,1)S(1)}, bf16[16,16,512]{2,1,0:T(8,128)(2,1)}, u32[]{:S(2)}) copy-start(bf16[16,16,512]{2,1,0:T(8,128)(2,1)} %param.14) | copy-start | bytes 786436
  11.1 1.9 %collective-permute-start = (f32[8,256]{1,0:T(8,128)S(1)}, f32[8,256]{1,0:T(8,128)S(1)}, u32[]{:S(2)}, u32[]{:S(2)}) collective-permute-start(f32[8,256]{1,0:T(8,128)S(1)} %get-tuple-element.33), channel_id=1, source_target_pairs={{0,1},{1,0},{2,3},{3,2},{4,5},{5,4},{6,7},{7,6},{8,9},{9,8},{10,11... | collective-permute-start | bytes 24584 | tf_op jit(solution)/shard_map/ppermute | solution.py:416
  11.2 3.7 %collective-permute-start.1 = (f32[8,256]{1,0:T(8,128)S(1)}, f32[8,256]{1,0:T(8,128)S(1)}, u32[]{:S(2)}, u32[]{:S(2)}) collective-permute-start(f32[8,256]{1,0:T(8,128)S(1)} %get-tuple-element.33), channel_id=1, source_target_pairs={{0,2},{1,3},{2,0},{3,1},{4,6},{5,7},{6,4},{7,5},{8,10},{9,11},{10,... | collective-permute-start | bytes 24584 | tf_op jit(solution)/shard_map/ppermute | solution.py:416
  11.7 3.2 %collective-permute-start.2 = (f32[8,256]{1,0:T(8,128)S(1)}, f32[8,256]{1,0:T(8,128)S(1)}, u32[]{:S(2)}, u32[]{:S(2)}) collective-permute-start(f32[8,256]{1,0:T(8,128)S(1)} %get-tuple-element.33), channel_id=1, source_target_pairs={{0,3},{1,2},{2,1},{3,0},{4,7},{5,6},{6,5},{7,4},{8,11},{9,10},{10,... | collective-permute-start | bytes 24584 | tf_op jit(solution)/shard_map/ppermute | solution.py:416
  14.9 6.6 %collective-permute-start.10 = (f32[32,256]{1,0:T(8,128)S(1)}, f32[32,256]{1,0:T(8,128)S(1)}, u32[]{:S(2)}, u32[]{:S(2)}) collective-permute-start(f32[32,256]{1,0:T(8,128)S(1)} %pad_maximum_fusion.refs_3_), channel_id=1, source_target_pairs={{0,12},{1,13},{2,14},{3,15},{4,8},{5,9},{6,10},{7,11},{8,4},{9,5},... | collective-permute-start | bytes 98312 | tf_op jit(solution)/shard_map/ppermute | solution.py:416
  17.6 4.3 %collective-permute-start.8 = (f32[32,256]{1,0:T(8,128)S(1)}, f32[32,256]{1,0:T(8,128)S(1)}, u32[]{:S(2)}, u32[]{:S(2)}) collective-permute-start(f32[32,256]{1,0:T(8,128)S(1)} %pad_maximum_fusion.refs_3_), channel_id=1, source_target_pairs={{0,4},{1,5},{2,6},{3,7},{4,0},{5,1},{6,2},{7,3},{8,12},{9,13},{10,... | collective-permute-start | bytes 98312 | tf_op jit(solution)/shard_map/ppermute | solution.py:416
  18.1 4.8 %collective-permute-start.9 = (f32[32,256]{1,0:T(8,128)S(1)}, f32[32,256]{1,0:T(8,128)S(1)}, u32[]{:S(2)}, u32[]{:S(2)}) collective-permute-start(f32[32,256]{1,0:T(8,128)S(1)} %pad_maximum_fusion.refs_3_), channel_id=1, source_target_pairs={{0,8},{1,9},{2,10},{3,11},{4,12},{5,13},{6,14},{7,15},{8,0},{9,1},... | collective-permute-start | bytes 98312 | tf_op jit(solution)/shard_map/ppermute | solution.py:416
  19.4 9.8 %collective-permute-start.5 = (bf16[256,512]{1,0:T(8,128)(2,1)}, bf16[256,512]{1,0:T(8,128)(2,1)S(1)}, u32[]{:S(2)}, u32[]{:S(2)}) collective-permute-start(bf16[256,512]{1,0:T(8,128)(2,1)} %collective-permute-done.3.refs_2_), channel_id=1, source_target_pairs={{0,4},{2,6},{4,8},{6,10},{8,12},{10,14},{12,0},{14,2},{1,5},{3,7},... | collective-permute-start | bytes 786440 | tf_op jit(solution)/shard_map/ppermute | solution.py:406
  20.1 10.8 %collective-permute-start.12 = (bf16[256,512]{1,0:T(8,128)(2,1)}, bf16[256,512]{1,0:T(8,128)(2,1)S(1)}, u32[]{:S(2)}, u32[]{:S(2)}) collective-permute-start(bf16[256,512]{1,0:T(8,128)(2,1)} %collective-permute-done.3.refs_2_), channel_id=1, source_target_pairs={{0,2},{2,0},{4,6},{6,4},{8,10},{10,8},{12,14},{14,12},{1,3},{3,1},... | collective-permute-start | bytes 786440 | tf_op jit(solution)/shard_map/ppermute | solution.py:406
  29.2 8.7 %collective-permute-start.6 = (bf16[256,512]{1,0:T(8,128)(2,1)S(1)}, bf16[256,512]{1,0:T(8,128)(2,1)S(1)}, u32[]{:S(2)}, u32[]{:S(2)}) collective-permute-start(bf16[256,512]{1,0:T(8,128)(2,1)S(1)} %collective-permute-done.5.refs_1_), channel_id=1, source_target_pairs={{0,4},{2,6},{4,8},{6,10},{8,12},{10,14},{12,0},{14,2},{1,5},{3,7},... | collective-permute-start | bytes 786440 | tf_op jit(solution)/shard_map/ppermute | solution.py:406
  29.9 9.2 %collective-permute-start.11 = (bf16[256,512]{1,0:T(8,128)(2,1)S(1)}, bf16[256,512]{1,0:T(8,128)(2,1)S(1)}, u32[]{:S(2)}, u32[]{:S(2)}) collective-permute-start(bf16[256,512]{1,0:T(8,128)(2,1)S(1)} %collective-permute-done.5.refs_1_), channel_id=1, source_target_pairs={{0,2},{2,0},{4,6},{6,4},{8,10},{10,8},{12,14},{14,12},{1,3},{3,1},... | collective-permute-start | bytes 786440 | tf_op jit(solution)/shard_map/ppermute | solution.py:406
  37.9 6.4 %collective-permute-start.7 = (bf16[256,512]{1,0:T(8,128)(2,1)S(1)}, bf16[256,512]{1,0:T(8,128)(2,1)S(1)}, u32[]{:S(2)}, u32[]{:S(2)}) collective-permute-start(bf16[256,512]{1,0:T(8,128)(2,1)S(1)} %collective-permute-done.6.refs_1_), channel_id=1, source_target_pairs={{0,2},{2,0},{4,6},{6,4},{8,10},{10,8},{12,14},{14,12},{1,3},{3,1},... | collective-permute-start | bytes 786440 | tf_op jit(solution)/shard_map/ppermute | solution.py:406
  44.3 5.3 %copy-start.1 = (f32[512,1024]{1,0:T(8,128)S(1)}, f32[512,1024]{1,0:T(8,128)}, u32[]{:S(2)}) copy-start(f32[512,1024]{1,0:T(8,128)} %embed_moment.1) | copy-start | bytes 6291460
  44.3 5.3 %copy-start.4 = (f32[1024,128]{1,0:T(8,128)S(1)}, f32[1024,128]{1,0:T(8,128)}, u32[]{:S(2)}) copy-start(f32[1024,128]{1,0:T(8,128)} %master_policy.1) | copy-start | bytes 1572868
  44.3 5.3 %copy-start.5 = (f32[1024,128]{1,0:T(8,128)S(1)}, f32[1024,128]{1,0:T(8,128)}, u32[]{:S(2)}) copy-start(f32[1024,128]{1,0:T(8,128)} %policy_moment.1) | copy-start | bytes 1572868
  44.3 5.3 %copy-start.9 = (bf16[256,512]{1,0:T(8,128)(2,1)S(1)}, bf16[256,512]{1,0:T(8,128)(2,1)}, u32[]{:S(2)}) copy-start(bf16[256,512]{1,0:T(8,128)(2,1)} %next_obs.1) | copy-start | bytes 786436
  44.3 5.3 %copy-start.13 = (f32[1024]{0:T(1024)S(1)}, f32[1024]{0:T(1024)}, u32[]{:S(2)}) copy-start(f32[1024]{0:T(1024)} %param.26) | copy-start | bytes 12292
  46.4 3.1 %collective-permute-start.13 = (bf16[656,1024]{1,0:T(8,128)(2,1)S(1)}, bf16[656,1024]{1,0:T(8,128)(2,1)S(1)}, u32[]{:S(2)}, u32[]{:S(2)}) collective-permute-start(bf16[656,1024]{1,0:T(8,128)(2,1)S(1)} %fourth.1.mine), channel_id=1, source_target_pairs={{0,1},{1,0},{2,3},{3,2},{4,5},{5,4},{6,7},{7,6},{8,9},{9,8},{10,11... | collective-permute-start | bytes 4030472 | tf_op jit(solution)/shard_map/ppermute | solution.py:463

commit v4 on v3

--- a/solution.py
+++ b/solution.py
@@ -54,7 +54,7 @@
         select_kernel,
         out_shape=(jax.ShapeDtypeStruct((slots, rows), F32), jax.ShapeDtypeStruct((traj, rows), F32)),
         out_specs=(VMEM, VMEM),
-        cost_estimate=cost(6),
+        cost_estimate=cost(40),
         name="select",
     )()
 
@@ -205,16 +205,21 @@
     return grad, scale * (values - targets)
 
 
-def work(slots, frames, side, weights, embed_t, head, head_t, frames_t, hidden_t, preact_t, add):
-    width, feats = embed_t.shape
-    nact = head_t.shape[0] - PAD
+def forward(frames, embed_t, head_t, frames_t, hidden_t):
+    width = embed_t.shape[0]
     tile = 256
     for index, block in enumerate(frames):
         frames_t[:, index * BLOCK : (index + 1) * BLOCK] = block.T
     for start in range(0, width, tile):
         here = slice(start, start + tile)
         hidden_t[here, :] = jnp.maximum(mm(embed_t[here, :], frames_t[...]), 0.0).astype(BF16)
-    logits = mm(head_t[...], hidden_t[...])
+    return mm(head_t[...], hidden_t[...])
+
+
+def backward(slots, logits, side, weights, head, frames_t, hidden_t, preact_t, add):
+    width, feats = head.shape[0], frames_t.shape[0]
+    nact = logits.shape[0] - PAD
+    tile = 256
     grad, grad_values = vtrace(
         slots, nact, side, weights, logits[0:nact, :], logits[nact : nact + 1, :]
     )
@@ -225,41 +230,15 @@
         back = mm(head[here, :], grad_t)
         alive = hidden_t[here, :].astype(F32) > 0.0
         preact_t[here, :] = jnp.where(alive, back, 0.0).astype(BF16)
-    for index in range(len(frames)):
+    for index in range(frames_t.shape[1] // BLOCK):
         lanes = slice(index * BLOCK, (index + 1) * BLOCK)
         add(index, slice(0, feats), mm_nt(frames_t[:, lanes], preact_t[:, lanes]))
         add(index, slice(feats, feats + nact + PAD), mm_nt(grad_t[:, lanes], hidden_t[:, lanes]))
 
 
 def work(slots, frames, side, weights, embed_t, head, head_t, frames_t, hidden_t, preact_t, add):
-    width, feats = embed_t.shape
-    nact = head_t.shape[0] - PAD
-    tile = 256
-    for index, block in enumerate(frames):
-        frames_t[:, index * BLOCK : (index + 1) * BLOCK] = block.T
-    for start in range(0, width, tile):
-        here = slice(start, start + tile)
-        hidden_t[here, :] = jnp.maximum(mm(embed_t[here, :], frames_t[...]), 0.0).astype(BF16)
-    logits = mm(head_t[...], hidden_t[...])
-    grad, grad_values = vtrace(
-        slots, nact, side, weights, logits[0:nact, :], logits[nact : nact + 1, :]
-    )
-    pad = jnp.zeros((PAD - 1, grad.shape[1]), F32)
-    grad_t = jnp.concatenate([grad, grad_values, pad], axis=0).astype(BF16)
-    for start in range(0, width, tile):
-        here = slice(start, start + tile)
-        back = mm(head[here, :], grad_t)
-        alive = hidden_t[here, :].astype(F32) > 0.0
-        preact_t[here, :] = jnp.where(alive, back, 0.0).astype(BF16)
-    for index in range(len(frames)):
-        lanes = slice(index * BLOCK, (index + 1) * BLOCK)
-        add(index, slice(0, feats), mm_nt(frames_t[:, lanes], preact_t[:, lanes]))
-        add(index, slice(feats, feats + nact + PAD), mm_nt(grad_t[:, lanes], hidden_t[:, lanes]))
-
-
-def on_mid():
-    line = lax.div(lax.axis_index("hst"), 2)
-    return jnp.logical_or(line == 1, line == 2)
+    logits = forward(frames, embed_t, head_t, frames_t, hidden_t)
+    backward(slots, logits, side, weights, head, frames_t, hidden_t, preact_t, add)
 
 
 def side_of(sides, back, flip):
@@ -269,8 +248,30 @@
     return sides[pl.ds(pl.multiple_of(16 * mask, 8), 8), :]
 
 
+def ahead_kernel(own, own_y, one, embed_t, head_t, frames_t, hidden_t, logits):
+    logits[...] = forward((own[...], own_y[...], one[...]), embed_t, head_t, frames_t, hidden_t)
+
+
+def ahead(frames, embed_t, head_t):
+    width, feats = embed_t.shape
+    rows = len(frames) * BLOCK
+    return pl.pallas_call(
+        ahead_kernel,
+        out_shape=(
+            jax.ShapeDtypeStruct((feats, rows), BF16),
+            jax.ShapeDtypeStruct((width, rows), BF16),
+            jax.ShapeDtypeStruct((head_t.shape[0], rows), F32),
+        ),
+        in_specs=[VMEM] * 5,
+        out_specs=(VMEM,) * 3,
+        compiler_params=params(20),
+        cost_estimate=cost(1.6),
+        name="ahead",
+    )(*frames, embed_t, head_t)
+
+
 def first_kernel(slots, *refs):
-    (own, own_y, one, *pieces), mats, (out, other, weights, sides), scratch = (
+    (frames_t, hidden_t, logits, *pieces), mats, (out, other, weights, sides), scratch = (
         refs[0:7], refs[7:10], refs[10:14], refs[14:17])
     start = 0
     for piece in pieces:
@@ -287,7 +288,7 @@
             other[rows, :] = value
 
     side = jnp.concatenate([side_of(sides, *at) for at in ((0, 0), (0, 1), (1, 0))], axis=1)
-    work(slots, (own[...], own_y[...], one[...]), side, weights, *mats, *scratch, add)
+    backward(slots, logits[...], side, weights, mats[1], frames_t, hidden_t, scratch[2], add)
 
 
 def second_kernel(slots, *refs):
@@ -421,13 +422,15 @@
     three = send(two, along)
     two_y = send(two, across)
     three_y = send(three, across)
+    done = ahead((own, own_y, one), mats[0], mats[2])
+    pieces, two = lax.optimization_barrier((pieces, two))
 
     width, feats = mats[0].shape
     grads = jax.ShapeDtypeStruct((feats + mats[2].shape[0], width), F32)
     weights = jax.ShapeDtypeStruct((8 * n_cores, 128), F32)
     sides = jax.ShapeDtypeStruct((64 * n_cores, side.shape[1]), F32)
     own_sum, one_sum, weights, sides = call(
-        first_kernel, "first", slots, 3, (own, own_y, one, *pieces), mats,
+        first_kernel, "first", slots, 3, (*done, *pieces), mats,
         (grads, grads, weights, sides),
     )
     one_sum, two_sum = call(

time: 53.4 us -> 54.6 us (1.022)
  starting transfers between devices: 16 us -> 17.2 us
    pallas_call x0 -> x1, Pallas kernels: none -> 2.33 us  [ahead(): pl.pallas_call(ahead_kernel, out_shape=(jax.ShapeDtypeStruct((feats, rows...]
    pallas_call x4, Pallas kernels: 12.8 us -> 10.5 us  [call(): pl.pallas_call(functools.partial(kernel, slots), out_shape=outs, in_specs...]
    ppermute x7, waiting for transfers between devices: 7.74 us -> 5.81 us  [send(): return lax.ppermute(array, 'hst', pairs)]
    ppermute x6, waiting for transfers between devices: 3.35 us -> 5.28 us  [gathered_grads(): lax.ppermute(held, AXES, [(at, at ^ scale * step) for at in range(8 * n_c...]
    ppermute x7, starting transfers between devices: 9.58 us -> 10.8 us  [send(): return lax.ppermute(array, 'hst', pairs)]
  transfers between devices with their start and end apart: 14 -> 14, of which waited for: 7 -> 6; matrix products, arithmetic and copies ran while one was open for 0% -> 0% of each run, Pallas kernels for 24% -> 24%
where the time goes in v4:
time: 54.6 us; the launch traced here: 54.3 us
  Pallas kernels  18.6 us (34%)
  starting transfers between devices  17.2 us (32%)
  waiting for transfers between devices  14.2 us (26%)
  local copies, waits for them, and re-layouts  3.48 us (6%)
  between operations  0.85 us (2%)
    ppermute x7, starting transfers between devices, send(): return lax.ppermute(array, 'hst', pairs)  10.8 us
    pallas_call x4, Pallas kernels, call(): pl.pallas_call(functools.partial(kernel, slots), out_shape=outs, in_specs...  10.5 us
    ppermute x6, starting transfers between devices, gathered_grads(): lax.ppermute(held, AXES, [(at, at ^ scale * step) for at in range(8 * n_c...  6.32 us
    ppermute x7, waiting for transfers between devices, send(): return lax.ppermute(array, 'hst', pairs)  5.81 us
    ppermute x6, waiting for transfers between devices, gathered_grads(): lax.ppermute(held, AXES, [(at, at ^ scale * step) for at in range(8 * n_c...  5.28 us
    unnamed x36, local copies, waits for them, and re-layouts  3.48 us
    pallas_call x1, Pallas kernels, update(): pl.pallas_call(functools.partial(update_kernel, feats, nact), out_shape=(...  3.47 us
    ppermute x1, waiting for transfers between devices, body(): theirs = lax.ppermute(mine, 'cores', [(0, 1), (1, 0)])  3.07 us
  transfers between devices with their start and end apart: 14, of which 6 were waited for; matrix products, arithmetic and copies ran while one was open for 0% of the time, Pallas kernels for 24%

profile of v4, /device:TPU:0, one launch (start us, length us, event | category | flops | bytes accessed | tf_op | source)
XLA Modules:
  0.0 54.3 jit_solution(16640893629348787006)
XLA Ops:
  0.7 3.1 %collective-permute-start.3 = (bf16[256,512]{1,0:T(8,128)(2,1)}, bf16[256,512]{1,0:T(8,128)(2,1)}, u32[]{:S(2)}, u32[]{:S(2)}) collective-permute-start(bf16[256,512]{1,0:T(8,128)(2,1)} %bitcast.7), channel_id=1, source_target_pairs={{0,4},{2,6},{4,8},{6,10},{8,12},{10,14},{12,0},{14,2},{1,5},{3,7},... | collective-permute-start | bytes 786440 | tf_op jit(solution)/shard_map/ppermute | solution.py:407
  3.8 1.5 %collective-permute-start.4 = (bf16[256,512]{1,0:T(8,128)(2,1)}, bf16[256,512]{1,0:T(8,128)(2,1)}, u32[]{:S(2)}, u32[]{:S(2)}) collective-permute-start(bf16[256,512]{1,0:T(8,128)(2,1)} %bitcast.8), channel_id=1, source_target_pairs={{0,2},{2,0},{4,6},{6,4},{8,10},{10,8},{12,14},{14,12},{1,3},{3,1},... | collective-permute-start | bytes 786440 | tf_op jit(solution)/shard_map/ppermute | solution.py:407
  5.3 0.6 %select.1 = (f32[16,256]{1,0:T(8,128)}, f32[16,256]{1,0:T(8,128)}) custom-call(), custom_call_target="tpu_custom_call" | custom-call | flops 44000002048 | tf_op jit(solution)/shard_map/select/pallas_call | solution.py:53
  6.0 1.0 %copy-done.3 = f32[1024,128]{1,0:T(8,128)S(1)} copy-done((f32[1024,128]{1,0:T(8,128)S(1)}, f32[1024,128]{1,0:T(8,128)}, u32[]{:S(2)}) %copy-start.3) | copy-done | bytes 524312
  7.0 0.9 %copy-done.7 = bf16[16,16,512]{2,1,0:T(8,128)(2,1)S(1)} copy-done((bf16[16,16,512]{2,1,0:T(8,128)(2,1)S(1)}, bf16[16,16,512]{2,1,0:T(8,128)(2,1)}, u32[]{:S(2)}) %copy-start.7) | copy-done | bytes 262168
  8.0 0.7 %copy-done.16 = f32[16,256]{1,0:T(8,128)S(1)} copy-done((f32[16,256]{1,0:T(8,128)S(1)}, f32[16,256]{1,0:T(8,128)}, u32[]{:S(2)}) %copy-start.16) | copy-done | bytes 16408
  8.7 0.7 %copy-done.17 = f32[16,256]{1,0:T(8,128)S(1)} copy-done((f32[16,256]{1,0:T(8,128)S(1)}, f32[16,256]{1,0:T(8,128)}, u32[]{:S(2)}) %copy-start.17) | copy-done | bytes 16408
  9.4 1.7 %prepare.1 = (f32[8,256]{1,0:T(8,128)S(1)}, bf16[1024,512]{1,0:T(8,128)(2,1)S(1)}, bf16[1024,144]{1,0:T(8,128)(2,1)S(1)}, bf16[144,1024]{1,0:T(8,128)(2,1)S(1)}) custom-call(s32[1,16]{1,0:T(1,128)S(1)} %bitcast.14, s32[1,16]{1,0:T(1,128)S(1)} %bitcast.15, s32[16,16]{1,0:T(8,128)S(1)} %copy-done.10, f32[16,16]{1,0:T(8,128)S(1)} %copy-done.11, ...), custom_call_target="tpu_custom_call" | custom-call | flops 3300000000 | tf_op jit(solution)/shard_map/prepare/pallas_call | solution.py:133
  11.1 0.1 collective-permute-start
  11.2 0.6 %collective-permute-start.1 = (f32[8,256]{1,0:T(8,128)S(1)}, f32[8,256]{1,0:T(8,128)S(1)}, u32[]{:S(2)}, u32[]{:S(2)}) collective-permute-start(f32[8,256]{1,0:T(8,128)S(1)} %get-tuple-element.41), channel_id=1, source_target_pairs={{0,2},{1,3},{2,0},{3,1},{4,6},{5,7},{6,4},{7,5},{8,10},{9,11},{10,... | collective-permute-start | bytes 24584 | tf_op jit(solution)/shard_map/ppermute | solution.py:417
  11.7 1.3 %collective-permute-start.2 = (f32[8,256]{1,0:T(8,128)S(1)}, f32[8,256]{1,0:T(8,128)S(1)}, u32[]{:S(2)}, u32[]{:S(2)}) collective-permute-start(f32[8,256]{1,0:T(8,128)S(1)} %get-tuple-element.41), channel_id=1, source_target_pairs={{0,3},{1,2},{2,1},{3,0},{4,7},{5,6},{6,5},{7,4},{8,11},{9,10},{10,... | collective-permute-start | bytes 24584 | tf_op jit(solution)/shard_map/ppermute | solution.py:417
  13.0 1.9 %collective-permute-done.1 = f32[8,256]{1,0:T(8,128)S(1)} collective-permute-done((f32[8,256]{1,0:T(8,128)S(1)}, f32[8,256]{1,0:T(8,128)S(1)}, u32[]{:S(2)}, u32[]{:S(2)}) %collective-permute-start.1) | collective-permute-done | bytes 8224 | tf_op jit(solution)/shard_map/ppermute | solution.py:417
  14.9 1.6 %collective-permute-start.5 = (bf16[256,512]{1,0:T(8,128)(2,1)}, bf16[256,512]{1,0:T(8,128)(2,1)S(1)}, u32[]{:S(2)}, u32[]{:S(2)}) collective-permute-start(bf16[256,512]{1,0:T(8,128)(2,1)} %collective-permute-done.3.one), channel_id=1, source_target_pairs={{0,4},{2,6},{4,8},{6,10},{8,12},{10,14},{12,0},{14,2},{1,5},{3,7},... | collective-permute-start | bytes 786440 | tf_op jit(solution)/shard_map/ppermute | solution.py:407
  16.6 2.2 %collective-permute-start.10 = (f32[32,256]{1,0:T(8,128)S(1)}, f32[32,256]{1,0:T(8,128)S(1)}, u32[]{:S(2)}, u32[]{:S(2)}) collective-permute-start(f32[32,256]{1,0:T(8,128)S(1)} %pad_maximum_fusion.refs_3_), channel_id=1, source_target_pairs={{0,12},{1,13},{2,14},{3,15},{4,8},{5,9},{6,10},{7,11},{8,4},{9,5},... | collective-permute-start | bytes 98312 | tf_op jit(solution)/shard_map/ppermute | solution.py:417
  18.8 2.1 %collective-permute-start.9 = (f32[32,256]{1,0:T(8,128)S(1)}, f32[32,256]{1,0:T(8,128)S(1)}, u32[]{:S(2)}, u32[]{:S(2)}) collective-permute-start(f32[32,256]{1,0:T(8,128)S(1)} %pad_maximum_fusion.refs_3_), channel_id=1, source_target_pairs={{0,8},{1,9},{2,10},{3,11},{4,12},{5,13},{6,14},{7,15},{8,0},{9,1},... | collective-permute-start | bytes 98312 | tf_op jit(solution)/shard_map/ppermute | solution.py:417
  20.9 1.4 %collective-permute-start.12 = (bf16[256,512]{1,0:T(8,128)(2,1)}, bf16[256,512]{1,0:T(8,128)(2,1)S(1)}, u32[]{:S(2)}, u32[]{:S(2)}) collective-permute-start(bf16[256,512]{1,0:T(8,128)(2,1)} %collective-permute-done.3.one), channel_id=1, source_target_pairs={{0,2},{2,0},{4,6},{6,4},{8,10},{10,8},{12,14},{14,12},{1,3},{3,1},... | collective-permute-start | bytes 786440 | tf_op jit(solution)/shard_map/ppermute | solution.py:407
  22.4 2.3 %ahead.1 = (bf16[512,768]{1,0:T(8,128)(2,1)S(1)}, bf16[1024,768]{1,0:T(8,128)(2,1)S(1)}, f32[144,768]{1,0:T(8,128)S(1)}) custom-call(bf16[256,512]{1,0:T(8,128)(2,1)S(1)} %bitcast.10, bf16[256,512]{1,0:T(8,128)(2,1)} %collective-permute-done.4.own_y, bf16[256,512]{1,0:T(8,128)(2,1)} %collective-permute-done.3.one, ...), custom_call_target="tpu_custom_call" | custom-call | flops 1760000000 | tf_op jit(solution)/shard_map/ahead/pallas_call | solution.py:258
  24.7 2.1 %collective-permute-done.10.refs_6_ = f32[32,256]{1,0:T(8,128)S(1)} collective-permute-done((f32[32,256]{1,0:T(8,128)S(1)}, f32[32,256]{1,0:T(8,128)S(1)}, u32[]{:S(2)}, u32[]{:S(2)}) %collective-permute-start.10) | collective-permute-done | bytes 32800 | tf_op jit(solution)/shard_map/ppermute | solution.py:417
  26.9 1.3 %collective-permute-done.9.refs_5_ = f32[32,256]{1,0:T(8,128)S(1)} collective-permute-done((f32[32,256]{1,0:T(8,128)S(1)}, f32[32,256]{1,0:T(8,128)S(1)}, u32[]{:S(2)}, u32[]{:S(2)}) %collective-permute-start.9) | collective-permute-done | bytes 32800 | tf_op jit(solution)/shard_map/ppermute | solution.py:417
  28.1 0.2 collective-permute-start.6
  28.3 1.5 %collective-permute-start.11 = (bf16[256,512]{1,0:T(8,128)(2,1)S(1)}, bf16[256,512]{1,0:T(8,128)(2,1)S(1)}, u32[]{:S(2)}, u32[]{:S(2)}) collective-permute-start(bf16[256,512]{1,0:T(8,128)(2,1)S(1)} %collective-permute-done.5.refs_1_), channel_id=1, source_target_pairs={{0,2},{2,0},{4,6},{6,4},{8,10},{10,8},{12,14},{14,12},{1,3},{3,1},... | collective-permute-start | bytes 786440 | tf_op jit(solution)/shard_map/ppermute | solution.py:407
  29.8 2.6 %first.1 = (f32[656,1024]{1,0:T(8,128)S(1)}, f32[656,1024]{1,0:T(8,128)S(1)}, f32[16,128]{1,0:T(8,128)S(1)}, f32[128,256]{1,0:T(8,128)S(1)}) custom-call(bf16[512,768]{1,0:T(8,128)(2,1)S(1)} %get-tuple-element.46.refs_0_, bf16[1024,768]{1,0:T(8,128)(2,1)S(1)} %get-tuple-element.47.refs_1_, f32[144,768]{1,0:T(8,128)S(1)} %get-tuple-element.48.refs_2_, ...), custom_call_target="tpu_custom_call" | custom-call | flops 4400000000 | tf_op jit(solution)/shard_map/first/pallas_call | solution.py:348
  32.4 2.9 %second.1 = (f32[656,1024]{1,0:T(8,128)S(1)}, f32[656,1024]{1,0:T(8,128)S(1)}) custom-call(bf16[256,512]{1,0:T(8,128)(2,1)S(1)} %collective-permute-done.12.refs_0_, bf16[256,512]{1,0:T(8,128)(2,1)S(1)} %collective-permute-done.5.refs_1_, f32[128,256]{1,0:T(8,128)S(1)} %get-tuple-element.55.refs_2_.refs_1_, f32[16,128]{1,0:T(8,128)S(1)} %get-tuple-element.56.refs_3_.refs_2_, ...), custom_call_target="tpu_custom_call" | custom-call | flops 3080000000 | tf_op jit(solution)/shard_map/second/pallas_call | solution.py:348
  35.3 2.9 %collective-permute-done.6.refs_1_ = bf16[256,512]{1,0:T(8,128)(2,1)S(1)} collective-permute-done((bf16[256,512]{1,0:T(8,128)(2,1)S(1)}, bf16[256,512]{1,0:T(8,128)(2,1)S(1)}, u32[]{:S(2)}, u32[]{:S(2)}) %collective-permute-start.6) | collective-permute-done | bytes 262176 | tf_op jit(solution)/shard_map/ppermute | solution.py:407
  38.1 1.5 %collective-permute-start.7 = (bf16[256,512]{1,0:T(8,128)(2,1)S(1)}, bf16[256,512]{1,0:T(8,128)(2,1)S(1)}, u32[]{:S(2)}, u32[]{:S(2)}) collective-permute-start(bf16[256,512]{1,0:T(8,128)(2,1)S(1)} %collective-permute-done.6.refs_1_), channel_id=1, source_target_pairs={{0,2},{2,0},{4,6},{6,4},{8,10},{10,8},{12,14},{14,12},{1,3},{3,1},... | collective-permute-start | bytes 786440 | tf_op jit(solution)/shard_map/ppermute | solution.py:407
  39.6 3.0 %third.1 = (f32[656,1024]{1,0:T(8,128)S(1)}, f32[656,1024]{1,0:T(8,128)S(1)}) custom-call(bf16[256,512]{1,0:T(8,128)(2,1)S(1)} %collective-permute-done.11.refs_0_, bf16[256,512]{1,0:T(8,128)(2,1)S(1)} %collective-permute-done.6.refs_1_, f32[128,256]{1,0:T(8,128)S(1)} %get-tuple-element.55.refs_2_.refs_1_, f32[16,128]{1,0:T(8,128)S(1)} %get-tuple-element.56.refs_3_.refs_2_, ...), custom_call_target="tpu_custom_call" | custom-call | flops 3080000000 | tf_op jit(solution)/shard_map/third/pallas_call | solution.py:348
  42.6 2.9 %collective-permute-done.7.refs_0_ = bf16[256,512]{1,0:T(8,128)(2,1)S(1)} collective-permute-done((bf16[256,512]{1,0:T(8,128)(2,1)S(1)}, bf16[256,512]{1,0:T(8,128)(2,1)S(1)}, u32[]{:S(2)}, u32[]{:S(2)}) %collective-permute-start.7) | collective-permute-done | bytes 262176 | tf_op jit(solution)/shard_map/ppermute | solution.py:407
  45.5 0.0 copy-start.13
  45.6 2.1 %fourth.1.mine = bf16[656,1024]{1,0:T(8,128)(2,1)S(1)} custom-call(bf16[256,512]{1,0:T(8,128)(2,1)S(1)} %collective-permute-done.7.refs_0_, f32[128,256]{1,0:T(8,128)S(1)} %get-tuple-element.55.refs_2_.refs_1_, f32[16,128]{1,0:T(8,128)S(1)} %get-tuple-element.56.refs_3_.refs_2_, f32[656,1024]{1,0:T(8,128)S(1)} %get-tuple-element.61.refs_3_, ...), custom_call_target="tpu_custom_call" | custom-call | flops 1760000000 | tf_op jit(solution)/shard_map/fourth/pallas_call | solution.py:348
  47.6 0.1 collective-permute-start.13
  47.7 3.1 %collective-permute-done.13.theirs = bf16[656,1024]{1,0:T(8,128)(2,1)S(1)} collective-permute-done((bf16[656,1024]{1,0:T(8,128)(2,1)S(1)}, bf16[656,1024]{1,0:T(8,128)(2,1)S(1)}, u32[]{:S(2)}, u32[]{:S(2)}) %collective-permute-start.13) | collective-permute-done | bytes 1343520 | tf_op jit(solution)/shard_map/ppermute | solution.py:466
  50.8 3.5 %update.1 = (bf16[256,128]{1,0:T(8,128)(2,1)}, f32[512,1024]{1,0:T(8,128)}, f32[1024,128]{1,0:T(8,128)}, f32[1,1024]{1,0:T(1,128)}, f32[512,1024]{1,0:T(8,128)}, /*index=5*/f32[1024,128]{1,0:T(8,128)}, f32[1,1024]{1,0:T(1,128)}) custom-call(bf16[656,1024]{1,0:T(8,128)(2,1)S(1)} %fourth.1.mine, bf16[656,1024]{1,0:T(8,128)(2,1)S(1)} %collective-permute-done.13.theirs, ...), custom_call_target="tpu_custom_call" | custom-call | flops 3740000000 | tf_op jit(solution)/shard_map/update/pallas_call | solution.py:391
  (41 shorter events, 0.1 us)
Async XLA Ops:
  0.6 5.3 %copy-start = (f32[512,1024]{1,0:T(8,128)S(1)}, f32[512,1024]{1,0:T(8,128)}, u32[]{:S(2)}) copy-start(f32[512,1024]{1,0:T(8,128)} %master_embed.1) | copy-start | bytes 6291460
  0.6 5.3 %copy-start.2 = (bf16[512,1024]{1,0:T(8,128)(2,1)S(1)}, bf16[512,1024]{1,0:T(8,128)(2,1)}, u32[]{:S(2)}) copy-start(bf16[512,1024]{1,0:T(8,128)(2,1)} %actor_embed_at.1) | copy-start | bytes 3145732
  0.7 5.3 %copy-start.6 = (bf16[1024,128]{1,0:T(8,128)(2,1)S(1)}, bf16[1024,128]{1,0:T(8,128)(2,1)}, u32[]{:S(2)}) copy-start(bf16[1024,128]{1,0:T(8,128)(2,1)} %actor_policy_at.1) | copy-start | bytes 786436
  0.7 5.3 %copy-start.10 = (s32[16,16]{1,0:T(8,128)S(1)}, s32[16,16]{1,0:T(8,128)}, u32[]{:S(2)}) copy-start(s32[16,16]{1,0:T(8,128)} %actions_at.1) | copy-start | bytes 3076
  0.7 5.3 %copy-start.11 = (f32[16,16]{1,0:T(8,128)S(1)}, f32[16,16]{1,0:T(8,128)}, u32[]{:S(2)}) copy-start(f32[16,16]{1,0:T(8,128)} %rewards_at.1) | copy-start | bytes 3076
  0.7 5.3 %copy-start.12 = (f32[1024]{0:T(1024)S(1)}, f32[1024]{0:T(1024)}, u32[]{:S(2)}) copy-start(f32[1024]{0:T(1024)} %param.23) | copy-start | bytes 12292
  0.7 5.3 %copy-start.14 = (s32[16]{0:T(128)S(1)}, s32[16]{0:T(128)}, u32[]{:S(2)}) copy-start(s32[16]{0:T(128)} %param.15) | copy-start | bytes 196
  0.7 5.3 %copy-start.15 = (s32[16]{0:T(128)S(1)}, s32[16]{0:T(128)}, u32[]{:S(2)}) copy-start(s32[16]{0:T(128)} %param.18) | copy-start | bytes 196
  0.7 14.2 %collective-permute-start.3 = (bf16[256,512]{1,0:T(8,128)(2,1)}, bf16[256,512]{1,0:T(8,128)(2,1)}, u32[]{:S(2)}, u32[]{:S(2)}) collective-permute-start(bf16[256,512]{1,0:T(8,128)(2,1)} %bitcast.7), channel_id=1, source_target_pairs={{0,4},{2,6},{4,8},{6,10},{8,12},{10,14},{12,0},{14,2},{1,5},{3,7},... | collective-permute-start | bytes 786440 | tf_op jit(solution)/shard_map/ppermute | solution.py:407
  3.8 11.1 %collective-permute-start.4 = (bf16[256,512]{1,0:T(8,128)(2,1)}, bf16[256,512]{1,0:T(8,128)(2,1)}, u32[]{:S(2)}, u32[]{:S(2)}) collective-permute-start(bf16[256,512]{1,0:T(8,128)(2,1)} %bitcast.8), channel_id=1, source_target_pairs={{0,2},{2,0},{4,6},{6,4},{8,10},{10,8},{12,14},{14,12},{1,3},{3,1},... | collective-permute-start | bytes 786440 | tf_op jit(solution)/shard_map/ppermute | solution.py:407
  6.0 1.0 %copy-start.3 = (f32[1024,128]{1,0:T(8,128)S(1)}, f32[1024,128]{1,0:T(8,128)}, u32[]{:S(2)}) copy-start(f32[1024,128]{1,0:T(8,128)} %master_policy.1) | copy-start | bytes 1572868
  7.0 0.9 %copy-start.7 = (bf16[16,16,512]{2,1,0:T(8,128)(2,1)S(1)}, bf16[16,16,512]{2,1,0:T(8,128)(2,1)}, u32[]{:S(2)}) copy-start(bf16[16,16,512]{2,1,0:T(8,128)(2,1)} %param.14) | copy-start | bytes 786436
  8.0 0.7 %copy-start.16 = (f32[16,256]{1,0:T(8,128)S(1)}, f32[16,256]{1,0:T(8,128)}, u32[]{:S(2)}) copy-start(f32[16,256]{1,0:T(8,128)} %get-tuple-element.39.spread) | copy-start | bytes 49156
  8.7 0.7 %copy-start.17 = (f32[16,256]{1,0:T(8,128)S(1)}, f32[16,256]{1,0:T(8,128)}, u32[]{:S(2)}) copy-start(f32[16,256]{1,0:T(8,128)} %get-tuple-element.40.owner) | copy-start | bytes 49156
  9.4 12.9 %copy-start.8 = (bf16[16,16,512]{2,1,0:T(8,128)(2,1)S(1)}, bf16[16,16,512]{2,1,0:T(8,128)(2,1)}, u32[]{:S(2)}) copy-start(bf16[16,16,512]{2,1,0:T(8,128)(2,1)} %param.14) | copy-start | bytes 786436
  11.1 1.9 %collective-permute-start = (f32[8,256]{1,0:T(8,128)S(1)}, f32[8,256]{1,0:T(8,128)S(1)}, u32[]{:S(2)}, u32[]{:S(2)}) collective-permute-start(f32[8,256]{1,0:T(8,128)S(1)} %get-tuple-element.41), channel_id=1, source_target_pairs={{0,1},{1,0},{2,3},{3,2},{4,5},{5,4},{6,7},{7,6},{8,9},{9,8},{10,11... | collective-permute-start | bytes 24584 | tf_op jit(solution)/shard_map/ppermute | solution.py:417
  11.2 3.7 %collective-permute-start.1 = (f32[8,256]{1,0:T(8,128)S(1)}, f32[8,256]{1,0:T(8,128)S(1)}, u32[]{:S(2)}, u32[]{:S(2)}) collective-permute-start(f32[8,256]{1,0:T(8,128)S(1)} %get-tuple-element.41), channel_id=1, source_target_pairs={{0,2},{1,3},{2,0},{3,1},{4,6},{5,7},{6,4},{7,5},{8,10},{9,11},{10,... | collective-permute-start | bytes 24584 | tf_op jit(solution)/shard_map/ppermute | solution.py:417
  11.7 3.2 %collective-permute-start.2 = (f32[8,256]{1,0:T(8,128)S(1)}, f32[8,256]{1,0:T(8,128)S(1)}, u32[]{:S(2)}, u32[]{:S(2)}) collective-permute-start(f32[8,256]{1,0:T(8,128)S(1)} %get-tuple-element.41), channel_id=1, source_target_pairs={{0,3},{1,2},{2,1},{3,0},{4,7},{5,6},{6,5},{7,4},{8,11},{9,10},{10,... | collective-permute-start | bytes 24584 | tf_op jit(solution)/shard_map/ppermute | solution.py:417
  14.9 13.2 %collective-permute-start.5 = (bf16[256,512]{1,0:T(8,128)(2,1)}, bf16[256,512]{1,0:T(8,128)(2,1)S(1)}, u32[]{:S(2)}, u32[]{:S(2)}) collective-permute-start(bf16[256,512]{1,0:T(8,128)(2,1)} %collective-permute-done.3.one), channel_id=1, source_target_pairs={{0,4},{2,6},{4,8},{6,10},{8,12},{10,14},{12,0},{14,2},{1,5},{3,7},... | collective-permute-start | bytes 786440 | tf_op jit(solution)/shard_map/ppermute | solution.py:407
  16.6 10.3 %collective-permute-start.10 = (f32[32,256]{1,0:T(8,128)S(1)}, f32[32,256]{1,0:T(8,128)S(1)}, u32[]{:S(2)}, u32[]{:S(2)}) collective-permute-start(f32[32,256]{1,0:T(8,128)S(1)} %pad_maximum_fusion.refs_3_), channel_id=1, source_target_pairs={{0,12},{1,13},{2,14},{3,15},{4,8},{5,9},{6,10},{7,11},{8,4},{9,5},... | collective-permute-start | bytes 98312 | tf_op jit(solution)/shard_map/ppermute | solution.py:417
  18.8 8.0 %collective-permute-start.8 = (f32[32,256]{1,0:T(8,128)S(1)}, f32[32,256]{1,0:T(8,128)S(1)}, u32[]{:S(2)}, u32[]{:S(2)}) collective-permute-start(f32[32,256]{1,0:T(8,128)S(1)} %pad_maximum_fusion.refs_3_), channel_id=1, source_target_pairs={{0,4},{1,5},{2,6},{3,7},{4,0},{5,1},{6,2},{7,3},{8,12},{9,13},{10,... | collective-permute-start | bytes 98312 | tf_op jit(solution)/shard_map/ppermute | solution.py:417
  18.8 9.3 %collective-permute-start.9 = (f32[32,256]{1,0:T(8,128)S(1)}, f32[32,256]{1,0:T(8,128)S(1)}, u32[]{:S(2)}, u32[]{:S(2)}) collective-permute-start(f32[32,256]{1,0:T(8,128)S(1)} %pad_maximum_fusion.refs_3_), channel_id=1, source_target_pairs={{0,8},{1,9},{2,10},{3,11},{4,12},{5,13},{6,14},{7,15},{8,0},{9,1},... | collective-permute-start | bytes 98312 | tf_op jit(solution)/shard_map/ppermute | solution.py:417
  20.9 11.4 %collective-permute-start.12 = (bf16[256,512]{1,0:T(8,128)(2,1)}, bf16[256,512]{1,0:T(8,128)(2,1)S(1)}, u32[]{:S(2)}, u32[]{:S(2)}) collective-permute-start(bf16[256,512]{1,0:T(8,128)(2,1)} %collective-permute-done.3.one), channel_id=1, source_target_pairs={{0,2},{2,0},{4,6},{6,4},{8,10},{10,8},{12,14},{14,12},{1,3},{3,1},... | collective-permute-start | bytes 786440 | tf_op jit(solution)/shard_map/ppermute | solution.py:407
  28.1 10.0 %collective-permute-start.6 = (bf16[256,512]{1,0:T(8,128)(2,1)S(1)}, bf16[256,512]{1,0:T(8,128)(2,1)S(1)}, u32[]{:S(2)}, u32[]{:S(2)}) collective-permute-start(bf16[256,512]{1,0:T(8,128)(2,1)S(1)} %collective-permute-done.5.refs_1_), channel_id=1, source_target_pairs={{0,4},{2,6},{4,8},{6,10},{8,12},{10,14},{12,0},{14,2},{1,5},{3,7},... | collective-permute-start | bytes 786440 | tf_op jit(solution)/shard_map/ppermute | solution.py:407
  28.3 11.3 %collective-permute-start.11 = (bf16[256,512]{1,0:T(8,128)(2,1)S(1)}, bf16[256,512]{1,0:T(8,128)(2,1)S(1)}, u32[]{:S(2)}, u32[]{:S(2)}) collective-permute-start(bf16[256,512]{1,0:T(8,128)(2,1)S(1)} %collective-permute-done.5.refs_1_), channel_id=1, source_target_pairs={{0,2},{2,0},{4,6},{6,4},{8,10},{10,8},{12,14},{14,12},{1,3},{3,1},... | collective-permute-start | bytes 786440 | tf_op jit(solution)/shard_map/ppermute | solution.py:407
  38.1 7.4 %collective-permute-start.7 = (bf16[256,512]{1,0:T(8,128)(2,1)S(1)}, bf16[256,512]{1,0:T(8,128)(2,1)S(1)}, u32[]{:S(2)}, u32[]{:S(2)}) collective-permute-start(bf16[256,512]{1,0:T(8,128)(2,1)S(1)} %collective-permute-done.6.refs_1_), channel_id=1, source_target_pairs={{0,2},{2,0},{4,6},{6,4},{8,10},{10,8},{12,14},{14,12},{1,3},{3,1},... | collective-permute-start | bytes 786440 | tf_op jit(solution)/shard_map/ppermute | solution.py:407
  45.5 5.3 %copy-start.1 = (f32[512,1024]{1,0:T(8,128)S(1)}, f32[512,1024]{1,0:T(8,128)}, u32[]{:S(2)}) copy-start(f32[512,1024]{1,0:T(8,128)} %embed_moment.1) | copy-start | bytes 6291460
  45.5 5.3 %copy-start.4 = (f32[1024,128]{1,0:T(8,128)S(1)}, f32[1024,128]{1,0:T(8,128)}, u32[]{:S(2)}) copy-start(f32[1024,128]{1,0:T(8,128)} %master_policy.1) | copy-start | bytes 1572868
  45.5 5.3 %copy-start.5 = (f32[1024,128]{1,0:T(8,128)S(1)}, f32[1024,128]{1,0:T(8,128)}, u32[]{:S(2)}) copy-start(f32[1024,128]{1,0:T(8,128)} %policy_moment.1) | copy-start | bytes 1572868
  45.5 5.3 %copy-start.9 = (bf16[256,512]{1,0:T(8,128)(2,1)S(1)}, bf16[256,512]{1,0:T(8,128)(2,1)}, u32[]{:S(2)}) copy-start(bf16[256,512]{1,0:T(8,128)(2,1)} %next_obs.1) | copy-start | bytes 786436
  45.5 5.3 %copy-start.13 = (f32[1024]{0:T(1024)S(1)}, f32[1024]{0:T(1024)}, u32[]{:S(2)}) copy-start(f32[1024]{0:T(1024)} %param.26) | copy-start | bytes 12292
  47.6 3.1 %collective-permute-start.13 = (bf16[656,1024]{1,0:T(8,128)(2,1)S(1)}, bf16[656,1024]{1,0:T(8,128)(2,1)S(1)}, u32[]{:S(2)}, u32[]{:S(2)}) collective-permute-start(bf16[656,1024]{1,0:T(8,128)(2,1)S(1)} %fourth.1.mine), channel_id=1, source_target_pairs={{0,1},{1,0},{2,3},{3,2},{4,5},{5,4},{6,7},{7,6},{8,9},{9,8},{10,11... | collective-permute-start | bytes 4030472 | tf_op jit(solution)/shard_map/ppermute | solution.py:466

commit v5 on v4

--- a/solution.py
+++ b/solution.py
@@ -17,8 +17,9 @@
 VMEM = pl.BlockSpec(memory_space=pltpu.VMEM)
 MIB = 2**20
 BLOCK = 256
+HALF = 128
 PAD = 16
-BEHAVE, ACTION, REWARD, LENGTH, ASSIGN = range(5)
+BEHAVE, ACTION, REWARD, LENGTH, ASSIGN, LENGTH_2, ASSIGN_2 = range(7)
 
 
 def iota(shape, dim):
@@ -54,31 +55,17 @@
         select_kernel,
         out_shape=(jax.ShapeDtypeStruct((slots, rows), F32), jax.ShapeDtypeStruct((traj, rows), F32)),
         out_specs=(VMEM, VMEM),
+        compiler_params=params(4),
         cost_estimate=cost(40),
         name="select",
     )()
 
 
-def prepare_kernel(
-    lengths_at, assign_at, actions_at, rewards_at, obs_at, actor_embed_at, actor_policy_at,
-    master_embed_at, master_policy_at, master_value_at, spread, owner,
-    side, embed_t, head, head_t, *scratch,
+def side_kernel(
+    lengths, assign, lengths_2, assign_2, actions, rewards, actor_embed, actor_policy,
+    spread, owner, *refs,
 ):
-    sources = (
-        lengths_at, assign_at, actions_at, rewards_at, obs_at, actor_embed_at, actor_policy_at,
-        master_embed_at, master_policy_at, master_value_at,
-    )
-    held, sems = scratch[:-1], scratch[-1]
-    copies = [
-        pltpu.make_async_copy(source, target, sems.at[index])
-        for index, (source, target) in enumerate(zip(sources, held))
-    ]
-    for copy in copies:
-        copy.start()
-    (lengths, assign, actions, rewards, obs, actor_embed, actor_policy,
-     master_embed, master_policy, master_value) = held
-    for copy in copies[:7]:
-        copy.wait()
+    halves, side = refs[:-1], refs[-1]
 
     def flat(series):
         wide = jnp.dot(
@@ -93,7 +80,8 @@
         )
 
     action = flat(actions[...].astype(F32))
-    hidden = jnp.maximum(mm(obs[...], actor_embed[...]), 0.0).astype(BF16)
+    obs = jnp.concatenate([half[...] for half in halves], axis=0)
+    hidden = jnp.maximum(mm(obs, actor_embed[...]), 0.0).astype(BF16)
     logits = mm(hidden, actor_policy[...]).T
     top = jnp.max(logits, axis=0, keepdims=True)
     shifted = logits - top
@@ -107,9 +95,24 @@
     side[REWARD : REWARD + 1, :] = flat(rewards[...])
     side[LENGTH : LENGTH + 1, :] = repeat(lengths[...])
     side[ASSIGN : ASSIGN + 1, :] = repeat(assign[...])
-
-    for copy in copies[7:]:
-        copy.wait()
+    side[LENGTH_2 : LENGTH_2 + 1, :] = repeat(lengths_2[...])
+    side[ASSIGN_2 : ASSIGN_2 + 1, :] = repeat(assign_2[...])
+
+
+def side_data(spread, owner, halves, *args):
+    count = len(args) + 2 + len(halves)
+    return pl.pallas_call(
+        side_kernel,
+        out_shape=jax.ShapeDtypeStruct((8, spread.shape[1]), F32),
+        in_specs=[VMEM] * count,
+        out_specs=VMEM,
+        compiler_params=params(12),
+        cost_estimate=cost(1.3),
+        name="side",
+    )(*args, spread, owner, *halves)
+
+
+def convert_kernel(master_embed, master_policy, master_value, embed_t, head, head_t):
     embed_t[...] = master_embed[...].T.astype(BF16)
     nact = master_policy.shape[1]
     wide = jnp.concatenate(
@@ -125,27 +128,22 @@
     head[:, nact:] = wide[nact:, :].T.astype(BF16)
 
 
-def prepare(*args):
-    masks = select(*args[2].shape)
-    rows = args[4].shape[0]
-    feats, width = args[7].shape
-    nact = args[8].shape[1]
-    return pl.pallas_call(
-        prepare_kernel,
+def convert(master_embed, master_policy, master_value):
+    feats, width = master_embed.shape
+    nact = master_policy.shape[1]
+    return pl.pallas_call(
+        convert_kernel,
         out_shape=(
-            jax.ShapeDtypeStruct((8, rows), F32),
             jax.ShapeDtypeStruct((width, feats), BF16),
             jax.ShapeDtypeStruct((width, nact + PAD), BF16),
             jax.ShapeDtypeStruct((nact + PAD, width), BF16),
         ),
-        in_specs=[pl.BlockSpec(memory_space=pl.ANY)] * len(args) + [VMEM] * 2,
-        out_specs=(VMEM,) * 4,
-        scratch_shapes=[pltpu.VMEM(arg.shape, arg.dtype) for arg in args]
-        + [pltpu.SemaphoreType.DMA((len(args),))],
-        compiler_params=params(16),
-        cost_estimate=cost(3),
-        name="prepare",
-    )(*args, *masks)
+        in_specs=[VMEM] * 3,
+        out_specs=(VMEM,) * 3,
+        compiler_params=params(12),
+        cost_estimate=cost(0.6),
+        name="convert",
+    )(master_embed, master_policy, master_value)
 
 
 def learner_weights(slots, sides, out):
@@ -153,9 +151,10 @@
     total = jnp.zeros((learners, rows), F32)
     first = lax.rem(iota((1, rows), 1), slots) == 0
     for place in range(0, sides.shape[0], 8):
-        assign = sides[place + ASSIGN : place + ASSIGN + 1, :].astype(jnp.int32)
-        length = jnp.where(first, sides[place + LENGTH : place + LENGTH + 1, :], 0.0)
-        total = total + jnp.where(iota((learners, rows), 0) == assign, length, 0.0)
+        for length_at, assign_at in ((LENGTH, ASSIGN), (LENGTH_2, ASSIGN_2)):
+            assign = sides[place + assign_at : place + assign_at + 1, :].astype(jnp.int32)
+            length = jnp.where(first, sides[place + length_at : place + length_at + 1, :], 0.0)
+            total = total + jnp.where(iota((learners, rows), 0) == assign, length, 0.0)
     summed = jnp.sum(total, axis=1, keepdims=True)
     out[...] = jnp.broadcast_to(1.0 / (learners * summed), out.shape)
 
@@ -208,8 +207,8 @@
 def forward(frames, embed_t, head_t, frames_t, hidden_t):
     width = embed_t.shape[0]
     tile = 256
-    for index, block in enumerate(frames):
-        frames_t[:, index * BLOCK : (index + 1) * BLOCK] = block.T
+    for index, half in enumerate(frames):
+        frames_t[:, index * HALF : (index + 1) * HALF] = half[...].T
     for start in range(0, width, tile):
         here = slice(start, start + tile)
         hidden_t[here, :] = jnp.maximum(mm(embed_t[here, :], frames_t[...]), 0.0).astype(BF16)
@@ -241,20 +240,28 @@
     backward(slots, logits, side, weights, head, frames_t, hidden_t, preact_t, add)
 
 
-def side_of(sides, back, flip):
-    line = lax.div(lax.axis_index("hst"), 2)
-    there = lax.bitwise_and(line + 4 - back, 3)
-    mask = 2 * lax.bitwise_xor(line, there) + flip
-    return sides[pl.ds(pl.multiple_of(16 * mask, 8), 8), :]
-
-
-def ahead_kernel(own, own_y, one, embed_t, head_t, frames_t, hidden_t, logits):
-    logits[...] = forward((own[...], own_y[...], one[...]), embed_t, head_t, frames_t, hidden_t)
+def ring_place(hst):
+    line, across = lax.div(hst, 2), lax.rem(hst, 2)
+    return jnp.where(across == 0, line, 7 - line)
+
+
+def side_of(sides, step):
+    hst = lax.axis_index("hst")
+    way = jnp.where(lax.axis_index("cores") == 0, 7, 1)
+    there = lax.bitwise_and(ring_place(hst) + way * step, 7)
+    chip = jnp.where(there < 4, 2 * there, 2 * (7 - there) + 1)
+    mask = lax.bitwise_xor(hst, chip)
+    return sides[pl.ds(pl.multiple_of(8 * mask, 8), 8), :]
+
+
+def ahead_kernel(*refs):
+    (*frames, embed_t, head_t, frames_t, hidden_t, logits) = refs
+    logits[...] = forward(frames, embed_t, head_t, frames_t, hidden_t)
 
 
 def ahead(frames, embed_t, head_t):
     width, feats = embed_t.shape
-    rows = len(frames) * BLOCK
+    rows = len(frames) * HALF
     return pl.pallas_call(
         ahead_kernel,
         out_shape=(
@@ -262,7 +269,7 @@
             jax.ShapeDtypeStruct((width, rows), BF16),
             jax.ShapeDtypeStruct((head_t.shape[0], rows), F32),
         ),
-        in_specs=[VMEM] * 5,
+        in_specs=[VMEM] * (len(frames) + 2),
         out_specs=(VMEM,) * 3,
         compiler_params=params(20),
         cost_estimate=cost(1.6),
@@ -271,8 +278,8 @@
 
 
 def first_kernel(slots, *refs):
-    (frames_t, hidden_t, logits, *pieces), mats, (out, other, weights, sides), scratch = (
-        refs[0:7], refs[7:10], refs[10:14], refs[14:17])
+    (frames_t, hidden_t, logits, *pieces), mats, outs, (weights, sides), scratch = (
+        refs[0:7], refs[7:10], refs[10:13], refs[13:15], refs[15:18])
     start = 0
     for piece in pieces:
         sides[start : start + piece.shape[0], :] = piece[...]
@@ -280,55 +287,50 @@
     learner_weights(slots, sides, weights)
 
     def add(index, rows, value):
-        if index == 0:
-            out[rows, :] = value
-        elif index == 1:
-            out[rows, :] += value
-        else:
-            other[rows, :] = value
-
-    side = jnp.concatenate([side_of(sides, *at) for at in ((0, 0), (0, 1), (1, 0))], axis=1)
+        outs[index][rows, :] = value
+
+    side = jnp.concatenate([side_of(sides, step) for step in (0, 1, 2)], axis=1)
     backward(slots, logits[...], side, weights, mats[1], frames_t, hidden_t, scratch[2], add)
 
 
 def second_kernel(slots, *refs):
-    (one_y, two, sides, weights, one_sum), mats, (out, other), scratch = (
-        refs[0:5], refs[5:8], refs[8:10], refs[10:13])
+    frames, (sides, weights, sum_0), mats, (sum_04, sum_3), scratch = (
+        refs[0:4], refs[4:7], refs[7:10], refs[10:12], refs[12:15])
 
     def add(index, rows, value):
         if index == 0:
-            out[rows, :] = one_sum[rows, :] + value
+            sum_3[rows, :] = value
         else:
-            other[rows, :] = value
-
-    side = jnp.concatenate([side_of(sides, 1, 1), side_of(sides, 2, 0)], axis=1)
-    work(slots, (one_y[...], two[...]), side, weights, *mats, *scratch, add)
+            sum_04[rows, :] = sum_0[rows, :] + value
+
+    side = jnp.concatenate([side_of(sides, 3), side_of(sides, 4)], axis=1)
+    work(slots, frames, side, weights, *mats, *scratch, add)
 
 
 def third_kernel(slots, *refs):
-    (two_y, three, sides, weights, own_sum, two_sum), mats, (out, other), scratch = (
-        refs[0:6], refs[6:9], refs[9:11], refs[11:14])
+    frames, (sides, weights, sum_04, sum_1, sum_2), mats, (even, sum_15), scratch = (
+        refs[0:4], refs[4:9], refs[9:12], refs[12:14], refs[14:17])
 
     def add(index, rows, value):
         if index == 0:
-            out[rows, :] = own_sum[rows, :] + (two_sum[rows, :] + value)
+            sum_15[rows, :] = sum_1[rows, :] + value
         else:
-            other[rows, :] = value
-
-    side = jnp.concatenate([side_of(sides, 2, 1), side_of(sides, 3, 0)], axis=1)
-    work(slots, (two_y[...], three[...]), side, weights, *mats, *scratch, add)
+            even[rows, :] = sum_04[rows, :] + (sum_2[rows, :] + value)
+
+    side = jnp.concatenate([side_of(sides, 5), side_of(sides, 6)], axis=1)
+    work(slots, frames, side, weights, *mats, *scratch, add)
 
 
 def fourth_kernel(slots, *refs):
-    (three_y, sides, weights, even_sum, one_sum, three_sum), mats, out, scratch = (
-        refs[0:6], refs[6:9], refs[9], refs[10:13])
+    frames, (sides, weights, even, sum_15, sum_3), mats, out, scratch = (
+        refs[0:2], refs[2:7], refs[7:10], refs[10], refs[11:14])
 
     def add(index, rows, value):
         out[rows, :] = (
-            even_sum[rows, :] + (one_sum[rows, :] + (three_sum[rows, :] + value))
+            even[rows, :] + (sum_15[rows, :] + (sum_3[rows, :] + value))
         ).astype(BF16)
 
-    work(slots, (three_y[...],), side_of(sides, 3, 1), weights, *mats, *scratch, add)
+    work(slots, frames, side_of(sides, 7), weights, *mats, *scratch, add)
 
 
 def local_kernel(slots, frames, side, weights, embed_t, head, head_t, out, *scratch):
@@ -338,8 +340,8 @@
         else:
             out[rows, :] += value
 
-    blocks = [frames[index] for index in range(frames.shape[0])]
-    work(slots, blocks, side, weights, embed_t, head, head_t, *scratch, add)
+    halves = [frames.at[index] for index in range(frames.shape[0])]
+    work(slots, halves, side, weights, embed_t, head, head_t, *scratch, add)
 
 
 def call(kernel, name, slots, blocks, args, mats, outs):
@@ -399,51 +401,44 @@
     )(mine, theirs, *args)
 
 
-def gathered_grads(slots, n_cores, own, side, mats):
-    across = [(place, place ^ 1) for place in range(8)]
-    along = [(place, (place + 2) % 8) for place in range(8)]
-
-    def send(array, pairs):
-        return lax.ppermute(array, "hst", pairs)
-
-    one = send(own, along)
-    own_y = send(own, across)
+def gathered_grads(slots, halves, side, mats):
+    cycle = [0, 2, 4, 6, 7, 5, 3, 1]
+    ring = [
+        (2 * cycle[place] + core, 2 * cycle[(place + way) % 8] + core)
+        for place in range(8)
+        for core, way in ((0, 1), (1, -1))
+    ]
+
+    def send(blocks):
+        return [lax.ppermute(half, AXES, ring) for half in blocks]
+
+    blocks = [halves]
+    for step in range(7):
+        blocks.append(send(blocks[-1]))
     pieces = [side]
-    for scale in (1, 4):
-        held = pieces[0] if scale == 1 else jnp.concatenate(pieces, axis=0)
-        if scale == 4:
-            held, one, own_y = lax.optimization_barrier((held, one, own_y))
-        pieces = [held] + [
-            lax.ppermute(held, AXES, [(at, at ^ (scale * step)) for at in range(8 * n_cores)])
-            for step in (1, 2, 3)
-        ]
-    two = send(one, along)
-    one_y = send(one, across)
-    three = send(two, along)
-    two_y = send(two, across)
-    three_y = send(three, across)
-    done = ahead((own, own_y, one), mats[0], mats[2])
-    pieces, two = lax.optimization_barrier((pieces, two))
+    for mask in (1, 2, 4):
+        held = pieces[0] if mask == 1 else jnp.concatenate(pieces, axis=0)
+        pieces.append(lax.ppermute(held, "hst", [(at, at ^ mask) for at in range(8)]))
 
     width, feats = mats[0].shape
     grads = jax.ShapeDtypeStruct((feats + mats[2].shape[0], width), F32)
-    weights = jax.ShapeDtypeStruct((8 * n_cores, 128), F32)
-    sides = jax.ShapeDtypeStruct((64 * n_cores, side.shape[1]), F32)
-    own_sum, one_sum, weights, sides = call(
+    weights = jax.ShapeDtypeStruct((16, 128), F32)
+    sides = jax.ShapeDtypeStruct((64, side.shape[1]), F32)
+    done = ahead(blocks[0] + blocks[1] + blocks[2], mats[0], mats[2])
+    sum_0, sum_1, sum_2, weights, sides = call(
         first_kernel, "first", slots, 3, (*done, *pieces), mats,
-        (grads, grads, weights, sides),
-    )
-    one_sum, two_sum = call(
-        second_kernel, "second", slots, 2, (one_y, two, sides, weights, one_sum), mats,
+        (grads, grads, grads, weights, sides),
+    )
+    sum_04, sum_3 = call(
+        second_kernel, "second", slots, 2, (*blocks[3], *blocks[4], sides, weights, sum_0), mats,
         (grads, grads),
     )
-    even_sum, three_sum = call(
-        third_kernel, "third", slots, 2, (two_y, three, sides, weights, own_sum, two_sum), mats,
-        (grads, grads),
+    even, sum_15 = call(
+        third_kernel, "third", slots, 2,
+        (*blocks[5], *blocks[6], sides, weights, sum_04, sum_1, sum_2), mats, (grads, grads),
     )
     return call(
-        fourth_kernel, "fourth", slots, 1,
-        (three_y, sides, weights, even_sum, one_sum, three_sum), mats,
+        fourth_kernel, "fourth", slots, 1, (*blocks[7], sides, weights, even, sum_15, sum_3), mats,
         jax.ShapeDtypeStruct(grads.shape, BF16),
     )
 
@@ -457,20 +452,26 @@
     rows = traj * slots
     own = observations.reshape(rows, feats)
     value_row = master_value.reshape(1, -1)
-    side, *mats = prepare(
-        lengths.reshape(1, -1), assign.reshape(1, -1), actions, rewards, own,
-        actor_embed, actor_policy, master_embed, master_policy, value_row,
-    )
-    if n_hst == 8 and n_cores == 2 and rows == BLOCK:
-        mine = gathered_grads(slots, n_cores, own, side, mats)
-        theirs = lax.ppermute(mine, "cores", [(0, 1), (1, 0)])
+    spread, owner = select(traj, slots)
+    flip = [(core, core ^ 1) for core in range(n_cores)]
+    there = [lax.ppermute(array, "cores", flip) for array in (lengths, assign)]
+    gather = n_hst == 8 and n_cores == 2 and rows == BLOCK
+    halves = [own[start : start + HALF] for start in range(0, rows, HALF)]
+    side = side_data(
+        spread, owner, halves, *[array.reshape(1, -1) for array in (lengths, assign, *there)],
+        actions, rewards, actor_embed, actor_policy,
+    )
+    mats = convert(master_embed, master_policy, value_row)
+    if gather:
+        mine = gathered_grads(slots, halves, side, mats)
+        theirs = lax.ppermute(mine, "cores", flip)
     else:
         named = (assign[:, None] == jnp.arange(learners)[None, :]).astype(F32)
         totals = lax.psum(jnp.sum(named * lengths[:, None].astype(F32), axis=0), AXES)
         weights = jnp.broadcast_to((1.0 / (learners * totals))[:, None], (learners, 128))
         grads = call(
             local_kernel, "local", slots, rows // BLOCK,
-            (own.reshape(-1, BLOCK, feats), side, weights), mats,
+            (own.reshape(-1, HALF, feats), side, weights), mats,
             jax.ShapeDtypeStruct((feats + mats[2].shape[0], mats[0].shape[0]), F32),
         )
         mine = lax.psum(grads, AXES)

time: 54.6 us -> 54 us (0.989)
  starting transfers between devices: 17.2 us -> 26 us
  waiting for transfers between devices: 14.2 us -> 9.23 us
  local copies, waits for them, and re-layouts: 3.48 us -> 1.04 us
  Pallas kernels: 18.6 us -> 16.8 us
    ppermute x14 -> x20, starting transfers between devices: 17.2 us -> 26 us  [the longest x14 21.7 us: send(): return [lax.ppermute(half, AXES, ring) for half in blocks]]
    ppermute x14 -> x20, waiting for transfers between devices: 14.2 us -> 9.23 us  [the longest x3 3.21 us: gathered_grads(): lax.ppermute(held, 'hst', [(at, at ^ mask) for at in range(8)])]
    unnamed x36 -> x26, local copies, waits for them, and re-layouts: 3.48 us -> 0.06 us
    slice x0 -> x1, local copies, waits for them, and re-layouts: none -> 0.98 us  [body(): halves = [own[start:start + HALF] for start in range(0, rows, HALF)]]
    pallas_call x1, Pallas kernels: 2.33 us -> 1.36 us  [ahead(): pl.pallas_call(ahead_kernel, out_shape=(jax.ShapeDtypeStruct((feats, rows...]
    pallas_call x1, Pallas kernels: 0.62 us -> 0.01 us  [select(): pl.pallas_call(select_kernel, out_shape=(jax.ShapeDtypeStruct((slots, row...]
    pallas_call x1 -> x2, Pallas kernels: 1.66 us -> 1.25 us  [the longest x1 0.75 us: side_data(): pl.pallas_call(side_kernel, out_shape=jax.ShapeDtypeStruct((8, spread.sha...]
  transfers between devices with their start and end apart: 14 -> 20, of which waited for: 6 -> 6; matrix products, arithmetic and copies ran while one was open for 0% -> 2% of each run, Pallas kernels for 24% -> 21%
where the time goes in v5:
time: 54 us; the launch traced here: 53.9 us
  starting transfers between devices  26 us (48%)
  Pallas kernels  16.8 us (31%)
  waiting for transfers between devices  9.23 us (17%)
  local copies, waits for them, and re-layouts  1.04 us (2%)
  between operations  0.82 us (2%)
    ppermute x14, starting transfers between devices, send(): return [lax.ppermute(half, AXES, ring) for half in blocks]  21.7 us
    pallas_call x4, Pallas kernels, call(): pl.pallas_call(functools.partial(kernel, slots), out_shape=outs, in_specs...  10.8 us
    ppermute x3, starting transfers between devices, gathered_grads(): lax.ppermute(held, 'hst', [(at, at ^ mask) for at in range(8)])  3.65 us
    pallas_call x1, Pallas kernels, update(): pl.pallas_call(functools.partial(update_kernel, feats, nact), out_shape=(...  3.4 us
    ppermute x3, waiting for transfers between devices, gathered_grads(): lax.ppermute(held, 'hst', [(at, at ^ mask) for at in range(8)])  3.21 us
    ppermute x1, waiting for transfers between devices, body(): theirs = lax.ppermute(mine, 'cores', flip)  3.07 us
    ppermute x14, waiting for transfers between devices, send(): return [lax.ppermute(half, AXES, ring) for half in blocks]  2.95 us
    pallas_call x1, Pallas kernels, ahead(): pl.pallas_call(ahead_kernel, out_shape=(jax.ShapeDtypeStruct((feats, rows...  1.36 us
  transfers between devices with their start and end apart: 20, of which 6 were waited for; matrix products, arithmetic and copies ran while one was open for 2% of the time, Pallas kernels for 21%

profile of v5, /device:TPU:0, one launch (start us, length us, event | category | flops | bytes accessed | tf_op | source)
XLA Modules:
  0.0 53.9 jit_solution(17486161081714601296)
XLA Ops:
  0.6 0.5 collective-permute-start.14
  1.2 1.0 %fusion = (bf16[8,16,512]{2,1,0:T(8,128)(2,1)S(1)}, bf16[8,16,512]{2,1,0:T(8,128)(2,1)S(1)}) fusion(bf16[16,16,512]{2,1,0:T(8,128)(2,1)} %param.14), kind=kLoop, calls=%fused_computation.2 | loop fusion | bytes 524288 | tf_op jit(solution)/shard_map/slice | solution.py:459
  2.2 3.1 %collective-permute-start = (bf16[128,512]{1,0:T(8,128)(2,1)S(1)}, bf16[128,512]{1,0:T(8,128)(2,1)S(1)}, u32[]{:S(2)}, u32[]{:S(2)}) collective-permute-start(bf16[128,512]{1,0:T(8,128)(2,1)S(1)} %bitcast.13), channel_id=1, source_target_pairs={{0,4},{1,3},{4,8},{5,1},{8,12},{9,5},{12,14},{13,9},{14,10},{15,13... | collective-permute-start | bytes 393224 | tf_op jit(solution)/shard_map/ppermute | solution.py:413
  5.3 1.6 %collective-permute-start.7 = (bf16[128,512]{1,0:T(8,128)(2,1)S(1)}, bf16[128,512]{1,0:T(8,128)(2,1)S(1)}, u32[]{:S(2)}, u32[]{:S(2)}) collective-permute-start(bf16[128,512]{1,0:T(8,128)(2,1)S(1)} %bitcast.10), channel_id=1, source_target_pairs={{0,4},{1,3},{4,8},{5,1},{8,12},{9,5},{12,14},{13,9},{14,10},{15,13... | collective-permute-start | bytes 393224 | tf_op jit(solution)/shard_map/ppermute | solution.py:413
  7.0 1.2 %collective-permute-done.refs_2_ = bf16[128,512]{1,0:T(8,128)(2,1)S(1)} collective-permute-done((bf16[128,512]{1,0:T(8,128)(2,1)S(1)}, bf16[128,512]{1,0:T(8,128)(2,1)S(1)}, u32[]{:S(2)}, u32[]{:S(2)}) %collective-permute-start) | collective-permute-done | bytes 131104 | tf_op jit(solution)/shard_map/ppermute | solution.py:413
  8.2 2.1 %collective-permute-start.1 = (bf16[128,512]{1,0:T(8,128)(2,1)S(1)}, bf16[128,512]{1,0:T(8,128)(2,1)S(1)}, u32[]{:S(2)}, u32[]{:S(2)}) collective-permute-start(bf16[128,512]{1,0:T(8,128)(2,1)S(1)} %collective-permute-done.refs_2_), channel_id=1, source_target_pairs={{0,4},{1,3},{4,8},{5,1},{8,12},{9,5},{12,14},{13,9},{14,10},{15,13... | collective-permute-start | bytes 393224 | tf_op jit(solution)/shard_map/ppermute | solution.py:413
  10.3 1.6 %collective-permute-start.8 = (bf16[128,512]{1,0:T(8,128)(2,1)S(1)}, bf16[128,512]{1,0:T(8,128)(2,1)S(1)}, u32[]{:S(2)}, u32[]{:S(2)}) collective-permute-start(bf16[128,512]{1,0:T(8,128)(2,1)S(1)} %collective-permute-done.7.refs_3_), channel_id=1, source_target_pairs={{0,4},{1,3},{4,8},{5,1},{8,12},{9,5},{12,14},{13,9},{14,10},{15,13... | collective-permute-start | bytes 393224 | tf_op jit(solution)/shard_map/ppermute | solution.py:413
  12.0 0.8 %side.1.refs_3_ = f32[8,256]{1,0:T(8,128)S(1)} custom-call(s32[1,16]{1,0:T(1,128)S(1)} %bitcast.19, s32[1,16]{1,0:T(1,128)S(1)} %bitcast.20, s32[1,16]{1,0:T(1,128)S(1)} %bitcast.21, s32[1,16]{1,0:T(1,128)S(1)} %bitcast.22, s32[16,16]{1,0:T(8,128)S(1)} %copy-done.8, f32[16,16]{1,0:T(8,128)S(1)} %copy-done.9, bf16[512,1024]{1,0:T(8,128)(2,1)S(1)} %copy-done.4, ...), custom_call_target="tpu_custom_call" | custom-call | flops 1430000000 | tf_op jit(solution)/shard_map/side/pallas_call | solution.py:104
  12.7 0.5 collective-permute-start.16
  13.2 3.2 %collective-permute-done.16.refs_4_ = f32[8,256]{1,0:T(8,128)S(1)} collective-permute-done((f32[8,256]{1,0:T(8,128)S(1)}, f32[8,256]{1,0:T(8,128)S(1)}, u32[]{:S(2)}, u32[]{:S(2)}) %collective-permute-start.16) | collective-permute-done | bytes 8224 | tf_op jit(solution)/shard_map/ppermute | solution.py:421
  16.4 1.6 %collective-permute-start.17 = (f32[16,256]{1,0:T(8,128)S(1)}, f32[16,256]{1,0:T(8,128)S(1)}, u32[]{:S(2)}, u32[]{:S(2)}) collective-permute-start(f32[16,256]{1,0:T(8,128)S(1)} %pad_maximum_fusion.1), channel_id=1, source_target_pairs={{0,4},{2,6},{4,0},{6,2},{8,12},{10,14},{12,8},{14,10},{1,5},{3,7},... | collective-permute-start | bytes 49160 | tf_op jit(solution)/shard_map/ppermute | solution.py:421
  18.0 0.5 collective-permute-start.9
  18.5 2.4 %collective-permute-start.2 = (bf16[128,512]{1,0:T(8,128)(2,1)S(1)}, bf16[128,512]{1,0:T(8,128)(2,1)S(1)}, u32[]{:S(2)}, u32[]{:S(2)}) collective-permute-start(bf16[128,512]{1,0:T(8,128)(2,1)S(1)} %collective-permute-done.1.refs_4_), channel_id=1, source_target_pairs={{0,4},{1,3},{4,8},{5,1},{8,12},{9,5},{12,14},{13,9},{14,10},{15,13... | collective-permute-start | bytes 393224 | tf_op jit(solution)/shard_map/ppermute | solution.py:413
  20.9 0.5 convert.1
  21.4 1.6 %collective-permute-start.18 = (f32[32,256]{1,0:T(8,128)S(1)}, f32[32,256]{1,0:T(8,128)S(1)}, u32[]{:S(2)}, u32[]{:S(2)}) collective-permute-start(f32[32,256]{1,0:T(8,128)S(1)} %pad_maximum_fusion), channel_id=1, source_target_pairs={{0,8},{2,10},{4,12},{6,14},{8,0},{10,2},{12,4},{14,6},{1,9},{3,11}... | collective-permute-start | bytes 98312 | tf_op jit(solution)/shard_map/ppermute | solution.py:421
  23.0 1.4 %collective-permute-start.10 = (bf16[128,512]{1,0:T(8,128)(2,1)S(1)}, bf16[128,512]{1,0:T(8,128)(2,1)S(1)}, u32[]{:S(2)}, u32[]{:S(2)}) collective-permute-start(bf16[128,512]{1,0:T(8,128)(2,1)S(1)} %collective-permute-done.9.refs_1_), channel_id=1, source_target_pairs={{0,4},{1,3},{4,8},{5,1},{8,12},{9,5},{12,14},{13,9},{14,10},{15,13... | collective-permute-start | bytes 393224 | tf_op jit(solution)/shard_map/ppermute | solution.py:413
  24.4 1.4 %collective-permute-start.3 = (bf16[128,512]{1,0:T(8,128)(2,1)S(1)}, bf16[128,512]{1,0:T(8,128)(2,1)S(1)}, u32[]{:S(2)}, u32[]{:S(2)}) collective-permute-start(bf16[128,512]{1,0:T(8,128)(2,1)S(1)} %collective-permute-done.2.refs_0_), channel_id=1, source_target_pairs={{0,4},{1,3},{4,8},{5,1},{8,12},{9,5},{12,14},{13,9},{14,10},{15,13... | collective-permute-start | bytes 393224 | tf_op jit(solution)/shard_map/ppermute | solution.py:413
  25.8 1.4 %ahead.1 = (bf16[512,768]{1,0:T(8,128)(2,1)S(1)}, bf16[1024,768]{1,0:T(8,128)(2,1)S(1)}, f32[144,768]{1,0:T(8,128)S(1)}) custom-call(bf16[128,512]{1,0:T(8,128)(2,1)S(1)} %bitcast.15, bf16[128,512]{1,0:T(8,128)(2,1)S(1)} %bitcast.12, bf16[128,512]{1,0:T(8,128)(2,1)S(1)} %collective-permute-done.refs_2_, bf16[128,512]{1,0:T(8,128)(2,1)S(1)} %collective-permute-done.7.refs_3_, ...), custom_call_target="tpu_custom_call" | custom-call | flops 1760000000 | tf_op jit(solution)/shard_map/ahead/pallas_call | solution.py:265
  27.2 0.8 %collective-permute-done.10.refs_3_ = bf16[128,512]{1,0:T(8,128)(2,1)S(1)} collective-permute-done((bf16[128,512]{1,0:T(8,128)(2,1)S(1)}, bf16[128,512]{1,0:T(8,128)(2,1)S(1)}, u32[]{:S(2)}, u32[]{:S(2)}) %collective-permute-start.10) | collective-permute-done | bytes 131104 | tf_op jit(solution)/shard_map/ppermute | solution.py:413
  28.0 1.4 %collective-permute-start.11 = (bf16[128,512]{1,0:T(8,128)(2,1)S(1)}, bf16[128,512]{1,0:T(8,128)(2,1)S(1)}, u32[]{:S(2)}, u32[]{:S(2)}) collective-permute-start(bf16[128,512]{1,0:T(8,128)(2,1)S(1)} %collective-permute-done.10.refs_3_), channel_id=1, source_target_pairs={{0,4},{1,3},{4,8},{5,1},{8,12},{9,5},{12,14},{13,9},{14,10},{15,13... | collective-permute-start | bytes 393224 | tf_op jit(solution)/shard_map/ppermute | solution.py:413
  29.4 1.4 %collective-permute-start.4 = (bf16[128,512]{1,0:T(8,128)(2,1)S(1)}, bf16[128,512]{1,0:T(8,128)(2,1)S(1)}, u32[]{:S(2)}, u32[]{:S(2)}) collective-permute-start(bf16[128,512]{1,0:T(8,128)(2,1)S(1)} %collective-permute-done.3.refs_2_), channel_id=1, source_target_pairs={{0,4},{1,3},{4,8},{5,1},{8,12},{9,5},{12,14},{13,9},{14,10},{15,13... | collective-permute-start | bytes 393224 | tf_op jit(solution)/shard_map/ppermute | solution.py:413
  30.8 2.6 %first.1 = (f32[656,1024]{1,0:T(8,128)S(1)}, f32[656,1024]{1,0:T(8,128)S(1)}, f32[656,1024]{1,0:T(8,128)S(1)}, f32[16,128]{1,0:T(8,128)S(1)}, f32[64,256]{1,0:T(8,128)S(1)}) custom-call(bf16[512,768]{1,0:T(8,128)(2,1)S(1)} %get-tuple-element.33.refs_0_, bf16[1024,768]{1,0:T(8,128)(2,1)S(1)} %get-tuple-element.34.refs_1_, ...), custom_call_target="tpu_custom_call" | custom-call | flops 4400000000 | tf_op jit(solution)/shard_map/first/pallas_call | solution.py:350
  33.4 1.4 %collective-permute-start.12 = (bf16[128,512]{1,0:T(8,128)(2,1)S(1)}, bf16[128,512]{1,0:T(8,128)(2,1)S(1)}, u32[]{:S(2)}, u32[]{:S(2)}) collective-permute-start(bf16[128,512]{1,0:T(8,128)(2,1)S(1)} %collective-permute-done.11.refs_1_), channel_id=1, source_target_pairs={{0,4},{1,3},{4,8},{5,1},{8,12},{9,5},{12,14},{13,9},{14,10},{15,13... | collective-permute-start | bytes 393224 | tf_op jit(solution)/shard_map/ppermute | solution.py:413
  34.8 0.9 %collective-permute-start.5 = (bf16[128,512]{1,0:T(8,128)(2,1)S(1)}, bf16[128,512]{1,0:T(8,128)(2,1)S(1)}, u32[]{:S(2)}, u32[]{:S(2)}) collective-permute-start(bf16[128,512]{1,0:T(8,128)(2,1)S(1)} %collective-permute-done.4.refs_0_), channel_id=1, source_target_pairs={{0,4},{1,3},{4,8},{5,1},{8,12},{9,5},{12,14},{13,9},{14,10},{15,13... | collective-permute-start | bytes 393224 | tf_op jit(solution)/shard_map/ppermute | solution.py:413
  35.8 2.9 %second.1 = (f32[656,1024]{1,0:T(8,128)S(1)}, f32[656,1024]{1,0:T(8,128)S(1)}) custom-call(bf16[128,512]{1,0:T(8,128)(2,1)S(1)} %collective-permute-done.2.refs_0_, bf16[128,512]{1,0:T(8,128)(2,1)S(1)} %collective-permute-done.9.refs_1_, bf16[128,512]{1,0:T(8,128)(2,1)S(1)} %collective-permute-done.3.refs_2_, ...), custom_call_target="tpu_custom_call" | custom-call | flops 3080000000 | tf_op jit(solution)/shard_map/second/pallas_call | solution.py:350
  38.7 1.5 %collective-permute-start.13 = (bf16[128,512]{1,0:T(8,128)(2,1)S(1)}, bf16[128,512]{1,0:T(8,128)(2,1)S(1)}, u32[]{:S(2)}, u32[]{:S(2)}) collective-permute-start(bf16[128,512]{1,0:T(8,128)(2,1)S(1)} %collective-permute-done.12.refs_3_), channel_id=1, source_target_pairs={{0,4},{1,3},{4,8},{5,1},{8,12},{9,5},{12,14},{13,9},{14,10},{15,13... | collective-permute-start | bytes 393224 | tf_op jit(solution)/shard_map/ppermute | solution.py:413
  40.2 1.0 %collective-permute-start.6 = (bf16[128,512]{1,0:T(8,128)(2,1)S(1)}, bf16[128,512]{1,0:T(8,128)(2,1)S(1)}, u32[]{:S(2)}, u32[]{:S(2)}) collective-permute-start(bf16[128,512]{1,0:T(8,128)(2,1)S(1)} %collective-permute-done.5.refs_2_), channel_id=1, source_target_pairs={{0,4},{1,3},{4,8},{5,1},{8,12},{9,5},{12,14},{13,9},{14,10},{15,13... | collective-permute-start | bytes 393224 | tf_op jit(solution)/shard_map/ppermute | solution.py:413
  41.2 3.1 %third.1 = (f32[656,1024]{1,0:T(8,128)S(1)}, f32[656,1024]{1,0:T(8,128)S(1)}) custom-call(bf16[128,512]{1,0:T(8,128)(2,1)S(1)} %collective-permute-done.4.refs_0_, bf16[128,512]{1,0:T(8,128)(2,1)S(1)} %collective-permute-done.11.refs_1_, bf16[128,512]{1,0:T(8,128)(2,1)S(1)} %collective-permute-done.5.refs_2_, ...), custom_call_target="tpu_custom_call" | custom-call | flops 3080000000 | tf_op jit(solution)/shard_map/third/pallas_call | solution.py:350
  44.3 0.8 %collective-permute-done.6.refs_0_ = bf16[128,512]{1,0:T(8,128)(2,1)S(1)} collective-permute-done((bf16[128,512]{1,0:T(8,128)(2,1)S(1)}, bf16[128,512]{1,0:T(8,128)(2,1)S(1)}, u32[]{:S(2)}, u32[]{:S(2)}) %collective-permute-start.6) | collective-permute-done | bytes 131104 | tf_op jit(solution)/shard_map/ppermute | solution.py:413
  45.1 2.2 %fourth.1.mine = bf16[656,1024]{1,0:T(8,128)(2,1)S(1)} custom-call(bf16[128,512]{1,0:T(8,128)(2,1)S(1)} %collective-permute-done.6.refs_0_, bf16[128,512]{1,0:T(8,128)(2,1)S(1)} %collective-permute-done.13.refs_1_, f32[64,256]{1,0:T(8,128)S(1)} %get-tuple-element.39.refs_4_.refs_2_, f32[16,128]{1,0:T(8,128)S(1)} %get-tuple-element.40.refs_5_.refs_3_, ...), custom_call_target="tpu_custom_call" | custom-call | flops 1760000000 | tf_op jit(solution)/shard_map/fourth/pallas_call | solution.py:350
  47.4 3.1 %collective-permute-done.19.theirs = bf16[656,1024]{1,0:T(8,128)(2,1)S(1)} collective-permute-done((bf16[656,1024]{1,0:T(8,128)(2,1)S(1)}, bf16[656,1024]{1,0:T(8,128)(2,1)S(1)}, u32[]{:S(2)}, u32[]{:S(2)}) %collective-permute-start.19) | collective-permute-done | bytes 1343520 | tf_op jit(solution)/shard_map/ppermute | solution.py:467
  50.5 3.4 %update.1 = (bf16[256,128]{1,0:T(8,128)(2,1)}, f32[512,1024]{1,0:T(8,128)}, f32[1024,128]{1,0:T(8,128)}, f32[1,1024]{1,0:T(1,128)}, f32[512,1024]{1,0:T(8,128)}, /*index=5*/f32[1024,128]{1,0:T(8,128)}, f32[1,1024]{1,0:T(1,128)}) custom-call(bf16[656,1024]{1,0:T(8,128)(2,1)S(1)} %fourth.1.mine, bf16[656,1024]{1,0:T(8,128)(2,1)S(1)} %collective-permute-done.19.theirs, ...), custom_call_target="tpu_custom_call" | custom-call | flops 3740000000 | tf_op jit(solution)/shard_map/update/pallas_call | solution.py:393
  (46 shorter events, 0.4 us)
Async XLA Ops:
  0.6 11.3 %collective-permute-start.14 = (s32[16]{0:T(128)}, s32[16]{0:T(128)S(1)}, u32[]{:S(2)}, u32[]{:S(2)}) collective-permute-start(s32[16]{0:T(128)} %param.15), channel_id=1, source_target_pairs={{0,1},{1,0},{2,3},{3,2},{4,5},{5,4},{6,7},{7,6},{8,9},{9,8},{10,11... | collective-permute-start | bytes 200 | tf_op jit(solution)/shard_map/ppermute | solution.py:457
  1.1 10.8 %collective-permute-start.15 = (s32[16]{0:T(128)}, s32[16]{0:T(128)S(1)}, u32[]{:S(2)}, u32[]{:S(2)}) collective-permute-start(s32[16]{0:T(128)} %param.18), channel_id=1, source_target_pairs={{0,1},{1,0},{2,3},{3,2},{4,5},{5,4},{6,7},{7,6},{8,9},{9,8},{10,11... | collective-permute-start | bytes 200 | tf_op jit(solution)/shard_map/ppermute | solution.py:457
  2.2 5.9 %collective-permute-start = (bf16[128,512]{1,0:T(8,128)(2,1)S(1)}, bf16[128,512]{1,0:T(8,128)(2,1)S(1)}, u32[]{:S(2)}, u32[]{:S(2)}) collective-permute-start(bf16[128,512]{1,0:T(8,128)(2,1)S(1)} %bitcast.13), channel_id=1, source_target_pairs={{0,4},{1,3},{4,8},{5,1},{8,12},{9,5},{12,14},{13,9},{14,10},{15,13... | collective-permute-start | bytes 393224 | tf_op jit(solution)/shard_map/ppermute | solution.py:413
  5.3 6.6 %copy-start.4 = (bf16[512,1024]{1,0:T(8,128)(2,1)S(1)}, bf16[512,1024]{1,0:T(8,128)(2,1)}, u32[]{:S(2)}) copy-start(bf16[512,1024]{1,0:T(8,128)(2,1)} %actor_embed.1) | copy-start | bytes 3145732
  5.3 6.6 %copy-start.6 = (bf16[1024,128]{1,0:T(8,128)(2,1)S(1)}, bf16[1024,128]{1,0:T(8,128)(2,1)}, u32[]{:S(2)}) copy-start(bf16[1024,128]{1,0:T(8,128)(2,1)} %actor_policy.1) | copy-start | bytes 786436
  5.3 6.7 %copy-start.8 = (s32[16,16]{1,0:T(8,128)S(1)}, s32[16,16]{1,0:T(8,128)}, u32[]{:S(2)}) copy-start(s32[16,16]{1,0:T(8,128)} %actions.1) | copy-start | bytes 3076
  5.3 6.7 %copy-start.9 = (f32[16,16]{1,0:T(8,128)S(1)}, f32[16,16]{1,0:T(8,128)}, u32[]{:S(2)}) copy-start(f32[16,16]{1,0:T(8,128)} %rewards.1) | copy-start | bytes 3076
  5.3 6.7 %copy-start.11 = (s32[16]{0:T(128)S(1)}, s32[16]{0:T(128)}, u32[]{:S(2)}) copy-start(s32[16]{0:T(128)} %param.15) | copy-start | bytes 196
  5.3 6.7 %copy-start.12 = (s32[16]{0:T(128)S(1)}, s32[16]{0:T(128)}, u32[]{:S(2)}) copy-start(s32[16]{0:T(128)} %param.18) | copy-start | bytes 196
  5.3 5.0 %collective-permute-start.7 = (bf16[128,512]{1,0:T(8,128)(2,1)S(1)}, bf16[128,512]{1,0:T(8,128)(2,1)S(1)}, u32[]{:S(2)}, u32[]{:S(2)}) collective-permute-start(bf16[128,512]{1,0:T(8,128)(2,1)S(1)} %bitcast.10), channel_id=1, source_target_pairs={{0,4},{1,3},{4,8},{5,1},{8,12},{9,5},{12,14},{13,9},{14,10},{15,13... | collective-permute-start | bytes 393224 | tf_op jit(solution)/shard_map/ppermute | solution.py:413
  6.9 13.9 %copy-start = (f32[512,1024]{1,0:T(8,128)S(1)}, f32[512,1024]{1,0:T(8,128)}, u32[]{:S(2)}) copy-start(f32[512,1024]{1,0:T(8,128)} %master_embed.3) | copy-start | bytes 6291460
  6.9 13.9 %copy-start.1 = (f32[1024,128]{1,0:T(8,128)S(1)}, f32[1024,128]{1,0:T(8,128)}, u32[]{:S(2)}) copy-start(f32[1024,128]{1,0:T(8,128)} %master_policy.3) | copy-start | bytes 1572868
  7.0 13.9 %copy-start.2 = (f32[1024]{0:T(1024)S(1)}, f32[1024]{0:T(1024)}, u32[]{:S(2)}) copy-start(f32[1024]{0:T(1024)} %param.23) | copy-start | bytes 12292
  8.2 10.3 %collective-permute-start.1 = (bf16[128,512]{1,0:T(8,128)(2,1)S(1)}, bf16[128,512]{1,0:T(8,128)(2,1)S(1)}, u32[]{:S(2)}, u32[]{:S(2)}) collective-permute-start(bf16[128,512]{1,0:T(8,128)(2,1)S(1)} %collective-permute-done.refs_2_), channel_id=1, source_target_pairs={{0,4},{1,3},{4,8},{5,1},{8,12},{9,5},{12,14},{13,9},{14,10},{15,13... | collective-permute-start | bytes 393224 | tf_op jit(solution)/shard_map/ppermute | solution.py:413
  10.3 7.7 %collective-permute-start.8 = (bf16[128,512]{1,0:T(8,128)(2,1)S(1)}, bf16[128,512]{1,0:T(8,128)(2,1)S(1)}, u32[]{:S(2)}, u32[]{:S(2)}) collective-permute-start(bf16[128,512]{1,0:T(8,128)(2,1)S(1)} %collective-permute-done.7.refs_3_), channel_id=1, source_target_pairs={{0,4},{1,3},{4,8},{5,1},{8,12},{9,5},{12,14},{13,9},{14,10},{15,13... | collective-permute-start | bytes 393224 | tf_op jit(solution)/shard_map/ppermute | solution.py:413
  12.7 3.7 %collective-permute-start.16 = (f32[8,256]{1,0:T(8,128)S(1)}, f32[8,256]{1,0:T(8,128)S(1)}, u32[]{:S(2)}, u32[]{:S(2)}) collective-permute-start(f32[8,256]{1,0:T(8,128)S(1)} %side.1.refs_3_), channel_id=1, source_target_pairs={{0,2},{2,0},{4,6},{6,4},{8,10},{10,8},{12,14},{14,12},{1,3},{3,1},... | collective-permute-start | bytes 24584 | tf_op jit(solution)/shard_map/ppermute | solution.py:421
  16.4 4.9 %collective-permute-start.17 = (f32[16,256]{1,0:T(8,128)S(1)}, f32[16,256]{1,0:T(8,128)S(1)}, u32[]{:S(2)}, u32[]{:S(2)}) collective-permute-start(f32[16,256]{1,0:T(8,128)S(1)} %pad_maximum_fusion.1), channel_id=1, source_target_pairs={{0,4},{2,6},{4,0},{6,2},{8,12},{10,14},{12,8},{14,10},{1,5},{3,7},... | collective-permute-start | bytes 49160 | tf_op jit(solution)/shard_map/ppermute | solution.py:421
  18.0 5.0 %collective-permute-start.9 = (bf16[128,512]{1,0:T(8,128)(2,1)S(1)}, bf16[128,512]{1,0:T(8,128)(2,1)S(1)}, u32[]{:S(2)}, u32[]{:S(2)}) collective-permute-start(bf16[128,512]{1,0:T(8,128)(2,1)S(1)} %collective-permute-done.8.refs_5_), channel_id=1, source_target_pairs={{0,4},{1,3},{4,8},{5,1},{8,12},{9,5},{12,14},{13,9},{14,10},{15,13... | collective-permute-start | bytes 393224 | tf_op jit(solution)/shard_map/ppermute | solution.py:413
  18.5 5.9 %collective-permute-start.2 = (bf16[128,512]{1,0:T(8,128)(2,1)S(1)}, bf16[128,512]{1,0:T(8,128)(2,1)S(1)}, u32[]{:S(2)}, u32[]{:S(2)}) collective-permute-start(bf16[128,512]{1,0:T(8,128)(2,1)S(1)} %collective-permute-done.1.refs_4_), channel_id=1, source_target_pairs={{0,4},{1,3},{4,8},{5,1},{8,12},{9,5},{12,14},{13,9},{14,10},{15,13... | collective-permute-start | bytes 393224 | tf_op jit(solution)/shard_map/ppermute | solution.py:413
  21.4 9.4 %collective-permute-start.18 = (f32[32,256]{1,0:T(8,128)S(1)}, f32[32,256]{1,0:T(8,128)S(1)}, u32[]{:S(2)}, u32[]{:S(2)}) collective-permute-start(f32[32,256]{1,0:T(8,128)S(1)} %pad_maximum_fusion), channel_id=1, source_target_pairs={{0,8},{2,10},{4,12},{6,14},{8,0},{10,2},{12,4},{14,6},{1,9},{3,11}... | collective-permute-start | bytes 98312 | tf_op jit(solution)/shard_map/ppermute | solution.py:421
  23.0 5.0 %collective-permute-start.10 = (bf16[128,512]{1,0:T(8,128)(2,1)S(1)}, bf16[128,512]{1,0:T(8,128)(2,1)S(1)}, u32[]{:S(2)}, u32[]{:S(2)}) collective-permute-start(bf16[128,512]{1,0:T(8,128)(2,1)S(1)} %collective-permute-done.9.refs_1_), channel_id=1, source_target_pairs={{0,4},{1,3},{4,8},{5,1},{8,12},{9,5},{12,14},{13,9},{14,10},{15,13... | collective-permute-start | bytes 393224 | tf_op jit(solution)/shard_map/ppermute | solution.py:413
  24.4 5.0 %collective-permute-start.3 = (bf16[128,512]{1,0:T(8,128)(2,1)S(1)}, bf16[128,512]{1,0:T(8,128)(2,1)S(1)}, u32[]{:S(2)}, u32[]{:S(2)}) collective-permute-start(bf16[128,512]{1,0:T(8,128)(2,1)S(1)} %collective-permute-done.2.refs_0_), channel_id=1, source_target_pairs={{0,4},{1,3},{4,8},{5,1},{8,12},{9,5},{12,14},{13,9},{14,10},{15,13... | collective-permute-start | bytes 393224 | tf_op jit(solution)/shard_map/ppermute | solution.py:413
  28.0 5.4 %collective-permute-start.11 = (bf16[128,512]{1,0:T(8,128)(2,1)S(1)}, bf16[128,512]{1,0:T(8,128)(2,1)S(1)}, u32[]{:S(2)}, u32[]{:S(2)}) collective-permute-start(bf16[128,512]{1,0:T(8,128)(2,1)S(1)} %collective-permute-done.10.refs_3_), channel_id=1, source_target_pairs={{0,4},{1,3},{4,8},{5,1},{8,12},{9,5},{12,14},{13,9},{14,10},{15,13... | collective-permute-start | bytes 393224 | tf_op jit(solution)/shard_map/ppermute | solution.py:413
  29.4 5.5 %collective-permute-start.4 = (bf16[128,512]{1,0:T(8,128)(2,1)S(1)}, bf16[128,512]{1,0:T(8,128)(2,1)S(1)}, u32[]{:S(2)}, u32[]{:S(2)}) collective-permute-start(bf16[128,512]{1,0:T(8,128)(2,1)S(1)} %collective-permute-done.3.refs_2_), channel_id=1, source_target_pairs={{0,4},{1,3},{4,8},{5,1},{8,12},{9,5},{12,14},{13,9},{14,10},{15,13... | collective-permute-start | bytes 393224 | tf_op jit(solution)/shard_map/ppermute | solution.py:413
  33.4 5.3 %collective-permute-start.12 = (bf16[128,512]{1,0:T(8,128)(2,1)S(1)}, bf16[128,512]{1,0:T(8,128)(2,1)S(1)}, u32[]{:S(2)}, u32[]{:S(2)}) collective-permute-start(bf16[128,512]{1,0:T(8,128)(2,1)S(1)} %collective-permute-done.11.refs_1_), channel_id=1, source_target_pairs={{0,4},{1,3},{4,8},{5,1},{8,12},{9,5},{12,14},{13,9},{14,10},{15,13... | collective-permute-start | bytes 393224 | tf_op jit(solution)/shard_map/ppermute | solution.py:413
  34.8 5.3 %collective-permute-start.5 = (bf16[128,512]{1,0:T(8,128)(2,1)S(1)}, bf16[128,512]{1,0:T(8,128)(2,1)S(1)}, u32[]{:S(2)}, u32[]{:S(2)}) collective-permute-start(bf16[128,512]{1,0:T(8,128)(2,1)S(1)} %collective-permute-done.4.refs_0_), channel_id=1, source_target_pairs={{0,4},{1,3},{4,8},{5,1},{8,12},{9,5},{12,14},{13,9},{14,10},{15,13... | collective-permute-start | bytes 393224 | tf_op jit(solution)/shard_map/ppermute | solution.py:413
  38.7 5.6 %collective-permute-start.13 = (bf16[128,512]{1,0:T(8,128)(2,1)S(1)}, bf16[128,512]{1,0:T(8,128)(2,1)S(1)}, u32[]{:S(2)}, u32[]{:S(2)}) collective-permute-start(bf16[128,512]{1,0:T(8,128)(2,1)S(1)} %collective-permute-done.12.refs_3_), channel_id=1, source_target_pairs={{0,4},{1,3},{4,8},{5,1},{8,12},{9,5},{12,14},{13,9},{14,10},{15,13... | collective-permute-start | bytes 393224 | tf_op jit(solution)/shard_map/ppermute | solution.py:413
  40.2 5.0 %collective-permute-start.6 = (bf16[128,512]{1,0:T(8,128)(2,1)S(1)}, bf16[128,512]{1,0:T(8,128)(2,1)S(1)}, u32[]{:S(2)}, u32[]{:S(2)}) collective-permute-start(bf16[128,512]{1,0:T(8,128)(2,1)S(1)} %collective-permute-done.5.refs_2_), channel_id=1, source_target_pairs={{0,4},{1,3},{4,8},{5,1},{8,12},{9,5},{12,14},{13,9},{14,10},{15,13... | collective-permute-start | bytes 393224 | tf_op jit(solution)/shard_map/ppermute | solution.py:413
  45.1 5.3 %copy-start.5 = (f32[1024,128]{1,0:T(8,128)S(1)}, f32[1024,128]{1,0:T(8,128)}, u32[]{:S(2)}) copy-start(f32[1024,128]{1,0:T(8,128)} %policy_moment.1) | copy-start | bytes 1572868
  45.1 5.3 %copy-start.7 = (bf16[256,512]{1,0:T(8,128)(2,1)S(1)}, bf16[256,512]{1,0:T(8,128)(2,1)}, u32[]{:S(2)}) copy-start(bf16[256,512]{1,0:T(8,128)(2,1)} %next_obs.1) | copy-start | bytes 786436
  45.1 5.3 %copy-start.10 = (f32[1024]{0:T(1024)S(1)}, f32[1024]{0:T(1024)}, u32[]{:S(2)}) copy-start(f32[1024]{0:T(1024)} %param.26) | copy-start | bytes 12292
  47.3 3.1 %collective-permute-start.19 = (bf16[656,1024]{1,0:T(8,128)(2,1)S(1)}, bf16[656,1024]{1,0:T(8,128)(2,1)S(1)}, u32[]{:S(2)}, u32[]{:S(2)}) collective-permute-start(bf16[656,1024]{1,0:T(8,128)(2,1)S(1)} %fourth.1.mine), channel_id=1, source_target_pairs={{0,1},{1,0},{2,3},{3,2},{4,5},{5,4},{6,7},{7,6},{8,9},{9,8},{10,11... | collective-permute-start | bytes 4030472 | tf_op jit(solution)/shard_map/ppermute | solution.py:467
  (1 other events, 5.3 us)

commit v6 on v5

--- a/solution.py
+++ b/solution.py
@@ -17,7 +17,6 @@
 VMEM = pl.BlockSpec(memory_space=pltpu.VMEM)
 MIB = 2**20
 BLOCK = 256
-HALF = 128
 PAD = 16
 BEHAVE, ACTION, REWARD, LENGTH, ASSIGN, LENGTH_2, ASSIGN_2 = range(7)
 
@@ -63,9 +62,8 @@
 
 def side_kernel(
     lengths, assign, lengths_2, assign_2, actions, rewards, actor_embed, actor_policy,
-    spread, owner, *refs,
+    spread, owner, obs, side,
 ):
-    halves, side = refs[:-1], refs[-1]
 
     def flat(series):
         wide = jnp.dot(
@@ -80,8 +78,7 @@
         )
 
     action = flat(actions[...].astype(F32))
-    obs = jnp.concatenate([half[...] for half in halves], axis=0)
-    hidden = jnp.maximum(mm(obs, actor_embed[...]), 0.0).astype(BF16)
+    hidden = jnp.maximum(mm(obs[...], actor_embed[...]), 0.0).astype(BF16)
     logits = mm(hidden, actor_policy[...]).T
     top = jnp.max(logits, axis=0, keepdims=True)
     shifted = logits - top
@@ -99,8 +96,8 @@
     side[ASSIGN_2 : ASSIGN_2 + 1, :] = repeat(assign_2[...])
 
 
-def side_data(spread, owner, halves, *args):
-    count = len(args) + 2 + len(halves)
+def side_data(spread, owner, obs, *args):
+    count = len(args) + 3
     return pl.pallas_call(
         side_kernel,
         out_shape=jax.ShapeDtypeStruct((8, spread.shape[1]), F32),
@@ -109,7 +106,7 @@
         compiler_params=params(12),
         cost_estimate=cost(1.3),
         name="side",
-    )(*args, spread, owner, *halves)
+    )(*args, spread, owner, obs)
 
 
 def convert_kernel(master_embed, master_policy, master_value, embed_t, head, head_t):
@@ -207,8 +204,8 @@
 def forward(frames, embed_t, head_t, frames_t, hidden_t):
     width = embed_t.shape[0]
     tile = 256
-    for index, half in enumerate(frames):
-        frames_t[:, index * HALF : (index + 1) * HALF] = half[...].T
+    for index, block in enumerate(frames):
+        frames_t[:, index * BLOCK : (index + 1) * BLOCK] = block[...].T
     for start in range(0, width, tile):
         here = slice(start, start + tile)
         hidden_t[here, :] = jnp.maximum(mm(embed_t[here, :], frames_t[...]), 0.0).astype(BF16)
@@ -240,18 +237,10 @@
     backward(slots, logits, side, weights, head, frames_t, hidden_t, preact_t, add)
 
 
-def ring_place(hst):
-    line, across = lax.div(hst, 2), lax.rem(hst, 2)
-    return jnp.where(across == 0, line, 7 - line)
-
-
-def side_of(sides, step):
-    hst = lax.axis_index("hst")
-    way = jnp.where(lax.axis_index("cores") == 0, 7, 1)
-    there = lax.bitwise_and(ring_place(hst) + way * step, 7)
-    chip = jnp.where(there < 4, 2 * there, 2 * (7 - there) + 1)
-    mask = lax.bitwise_xor(hst, chip)
-    return sides[pl.ds(pl.multiple_of(8 * mask, 8), 8), :]
+def side_of(sides, back, flip):
+    line = lax.div(lax.axis_index("hst"), 2)
+    there = lax.bitwise_xor(line, lax.bitwise_and(line + 4 - back, 3))
+    return sides[pl.ds(pl.multiple_of(8 * (4 * flip + there), 8), 8), :]
 
 
 def ahead_kernel(*refs):
@@ -261,7 +250,7 @@
 
 def ahead(frames, embed_t, head_t):
     width, feats = embed_t.shape
-    rows = len(frames) * HALF
+    rows = len(frames) * BLOCK
     return pl.pallas_call(
         ahead_kernel,
         out_shape=(
@@ -272,14 +261,14 @@
         in_specs=[VMEM] * (len(frames) + 2),
         out_specs=(VMEM,) * 3,
         compiler_params=params(20),
-        cost_estimate=cost(1.6),
+        cost_estimate=cost(0.1),
         name="ahead",
     )(*frames, embed_t, head_t)
 
 
 def first_kernel(slots, *refs):
-    (frames_t, hidden_t, logits, *pieces), mats, outs, (weights, sides), scratch = (
-        refs[0:7], refs[7:10], refs[10:13], refs[13:15], refs[15:18])
+    (frames_t, hidden_t, logits, *pieces), mats, (sum_0, sum_1, weights, sides), scratch = (
+        refs[0:5], refs[5:8], refs[8:12], refs[12:15])
     start = 0
     for piece in pieces:
         sides[start : start + piece.shape[0], :] = piece[...]
@@ -287,50 +276,55 @@
     learner_weights(slots, sides, weights)
 
     def add(index, rows, value):
-        outs[index][rows, :] = value
-
-    side = jnp.concatenate([side_of(sides, step) for step in (0, 1, 2)], axis=1)
+        if index == 0:
+            sum_0[rows, :] = value
+        elif index == 1:
+            sum_0[rows, :] += value
+        else:
+            sum_1[rows, :] = value
+
+    side = jnp.concatenate([side_of(sides, *at) for at in ((0, 0), (0, 1), (1, 0))], axis=1)
     backward(slots, logits[...], side, weights, mats[1], frames_t, hidden_t, scratch[2], add)
 
 
 def second_kernel(slots, *refs):
-    frames, (sides, weights, sum_0), mats, (sum_04, sum_3), scratch = (
-        refs[0:4], refs[4:7], refs[7:10], refs[10:12], refs[12:15])
+    frames, (sides, weights, sum_1), mats, (sum_1y, sum_2), scratch = (
+        refs[0:2], refs[2:5], refs[5:8], refs[8:10], refs[10:13])
 
     def add(index, rows, value):
         if index == 0:
-            sum_3[rows, :] = value
+            sum_1y[rows, :] = sum_1[rows, :] + value
         else:
-            sum_04[rows, :] = sum_0[rows, :] + value
-
-    side = jnp.concatenate([side_of(sides, 3), side_of(sides, 4)], axis=1)
+            sum_2[rows, :] = value
+
+    side = jnp.concatenate([side_of(sides, 1, 1), side_of(sides, 2, 0)], axis=1)
     work(slots, frames, side, weights, *mats, *scratch, add)
 
 
 def third_kernel(slots, *refs):
-    frames, (sides, weights, sum_04, sum_1, sum_2), mats, (even, sum_15), scratch = (
-        refs[0:4], refs[4:9], refs[9:12], refs[12:14], refs[14:17])
+    frames, (sides, weights, sum_0, sum_2), mats, (even, sum_3), scratch = (
+        refs[0:2], refs[2:6], refs[6:9], refs[9:11], refs[11:14])
 
     def add(index, rows, value):
         if index == 0:
-            sum_15[rows, :] = sum_1[rows, :] + value
+            even[rows, :] = sum_0[rows, :] + (sum_2[rows, :] + value)
         else:
-            even[rows, :] = sum_04[rows, :] + (sum_2[rows, :] + value)
-
-    side = jnp.concatenate([side_of(sides, 5), side_of(sides, 6)], axis=1)
+            sum_3[rows, :] = value
+
+    side = jnp.concatenate([side_of(sides, 2, 1), side_of(sides, 3, 0)], axis=1)
     work(slots, frames, side, weights, *mats, *scratch, add)
 
 
 def fourth_kernel(slots, *refs):
-    frames, (sides, weights, even, sum_15, sum_3), mats, out, scratch = (
-        refs[0:2], refs[2:7], refs[7:10], refs[10], refs[11:14])
+    frames, (sides, weights, even, sum_1y, sum_3), mats, out, scratch = (
+        refs[0:1], refs[1:6], refs[6:9], refs[9], refs[10:13])
 
     def add(index, rows, value):
         out[rows, :] = (
-            even[rows, :] + (sum_15[rows, :] + (sum_3[rows, :] + value))
+            even[rows, :] + (sum_1y[rows, :] + (sum_3[rows, :] + value))
         ).astype(BF16)
 
-    work(slots, frames, side_of(sides, 7), weights, *mats, *scratch, add)
+    work(slots, frames, side_of(sides, 3, 1), weights, *mats, *scratch, add)
 
 
 def local_kernel(slots, frames, side, weights, embed_t, head, head_t, out, *scratch):
@@ -340,8 +334,8 @@
         else:
             out[rows, :] += value
 
-    halves = [frames.at[index] for index in range(frames.shape[0])]
-    work(slots, halves, side, weights, embed_t, head, head_t, *scratch, add)
+    blocks = [frames.at[index] for index in range(frames.shape[0])]
+    work(slots, blocks, side, weights, embed_t, head, head_t, *scratch, add)
 
 
 def call(kernel, name, slots, blocks, args, mats, outs):
@@ -401,44 +395,44 @@
     )(mine, theirs, *args)
 
 
-def gathered_grads(slots, halves, side, mats):
-    cycle = [0, 2, 4, 6, 7, 5, 3, 1]
-    ring = [
-        (2 * cycle[place] + core, 2 * cycle[(place + way) % 8] + core)
-        for place in range(8)
-        for core, way in ((0, 1), (1, -1))
-    ]
-
-    def send(blocks):
-        return [lax.ppermute(half, AXES, ring) for half in blocks]
-
-    blocks = [halves]
-    for step in range(7):
-        blocks.append(send(blocks[-1]))
-    pieces = [side]
-    for mask in (1, 2, 4):
-        held = pieces[0] if mask == 1 else jnp.concatenate(pieces, axis=0)
-        pieces.append(lax.ppermute(held, "hst", [(at, at ^ mask) for at in range(8)]))
+def gathered_grads(slots, own, side, mats):
+    def exchange(array, mask):
+        return lax.ppermute(array, "hst", [(at, at ^ mask) for at in range(8)])
+
+    def shift(array, by):
+        return lax.ppermute(array, "hst", [(at, (at + 2 * by) % 8) for at in range(8)])
+
+    one = shift(own, 1)
+    own_y = exchange(own, 1)
+    pieces = [side] + [exchange(side, 2 * mask) for mask in (1, 2, 3)]
+    line = jnp.concatenate(pieces, axis=0)
+    line, one, again = lax.optimization_barrier((line, one, own))
+    line_y = exchange(line, 1)
+    three = shift(again, -1)
+    one_y = exchange(one, 1)
+    two = shift(one, 1)
+    three_y = exchange(three, 1)
+    two_y = exchange(two, 1)
 
     width, feats = mats[0].shape
     grads = jax.ShapeDtypeStruct((feats + mats[2].shape[0], width), F32)
     weights = jax.ShapeDtypeStruct((16, 128), F32)
     sides = jax.ShapeDtypeStruct((64, side.shape[1]), F32)
-    done = ahead(blocks[0] + blocks[1] + blocks[2], mats[0], mats[2])
-    sum_0, sum_1, sum_2, weights, sides = call(
-        first_kernel, "first", slots, 3, (*done, *pieces), mats,
-        (grads, grads, grads, weights, sides),
-    )
-    sum_04, sum_3 = call(
-        second_kernel, "second", slots, 2, (*blocks[3], *blocks[4], sides, weights, sum_0), mats,
+    done = ahead((own, own_y, one), mats[0], mats[2])
+    sum_0, sum_1, weights, sides = call(
+        first_kernel, "first", slots, 3, (*done, line, line_y), mats,
+        (grads, grads, weights, sides),
+    )
+    sum_1y, sum_2 = call(
+        second_kernel, "second", slots, 2, (one_y, two, sides, weights, sum_1), mats,
         (grads, grads),
     )
-    even, sum_15 = call(
-        third_kernel, "third", slots, 2,
-        (*blocks[5], *blocks[6], sides, weights, sum_04, sum_1, sum_2), mats, (grads, grads),
+    even, sum_3 = call(
+        third_kernel, "third", slots, 2, (two_y, three, sides, weights, sum_0, sum_2), mats,
+        (grads, grads),
     )
     return call(
-        fourth_kernel, "fourth", slots, 1, (*blocks[7], sides, weights, even, sum_15, sum_3), mats,
+        fourth_kernel, "fourth", slots, 1, (three_y, sides, weights, even, sum_1y, sum_3), mats,
         jax.ShapeDtypeStruct(grads.shape, BF16),
     )
 
@@ -456,14 +450,14 @@
     flip = [(core, core ^ 1) for core in range(n_cores)]
     there = [lax.ppermute(array, "cores", flip) for array in (lengths, assign)]
     gather = n_hst == 8 and n_cores == 2 and rows == BLOCK
-    halves = [own[start : start + HALF] for start in range(0, rows, HALF)]
     side = side_data(
-        spread, owner, halves, *[array.reshape(1, -1) for array in (lengths, assign, *there)],
+        spread, owner, own, *[array.reshape(1, -1) for array in (lengths, assign, *there)],
         actions, rewards, actor_embed, actor_policy,
     )
     mats = convert(master_embed, master_policy, value_row)
+    side, mats = lax.optimization_barrier((side, mats))
     if gather:
-        mine = gathered_grads(slots, halves, side, mats)
+        mine = gathered_grads(slots, own, side, mats)
         theirs = lax.ppermute(mine, "cores", flip)
     else:
         named = (assign[:, None] == jnp.arange(learners)[None, :]).astype(F32)
@@ -471,7 +465,7 @@
         weights = jnp.broadcast_to((1.0 / (learners * totals))[:, None], (learners, 128))
         grads = call(
             local_kernel, "local", slots, rows // BLOCK,
-            (own.reshape(-1, HALF, feats), side, weights), mats,
+            (own.reshape(-1, BLOCK, feats), side, weights), mats,
             jax.ShapeDtypeStruct((feats + mats[2].shape[0], mats[0].shape[0]), F32),
         )
         mine = lax.psum(grads, AXES)

time: 54 us -> 48.6 us (0.900)
  starting transfers between devices: 26 us -> 17.5 us
  waiting for transfers between devices: 9.23 us -> 13.2 us
  local copies, waits for them, and re-layouts: 1.04 us -> 0.46 us
    ppermute x17 -> x11, starting transfers between devices: 25.4 us -> 16.9 us  [the longest x8 10 us: exchange(): return lax.ppermute(array, 'hst', [(at, at ^ mask) for at in range(8)])]
    ppermute x17 -> x11, waiting for transfers between devices: 6.15 us -> 9.76 us  [the longest x8 7.32 us: exchange(): return lax.ppermute(array, 'hst', [(at, at ^ mask) for at in range(8)])]
    slice x1 -> x0, local copies, waits for them, and re-layouts: 0.98 us -> none  [body(): halves = [own[start:start + HALF] for start in range(0, rows, HALF)]]
  transfers between devices with their start and end apart: 20 -> 14, of which waited for: 6 -> 10; matrix products, arithmetic and copies ran while one was open for 2% -> 0% of each run, Pallas kernels for 21% -> 23%
where the time goes in v6:
time: 48.6 us; the launch traced here: 48.5 us
  starting transfers between devices  17.5 us (36%)
  Pallas kernels  16.5 us (34%)
  waiting for transfers between devices  13.2 us (27%)
  between operations  0.81 us (2%)
    pallas_call x4, Pallas kernels, call(): pl.pallas_call(functools.partial(kernel, slots), out_shape=outs, in_specs...  10.5 us
    ppermute x8, starting transfers between devices, exchange(): return lax.ppermute(array, 'hst', [(at, at ^ mask) for at in range(8)])  10 us
    ppermute x8, waiting for transfers between devices, exchange(): return lax.ppermute(array, 'hst', [(at, at ^ mask) for at in range(8)])  7.32 us
    ppermute x3, starting transfers between devices, shift(): lax.ppermute(array, 'hst', [(at, (at + 2 * by) % 8) for at in range(8)])  6.91 us
    pallas_call x1, Pallas kernels, update(): pl.pallas_call(functools.partial(update_kernel, feats, nact), out_shape=(...  3.42 us
    ppermute x1, waiting for transfers between devices, body(): theirs = lax.ppermute(mine, 'cores', flip)  3.07 us
    ppermute x3, waiting for transfers between devices, shift(): lax.ppermute(array, 'hst', [(at, (at + 2 * by) % 8) for at in range(8)])  2.43 us
    pallas_call x1, Pallas kernels, ahead(): pl.pallas_call(ahead_kernel, out_shape=(jax.ShapeDtypeStruct((feats, rows...  1.31 us
  transfers between devices with their start and end apart: 14, of which 10 were waited for; matrix products, arithmetic and copies ran while one was open for 0% of the time, Pallas kernels for 23%

profile of v6, /device:TPU:0, one launch (start us, length us, event | category | flops | bytes accessed | tf_op | source)
XLA Modules:
  0.0 48.5 jit_solution(12118368571181580356)
XLA Ops:
  0.7 3.1 %collective-permute-start.5 = (bf16[256,512]{1,0:T(8,128)(2,1)}, bf16[256,512]{1,0:T(8,128)(2,1)S(1)}, u32[]{:S(2)}, u32[]{:S(2)}) collective-permute-start(bf16[256,512]{1,0:T(8,128)(2,1)} %bitcast.9), channel_id=1, source_target_pairs={{0,4},{2,6},{4,8},{6,10},{8,12},{10,14},{12,0},{14,2},{1,5},{3,7},... | collective-permute-start | bytes 786440 | tf_op jit(solution)/shard_map/ppermute | solution.py:403
  3.7 1.5 %collective-permute-start.8 = (bf16[256,512]{1,0:T(8,128)(2,1)}, bf16[256,512]{1,0:T(8,128)(2,1)S(1)}, u32[]{:S(2)}, u32[]{:S(2)}) collective-permute-start(bf16[256,512]{1,0:T(8,128)(2,1)} %bitcast.10), channel_id=1, source_target_pairs={{0,2},{2,0},{4,6},{6,4},{8,10},{10,8},{12,14},{14,12},{1,3},{3,1},... | collective-permute-start | bytes 786440 | tf_op jit(solution)/shard_map/ppermute | solution.py:400
  5.3 0.5 %collective-permute-start.1 = (s32[16]{0:T(128)}, s32[16]{0:T(128)S(1)}, u32[]{:S(2)}, u32[]{:S(2)}) collective-permute-start(s32[16]{0:T(128)} %param.18), channel_id=1, source_target_pairs={{0,1},{1,0},{2,3},{3,2},{4,5},{5,4},{6,7},{7,6},{8,9},{9,8},{10,11... | collective-permute-start | bytes 200 | tf_op jit(solution)/shard_map/ppermute | solution.py:451
  5.9 0.5 %convert.1 = (bf16[1024,512]{1,0:T(8,128)(2,1)S(1)}, bf16[1024,144]{1,0:T(8,128)(2,1)S(1)}, bf16[144,1024]{1,0:T(8,128)(2,1)S(1)}) custom-call(f32[512,1024]{1,0:T(8,128)S(1)} %copy-done, f32[1024,128]{1,0:T(8,128)S(1)} %copy-done.1, f32[1,1024]{1,0:T(1,128)S(1)} %bitcast.14), custom_call_target="tpu_custom_call" | custom-call | flops 660000000 | tf_op jit(solution)/shard_map/convert/pallas_call | solution.py:131
  6.4 0.1 collective-permute-done
  6.5 0.2 collective-permute-done.1
  6.7 0.4 copy-done.5
  7.1 0.0 copy-done.7
  7.1 0.8 %side.1 = f32[8,256]{1,0:T(8,128)S(1)} custom-call(s32[1,16]{1,0:T(1,128)S(1)} %bitcast.17, s32[1,16]{1,0:T(1,128)S(1)} %bitcast.18, s32[1,16]{1,0:T(1,128)S(1)} %bitcast.19, s32[1,16]{1,0:T(1,128)S(1)} %bitcast.20, s32[16,16]{1,0:T(8,128)S(1)} %copy-done.9, f32[16,16]{1,0:T(8,128)S(1)} %copy-done.10, bf16[512,1024]{1,0:T(8,128)(2,1)S(1)} %copy-done.5, ...), custom_call_target="tpu_custom_call" | custom-call | flops 1430000000 | tf_op jit(solution)/shard_map/side/pallas_call | solution.py:101
  7.9 1.6 %collective-permute-start.2 = (f32[8,256]{1,0:T(8,128)S(1)}, f32[8,256]{1,0:T(8,128)S(1)}, u32[]{:S(2)}, u32[]{:S(2)}) collective-permute-start(f32[8,256]{1,0:T(8,128)S(1)} %side.1), channel_id=1, source_target_pairs={{0,4},{2,6},{4,0},{6,2},{8,12},{10,14},{12,8},{14,10},{1,5},{3,7},... | collective-permute-start | bytes 24584 | tf_op jit(solution)/shard_map/ppermute | solution.py:400
  9.5 1.2 %collective-permute-start.3 = (f32[8,256]{1,0:T(8,128)S(1)}, f32[8,256]{1,0:T(8,128)S(1)}, u32[]{:S(2)}, u32[]{:S(2)}) collective-permute-start(f32[8,256]{1,0:T(8,128)S(1)} %side.1), channel_id=1, source_target_pairs={{0,8},{2,10},{4,12},{6,14},{8,0},{10,2},{12,4},{14,6},{1,9},{3,11}... | collective-permute-start | bytes 24584 | tf_op jit(solution)/shard_map/ppermute | solution.py:400
  10.8 1.6 %collective-permute-start.4 = (f32[8,256]{1,0:T(8,128)S(1)}, f32[8,256]{1,0:T(8,128)S(1)}, u32[]{:S(2)}, u32[]{:S(2)}) collective-permute-start(f32[8,256]{1,0:T(8,128)S(1)} %side.1), channel_id=1, source_target_pairs={{0,12},{2,14},{4,8},{6,10},{8,4},{10,6},{12,0},{14,2},{1,13},{3,15... | collective-permute-start | bytes 24584 | tf_op jit(solution)/shard_map/ppermute | solution.py:400
  12.3 0.1 collective-permute-done.2
  12.5 1.7 %collective-permute-done.3 = f32[8,256]{1,0:T(8,128)S(1)} collective-permute-done((f32[8,256]{1,0:T(8,128)S(1)}, f32[8,256]{1,0:T(8,128)S(1)}, u32[]{:S(2)}, u32[]{:S(2)}) %collective-permute-start.3) | collective-permute-done | bytes 8224 | tf_op jit(solution)/shard_map/ppermute | solution.py:400
  14.1 2.1 %collective-permute-done.4 = f32[8,256]{1,0:T(8,128)S(1)} collective-permute-done((f32[8,256]{1,0:T(8,128)S(1)}, f32[8,256]{1,0:T(8,128)S(1)}, u32[]{:S(2)}, u32[]{:S(2)}) %collective-permute-start.4) | collective-permute-done | bytes 8224 | tf_op jit(solution)/shard_map/ppermute | solution.py:400
  16.2 0.5 %collective-permute-start.9 = (f32[32,256]{1,0:T(8,128)S(1)}, f32[32,256]{1,0:T(8,128)S(1)}, u32[]{:S(2)}, u32[]{:S(2)}) collective-permute-start(f32[32,256]{1,0:T(8,128)S(1)} %pad_maximum_fusion.refs_3_), channel_id=1, source_target_pairs={{0,2},{2,0},{4,6},{6,4},{8,10},{10,8},{12,14},{14,12},{1,3},{3,1},... | collective-permute-start | bytes 98312 | tf_op jit(solution)/shard_map/ppermute | solution.py:400
  16.7 1.5 %collective-permute-start.12 = (bf16[256,512]{1,0:T(8,128)(2,1)S(1)}, bf16[256,512]{1,0:T(8,128)(2,1)S(1)}, u32[]{:S(2)}, u32[]{:S(2)}) collective-permute-start(bf16[256,512]{1,0:T(8,128)(2,1)S(1)} %collective-permute-done.5.refs_2_), channel_id=1, source_target_pairs={{0,2},{2,0},{4,6},{6,4},{8,10},{10,8},{12,14},{14,12},{1,3},{3,1},... | collective-permute-start | bytes 786440 | tf_op jit(solution)/shard_map/ppermute | solution.py:400
  18.3 3.8 %collective-permute-start.6 = (bf16[256,512]{1,0:T(8,128)(2,1)S(1)}, bf16[256,512]{1,0:T(8,128)(2,1)S(1)}, u32[]{:S(2)}, u32[]{:S(2)}) collective-permute-start(bf16[256,512]{1,0:T(8,128)(2,1)S(1)} %bitcast.12), channel_id=1, source_target_pairs={{0,12},{2,14},{4,0},{6,2},{8,4},{10,6},{12,8},{14,10},{1,13},{3,15... | collective-permute-start | bytes 786440 | tf_op jit(solution)/shard_map/ppermute | solution.py:403
  22.1 1.3 %ahead.1 = (bf16[512,768]{1,0:T(8,128)(2,1)S(1)}, bf16[1024,768]{1,0:T(8,128)(2,1)S(1)}, f32[144,768]{1,0:T(8,128)S(1)}) custom-call(bf16[256,512]{1,0:T(8,128)(2,1)S(1)} %bitcast.13, bf16[256,512]{1,0:T(8,128)(2,1)S(1)} %collective-permute-done.8.refs_1_, bf16[256,512]{1,0:T(8,128)(2,1)S(1)} %collective-permute-done.5.refs_2_, ...), custom_call_target="tpu_custom_call" | custom-call | flops 110000000 | tf_op jit(solution)/shard_map/ahead/pallas_call | solution.py:254
  23.4 2.6 %first.1 = (f32[656,1024]{1,0:T(8,128)S(1)}, f32[656,1024]{1,0:T(8,128)S(1)}, f32[16,128]{1,0:T(8,128)S(1)}, f32[64,256]{1,0:T(8,128)S(1)}) custom-call(bf16[512,768]{1,0:T(8,128)(2,1)S(1)} %get-tuple-element.47.refs_0_, bf16[1024,768]{1,0:T(8,128)(2,1)S(1)} %get-tuple-element.48.refs_1_, f32[144,768]{1,0:T(8,128)S(1)} %get-tuple-element.49.refs_2_, ...), custom_call_target="tpu_custom_call" | custom-call | flops 4400000000 | tf_op jit(solution)/shard_map/first/pallas_call | solution.py:344
  26.0 1.7 %collective-permute-done.10.refs_1_ = bf16[256,512]{1,0:T(8,128)(2,1)S(1)} collective-permute-done((bf16[256,512]{1,0:T(8,128)(2,1)S(1)}, bf16[256,512]{1,0:T(8,128)(2,1)S(1)}, u32[]{:S(2)}, u32[]{:S(2)}) %collective-permute-start.10) | collective-permute-done | bytes 262176 | tf_op jit(solution)/shard_map/ppermute | solution.py:403
  27.8 1.5 %collective-permute-start.11 = (bf16[256,512]{1,0:T(8,128)(2,1)S(1)}, bf16[256,512]{1,0:T(8,128)(2,1)S(1)}, u32[]{:S(2)}, u32[]{:S(2)}) collective-permute-start(bf16[256,512]{1,0:T(8,128)(2,1)S(1)} %collective-permute-done.10.refs_1_), channel_id=1, source_target_pairs={{0,2},{2,0},{4,6},{6,4},{8,10},{10,8},{12,14},{14,12},{1,3},{3,1},... | collective-permute-start | bytes 786440 | tf_op jit(solution)/shard_map/ppermute | solution.py:400
  29.3 0.7 %collective-permute-done.6.refs_1_ = bf16[256,512]{1,0:T(8,128)(2,1)S(1)} collective-permute-done((bf16[256,512]{1,0:T(8,128)(2,1)S(1)}, bf16[256,512]{1,0:T(8,128)(2,1)S(1)}, u32[]{:S(2)}, u32[]{:S(2)}) %collective-permute-start.6) | collective-permute-done | bytes 262176 | tf_op jit(solution)/shard_map/ppermute | solution.py:403
  30.0 0.5 %collective-permute-start.7 = (bf16[256,512]{1,0:T(8,128)(2,1)S(1)}, bf16[256,512]{1,0:T(8,128)(2,1)S(1)}, u32[]{:S(2)}, u32[]{:S(2)}) collective-permute-start(bf16[256,512]{1,0:T(8,128)(2,1)S(1)} %collective-permute-done.6.refs_1_), channel_id=1, source_target_pairs={{0,2},{2,0},{4,6},{6,4},{8,10},{10,8},{12,14},{14,12},{1,3},{3,1},... | collective-permute-start | bytes 786440 | tf_op jit(solution)/shard_map/ppermute | solution.py:400
  30.5 2.9 %second.1 = (f32[656,1024]{1,0:T(8,128)S(1)}, f32[656,1024]{1,0:T(8,128)S(1)}) custom-call(bf16[256,512]{1,0:T(8,128)(2,1)S(1)} %collective-permute-done.12.refs_0_, bf16[256,512]{1,0:T(8,128)(2,1)S(1)} %collective-permute-done.10.refs_1_, f32[64,256]{1,0:T(8,128)S(1)} %get-tuple-element.52.refs_2_.refs_1_, f32[16,128]{1,0:T(8,128)S(1)} %get-tuple-element.53.refs_3_.refs_2_, ...), custom_call_target="tpu_custom_call" | custom-call | flops 3080000000 | tf_op jit(solution)/shard_map/second/pallas_call | solution.py:344
  33.3 3.1 %collective-permute-done.11.refs_0_ = bf16[256,512]{1,0:T(8,128)(2,1)S(1)} collective-permute-done((bf16[256,512]{1,0:T(8,128)(2,1)S(1)}, bf16[256,512]{1,0:T(8,128)(2,1)S(1)}, u32[]{:S(2)}, u32[]{:S(2)}) %collective-permute-start.11) | collective-permute-done | bytes 262176 | tf_op jit(solution)/shard_map/ppermute | solution.py:400
  36.4 3.0 %third.1 = (f32[656,1024]{1,0:T(8,128)S(1)}, f32[656,1024]{1,0:T(8,128)S(1)}) custom-call(bf16[256,512]{1,0:T(8,128)(2,1)S(1)} %collective-permute-done.11.refs_0_, bf16[256,512]{1,0:T(8,128)(2,1)S(1)} %collective-permute-done.6.refs_1_, f32[64,256]{1,0:T(8,128)S(1)} %get-tuple-element.52.refs_2_.refs_1_, f32[16,128]{1,0:T(8,128)S(1)} %get-tuple-element.53.refs_3_.refs_2_, ...), custom_call_target="tpu_custom_call" | custom-call | flops 3080000000 | tf_op jit(solution)/shard_map/third/pallas_call | solution.py:344
  39.4 0.4 collective-permute-done.7.refs_0_
  39.8 2.1 %fourth.1.mine = bf16[656,1024]{1,0:T(8,128)(2,1)S(1)} custom-call(bf16[256,512]{1,0:T(8,128)(2,1)S(1)} %collective-permute-done.7.refs_0_, f32[64,256]{1,0:T(8,128)S(1)} %get-tuple-element.52.refs_2_.refs_1_, f32[16,128]{1,0:T(8,128)S(1)} %get-tuple-element.53.refs_3_.refs_2_, f32[656,1024]{1,0:T(8,128)S(1)} %get-tuple-element.57.refs_3_, ...), custom_call_target="tpu_custom_call" | custom-call | flops 1760000000 | tf_op jit(solution)/shard_map/fourth/pallas_call | solution.py:344
  41.9 0.1 collective-permute-start.13
  41.9 3.1 %collective-permute-done.13.theirs = bf16[656,1024]{1,0:T(8,128)(2,1)S(1)} collective-permute-done((bf16[656,1024]{1,0:T(8,128)(2,1)S(1)}, bf16[656,1024]{1,0:T(8,128)(2,1)S(1)}, u32[]{:S(2)}, u32[]{:S(2)}) %collective-permute-start.13) | collective-permute-done | bytes 1343520 | tf_op jit(solution)/shard_map/ppermute | solution.py:461
  45.0 3.4 %update.1 = (bf16[256,128]{1,0:T(8,128)(2,1)}, f32[512,1024]{1,0:T(8,128)}, f32[1024,128]{1,0:T(8,128)}, f32[1,1024]{1,0:T(1,128)}, f32[512,1024]{1,0:T(8,128)}, /*index=5*/f32[1024,128]{1,0:T(8,128)}, f32[1,1024]{1,0:T(1,128)}) custom-call(bf16[656,1024]{1,0:T(8,128)(2,1)S(1)} %fourth.1.mine, bf16[656,1024]{1,0:T(8,128)(2,1)S(1)} %collective-permute-done.13.theirs, ...), custom_call_target="tpu_custom_call" | custom-call | flops 3740000000 | tf_op jit(solution)/shard_map/update/pallas_call | solution.py:387
  (34 shorter events, 0.1 us)
Async XLA Ops:
  0.6 5.2 %copy-start = (f32[512,1024]{1,0:T(8,128)S(1)}, f32[512,1024]{1,0:T(8,128)}, u32[]{:S(2)}) copy-start(f32[512,1024]{1,0:T(8,128)} %master_embed.3) | copy-start | bytes 6291460
  0.6 5.2 %copy-start.1 = (f32[1024,128]{1,0:T(8,128)S(1)}, f32[1024,128]{1,0:T(8,128)}, u32[]{:S(2)}) copy-start(f32[1024,128]{1,0:T(8,128)} %master_policy.3) | copy-start | bytes 1572868
  0.7 5.2 %copy-start.3 = (f32[1024]{0:T(1024)S(1)}, f32[1024]{0:T(1024)}, u32[]{:S(2)}) copy-start(f32[1024]{0:T(1024)} %param.23) | copy-start | bytes 12292
  0.7 15.6 %collective-permute-start.5 = (bf16[256,512]{1,0:T(8,128)(2,1)}, bf16[256,512]{1,0:T(8,128)(2,1)S(1)}, u32[]{:S(2)}, u32[]{:S(2)}) collective-permute-start(bf16[256,512]{1,0:T(8,128)(2,1)} %bitcast.9), channel_id=1, source_target_pairs={{0,4},{2,6},{4,8},{6,10},{8,12},{10,14},{12,0},{14,2},{1,5},{3,7},... | collective-permute-start | bytes 786440 | tf_op jit(solution)/shard_map/ppermute | solution.py:403
  3.7 18.3 %collective-permute-start.8 = (bf16[256,512]{1,0:T(8,128)(2,1)}, bf16[256,512]{1,0:T(8,128)(2,1)S(1)}, u32[]{:S(2)}, u32[]{:S(2)}) collective-permute-start(bf16[256,512]{1,0:T(8,128)(2,1)} %bitcast.10), channel_id=1, source_target_pairs={{0,2},{2,0},{4,6},{6,4},{8,10},{10,8},{12,14},{14,12},{1,3},{3,1},... | collective-permute-start | bytes 786440 | tf_op jit(solution)/shard_map/ppermute | solution.py:400
  5.3 1.3 %collective-permute-start = (s32[16]{0:T(128)}, s32[16]{0:T(128)S(1)}, u32[]{:S(2)}, u32[]{:S(2)}) collective-permute-start(s32[16]{0:T(128)} %param.15), channel_id=1, source_target_pairs={{0,1},{1,0},{2,3},{3,2},{4,5},{5,4},{6,7},{7,6},{8,9},{9,8},{10,11... | collective-permute-start | bytes 200 | tf_op jit(solution)/shard_map/ppermute | solution.py:451
  5.3 1.5 %collective-permute-start.1 = (s32[16]{0:T(128)}, s32[16]{0:T(128)S(1)}, u32[]{:S(2)}, u32[]{:S(2)}) collective-permute-start(s32[16]{0:T(128)} %param.18), channel_id=1, source_target_pairs={{0,1},{1,0},{2,3},{3,2},{4,5},{5,4},{6,7},{7,6},{8,9},{9,8},{10,11... | collective-permute-start | bytes 200 | tf_op jit(solution)/shard_map/ppermute | solution.py:451
  5.8 1.0 %copy-start.2 = (bf16[16,16,512]{2,1,0:T(8,128)(2,1)S(1)}, bf16[16,16,512]{2,1,0:T(8,128)(2,1)}, u32[]{:S(2)}) copy-start(bf16[16,16,512]{2,1,0:T(8,128)(2,1)} %param.14) | copy-start | bytes 786436
  5.8 1.3 %copy-start.5 = (bf16[512,1024]{1,0:T(8,128)(2,1)S(1)}, bf16[512,1024]{1,0:T(8,128)(2,1)}, u32[]{:S(2)}) copy-start(bf16[512,1024]{1,0:T(8,128)(2,1)} %actor_embed.1) | copy-start | bytes 3145732
  5.8 1.3 %copy-start.7 = (bf16[1024,128]{1,0:T(8,128)(2,1)S(1)}, bf16[1024,128]{1,0:T(8,128)(2,1)}, u32[]{:S(2)}) copy-start(bf16[1024,128]{1,0:T(8,128)(2,1)} %actor_policy.1) | copy-start | bytes 786436
  5.8 1.3 %copy-start.9 = (s32[16,16]{1,0:T(8,128)S(1)}, s32[16,16]{1,0:T(8,128)}, u32[]{:S(2)}) copy-start(s32[16,16]{1,0:T(8,128)} %actions.1) | copy-start | bytes 3076
  5.8 1.3 %copy-start.10 = (f32[16,16]{1,0:T(8,128)S(1)}, f32[16,16]{1,0:T(8,128)}, u32[]{:S(2)}) copy-start(f32[16,16]{1,0:T(8,128)} %rewards.1) | copy-start | bytes 3076
  5.8 1.3 %copy-start.12 = (s32[16]{0:T(128)S(1)}, s32[16]{0:T(128)}, u32[]{:S(2)}) copy-start(s32[16]{0:T(128)} %param.15) | copy-start | bytes 196
  5.8 1.3 %copy-start.13 = (s32[16]{0:T(128)S(1)}, s32[16]{0:T(128)}, u32[]{:S(2)}) copy-start(s32[16]{0:T(128)} %param.18) | copy-start | bytes 196
  7.9 4.6 %collective-permute-start.2 = (f32[8,256]{1,0:T(8,128)S(1)}, f32[8,256]{1,0:T(8,128)S(1)}, u32[]{:S(2)}, u32[]{:S(2)}) collective-permute-start(f32[8,256]{1,0:T(8,128)S(1)} %side.1), channel_id=1, source_target_pairs={{0,4},{2,6},{4,0},{6,2},{8,12},{10,14},{12,8},{14,10},{1,5},{3,7},... | collective-permute-start | bytes 24584 | tf_op jit(solution)/shard_map/ppermute | solution.py:400
  9.5 4.6 %collective-permute-start.3 = (f32[8,256]{1,0:T(8,128)S(1)}, f32[8,256]{1,0:T(8,128)S(1)}, u32[]{:S(2)}, u32[]{:S(2)}) collective-permute-start(f32[8,256]{1,0:T(8,128)S(1)} %side.1), channel_id=1, source_target_pairs={{0,8},{2,10},{4,12},{6,14},{8,0},{10,2},{12,4},{14,6},{1,9},{3,11}... | collective-permute-start | bytes 24584 | tf_op jit(solution)/shard_map/ppermute | solution.py:400
  10.8 5.4 %collective-permute-start.4 = (f32[8,256]{1,0:T(8,128)S(1)}, f32[8,256]{1,0:T(8,128)S(1)}, u32[]{:S(2)}, u32[]{:S(2)}) collective-permute-start(f32[8,256]{1,0:T(8,128)S(1)} %side.1), channel_id=1, source_target_pairs={{0,12},{2,14},{4,8},{6,10},{8,4},{10,6},{12,0},{14,2},{1,13},{3,15... | collective-permute-start | bytes 24584 | tf_op jit(solution)/shard_map/ppermute | solution.py:400
  16.2 7.2 %collective-permute-start.9 = (f32[32,256]{1,0:T(8,128)S(1)}, f32[32,256]{1,0:T(8,128)S(1)}, u32[]{:S(2)}, u32[]{:S(2)}) collective-permute-start(f32[32,256]{1,0:T(8,128)S(1)} %pad_maximum_fusion.refs_3_), channel_id=1, source_target_pairs={{0,2},{2,0},{4,6},{6,4},{8,10},{10,8},{12,14},{14,12},{1,3},{3,1},... | collective-permute-start | bytes 98312 | tf_op jit(solution)/shard_map/ppermute | solution.py:400
  16.7 11.0 %collective-permute-start.10 = (bf16[256,512]{1,0:T(8,128)(2,1)S(1)}, bf16[256,512]{1,0:T(8,128)(2,1)S(1)}, u32[]{:S(2)}, u32[]{:S(2)}) collective-permute-start(bf16[256,512]{1,0:T(8,128)(2,1)S(1)} %collective-permute-done.5.refs_2_), channel_id=1, source_target_pairs={{0,4},{2,6},{4,8},{6,10},{8,12},{10,14},{12,0},{14,2},{1,5},{3,7},... | collective-permute-start | bytes 786440 | tf_op jit(solution)/shard_map/ppermute | solution.py:403
  16.7 13.7 %collective-permute-start.12 = (bf16[256,512]{1,0:T(8,128)(2,1)S(1)}, bf16[256,512]{1,0:T(8,128)(2,1)S(1)}, u32[]{:S(2)}, u32[]{:S(2)}) collective-permute-start(bf16[256,512]{1,0:T(8,128)(2,1)S(1)} %collective-permute-done.5.refs_2_), channel_id=1, source_target_pairs={{0,2},{2,0},{4,6},{6,4},{8,10},{10,8},{12,14},{14,12},{1,3},{3,1},... | collective-permute-start | bytes 786440 | tf_op jit(solution)/shard_map/ppermute | solution.py:400
  18.3 11.7 %collective-permute-start.6 = (bf16[256,512]{1,0:T(8,128)(2,1)S(1)}, bf16[256,512]{1,0:T(8,128)(2,1)S(1)}, u32[]{:S(2)}, u32[]{:S(2)}) collective-permute-start(bf16[256,512]{1,0:T(8,128)(2,1)S(1)} %bitcast.12), channel_id=1, source_target_pairs={{0,12},{2,14},{4,0},{6,2},{8,4},{10,6},{12,8},{14,10},{1,13},{3,15... | collective-permute-start | bytes 786440 | tf_op jit(solution)/shard_map/ppermute | solution.py:403
  27.8 8.7 %collective-permute-start.11 = (bf16[256,512]{1,0:T(8,128)(2,1)S(1)}, bf16[256,512]{1,0:T(8,128)(2,1)S(1)}, u32[]{:S(2)}, u32[]{:S(2)}) collective-permute-start(bf16[256,512]{1,0:T(8,128)(2,1)S(1)} %collective-permute-done.10.refs_1_), channel_id=1, source_target_pairs={{0,2},{2,0},{4,6},{6,4},{8,10},{10,8},{12,14},{14,12},{1,3},{3,1},... | collective-permute-start | bytes 786440 | tf_op jit(solution)/shard_map/ppermute | solution.py:400
  30.0 9.8 %collective-permute-start.7 = (bf16[256,512]{1,0:T(8,128)(2,1)S(1)}, bf16[256,512]{1,0:T(8,128)(2,1)S(1)}, u32[]{:S(2)}, u32[]{:S(2)}) collective-permute-start(bf16[256,512]{1,0:T(8,128)(2,1)S(1)} %collective-permute-done.6.refs_1_), channel_id=1, source_target_pairs={{0,2},{2,0},{4,6},{6,4},{8,10},{10,8},{12,14},{14,12},{1,3},{3,1},... | collective-permute-start | bytes 786440 | tf_op jit(solution)/shard_map/ppermute | solution.py:400
  39.7 5.3 %copy-start.4 = (f32[512,1024]{1,0:T(8,128)S(1)}, f32[512,1024]{1,0:T(8,128)}, u32[]{:S(2)}) copy-start(f32[512,1024]{1,0:T(8,128)} %embed_moment.1) | copy-start | bytes 6291460
  39.8 5.3 %copy-start.6 = (f32[1024,128]{1,0:T(8,128)S(1)}, f32[1024,128]{1,0:T(8,128)}, u32[]{:S(2)}) copy-start(f32[1024,128]{1,0:T(8,128)} %policy_moment.1) | copy-start | bytes 1572868
  39.8 5.3 %copy-start.8 = (bf16[256,512]{1,0:T(8,128)(2,1)S(1)}, bf16[256,512]{1,0:T(8,128)(2,1)}, u32[]{:S(2)}) copy-start(bf16[256,512]{1,0:T(8,128)(2,1)} %next_obs.1) | copy-start | bytes 786436
  39.8 5.3 %copy-start.11 = (f32[1024]{0:T(1024)S(1)}, f32[1024]{0:T(1024)}, u32[]{:S(2)}) copy-start(f32[1024]{0:T(1024)} %param.26) | copy-start | bytes 12292
  41.9 3.1 %collective-permute-start.13 = (bf16[656,1024]{1,0:T(8,128)(2,1)S(1)}, bf16[656,1024]{1,0:T(8,128)(2,1)S(1)}, u32[]{:S(2)}, u32[]{:S(2)}) collective-permute-start(bf16[656,1024]{1,0:T(8,128)(2,1)S(1)} %fourth.1.mine), channel_id=1, source_target_pairs={{0,1},{1,0},{2,3},{3,2},{4,5},{5,4},{6,7},{7,6},{8,9},{9,8},{10,11... | collective-permute-start | bytes 4030472 | tf_op jit(solution)/shard_map/ppermute | solution.py:461

commit v7 on v6

--- a/solution.py
+++ b/solution.py
@@ -18,6 +18,7 @@
 MIB = 2**20
 BLOCK = 256
 PAD = 16
+CHUNKS = 4
 BEHAVE, ACTION, REWARD, LENGTH, ASSIGN, LENGTH_2, ASSIGN_2 = range(7)
 
 
@@ -261,7 +262,7 @@
         in_specs=[VMEM] * (len(frames) + 2),
         out_specs=(VMEM,) * 3,
         compiler_params=params(20),
-        cost_estimate=cost(0.1),
+        cost_estimate=cost(0.2),
         name="ahead",
     )(*frames, embed_t, head_t)
 
@@ -288,43 +289,43 @@
 
 
 def second_kernel(slots, *refs):
-    frames, (sides, weights, sum_1), mats, (sum_1y, sum_2), scratch = (
+    frames, (sides, weights, sum_1), mats, (sum_1y, sum_3), scratch = (
         refs[0:2], refs[2:5], refs[5:8], refs[8:10], refs[10:13])
 
     def add(index, rows, value):
         if index == 0:
             sum_1y[rows, :] = sum_1[rows, :] + value
         else:
-            sum_2[rows, :] = value
-
-    side = jnp.concatenate([side_of(sides, 1, 1), side_of(sides, 2, 0)], axis=1)
+            sum_3[rows, :] = value
+
+    side = jnp.concatenate([side_of(sides, 1, 1), side_of(sides, 3, 0)], axis=1)
     work(slots, frames, side, weights, *mats, *scratch, add)
 
 
 def third_kernel(slots, *refs):
-    frames, (sides, weights, sum_0, sum_2), mats, (even, sum_3), scratch = (
+    frames, (sides, weights, sum_1y, sum_3), mats, (odd, sum_2), scratch = (
         refs[0:2], refs[2:6], refs[6:9], refs[9:11], refs[11:14])
 
     def add(index, rows, value):
         if index == 0:
-            even[rows, :] = sum_0[rows, :] + (sum_2[rows, :] + value)
+            odd[rows, :] = sum_1y[rows, :] + (sum_3[rows, :] + value)
         else:
-            sum_3[rows, :] = value
-
-    side = jnp.concatenate([side_of(sides, 2, 1), side_of(sides, 3, 0)], axis=1)
+            sum_2[rows, :] = value
+
+    side = jnp.concatenate([side_of(sides, 3, 1), side_of(sides, 2, 0)], axis=1)
     work(slots, frames, side, weights, *mats, *scratch, add)
 
 
 def fourth_kernel(slots, *refs):
-    frames, (sides, weights, even, sum_1y, sum_3), mats, out, scratch = (
+    frames, (sides, weights, odd, sum_0, sum_2), mats, out, scratch = (
         refs[0:1], refs[1:6], refs[6:9], refs[9], refs[10:13])
 
     def add(index, rows, value):
         out[rows, :] = (
-            even[rows, :] + (sum_1y[rows, :] + (sum_3[rows, :] + value))
+            odd[rows, :] + (sum_0[rows, :] + (sum_2[rows, :] + value))
         ).astype(BF16)
 
-    work(slots, frames, side_of(sides, 3, 1), weights, *mats, *scratch, add)
+    work(slots, frames, side_of(sides, 2, 1), weights, *mats, *scratch, add)
 
 
 def local_kernel(slots, frames, side, weights, embed_t, head, head_t, out, *scratch):
@@ -360,23 +361,49 @@
 def update_kernel(
     feats, nact, mine, theirs, master_embed, master_policy, master_value,
     embed_moment, policy_moment, value_moment, next_obs,
-    next_logits, new_embed, new_policy, new_value, new_em, new_pm, new_vm,
+    next_logits, new_embed_at, new_policy_at, new_value, new_em_at, new_pm_at, new_vm,
+    new_embed, new_policy, new_em, new_pm, sems,
 ):
-    def step(grad, moment, master, new_moment, new_master):
-        held = MOMENTUM * moment[...] + grad
-        new_moment[...] = held
-        fresh = master[...] - LEARN_RATE * held
-        new_master[...] = fresh
-        return fresh
+    copies = []
+
+    def store(source, target, rows):
+        copy = pltpu.make_async_copy(source.at[rows, :], target.at[rows, :], sems.at[len(copies)])
+        copy.start()
+        copies.append(copy)
 
     def grad(start, size):
         return mine[start : start + size, :].astype(F32) + theirs[start : start + size, :].astype(F32)
 
-    embed = step(grad(0, feats), embed_moment, master_embed, new_em, new_embed)
-    hidden = jnp.maximum(mm(next_obs[...], embed.astype(BF16)), 0.0).astype(BF16)
-    policy = step(grad(feats, nact).T, policy_moment, master_policy, new_pm, new_policy)
-    step(grad(feats + nact, PAD)[0:1, :], value_moment, master_value, new_vm, new_value)
-    next_logits[...] = mm(hidden, policy.astype(BF16)).astype(BF16)
+    def step(grad, moment, master):
+        held = MOMENTUM * moment + grad
+        return held, master - LEARN_RATE * held
+
+    def chunks(height):
+        return [pl.ds(start, height // CHUNKS) for start in range(0, height, height // CHUNKS)]
+
+    preact = None
+    for rows in chunks(feats):
+        held, fresh = step(grad(rows.start, rows.size), embed_moment[rows, :], master_embed[rows, :])
+        new_em[rows, :] = held
+        new_embed[rows, :] = fresh
+        store(new_em, new_em_at, rows)
+        store(new_embed, new_embed_at, rows)
+        part = mm(next_obs[:, rows], fresh.astype(BF16))
+        preact = part if preact is None else preact + part
+    policy_grad = grad(feats, nact).T
+    held, fresh = step(policy_grad, policy_moment[...], master_policy[...])
+    new_pm[...] = held
+    new_policy[...] = fresh
+    every = pl.ds(0, new_pm.shape[0])
+    store(new_pm, new_pm_at, every)
+    store(new_policy, new_policy_at, every)
+    new_vm[...], new_value[...] = step(
+        grad(feats + nact, PAD)[0:1, :], value_moment[...], master_value[...]
+    )
+    hidden = jnp.maximum(preact, 0.0).astype(BF16)
+    next_logits[...] = mm(hidden, fresh.astype(BF16)).astype(BF16)
+    for copy in copies:
+        copy.wait()
 
 
 def update(mine, theirs, *args):
@@ -384,35 +411,42 @@
     next_obs = args[6]
     feats, nact = embed.shape[0], policy.shape[1]
     shapes = [jax.ShapeDtypeStruct(array.shape, F32) for array in (embed, policy, value)]
+    anywhere = pl.BlockSpec(memory_space=pl.ANY)
+    specs = (anywhere, anywhere, VMEM)
+    held = [pltpu.VMEM(array.shape, F32) for array in (embed, policy)]
     return pl.pallas_call(
         functools.partial(update_kernel, feats, nact),
         out_shape=(jax.ShapeDtypeStruct((next_obs.shape[0], nact), BF16), *shapes, *shapes),
         in_specs=[VMEM] * 9,
-        out_specs=(VMEM,) * 7,
-        compiler_params=params(32),
+        out_specs=(VMEM, *specs, *specs),
+        scratch_shapes=[*held, *held, pltpu.SemaphoreType.DMA((2 * CHUNKS + 2,))],
+        compiler_params=params(24),
         cost_estimate=cost(3.4),
         name="update",
     )(mine, theirs, *args)
 
 
 def gathered_grads(slots, own, side, mats):
-    def exchange(array, mask):
-        return lax.ppermute(array, "hst", [(at, at ^ mask) for at in range(8)])
-
-    def shift(array, by):
-        return lax.ppermute(array, "hst", [(at, (at + 2 * by) % 8) for at in range(8)])
-
-    one = shift(own, 1)
-    own_y = exchange(own, 1)
-    pieces = [side] + [exchange(side, 2 * mask) for mask in (1, 2, 3)]
+    def exchange(array, mask, name):
+        with jax.named_scope(name):
+            return lax.ppermute(array, "hst", [(at, at ^ mask) for at in range(8)])
+
+    def shift(array, by, name):
+        with jax.named_scope(name):
+            return lax.ppermute(array, "hst", [(at, (at + 2 * by) % 8) for at in range(8)])
+
+    one = shift(own, 1, "one")
+    own_y = exchange(own, 1, "own_y")
+    pieces = [side] + [exchange(side, 2 * mask, "side_z") for mask in (1, 2, 3)]
     line = jnp.concatenate(pieces, axis=0)
-    line, one, again = lax.optimization_barrier((line, one, own))
-    line_y = exchange(line, 1)
-    three = shift(again, -1)
-    one_y = exchange(one, 1)
-    two = shift(one, 1)
-    three_y = exchange(three, 1)
-    two_y = exchange(two, 1)
+    line, _ = lax.optimization_barrier((line, side))
+    one, _ = lax.optimization_barrier((one, pieces[1]))
+    again, _ = lax.optimization_barrier((own, pieces[1]))
+    line_y = exchange(line, 1, "side_y")
+    three = shift(again, -1, "three")
+    one_y = exchange(one, 1, "one_y")
+    two = shift(one, 1, "two")
+    three_y = exchange(three, 1, "three_y")
 
     width, feats = mats[0].shape
     grads = jax.ShapeDtypeStruct((feats + mats[2].shape[0], width), F32)
@@ -423,16 +457,18 @@
         first_kernel, "first", slots, 3, (*done, line, line_y), mats,
         (grads, grads, weights, sides),
     )
-    sum_1y, sum_2 = call(
-        second_kernel, "second", slots, 2, (one_y, two, sides, weights, sum_1), mats,
+    sum_1y, sum_3 = call(
+        second_kernel, "second", slots, 2, (one_y, three, sides, weights, sum_1), mats,
         (grads, grads),
     )
-    even, sum_3 = call(
-        third_kernel, "third", slots, 2, (two_y, three, sides, weights, sum_0, sum_2), mats,
+    two, sum_3 = lax.optimization_barrier((two, sum_3))
+    two_y = exchange(two, 1, "two_y")
+    odd, sum_2 = call(
+        third_kernel, "third", slots, 2, (three_y, two, sides, weights, sum_1y, sum_3), mats,
         (grads, grads),
     )
     return call(
-        fourth_kernel, "fourth", slots, 1, (three_y, sides, weights, even, sum_1y, sum_3), mats,
+        fourth_kernel, "fourth", slots, 1, (two_y, sides, weights, odd, sum_0, sum_2), mats,
         jax.ShapeDtypeStruct(grads.shape, BF16),
     )
 

time: 48.6 us -> 45.7 us (0.940)
  waiting for transfers between devices: 13.2 us -> 10.2 us
  Pallas kernels: 16.5 us -> 17 us
    ppermute x3, starting transfers between devices: 6.91 us -> 3.96 us  [shift(): lax.ppermute(array, 'hst', [(at, (at + 2 * by) % 8) for at in range(8)])]
    ppermute x8, starting transfers between devices: 10 us -> 12.6 us  [exchange(): return lax.ppermute(array, 'hst', [(at, at ^ mask) for at in range(8)])]
    ppermute x8, waiting for transfers between devices: 7.32 us -> 5.45 us  [exchange(): return lax.ppermute(array, 'hst', [(at, at ^ mask) for at in range(8)])]
    ppermute x3, waiting for transfers between devices: 2.43 us -> 1.31 us  [shift(): lax.ppermute(array, 'hst', [(at, (at + 2 * by) % 8) for at in range(8)])]
  transfers between devices with their start and end apart: 14 -> 14, of which waited for: 10 -> 8; matrix products, arithmetic and copies ran while one was open for 0% -> 0% of each run, Pallas kernels for 23% -> 24%
where the time goes in v7:
time: 45.7 us; the launch traced here: 45.6 us
  starting transfers between devices  17.1 us (37%)
  Pallas kernels  17 us (37%)
  waiting for transfers between devices  10.2 us (22%)
  between operations  0.81 us (2%)
  local copies, waits for them, and re-layouts  0.46 us (1%)
    ppermute x8, starting transfers between devices, exchange(): return lax.ppermute(array, 'hst', [(at, at ^ mask) for at in range(8)])  12.6 us
    pallas_call x4, Pallas kernels, call(): pl.pallas_call(functools.partial(kernel, slots), out_shape=outs, in_specs...  10.6 us
    ppermute x8, waiting for transfers between devices, exchange(): return lax.ppermute(array, 'hst', [(at, at ^ mask) for at in range(8)])  5.45 us
    ppermute x3, starting transfers between devices, shift(): lax.ppermute(array, 'hst', [(at, (at + 2 * by) % 8) for at in range(8)])  3.96 us
    pallas_call x1, Pallas kernels, update(): pl.pallas_call(functools.partial(update_kernel, feats, nact), out_shape=(...  3.87 us
    ppermute x1, waiting for transfers between devices, body(): theirs = lax.ppermute(mine, 'cores', flip)  3.07 us
    ppermute x3, waiting for transfers between devices, shift(): lax.ppermute(array, 'hst', [(at, (at + 2 * by) % 8) for at in range(8)])  1.31 us
    pallas_call x1, Pallas kernels, ahead(): pl.pallas_call(ahead_kernel, out_shape=(jax.ShapeDtypeStruct((feats, rows...  1.31 us
  transfers between devices with their start and end apart: 14, of which 8 were waited for; matrix products, arithmetic and copies ran while one was open for 0% of the time, Pallas kernels for 24%

profile of v7, /device:TPU:0, one launch (start us, length us, event | category | flops | bytes accessed | tf_op | source)
XLA Modules:
  0.0 45.6 jit_solution(3861655395601341458)
XLA Ops:
  0.7 3.0 %collective-permute-start.7 = (bf16[256,512]{1,0:T(8,128)(2,1)}, bf16[256,512]{1,0:T(8,128)(2,1)S(1)}, u32[]{:S(2)}, u32[]{:S(2)}) collective-permute-start(bf16[256,512]{1,0:T(8,128)(2,1)} %bitcast.9), channel_id=1, source_target_pairs={{0,2},{2,0},{4,6},{6,4},{8,10},{10,8},{12,14},{14,12},{1,3},{3,1},... | collective-permute-start | bytes 786440 | tf_op jit(solution)/shard_map/own_y/ppermute | solution.py:432
  3.7 1.6 %collective-permute-start = (bf16[256,512]{1,0:T(8,128)(2,1)}, bf16[256,512]{1,0:T(8,128)(2,1)S(1)}, u32[]{:S(2)}, u32[]{:S(2)}) collective-permute-start(bf16[256,512]{1,0:T(8,128)(2,1)} %bitcast.10), channel_id=1, source_target_pairs={{0,4},{2,6},{4,8},{6,10},{8,12},{10,14},{12,0},{14,2},{1,5},{3,7},... | collective-permute-start | bytes 786440 | tf_op jit(solution)/shard_map/one/ppermute | solution.py:436
  5.3 0.5 %collective-permute-start.2 = (s32[16]{0:T(128)}, s32[16]{0:T(128)S(1)}, u32[]{:S(2)}, u32[]{:S(2)}) collective-permute-start(s32[16]{0:T(128)} %param.18), channel_id=1, source_target_pairs={{0,1},{1,0},{2,3},{3,2},{4,5},{5,4},{6,7},{7,6},{8,9},{9,8},{10,11... | collective-permute-start | bytes 200 | tf_op jit(solution)/shard_map/ppermute | solution.py:487
  5.8 0.0 copy-start.7
  5.8 0.0 copy-start.9
  5.9 0.5 %convert.1 = (bf16[1024,512]{1,0:T(8,128)(2,1)S(1)}, bf16[1024,144]{1,0:T(8,128)(2,1)S(1)}, bf16[144,1024]{1,0:T(8,128)(2,1)S(1)}) custom-call(f32[512,1024]{1,0:T(8,128)S(1)} %copy-done, f32[1024,128]{1,0:T(8,128)S(1)} %copy-done.1, f32[1,1024]{1,0:T(1,128)S(1)} %bitcast.14), custom_call_target="tpu_custom_call" | custom-call | flops 660000000 | tf_op jit(solution)/shard_map/convert/pallas_call | solution.py:132
  6.4 0.1 collective-permute-done.1
  6.5 0.2 collective-permute-done.2
  6.7 0.4 copy-done.5
  7.1 0.0 copy-done.7
  7.2 0.8 %side.1 = f32[8,256]{1,0:T(8,128)S(1)} custom-call(s32[1,16]{1,0:T(1,128)S(1)} %bitcast.17, s32[1,16]{1,0:T(1,128)S(1)} %bitcast.18, s32[1,16]{1,0:T(1,128)S(1)} %bitcast.19, s32[1,16]{1,0:T(1,128)S(1)} %bitcast.20, s32[16,16]{1,0:T(8,128)S(1)} %copy-done.9, f32[16,16]{1,0:T(8,128)S(1)} %copy-done.10, bf16[512,1024]{1,0:T(8,128)(2,1)S(1)} %copy-done.5, ...), custom_call_target="tpu_custom_call" | custom-call | flops 1430000000 | tf_op jit(solution)/shard_map/side/pallas_call | solution.py:102
  7.9 2.3 %collective-permute-start.9 = (f32[8,256]{1,0:T(8,128)S(1)}, f32[8,256]{1,0:T(8,128)S(1)}, u32[]{:S(2)}, u32[]{:S(2)}) collective-permute-start(f32[8,256]{1,0:T(8,128)S(1)} %side.1), channel_id=1, source_target_pairs={{0,12},{2,14},{4,8},{6,10},{8,4},{10,6},{12,0},{14,2},{1,13},{3,15... | collective-permute-start | bytes 24584 | tf_op jit(solution)/shard_map/side_z/ppermute | solution.py:432
  10.2 0.8 %collective-permute-start.8 = (f32[8,256]{1,0:T(8,128)S(1)}, f32[8,256]{1,0:T(8,128)S(1)}, u32[]{:S(2)}, u32[]{:S(2)}) collective-permute-start(f32[8,256]{1,0:T(8,128)S(1)} %side.1), channel_id=1, source_target_pairs={{0,8},{2,10},{4,12},{6,14},{8,0},{10,2},{12,4},{14,6},{1,9},{3,11}... | collective-permute-start | bytes 24584 | tf_op jit(solution)/shard_map/side_z/ppermute | solution.py:432
  11.0 1.3 %collective-permute-start.3 = (f32[8,256]{1,0:T(8,128)S(1)}, f32[8,256]{1,0:T(8,128)S(1)}, u32[]{:S(2)}, u32[]{:S(2)}) collective-permute-start(f32[8,256]{1,0:T(8,128)S(1)} %side.1), channel_id=1, source_target_pairs={{0,4},{2,6},{4,0},{6,2},{8,12},{10,14},{12,8},{14,10},{1,5},{3,7},... | collective-permute-start | bytes 24584 | tf_op jit(solution)/shard_map/side_z/ppermute | solution.py:432
  12.4 1.6 %collective-permute-done.9 = f32[8,256]{1,0:T(8,128)S(1)} collective-permute-done((f32[8,256]{1,0:T(8,128)S(1)}, f32[8,256]{1,0:T(8,128)S(1)}, u32[]{:S(2)}, u32[]{:S(2)}) %collective-permute-start.9) | collective-permute-done | bytes 8224 | tf_op jit(solution)/shard_map/side_z/ppermute | solution.py:432
  13.9 0.8 %collective-permute-done.8 = f32[8,256]{1,0:T(8,128)S(1)} collective-permute-done((f32[8,256]{1,0:T(8,128)S(1)}, f32[8,256]{1,0:T(8,128)S(1)}, u32[]{:S(2)}, u32[]{:S(2)}) %collective-permute-start.8) | collective-permute-done | bytes 8224 | tf_op jit(solution)/shard_map/side_z/ppermute | solution.py:432
  14.8 0.5 %collective-permute-start.10 = (f32[32,256]{1,0:T(8,128)S(1)}, f32[32,256]{1,0:T(8,128)S(1)}, u32[]{:S(2)}, u32[]{:S(2)}) collective-permute-start(f32[32,256]{1,0:T(8,128)S(1)} %pad_maximum_fusion.refs_3_), channel_id=1, source_target_pairs={{0,2},{2,0},{4,6},{6,4},{8,10},{10,8},{12,14},{14,12},{1,3},{3,1},... | collective-permute-start | bytes 98312 | tf_op jit(solution)/shard_map/side_y/ppermute | solution.py:432
  15.3 2.4 %collective-permute-start.6 = (bf16[256,512]{1,0:T(8,128)(2,1)S(1)}, bf16[256,512]{1,0:T(8,128)(2,1)S(1)}, u32[]{:S(2)}, u32[]{:S(2)}) collective-permute-start(bf16[256,512]{1,0:T(8,128)(2,1)S(1)} %bitcast.12), channel_id=1, source_target_pairs={{0,12},{2,14},{4,0},{6,2},{8,4},{10,6},{12,8},{14,10},{1,13},{3,15... | collective-permute-start | bytes 786440 | tf_op jit(solution)/shard_map/three/ppermute | solution.py:436
  17.7 1.5 %collective-permute-start.5 = (bf16[256,512]{1,0:T(8,128)(2,1)S(1)}, bf16[256,512]{1,0:T(8,128)(2,1)S(1)}, u32[]{:S(2)}, u32[]{:S(2)}) collective-permute-start(bf16[256,512]{1,0:T(8,128)(2,1)S(1)} %collective-permute-done.refs_2_), channel_id=1, source_target_pairs={{0,2},{2,0},{4,6},{6,4},{8,10},{10,8},{12,14},{14,12},{1,3},{3,1},... | collective-permute-start | bytes 786440 | tf_op jit(solution)/shard_map/one_y/ppermute | solution.py:432
  19.2 1.3 %ahead.1 = (bf16[512,768]{1,0:T(8,128)(2,1)S(1)}, bf16[1024,768]{1,0:T(8,128)(2,1)S(1)}, f32[144,768]{1,0:T(8,128)S(1)}) custom-call(bf16[256,512]{1,0:T(8,128)(2,1)S(1)} %bitcast.13, bf16[256,512]{1,0:T(8,128)(2,1)S(1)} %collective-permute-done.7.refs_1_, bf16[256,512]{1,0:T(8,128)(2,1)S(1)} %collective-permute-done.refs_2_, ...), custom_call_target="tpu_custom_call" | custom-call | flops 220000000 | tf_op jit(solution)/shard_map/ahead/pallas_call | solution.py:255
  20.5 2.6 %first.1 = (f32[656,1024]{1,0:T(8,128)S(1)}, f32[656,1024]{1,0:T(8,128)S(1)}, f32[16,128]{1,0:T(8,128)S(1)}, f32[64,256]{1,0:T(8,128)S(1)}) custom-call(bf16[512,768]{1,0:T(8,128)(2,1)S(1)} %get-tuple-element.49.refs_0_, bf16[1024,768]{1,0:T(8,128)(2,1)S(1)} %get-tuple-element.50.refs_1_, f32[144,768]{1,0:T(8,128)S(1)} %get-tuple-element.51.refs_2_, ...), custom_call_target="tpu_custom_call" | custom-call | flops 4400000000 | tf_op jit(solution)/shard_map/first/pallas_call | solution.py:345
  23.1 1.3 %collective-permute-done.6.refs_1_ = bf16[256,512]{1,0:T(8,128)(2,1)S(1)} collective-permute-done((bf16[256,512]{1,0:T(8,128)(2,1)S(1)}, bf16[256,512]{1,0:T(8,128)(2,1)S(1)}, u32[]{:S(2)}, u32[]{:S(2)}) %collective-permute-start.6) | collective-permute-done | bytes 262176 | tf_op jit(solution)/shard_map/three/ppermute | solution.py:436
  24.4 1.5 %collective-permute-start.12 = (bf16[256,512]{1,0:T(8,128)(2,1)S(1)}, bf16[256,512]{1,0:T(8,128)(2,1)S(1)}, u32[]{:S(2)}, u32[]{:S(2)}) collective-permute-start(bf16[256,512]{1,0:T(8,128)(2,1)S(1)} %collective-permute-done.6.refs_1_), channel_id=1, source_target_pairs={{0,2},{2,0},{4,6},{6,4},{8,10},{10,8},{12,14},{14,12},{1,3},{3,1},... | collective-permute-start | bytes 786440 | tf_op jit(solution)/shard_map/three_y/ppermute | solution.py:432
  25.9 2.9 %second.1 = (f32[656,1024]{1,0:T(8,128)S(1)}, f32[656,1024]{1,0:T(8,128)S(1)}) custom-call(bf16[256,512]{1,0:T(8,128)(2,1)S(1)} %collective-permute-done.5.refs_0_, bf16[256,512]{1,0:T(8,128)(2,1)S(1)} %collective-permute-done.6.refs_1_, f32[64,256]{1,0:T(8,128)S(1)} %get-tuple-element.54.refs_2_.refs_1_, f32[16,128]{1,0:T(8,128)S(1)} %get-tuple-element.55.refs_3_.refs_2_, ...), custom_call_target="tpu_custom_call" | custom-call | flops 3080000000 | tf_op jit(solution)/shard_map/second/pallas_call | solution.py:345
  28.8 1.6 %collective-permute-start.11 = (bf16[256,512]{1,0:T(8,128)(2,1)S(1)}, bf16[256,512]{1,0:T(8,128)(2,1)S(1)}, u32[]{:S(2)}, u32[]{:S(2)}) collective-permute-start(bf16[256,512]{1,0:T(8,128)(2,1)S(1)} %collective-permute-done.4.refs_1_), channel_id=1, source_target_pairs={{0,2},{2,0},{4,6},{6,4},{8,10},{10,8},{12,14},{14,12},{1,3},{3,1},... | collective-permute-start | bytes 786440 | tf_op jit(solution)/shard_map/two_y/ppermute | solution.py:432
  30.4 1.4 %collective-permute-done.12.refs_0_ = bf16[256,512]{1,0:T(8,128)(2,1)S(1)} collective-permute-done((bf16[256,512]{1,0:T(8,128)(2,1)S(1)}, bf16[256,512]{1,0:T(8,128)(2,1)S(1)}, u32[]{:S(2)}, u32[]{:S(2)}) %collective-permute-start.12) | collective-permute-done | bytes 262176 | tf_op jit(solution)/shard_map/three_y/ppermute | solution.py:432
  31.8 3.0 %third.1 = (f32[656,1024]{1,0:T(8,128)S(1)}, f32[656,1024]{1,0:T(8,128)S(1)}) custom-call(bf16[256,512]{1,0:T(8,128)(2,1)S(1)} %collective-permute-done.12.refs_0_, bf16[256,512]{1,0:T(8,128)(2,1)S(1)} %collective-permute-done.4.refs_1_, f32[64,256]{1,0:T(8,128)S(1)} %get-tuple-element.54.refs_2_.refs_1_, f32[16,128]{1,0:T(8,128)S(1)} %get-tuple-element.55.refs_3_.refs_2_, ...), custom_call_target="tpu_custom_call" | custom-call | flops 3080000000 | tf_op jit(solution)/shard_map/third/pallas_call | solution.py:345
  34.8 1.6 %collective-permute-done.11.refs_0_ = bf16[256,512]{1,0:T(8,128)(2,1)S(1)} collective-permute-done((bf16[256,512]{1,0:T(8,128)(2,1)S(1)}, bf16[256,512]{1,0:T(8,128)(2,1)S(1)}, u32[]{:S(2)}, u32[]{:S(2)}) %collective-permute-start.11) | collective-permute-done | bytes 262176 | tf_op jit(solution)/shard_map/two_y/ppermute | solution.py:432
  36.4 2.1 %fourth.1.mine = bf16[656,1024]{1,0:T(8,128)(2,1)S(1)} custom-call(bf16[256,512]{1,0:T(8,128)(2,1)S(1)} %collective-permute-done.11.refs_0_, f32[64,256]{1,0:T(8,128)S(1)} %get-tuple-element.54.refs_2_.refs_1_, f32[16,128]{1,0:T(8,128)S(1)} %get-tuple-element.55.refs_3_.refs_2_, f32[656,1024]{1,0:T(8,128)S(1)} %get-tuple-element.61.refs_3_, ...), custom_call_target="tpu_custom_call" | custom-call | flops 1760000000 | tf_op jit(solution)/shard_map/fourth/pallas_call | solution.py:345
  38.5 0.1 collective-permute-start.13
  38.6 3.1 %collective-permute-done.13.theirs = bf16[656,1024]{1,0:T(8,128)(2,1)S(1)} collective-permute-done((bf16[656,1024]{1,0:T(8,128)(2,1)S(1)}, bf16[656,1024]{1,0:T(8,128)(2,1)S(1)}, u32[]{:S(2)}, u32[]{:S(2)}) %collective-permute-start.13) | collective-permute-done | bytes 1343520 | tf_op jit(solution)/shard_map/ppermute | solution.py:497
  41.7 3.9 %update.1 = (bf16[256,128]{1,0:T(8,128)(2,1)}, f32[512,1024]{1,0:T(8,128)}, f32[1024,128]{1,0:T(8,128)}, f32[1,1024]{1,0:T(1,128)}, f32[512,1024]{1,0:T(8,128)}, /*index=5*/f32[1024,128]{1,0:T(8,128)}, f32[1,1024]{1,0:T(1,128)}) custom-call(bf16[656,1024]{1,0:T(8,128)(2,1)S(1)} %fourth.1.mine, bf16[656,1024]{1,0:T(8,128)(2,1)S(1)} %collective-permute-done.13.theirs, ...), custom_call_target="tpu_custom_call" | custom-call | flops 3740000000 | tf_op jit(solution)/shard_map/update/pallas_call | solution.py:417
  (34 shorter events, 0.1 us)
Async XLA Ops:
  0.6 5.2 %copy-start = (f32[512,1024]{1,0:T(8,128)S(1)}, f32[512,1024]{1,0:T(8,128)}, u32[]{:S(2)}) copy-start(f32[512,1024]{1,0:T(8,128)} %master_embed.3) | copy-start | bytes 6291460
  0.6 5.2 %copy-start.1 = (f32[1024,128]{1,0:T(8,128)S(1)}, f32[1024,128]{1,0:T(8,128)}, u32[]{:S(2)}) copy-start(f32[1024,128]{1,0:T(8,128)} %master_policy.3) | copy-start | bytes 1572868
  0.7 5.2 %copy-start.3 = (f32[1024]{0:T(1024)S(1)}, f32[1024]{0:T(1024)}, u32[]{:S(2)}) copy-start(f32[1024]{0:T(1024)} %param.23) | copy-start | bytes 12292
  0.7 18.5 %collective-permute-start.7 = (bf16[256,512]{1,0:T(8,128)(2,1)}, bf16[256,512]{1,0:T(8,128)(2,1)S(1)}, u32[]{:S(2)}, u32[]{:S(2)}) collective-permute-start(bf16[256,512]{1,0:T(8,128)(2,1)} %bitcast.9), channel_id=1, source_target_pairs={{0,2},{2,0},{4,6},{6,4},{8,10},{10,8},{12,14},{14,12},{1,3},{3,1},... | collective-permute-start | bytes 786440 | tf_op jit(solution)/shard_map/own_y/ppermute | solution.py:432
  3.7 14.0 %collective-permute-start = (bf16[256,512]{1,0:T(8,128)(2,1)}, bf16[256,512]{1,0:T(8,128)(2,1)S(1)}, u32[]{:S(2)}, u32[]{:S(2)}) collective-permute-start(bf16[256,512]{1,0:T(8,128)(2,1)} %bitcast.10), channel_id=1, source_target_pairs={{0,4},{2,6},{4,8},{6,10},{8,12},{10,14},{12,0},{14,2},{1,5},{3,7},... | collective-permute-start | bytes 786440 | tf_op jit(solution)/shard_map/one/ppermute | solution.py:436
  5.3 1.3 %collective-permute-start.1 = (s32[16]{0:T(128)}, s32[16]{0:T(128)S(1)}, u32[]{:S(2)}, u32[]{:S(2)}) collective-permute-start(s32[16]{0:T(128)} %param.15), channel_id=1, source_target_pairs={{0,1},{1,0},{2,3},{3,2},{4,5},{5,4},{6,7},{7,6},{8,9},{9,8},{10,11... | collective-permute-start | bytes 200 | tf_op jit(solution)/shard_map/ppermute | solution.py:487
  5.3 1.5 %collective-permute-start.2 = (s32[16]{0:T(128)}, s32[16]{0:T(128)S(1)}, u32[]{:S(2)}, u32[]{:S(2)}) collective-permute-start(s32[16]{0:T(128)} %param.18), channel_id=1, source_target_pairs={{0,1},{1,0},{2,3},{3,2},{4,5},{5,4},{6,7},{7,6},{8,9},{9,8},{10,11... | collective-permute-start | bytes 200 | tf_op jit(solution)/shard_map/ppermute | solution.py:487
  5.8 1.0 %copy-start.2 = (bf16[16,16,512]{2,1,0:T(8,128)(2,1)S(1)}, bf16[16,16,512]{2,1,0:T(8,128)(2,1)}, u32[]{:S(2)}) copy-start(bf16[16,16,512]{2,1,0:T(8,128)(2,1)} %param.14) | copy-start | bytes 786436
  5.8 1.3 %copy-start.5 = (bf16[512,1024]{1,0:T(8,128)(2,1)S(1)}, bf16[512,1024]{1,0:T(8,128)(2,1)}, u32[]{:S(2)}) copy-start(bf16[512,1024]{1,0:T(8,128)(2,1)} %actor_embed.1) | copy-start | bytes 3145732
  5.8 1.3 %copy-start.7 = (bf16[1024,128]{1,0:T(8,128)(2,1)S(1)}, bf16[1024,128]{1,0:T(8,128)(2,1)}, u32[]{:S(2)}) copy-start(bf16[1024,128]{1,0:T(8,128)(2,1)} %actor_policy.1) | copy-start | bytes 786436
  5.8 1.3 %copy-start.9 = (s32[16,16]{1,0:T(8,128)S(1)}, s32[16,16]{1,0:T(8,128)}, u32[]{:S(2)}) copy-start(s32[16,16]{1,0:T(8,128)} %actions.1) | copy-start | bytes 3076
  5.8 1.3 %copy-start.10 = (f32[16,16]{1,0:T(8,128)S(1)}, f32[16,16]{1,0:T(8,128)}, u32[]{:S(2)}) copy-start(f32[16,16]{1,0:T(8,128)} %rewards.1) | copy-start | bytes 3076
  5.8 1.3 %copy-start.12 = (s32[16]{0:T(128)S(1)}, s32[16]{0:T(128)}, u32[]{:S(2)}) copy-start(s32[16]{0:T(128)} %param.15) | copy-start | bytes 196
  5.9 1.3 %copy-start.13 = (s32[16]{0:T(128)S(1)}, s32[16]{0:T(128)}, u32[]{:S(2)}) copy-start(s32[16]{0:T(128)} %param.18) | copy-start | bytes 196
  7.9 6.0 %collective-permute-start.9 = (f32[8,256]{1,0:T(8,128)S(1)}, f32[8,256]{1,0:T(8,128)S(1)}, u32[]{:S(2)}, u32[]{:S(2)}) collective-permute-start(f32[8,256]{1,0:T(8,128)S(1)} %side.1), channel_id=1, source_target_pairs={{0,12},{2,14},{4,8},{6,10},{8,4},{10,6},{12,0},{14,2},{1,13},{3,15... | collective-permute-start | bytes 24584 | tf_op jit(solution)/shard_map/side_z/ppermute | solution.py:432
  10.2 4.5 %collective-permute-start.8 = (f32[8,256]{1,0:T(8,128)S(1)}, f32[8,256]{1,0:T(8,128)S(1)}, u32[]{:S(2)}, u32[]{:S(2)}) collective-permute-start(f32[8,256]{1,0:T(8,128)S(1)} %side.1), channel_id=1, source_target_pairs={{0,8},{2,10},{4,12},{6,14},{8,0},{10,2},{12,4},{14,6},{1,9},{3,11}... | collective-permute-start | bytes 24584 | tf_op jit(solution)/shard_map/side_z/ppermute | solution.py:432
  11.0 3.8 %collective-permute-start.3 = (f32[8,256]{1,0:T(8,128)S(1)}, f32[8,256]{1,0:T(8,128)S(1)}, u32[]{:S(2)}, u32[]{:S(2)}) collective-permute-start(f32[8,256]{1,0:T(8,128)S(1)} %side.1), channel_id=1, source_target_pairs={{0,4},{2,6},{4,0},{6,2},{8,12},{10,14},{12,8},{14,10},{1,5},{3,7},... | collective-permute-start | bytes 24584 | tf_op jit(solution)/shard_map/side_z/ppermute | solution.py:432
  14.8 5.7 %collective-permute-start.10 = (f32[32,256]{1,0:T(8,128)S(1)}, f32[32,256]{1,0:T(8,128)S(1)}, u32[]{:S(2)}, u32[]{:S(2)}) collective-permute-start(f32[32,256]{1,0:T(8,128)S(1)} %pad_maximum_fusion.refs_3_), channel_id=1, source_target_pairs={{0,2},{2,0},{4,6},{6,4},{8,10},{10,8},{12,14},{14,12},{1,3},{3,1},... | collective-permute-start | bytes 98312 | tf_op jit(solution)/shard_map/side_y/ppermute | solution.py:432
  15.3 9.1 %collective-permute-start.6 = (bf16[256,512]{1,0:T(8,128)(2,1)S(1)}, bf16[256,512]{1,0:T(8,128)(2,1)S(1)}, u32[]{:S(2)}, u32[]{:S(2)}) collective-permute-start(bf16[256,512]{1,0:T(8,128)(2,1)S(1)} %bitcast.12), channel_id=1, source_target_pairs={{0,12},{2,14},{4,0},{6,2},{8,4},{10,6},{12,8},{14,10},{1,13},{3,15... | collective-permute-start | bytes 786440 | tf_op jit(solution)/shard_map/three/ppermute | solution.py:436
  17.7 8.3 %collective-permute-start.5 = (bf16[256,512]{1,0:T(8,128)(2,1)S(1)}, bf16[256,512]{1,0:T(8,128)(2,1)S(1)}, u32[]{:S(2)}, u32[]{:S(2)}) collective-permute-start(bf16[256,512]{1,0:T(8,128)(2,1)S(1)} %collective-permute-done.refs_2_), channel_id=1, source_target_pairs={{0,2},{2,0},{4,6},{6,4},{8,10},{10,8},{12,14},{14,12},{1,3},{3,1},... | collective-permute-start | bytes 786440 | tf_op jit(solution)/shard_map/one_y/ppermute | solution.py:432
  19.2 9.7 %collective-permute-start.4 = (bf16[256,512]{1,0:T(8,128)(2,1)S(1)}, bf16[256,512]{1,0:T(8,128)(2,1)S(1)}, u32[]{:S(2)}, u32[]{:S(2)}) collective-permute-start(bf16[256,512]{1,0:T(8,128)(2,1)S(1)} %collective-permute-done.refs_2_), channel_id=1, source_target_pairs={{0,4},{2,6},{4,8},{6,10},{8,12},{10,14},{12,0},{14,2},{1,5},{3,7},... | collective-permute-start | bytes 786440 | tf_op jit(solution)/shard_map/two/ppermute | solution.py:436
  24.4 7.4 %collective-permute-start.12 = (bf16[256,512]{1,0:T(8,128)(2,1)S(1)}, bf16[256,512]{1,0:T(8,128)(2,1)S(1)}, u32[]{:S(2)}, u32[]{:S(2)}) collective-permute-start(bf16[256,512]{1,0:T(8,128)(2,1)S(1)} %collective-permute-done.6.refs_1_), channel_id=1, source_target_pairs={{0,2},{2,0},{4,6},{6,4},{8,10},{10,8},{12,14},{14,12},{1,3},{3,1},... | collective-permute-start | bytes 786440 | tf_op jit(solution)/shard_map/three_y/ppermute | solution.py:432
  28.8 7.6 %collective-permute-start.11 = (bf16[256,512]{1,0:T(8,128)(2,1)S(1)}, bf16[256,512]{1,0:T(8,128)(2,1)S(1)}, u32[]{:S(2)}, u32[]{:S(2)}) collective-permute-start(bf16[256,512]{1,0:T(8,128)(2,1)S(1)} %collective-permute-done.4.refs_1_), channel_id=1, source_target_pairs={{0,2},{2,0},{4,6},{6,4},{8,10},{10,8},{12,14},{14,12},{1,3},{3,1},... | collective-permute-start | bytes 786440 | tf_op jit(solution)/shard_map/two_y/ppermute | solution.py:432
  36.4 5.3 %copy-start.4 = (f32[512,1024]{1,0:T(8,128)S(1)}, f32[512,1024]{1,0:T(8,128)}, u32[]{:S(2)}) copy-start(f32[512,1024]{1,0:T(8,128)} %embed_moment.1) | copy-start | bytes 6291460
  36.4 5.3 %copy-start.6 = (f32[1024,128]{1,0:T(8,128)S(1)}, f32[1024,128]{1,0:T(8,128)}, u32[]{:S(2)}) copy-start(f32[1024,128]{1,0:T(8,128)} %policy_moment.1) | copy-start | bytes 1572868
  36.4 5.3 %copy-start.8 = (bf16[256,512]{1,0:T(8,128)(2,1)S(1)}, bf16[256,512]{1,0:T(8,128)(2,1)}, u32[]{:S(2)}) copy-start(bf16[256,512]{1,0:T(8,128)(2,1)} %next_obs.1) | copy-start | bytes 786436
  36.4 5.3 %copy-start.11 = (f32[1024]{0:T(1024)S(1)}, f32[1024]{0:T(1024)}, u32[]{:S(2)}) copy-start(f32[1024]{0:T(1024)} %param.26) | copy-start | bytes 12292
  38.5 3.1 %collective-permute-start.13 = (bf16[656,1024]{1,0:T(8,128)(2,1)S(1)}, bf16[656,1024]{1,0:T(8,128)(2,1)S(1)}, u32[]{:S(2)}, u32[]{:S(2)}) collective-permute-start(bf16[656,1024]{1,0:T(8,128)(2,1)S(1)} %fourth.1.mine), channel_id=1, source_target_pairs={{0,1},{1,0},{2,3},{3,2},{4,5},{5,4},{6,7},{7,6},{8,9},{9,8},{10,11... | collective-permute-start | bytes 4030472 | tf_op jit(solution)/shard_map/ppermute | solution.py:497

commit v8 on v7

--- a/solution.py
+++ b/solution.py
@@ -241,7 +241,7 @@
 def side_of(sides, back, flip):
     line = lax.div(lax.axis_index("hst"), 2)
     there = lax.bitwise_xor(line, lax.bitwise_and(line + 4 - back, 3))
-    return sides[pl.ds(pl.multiple_of(8 * (4 * flip + there), 8), 8), :]
+    return sides[pl.ds(pl.multiple_of(8 * (2 * there + flip), 8), 8), :]
 
 
 def ahead_kernel(*refs):
@@ -262,14 +262,14 @@
         in_specs=[VMEM] * (len(frames) + 2),
         out_specs=(VMEM,) * 3,
         compiler_params=params(20),
-        cost_estimate=cost(0.2),
+        cost_estimate=cost(1.6),
         name="ahead",
     )(*frames, embed_t, head_t)
 
 
 def first_kernel(slots, *refs):
     (frames_t, hidden_t, logits, *pieces), mats, (sum_0, sum_1, weights, sides), scratch = (
-        refs[0:5], refs[5:8], refs[8:12], refs[12:15])
+        refs[0:7], refs[7:10], refs[10:14], refs[14:17])
     start = 0
     for piece in pieces:
         sides[start : start + piece.shape[0], :] = piece[...]
@@ -362,7 +362,7 @@
     feats, nact, mine, theirs, master_embed, master_policy, master_value,
     embed_moment, policy_moment, value_moment, next_obs,
     next_logits, new_embed_at, new_policy_at, new_value, new_em_at, new_pm_at, new_vm,
-    new_embed, new_policy, new_em, new_pm, sems,
+    new_embed, new_policy, new_em, new_pm, rounded, sems,
 ):
     copies = []
 
@@ -381,15 +381,13 @@
     def chunks(height):
         return [pl.ds(start, height // CHUNKS) for start in range(0, height, height // CHUNKS)]
 
-    preact = None
     for rows in chunks(feats):
         held, fresh = step(grad(rows.start, rows.size), embed_moment[rows, :], master_embed[rows, :])
         new_em[rows, :] = held
         new_embed[rows, :] = fresh
+        rounded[rows, :] = fresh.astype(BF16)
         store(new_em, new_em_at, rows)
         store(new_embed, new_embed_at, rows)
-        part = mm(next_obs[:, rows], fresh.astype(BF16))
-        preact = part if preact is None else preact + part
     policy_grad = grad(feats, nact).T
     held, fresh = step(policy_grad, policy_moment[...], master_policy[...])
     new_pm[...] = held
@@ -400,7 +398,7 @@
     new_vm[...], new_value[...] = step(
         grad(feats + nact, PAD)[0:1, :], value_moment[...], master_value[...]
     )
-    hidden = jnp.maximum(preact, 0.0).astype(BF16)
+    hidden = jnp.maximum(mm(next_obs[...], rounded[...]), 0.0).astype(BF16)
     next_logits[...] = mm(hidden, fresh.astype(BF16)).astype(BF16)
     for copy in copies:
         copy.wait()
@@ -419,7 +417,7 @@
         out_shape=(jax.ShapeDtypeStruct((next_obs.shape[0], nact), BF16), *shapes, *shapes),
         in_specs=[VMEM] * 9,
         out_specs=(VMEM, *specs, *specs),
-        scratch_shapes=[*held, *held, pltpu.SemaphoreType.DMA((2 * CHUNKS + 2,))],
+        scratch_shapes=[*held, *held, pltpu.VMEM(embed.shape, BF16), pltpu.SemaphoreType.DMA((2 * CHUNKS + 2,))],
         compiler_params=params(24),
         cost_estimate=cost(3.4),
         name="update",
@@ -437,24 +435,22 @@
 
     one = shift(own, 1, "one")
     own_y = exchange(own, 1, "own_y")
-    pieces = [side] + [exchange(side, 2 * mask, "side_z") for mask in (1, 2, 3)]
-    line = jnp.concatenate(pieces, axis=0)
-    line, _ = lax.optimization_barrier((line, side))
-    one, _ = lax.optimization_barrier((one, pieces[1]))
-    again, _ = lax.optimization_barrier((own, pieces[1]))
-    line_y = exchange(line, 1, "side_y")
+    pair = jnp.concatenate([side, exchange(side, 1, "side_y")], axis=0)
+    pair, _, _ = lax.optimization_barrier((pair, one, own_y))
+    pieces = [pair] + [exchange(pair, 2 * mask, "side_z") for mask in (1, 2, 3)]
+    again, _ = lax.optimization_barrier((own, side))
     three = shift(again, -1, "three")
     one_y = exchange(one, 1, "one_y")
     two = shift(one, 1, "two")
     three_y = exchange(three, 1, "three_y")
-
+    pieces, one_y = lax.optimization_barrier((pieces, one_y))
     width, feats = mats[0].shape
     grads = jax.ShapeDtypeStruct((feats + mats[2].shape[0], width), F32)
     weights = jax.ShapeDtypeStruct((16, 128), F32)
     sides = jax.ShapeDtypeStruct((64, side.shape[1]), F32)
     done = ahead((own, own_y, one), mats[0], mats[2])
     sum_0, sum_1, weights, sides = call(
-        first_kernel, "first", slots, 3, (*done, line, line_y), mats,
+        first_kernel, "first", slots, 3, (*done, *pieces), mats,
         (grads, grads, weights, sides),
     )
     sum_1y, sum_3 = call(

time: 45.7 us -> 48.3 us (1.057)
  starting transfers between devices: 17.1 us -> 19.1 us
    ppermute x3, waiting for transfers between devices: 1.31 us -> 3.59 us  [shift(): lax.ppermute(array, 'hst', [(at, (at + 2 * by) % 8) for at in range(8)])]
    ppermute x8, waiting for transfers between devices: 5.45 us -> 3.51 us  [exchange(): return lax.ppermute(array, 'hst', [(at, at ^ mask) for at in range(8)])]
    ppermute x3, starting transfers between devices: 3.96 us -> 5.37 us  [shift(): lax.ppermute(array, 'hst', [(at, (at + 2 * by) % 8) for at in range(8)])]
    ppermute x8, starting transfers between devices: 12.6 us -> 13.2 us  [exchange(): return lax.ppermute(array, 'hst', [(at, at ^ mask) for at in range(8)])]
  transfers between devices with their start and end apart: 14 -> 14, of which waited for: 8 -> 6; matrix products, arithmetic and copies ran while one was open for 0% -> 0% of each run, Pallas kernels for 24% -> 23%
where the time goes in v8:
time: 48.3 us; the launch traced here: 48.1 us
  starting transfers between devices  19.1 us (40%)
  Pallas kernels  17.1 us (35%)
  waiting for transfers between devices  10.5 us (22%)
  between operations  0.98 us (2%)
    ppermute x8, starting transfers between devices, exchange(): return lax.ppermute(array, 'hst', [(at, at ^ mask) for at in range(8)])  13.2 us
    pallas_call x4, Pallas kernels, call(): pl.pallas_call(functools.partial(kernel, slots), out_shape=outs, in_specs...  10.5 us
    ppermute x3, starting transfers between devices, shift(): lax.ppermute(array, 'hst', [(at, (at + 2 * by) % 8) for at in range(8)])  5.37 us
    pallas_call x1, Pallas kernels, update(): pl.pallas_call(functools.partial(update_kernel, feats, nact), out_shape=(...  3.96 us
    ppermute x3, waiting for transfers between devices, shift(): lax.ppermute(array, 'hst', [(at, (at + 2 * by) % 8) for at in range(8)])  3.59 us
    ppermute x8, waiting for transfers between devices, exchange(): return lax.ppermute(array, 'hst', [(at, at ^ mask) for at in range(8)])  3.51 us
    ppermute x1, waiting for transfers between devices, body(): theirs = lax.ppermute(mine, 'cores', flip)  3.07 us
    pallas_call x1, Pallas kernels, ahead(): pl.pallas_call(ahead_kernel, out_shape=(jax.ShapeDtypeStruct((feats, rows...  1.31 us
  transfers between devices with their start and end apart: 14, of which 6 were waited for; matrix products, arithmetic and copies ran while one was open for 0% of the time, Pallas kernels for 23%

profile of v8, /device:TPU:0, one launch (start us, length us, event | category | flops | bytes accessed | tf_op | source)
XLA Modules:
  0.0 48.1 jit_solution(13011048294415685653)
XLA Ops:
  0.7 3.0 %collective-permute-start.5 = (bf16[256,512]{1,0:T(8,128)(2,1)}, bf16[256,512]{1,0:T(8,128)(2,1)S(1)}, u32[]{:S(2)}, u32[]{:S(2)}) collective-permute-start(bf16[256,512]{1,0:T(8,128)(2,1)} %bitcast.11), channel_id=1, source_target_pairs={{0,2},{2,0},{4,6},{6,4},{8,10},{10,8},{12,14},{14,12},{1,3},{3,1},... | collective-permute-start | bytes 786440 | tf_op jit(solution)/shard_map/own_y/ppermute | solution.py:430
  3.7 1.6 %collective-permute-start = (bf16[256,512]{1,0:T(8,128)(2,1)}, bf16[256,512]{1,0:T(8,128)(2,1)S(1)}, u32[]{:S(2)}, u32[]{:S(2)}) collective-permute-start(bf16[256,512]{1,0:T(8,128)(2,1)} %bitcast.12), channel_id=1, source_target_pairs={{0,4},{2,6},{4,8},{6,10},{8,12},{10,14},{12,0},{14,2},{1,5},{3,7},... | collective-permute-start | bytes 786440 | tf_op jit(solution)/shard_map/one/ppermute | solution.py:434
  5.3 0.5 %collective-permute-start.3 = (s32[16]{0:T(128)}, s32[16]{0:T(128)S(1)}, u32[]{:S(2)}, u32[]{:S(2)}) collective-permute-start(s32[16]{0:T(128)} %param.18), channel_id=1, source_target_pairs={{0,1},{1,0},{2,3},{3,2},{4,5},{5,4},{6,7},{7,6},{8,9},{9,8},{10,11... | collective-permute-start | bytes 200 | tf_op jit(solution)/shard_map/ppermute | solution.py:483
  5.8 0.0 copy-start.6
  5.8 0.0 copy-start.7
  5.8 0.0 copy-start.9
  5.8 0.0 copy-start.10
  5.9 0.5 %convert.1 = (bf16[1024,512]{1,0:T(8,128)(2,1)S(1)}, bf16[1024,144]{1,0:T(8,128)(2,1)S(1)}, bf16[144,1024]{1,0:T(8,128)(2,1)S(1)}) custom-call(f32[512,1024]{1,0:T(8,128)S(1)} %copy-done, f32[1024,128]{1,0:T(8,128)S(1)} %copy-done.1, f32[1,1024]{1,0:T(1,128)S(1)} %bitcast.9), custom_call_target="tpu_custom_call" | custom-call | flops 660000000 | tf_op jit(solution)/shard_map/convert/pallas_call | solution.py:132
  6.4 0.1 collective-permute-done.2
  6.5 0.2 collective-permute-done.3
  6.7 0.3 copy-done.4
  7.0 0.0 copy-done.6
  7.1 0.1 copy-done.7
  7.1 0.8 %side.1 = f32[8,256]{1,0:T(8,128)S(1)} custom-call(s32[1,16]{1,0:T(1,128)S(1)} %bitcast.17, s32[1,16]{1,0:T(1,128)S(1)} %bitcast.18, s32[1,16]{1,0:T(1,128)S(1)} %bitcast.19, s32[1,16]{1,0:T(1,128)S(1)} %bitcast.20, s32[16,16]{1,0:T(8,128)S(1)} %copy-done.9, f32[16,16]{1,0:T(8,128)S(1)} %copy-done.10, bf16[512,1024]{1,0:T(8,128)(2,1)S(1)} %copy-done.4, ...), custom_call_target="tpu_custom_call" | custom-call | flops 1430000000 | tf_op jit(solution)/shard_map/side/pallas_call | solution.py:102
  7.9 0.6 %collective-permute-start.4 = (f32[8,256]{1,0:T(8,128)S(1)}, f32[8,256]{1,0:T(8,128)S(1)}, u32[]{:S(2)}, u32[]{:S(2)}) collective-permute-start(f32[8,256]{1,0:T(8,128)S(1)} %side.1), channel_id=1, source_target_pairs={{0,2},{2,0},{4,6},{6,4},{8,10},{10,8},{12,14},{14,12},{1,3},{3,1},... | collective-permute-start | bytes 24584 | tf_op jit(solution)/shard_map/side_y/ppermute | solution.py:430
  8.5 2.2 %collective-permute-start.10 = (bf16[256,512]{1,0:T(8,128)(2,1)S(1)}, bf16[256,512]{1,0:T(8,128)(2,1)S(1)}, u32[]{:S(2)}, u32[]{:S(2)}) collective-permute-start(bf16[256,512]{1,0:T(8,128)(2,1)S(1)} %bitcast.14), channel_id=1, source_target_pairs={{0,12},{2,14},{4,0},{6,2},{8,4},{10,6},{12,8},{14,10},{1,13},{3,15... | collective-permute-start | bytes 786440 | tf_op jit(solution)/shard_map/three/ppermute | solution.py:434
  10.7 3.6 %collective-permute-done.refs_2_ = bf16[256,512]{1,0:T(8,128)(2,1)S(1)} collective-permute-done((bf16[256,512]{1,0:T(8,128)(2,1)}, bf16[256,512]{1,0:T(8,128)(2,1)S(1)}, u32[]{:S(2)}, u32[]{:S(2)}) %collective-permute-start) | collective-permute-done | bytes 262176 | tf_op jit(solution)/shard_map/one/ppermute | solution.py:434
  14.3 6.2 %collective-permute-start.8 = (f32[16,256]{1,0:T(8,128)S(1)}, f32[16,256]{1,0:T(8,128)S(1)}, u32[]{:S(2)}, u32[]{:S(2)}) collective-permute-start(f32[16,256]{1,0:T(8,128)S(1)} %pad_maximum_fusion.refs_3_), channel_id=1, source_target_pairs={{0,12},{2,14},{4,8},{6,10},{8,4},{10,6},{12,0},{14,2},{1,13},{3,15... | collective-permute-start | bytes 49160 | tf_op jit(solution)/shard_map/side_z/ppermute | solution.py:430
  20.5 0.6 %collective-permute-start.6 = (f32[16,256]{1,0:T(8,128)S(1)}, f32[16,256]{1,0:T(8,128)S(1)}, u32[]{:S(2)}, u32[]{:S(2)}) collective-permute-start(f32[16,256]{1,0:T(8,128)S(1)} %pad_maximum_fusion.refs_3_), channel_id=1, source_target_pairs={{0,4},{2,6},{4,0},{6,2},{8,12},{10,14},{12,8},{14,10},{1,5},{3,7},... | collective-permute-start | bytes 49160 | tf_op jit(solution)/shard_map/side_z/ppermute | solution.py:430
  21.1 1.3 %ahead.1 = (bf16[512,768]{1,0:T(8,128)(2,1)S(1)}, bf16[1024,768]{1,0:T(8,128)(2,1)S(1)}, f32[144,768]{1,0:T(8,128)S(1)}) custom-call(bf16[256,512]{1,0:T(8,128)(2,1)S(1)} %bitcast.15, bf16[256,512]{1,0:T(8,128)(2,1)S(1)} %collective-permute-done.5.refs_1_, bf16[256,512]{1,0:T(8,128)(2,1)S(1)} %collective-permute-done.refs_2_, ...), custom_call_target="tpu_custom_call" | custom-call | flops 1760000000 | tf_op jit(solution)/shard_map/ahead/pallas_call | solution.py:255
  22.4 1.6 %collective-permute-start.1 = (bf16[256,512]{1,0:T(8,128)(2,1)S(1)}, bf16[256,512]{1,0:T(8,128)(2,1)S(1)}, u32[]{:S(2)}, u32[]{:S(2)}) collective-permute-start(bf16[256,512]{1,0:T(8,128)(2,1)S(1)} %collective-permute-done.refs_2_), channel_id=1, source_target_pairs={{0,4},{2,6},{4,8},{6,10},{8,12},{10,14},{12,0},{14,2},{1,5},{3,7},... | collective-permute-start | bytes 786440 | tf_op jit(solution)/shard_map/two/ppermute | solution.py:434
  24.0 2.0 %collective-permute-start.12 = (bf16[256,512]{1,0:T(8,128)(2,1)S(1)}, bf16[256,512]{1,0:T(8,128)(2,1)S(1)}, u32[]{:S(2)}, u32[]{:S(2)}) collective-permute-start(bf16[256,512]{1,0:T(8,128)(2,1)S(1)} %collective-permute-done.10.refs_1_), channel_id=1, source_target_pairs={{0,2},{2,0},{4,6},{6,4},{8,10},{10,8},{12,14},{14,12},{1,3},{3,1},... | collective-permute-start | bytes 786440 | tf_op jit(solution)/shard_map/three_y/ppermute | solution.py:430
  26.1 0.7 %collective-permute-done.7.refs_5_ = f32[16,256]{1,0:T(8,128)S(1)} collective-permute-done((f32[16,256]{1,0:T(8,128)S(1)}, f32[16,256]{1,0:T(8,128)S(1)}, u32[]{:S(2)}, u32[]{:S(2)}) %collective-permute-start.7) | collective-permute-done | bytes 16416 | tf_op jit(solution)/shard_map/side_z/ppermute | solution.py:430
  26.8 2.6 %first.1 = (f32[656,1024]{1,0:T(8,128)S(1)}, f32[656,1024]{1,0:T(8,128)S(1)}, f32[16,128]{1,0:T(8,128)S(1)}, f32[64,256]{1,0:T(8,128)S(1)}) custom-call(bf16[512,768]{1,0:T(8,128)(2,1)S(1)} %get-tuple-element.54.refs_0_, bf16[1024,768]{1,0:T(8,128)(2,1)S(1)} %get-tuple-element.55.refs_1_, f32[144,768]{1,0:T(8,128)S(1)} %get-tuple-element.56.refs_2_, ...), custom_call_target="tpu_custom_call" | custom-call | flops 4400000000 | tf_op jit(solution)/shard_map/first/pallas_call | solution.py:345
  29.4 2.9 %second.1 = (f32[656,1024]{1,0:T(8,128)S(1)}, f32[656,1024]{1,0:T(8,128)S(1)}) custom-call(bf16[256,512]{1,0:T(8,128)(2,1)S(1)} %collective-permute-done.9.refs_0_, bf16[256,512]{1,0:T(8,128)(2,1)S(1)} %collective-permute-done.10.refs_1_, f32[64,256]{1,0:T(8,128)S(1)} %get-tuple-element.62.refs_2_.refs_1_, f32[16,128]{1,0:T(8,128)S(1)} %get-tuple-element.63.refs_3_.refs_2_, ...), custom_call_target="tpu_custom_call" | custom-call | flops 3080000000 | tf_op jit(solution)/shard_map/second/pallas_call | solution.py:345
  32.3 0.7 %collective-permute-start.11 = (bf16[256,512]{1,0:T(8,128)(2,1)S(1)}, bf16[256,512]{1,0:T(8,128)(2,1)S(1)}, u32[]{:S(2)}, u32[]{:S(2)}) collective-permute-start(bf16[256,512]{1,0:T(8,128)(2,1)S(1)} %collective-permute-done.1.refs_1_), channel_id=1, source_target_pairs={{0,2},{2,0},{4,6},{6,4},{8,10},{10,8},{12,14},{14,12},{1,3},{3,1},... | collective-permute-start | bytes 786440 | tf_op jit(solution)/shard_map/two_y/ppermute | solution.py:430
  33.0 3.0 %third.1 = (f32[656,1024]{1,0:T(8,128)S(1)}, f32[656,1024]{1,0:T(8,128)S(1)}) custom-call(bf16[256,512]{1,0:T(8,128)(2,1)S(1)} %collective-permute-done.12.refs_0_, bf16[256,512]{1,0:T(8,128)(2,1)S(1)} %collective-permute-done.1.refs_1_, f32[64,256]{1,0:T(8,128)S(1)} %get-tuple-element.62.refs_2_.refs_1_, f32[16,128]{1,0:T(8,128)S(1)} %get-tuple-element.63.refs_3_.refs_2_, ...), custom_call_target="tpu_custom_call" | custom-call | flops 3080000000 | tf_op jit(solution)/shard_map/third/pallas_call | solution.py:345
  36.0 2.8 %collective-permute-done.11.refs_0_ = bf16[256,512]{1,0:T(8,128)(2,1)S(1)} collective-permute-done((bf16[256,512]{1,0:T(8,128)(2,1)S(1)}, bf16[256,512]{1,0:T(8,128)(2,1)S(1)}, u32[]{:S(2)}, u32[]{:S(2)}) %collective-permute-start.11) | collective-permute-done | bytes 262176 | tf_op jit(solution)/shard_map/two_y/ppermute | solution.py:430
  38.7 2.1 %fourth.1.mine = bf16[656,1024]{1,0:T(8,128)(2,1)S(1)} custom-call(bf16[256,512]{1,0:T(8,128)(2,1)S(1)} %collective-permute-done.11.refs_0_, f32[64,256]{1,0:T(8,128)S(1)} %get-tuple-element.62.refs_2_.refs_1_, f32[16,128]{1,0:T(8,128)S(1)} %get-tuple-element.63.refs_3_.refs_2_, f32[656,1024]{1,0:T(8,128)S(1)} %get-tuple-element.69.refs_3_, ...), custom_call_target="tpu_custom_call" | custom-call | flops 1760000000 | tf_op jit(solution)/shard_map/fourth/pallas_call | solution.py:345
  40.8 0.1 collective-permute-start.13
  40.9 3.1 %collective-permute-done.13.theirs = bf16[656,1024]{1,0:T(8,128)(2,1)S(1)} collective-permute-done((bf16[656,1024]{1,0:T(8,128)(2,1)S(1)}, bf16[656,1024]{1,0:T(8,128)(2,1)S(1)}, u32[]{:S(2)}, u32[]{:S(2)}) %collective-permute-start.13) | collective-permute-done | bytes 1343520 | tf_op jit(solution)/shard_map/ppermute | solution.py:493
  44.0 4.0 %update.1 = (bf16[256,128]{1,0:T(8,128)(2,1)}, f32[512,1024]{1,0:T(8,128)}, f32[1024,128]{1,0:T(8,128)}, f32[1,1024]{1,0:T(1,128)}, f32[512,1024]{1,0:T(8,128)}, /*index=5*/f32[1024,128]{1,0:T(8,128)}, f32[1,1024]{1,0:T(1,128)}) custom-call(bf16[656,1024]{1,0:T(8,128)(2,1)S(1)} %fourth.1.mine, bf16[656,1024]{1,0:T(8,128)(2,1)S(1)} %collective-permute-done.13.theirs, ...), custom_call_target="tpu_custom_call" | custom-call | flops 3740000000 | tf_op jit(solution)/shard_map/update/pallas_call | solution.py:415
  (34 shorter events, 0.1 us)
Async XLA Ops:
  0.6 5.2 %copy-start = (f32[512,1024]{1,0:T(8,128)S(1)}, f32[512,1024]{1,0:T(8,128)}, u32[]{:S(2)}) copy-start(f32[512,1024]{1,0:T(8,128)} %master_embed.3) | copy-start | bytes 6291460
  0.6 5.2 %copy-start.1 = (f32[1024,128]{1,0:T(8,128)S(1)}, f32[1024,128]{1,0:T(8,128)}, u32[]{:S(2)}) copy-start(f32[1024,128]{1,0:T(8,128)} %master_policy.3) | copy-start | bytes 1572868
  0.7 5.2 %copy-start.2 = (f32[1024]{0:T(1024)S(1)}, f32[1024]{0:T(1024)}, u32[]{:S(2)}) copy-start(f32[1024]{0:T(1024)} %param.23) | copy-start | bytes 12292
  0.7 13.6 %collective-permute-start.5 = (bf16[256,512]{1,0:T(8,128)(2,1)}, bf16[256,512]{1,0:T(8,128)(2,1)S(1)}, u32[]{:S(2)}, u32[]{:S(2)}) collective-permute-start(bf16[256,512]{1,0:T(8,128)(2,1)} %bitcast.11), channel_id=1, source_target_pairs={{0,2},{2,0},{4,6},{6,4},{8,10},{10,8},{12,14},{14,12},{1,3},{3,1},... | collective-permute-start | bytes 786440 | tf_op jit(solution)/shard_map/own_y/ppermute | solution.py:430
  3.7 10.5 %collective-permute-start = (bf16[256,512]{1,0:T(8,128)(2,1)}, bf16[256,512]{1,0:T(8,128)(2,1)S(1)}, u32[]{:S(2)}, u32[]{:S(2)}) collective-permute-start(bf16[256,512]{1,0:T(8,128)(2,1)} %bitcast.12), channel_id=1, source_target_pairs={{0,4},{2,6},{4,8},{6,10},{8,12},{10,14},{12,0},{14,2},{1,5},{3,7},... | collective-permute-start | bytes 786440 | tf_op jit(solution)/shard_map/one/ppermute | solution.py:434
  5.3 1.3 %collective-permute-start.2 = (s32[16]{0:T(128)}, s32[16]{0:T(128)S(1)}, u32[]{:S(2)}, u32[]{:S(2)}) collective-permute-start(s32[16]{0:T(128)} %param.15), channel_id=1, source_target_pairs={{0,1},{1,0},{2,3},{3,2},{4,5},{5,4},{6,7},{7,6},{8,9},{9,8},{10,11... | collective-permute-start | bytes 200 | tf_op jit(solution)/shard_map/ppermute | solution.py:483
  5.3 1.5 %collective-permute-start.3 = (s32[16]{0:T(128)}, s32[16]{0:T(128)S(1)}, u32[]{:S(2)}, u32[]{:S(2)}) collective-permute-start(s32[16]{0:T(128)} %param.18), channel_id=1, source_target_pairs={{0,1},{1,0},{2,3},{3,2},{4,5},{5,4},{6,7},{7,6},{8,9},{9,8},{10,11... | collective-permute-start | bytes 200 | tf_op jit(solution)/shard_map/ppermute | solution.py:483
  5.8 1.2 %copy-start.4 = (bf16[512,1024]{1,0:T(8,128)(2,1)S(1)}, bf16[512,1024]{1,0:T(8,128)(2,1)}, u32[]{:S(2)}) copy-start(bf16[512,1024]{1,0:T(8,128)(2,1)} %actor_embed.1) | copy-start | bytes 3145732
  5.8 1.3 %copy-start.6 = (bf16[1024,128]{1,0:T(8,128)(2,1)S(1)}, bf16[1024,128]{1,0:T(8,128)(2,1)}, u32[]{:S(2)}) copy-start(bf16[1024,128]{1,0:T(8,128)(2,1)} %actor_policy.1) | copy-start | bytes 786436
  5.8 1.3 %copy-start.7 = (bf16[16,16,512]{2,1,0:T(8,128)(2,1)S(1)}, bf16[16,16,512]{2,1,0:T(8,128)(2,1)}, u32[]{:S(2)}) copy-start(bf16[16,16,512]{2,1,0:T(8,128)(2,1)} %param.14) | copy-start | bytes 786436
  5.8 1.3 %copy-start.9 = (s32[16,16]{1,0:T(8,128)S(1)}, s32[16,16]{1,0:T(8,128)}, u32[]{:S(2)}) copy-start(s32[16,16]{1,0:T(8,128)} %actions.1) | copy-start | bytes 3076
  5.8 1.3 %copy-start.10 = (f32[16,16]{1,0:T(8,128)S(1)}, f32[16,16]{1,0:T(8,128)}, u32[]{:S(2)}) copy-start(f32[16,16]{1,0:T(8,128)} %rewards.1) | copy-start | bytes 3076
  5.8 1.3 %copy-start.12 = (s32[16]{0:T(128)S(1)}, s32[16]{0:T(128)}, u32[]{:S(2)}) copy-start(s32[16]{0:T(128)} %param.15) | copy-start | bytes 196
  5.9 1.3 %copy-start.13 = (s32[16]{0:T(128)S(1)}, s32[16]{0:T(128)}, u32[]{:S(2)}) copy-start(s32[16]{0:T(128)} %param.18) | copy-start | bytes 196
  7.9 6.3 %collective-permute-start.4 = (f32[8,256]{1,0:T(8,128)S(1)}, f32[8,256]{1,0:T(8,128)S(1)}, u32[]{:S(2)}, u32[]{:S(2)}) collective-permute-start(f32[8,256]{1,0:T(8,128)S(1)} %side.1), channel_id=1, source_target_pairs={{0,2},{2,0},{4,6},{6,4},{8,10},{10,8},{12,14},{14,12},{1,3},{3,1},... | collective-permute-start | bytes 24584 | tf_op jit(solution)/shard_map/side_y/ppermute | solution.py:430
  8.5 13.9 %collective-permute-start.10 = (bf16[256,512]{1,0:T(8,128)(2,1)S(1)}, bf16[256,512]{1,0:T(8,128)(2,1)S(1)}, u32[]{:S(2)}, u32[]{:S(2)}) collective-permute-start(bf16[256,512]{1,0:T(8,128)(2,1)S(1)} %bitcast.14), channel_id=1, source_target_pairs={{0,12},{2,14},{4,0},{6,2},{8,4},{10,6},{12,8},{14,10},{1,13},{3,15... | collective-permute-start | bytes 786440 | tf_op jit(solution)/shard_map/three/ppermute | solution.py:434
  14.2 12.6 %collective-permute-start.9 = (bf16[256,512]{1,0:T(8,128)(2,1)S(1)}, bf16[256,512]{1,0:T(8,128)(2,1)S(1)}, u32[]{:S(2)}, u32[]{:S(2)}) collective-permute-start(bf16[256,512]{1,0:T(8,128)(2,1)S(1)} %collective-permute-done.refs_2_), channel_id=1, source_target_pairs={{0,2},{2,0},{4,6},{6,4},{8,10},{10,8},{12,14},{14,12},{1,3},{3,1},... | collective-permute-start | bytes 786440 | tf_op jit(solution)/shard_map/one_y/ppermute | solution.py:430
  14.3 9.8 %collective-permute-start.8 = (f32[16,256]{1,0:T(8,128)S(1)}, f32[16,256]{1,0:T(8,128)S(1)}, u32[]{:S(2)}, u32[]{:S(2)}) collective-permute-start(f32[16,256]{1,0:T(8,128)S(1)} %pad_maximum_fusion.refs_3_), channel_id=1, source_target_pairs={{0,12},{2,14},{4,8},{6,10},{8,4},{10,6},{12,0},{14,2},{1,13},{3,15... | collective-permute-start | bytes 49160 | tf_op jit(solution)/shard_map/side_z/ppermute | solution.py:430
  20.5 6.3 %collective-permute-start.7 = (f32[16,256]{1,0:T(8,128)S(1)}, f32[16,256]{1,0:T(8,128)S(1)}, u32[]{:S(2)}, u32[]{:S(2)}) collective-permute-start(f32[16,256]{1,0:T(8,128)S(1)} %pad_maximum_fusion.refs_3_), channel_id=1, source_target_pairs={{0,8},{2,10},{4,12},{6,14},{8,0},{10,2},{12,4},{14,6},{1,9},{3,11}... | collective-permute-start | bytes 49160 | tf_op jit(solution)/shard_map/side_z/ppermute | solution.py:430
  20.5 6.3 %collective-permute-start.6 = (f32[16,256]{1,0:T(8,128)S(1)}, f32[16,256]{1,0:T(8,128)S(1)}, u32[]{:S(2)}, u32[]{:S(2)}) collective-permute-start(f32[16,256]{1,0:T(8,128)S(1)} %pad_maximum_fusion.refs_3_), channel_id=1, source_target_pairs={{0,4},{2,6},{4,0},{6,2},{8,12},{10,14},{12,8},{14,10},{1,5},{3,7},... | collective-permute-start | bytes 49160 | tf_op jit(solution)/shard_map/side_z/ppermute | solution.py:430
  22.4 9.9 %collective-permute-start.1 = (bf16[256,512]{1,0:T(8,128)(2,1)S(1)}, bf16[256,512]{1,0:T(8,128)(2,1)S(1)}, u32[]{:S(2)}, u32[]{:S(2)}) collective-permute-start(bf16[256,512]{1,0:T(8,128)(2,1)S(1)} %collective-permute-done.refs_2_), channel_id=1, source_target_pairs={{0,4},{2,6},{4,8},{6,10},{8,12},{10,14},{12,0},{14,2},{1,5},{3,7},... | collective-permute-start | bytes 786440 | tf_op jit(solution)/shard_map/two/ppermute | solution.py:434
  24.0 9.0 %collective-permute-start.12 = (bf16[256,512]{1,0:T(8,128)(2,1)S(1)}, bf16[256,512]{1,0:T(8,128)(2,1)S(1)}, u32[]{:S(2)}, u32[]{:S(2)}) collective-permute-start(bf16[256,512]{1,0:T(8,128)(2,1)S(1)} %collective-permute-done.10.refs_1_), channel_id=1, source_target_pairs={{0,2},{2,0},{4,6},{6,4},{8,10},{10,8},{12,14},{14,12},{1,3},{3,1},... | collective-permute-start | bytes 786440 | tf_op jit(solution)/shard_map/three_y/ppermute | solution.py:430
  32.3 6.4 %collective-permute-start.11 = (bf16[256,512]{1,0:T(8,128)(2,1)S(1)}, bf16[256,512]{1,0:T(8,128)(2,1)S(1)}, u32[]{:S(2)}, u32[]{:S(2)}) collective-permute-start(bf16[256,512]{1,0:T(8,128)(2,1)S(1)} %collective-permute-done.1.refs_1_), channel_id=1, source_target_pairs={{0,2},{2,0},{4,6},{6,4},{8,10},{10,8},{12,14},{14,12},{1,3},{3,1},... | collective-permute-start | bytes 786440 | tf_op jit(solution)/shard_map/two_y/ppermute | solution.py:430
  38.7 5.3 %copy-start.3 = (f32[512,1024]{1,0:T(8,128)S(1)}, f32[512,1024]{1,0:T(8,128)}, u32[]{:S(2)}) copy-start(f32[512,1024]{1,0:T(8,128)} %embed_moment.1) | copy-start | bytes 6291460
  38.7 5.3 %copy-start.5 = (f32[1024,128]{1,0:T(8,128)S(1)}, f32[1024,128]{1,0:T(8,128)}, u32[]{:S(2)}) copy-start(f32[1024,128]{1,0:T(8,128)} %policy_moment.1) | copy-start | bytes 1572868
  38.7 5.3 %copy-start.8 = (bf16[256,512]{1,0:T(8,128)(2,1)S(1)}, bf16[256,512]{1,0:T(8,128)(2,1)}, u32[]{:S(2)}) copy-start(bf16[256,512]{1,0:T(8,128)(2,1)} %next_obs.1) | copy-start | bytes 786436
  38.7 5.3 %copy-start.11 = (f32[1024]{0:T(1024)S(1)}, f32[1024]{0:T(1024)}, u32[]{:S(2)}) copy-start(f32[1024]{0:T(1024)} %param.26) | copy-start | bytes 12292
  40.8 3.1 %collective-permute-start.13 = (bf16[656,1024]{1,0:T(8,128)(2,1)S(1)}, bf16[656,1024]{1,0:T(8,128)(2,1)S(1)}, u32[]{:S(2)}, u32[]{:S(2)}) collective-permute-start(bf16[656,1024]{1,0:T(8,128)(2,1)S(1)} %fourth.1.mine), channel_id=1, source_target_pairs={{0,1},{1,0},{2,3},{3,2},{4,5},{5,4},{6,7},{7,6},{8,9},{9,8},{10,11... | collective-permute-start | bytes 4030472 | tf_op jit(solution)/shard_map/ppermute | solution.py:493

commit v9 on v6

--- a/solution.py
+++ b/solution.py
@@ -237,10 +237,8 @@
     backward(slots, logits, side, weights, head, frames_t, hidden_t, preact_t, add)
 
 
-def side_of(sides, back, flip):
-    line = lax.div(lax.axis_index("hst"), 2)
-    there = lax.bitwise_xor(line, lax.bitwise_and(line + 4 - back, 3))
-    return sides[pl.ds(pl.multiple_of(8 * (4 * flip + there), 8), 8), :]
+def side_of(sides, mask):
+    return sides[8 * mask : 8 * mask + 8, :]
 
 
 def ahead_kernel(*refs):
@@ -261,14 +259,14 @@
         in_specs=[VMEM] * (len(frames) + 2),
         out_specs=(VMEM,) * 3,
         compiler_params=params(20),
-        cost_estimate=cost(0.1),
+        cost_estimate=cost(1.6),
         name="ahead",
     )(*frames, embed_t, head_t)
 
 
 def first_kernel(slots, *refs):
-    (frames_t, hidden_t, logits, *pieces), mats, (sum_0, sum_1, weights, sides), scratch = (
-        refs[0:5], refs[5:8], refs[8:12], refs[12:15])
+    (frames_t, hidden_t, logits, *pieces), mats, (sum_01, sum_2, weights, sides), scratch = (
+        refs[0:7], refs[7:10], refs[10:14], refs[14:17])
     start = 0
     for piece in pieces:
         sides[start : start + piece.shape[0], :] = piece[...]
@@ -277,54 +275,54 @@
 
     def add(index, rows, value):
         if index == 0:
-            sum_0[rows, :] = value
+            sum_01[rows, :] = value
         elif index == 1:
-            sum_0[rows, :] += value
+            sum_01[rows, :] += value
         else:
-            sum_1[rows, :] = value
-
-    side = jnp.concatenate([side_of(sides, *at) for at in ((0, 0), (0, 1), (1, 0))], axis=1)
+            sum_2[rows, :] = value
+
+    side = jnp.concatenate([side_of(sides, mask) for mask in (0, 1, 2)], axis=1)
     backward(slots, logits[...], side, weights, mats[1], frames_t, hidden_t, scratch[2], add)
 
 
 def second_kernel(slots, *refs):
-    frames, (sides, weights, sum_1), mats, (sum_1y, sum_2), scratch = (
-        refs[0:2], refs[2:5], refs[5:8], refs[8:10], refs[10:13])
+    frames, (sides, weights, sum_01, sum_2), mats, (sum_0123, sum_4), scratch = (
+        refs[0:2], refs[2:6], refs[6:9], refs[9:11], refs[11:14])
 
     def add(index, rows, value):
         if index == 0:
-            sum_1y[rows, :] = sum_1[rows, :] + value
+            sum_0123[rows, :] = sum_01[rows, :] + (sum_2[rows, :] + value)
         else:
-            sum_2[rows, :] = value
-
-    side = jnp.concatenate([side_of(sides, 1, 1), side_of(sides, 2, 0)], axis=1)
+            sum_4[rows, :] = value
+
+    side = jnp.concatenate([side_of(sides, 3), side_of(sides, 4)], axis=1)
     work(slots, frames, side, weights, *mats, *scratch, add)
 
 
 def third_kernel(slots, *refs):
-    frames, (sides, weights, sum_0, sum_2), mats, (even, sum_3), scratch = (
-        refs[0:2], refs[2:6], refs[6:9], refs[9:11], refs[11:14])
+    frames, (sides, weights, sum_4), mats, (sum_45, sum_6), scratch = (
+        refs[0:2], refs[2:5], refs[5:8], refs[8:10], refs[10:13])
 
     def add(index, rows, value):
         if index == 0:
-            even[rows, :] = sum_0[rows, :] + (sum_2[rows, :] + value)
+            sum_45[rows, :] = sum_4[rows, :] + value
         else:
-            sum_3[rows, :] = value
-
-    side = jnp.concatenate([side_of(sides, 2, 1), side_of(sides, 3, 0)], axis=1)
+            sum_6[rows, :] = value
+
+    side = jnp.concatenate([side_of(sides, 5), side_of(sides, 6)], axis=1)
     work(slots, frames, side, weights, *mats, *scratch, add)
 
 
 def fourth_kernel(slots, *refs):
-    frames, (sides, weights, even, sum_1y, sum_3), mats, out, scratch = (
+    frames, (sides, weights, sum_0123, sum_45, sum_6), mats, out, scratch = (
         refs[0:1], refs[1:6], refs[6:9], refs[9], refs[10:13])
 
     def add(index, rows, value):
         out[rows, :] = (
-            even[rows, :] + (sum_1y[rows, :] + (sum_3[rows, :] + value))
+            sum_0123[rows, :] + (sum_45[rows, :] + (sum_6[rows, :] + value))
         ).astype(BF16)
 
-    work(slots, frames, side_of(sides, 3, 1), weights, *mats, *scratch, add)
+    work(slots, frames, side_of(sides, 7), weights, *mats, *scratch, add)
 
 
 def local_kernel(slots, frames, side, weights, embed_t, head, head_t, out, *scratch):
@@ -396,43 +394,39 @@
 
 
 def gathered_grads(slots, own, side, mats):
-    def exchange(array, mask):
-        return lax.ppermute(array, "hst", [(at, at ^ mask) for at in range(8)])
-
-    def shift(array, by):
-        return lax.ppermute(array, "hst", [(at, (at + 2 * by) % 8) for at in range(8)])
-
-    one = shift(own, 1)
-    own_y = exchange(own, 1)
-    pieces = [side] + [exchange(side, 2 * mask) for mask in (1, 2, 3)]
-    line = jnp.concatenate(pieces, axis=0)
-    line, one, again = lax.optimization_barrier((line, one, own))
-    line_y = exchange(line, 1)
-    three = shift(again, -1)
-    one_y = exchange(one, 1)
-    two = shift(one, 1)
-    three_y = exchange(three, 1)
-    two_y = exchange(two, 1)
-
+    def exchange(array, mask, name):
+        with jax.named_scope(name):
+            return lax.ppermute(array, "hst", [(at, at ^ mask) for at in range(8)])
+
+    b2 = exchange(own, 2, "b2")
+    b1 = exchange(own, 1, "b1")
+    pair = jnp.concatenate([side, exchange(side, 1, "side_y")], axis=0)
+    pair, _, _ = lax.optimization_barrier((pair, b2, b1))
+    pieces = [pair] + [exchange(pair, 2 * mask, "side_z") for mask in (1, 2, 3)]
+    b4 = exchange(own, 4, "b4")
+    b3 = exchange(b2, 1, "b3")
+    b5 = exchange(b4, 1, "b5")
+    b6 = exchange(b4, 2, "b6")
+    pieces, b3 = lax.optimization_barrier((pieces, b3))
     width, feats = mats[0].shape
     grads = jax.ShapeDtypeStruct((feats + mats[2].shape[0], width), F32)
     weights = jax.ShapeDtypeStruct((16, 128), F32)
     sides = jax.ShapeDtypeStruct((64, side.shape[1]), F32)
-    done = ahead((own, own_y, one), mats[0], mats[2])
-    sum_0, sum_1, weights, sides = call(
-        first_kernel, "first", slots, 3, (*done, line, line_y), mats,
-        (grads, grads, weights, sides),
-    )
-    sum_1y, sum_2 = call(
-        second_kernel, "second", slots, 2, (one_y, two, sides, weights, sum_1), mats,
+    done = ahead((own, b1, b2), mats[0], mats[2])
+    sum_01, sum_2, weights, sides = call(
+        first_kernel, "first", slots, 3, (*done, *pieces), mats, (grads, grads, weights, sides),
+    )
+    sum_0123, sum_4 = call(
+        second_kernel, "second", slots, 2, (b3, b4, sides, weights, sum_01, sum_2), mats,
         (grads, grads),
     )
-    even, sum_3 = call(
-        third_kernel, "third", slots, 2, (two_y, three, sides, weights, sum_0, sum_2), mats,
-        (grads, grads),
+    b6, sum_4 = lax.optimization_barrier((b6, sum_4))
+    b7 = exchange(b6, 1, "b7")
+    sum_45, sum_6 = call(
+        third_kernel, "third", slots, 2, (b5, b6, sides, weights, sum_4), mats, (grads, grads),
     )
     return call(
-        fourth_kernel, "fourth", slots, 1, (three_y, sides, weights, even, sum_1y, sum_3), mats,
+        fourth_kernel, "fourth", slots, 1, (b7, sides, weights, sum_0123, sum_45, sum_6), mats,
         jax.ShapeDtypeStruct(grads.shape, BF16),
     )
 

time: 48.6 us -> 47 us (0.967)
  starting transfers between devices: 17.5 us -> 15.6 us
    ppermute x3 -> x0, starting transfers between devices: 6.91 us -> none  [shift(): lax.ppermute(array, 'hst', [(at, (at + 2 * by) % 8) for at in range(8)])]
    ppermute x8 -> x11, starting transfers between devices: 10 us -> 15.1 us  [exchange(): return lax.ppermute(array, 'hst', [(at, at ^ mask) for at in range(8)])]
    ppermute x8 -> x11, waiting for transfers between devices: 7.32 us -> 9.94 us  [exchange(): return lax.ppermute(array, 'hst', [(at, at ^ mask) for at in range(8)])]
    ppermute x3 -> x0, waiting for transfers between devices: 2.43 us -> none  [shift(): lax.ppermute(array, 'hst', [(at, (at + 2 * by) % 8) for at in range(8)])]
  transfers between devices with their start and end apart: 14 -> 14, of which waited for: 10 -> 6; matrix products, arithmetic and copies ran while one was open for 0% -> 0% of each run, Pallas kernels for 23% -> 24%
where the time goes in v9:
time: 47 us; the launch traced here: 46.8 us
  Pallas kernels  16.5 us (35%)
  starting transfers between devices  15.6 us (33%)
  waiting for transfers between devices  13.3 us (28%)
  between operations  0.84 us (2%)
    ppermute x11, starting transfers between devices, exchange(): return lax.ppermute(array, 'hst', [(at, at ^ mask) for at in range(8)])  15.1 us
    pallas_call x4, Pallas kernels, call(): pl.pallas_call(functools.partial(kernel, slots), out_shape=outs, in_specs...  10.6 us
    ppermute x11, waiting for transfers between devices, exchange(): return lax.ppermute(array, 'hst', [(at, at ^ mask) for at in range(8)])  9.94 us
    pallas_call x1, Pallas kernels, update(): pl.pallas_call(functools.partial(update_kernel, feats, nact), out_shape=(...  3.4 us
    ppermute x1, waiting for transfers between devices, body(): theirs = lax.ppermute(mine, 'cores', flip)  3.07 us
    pallas_call x1, Pallas kernels, ahead(): pl.pallas_call(ahead_kernel, out_shape=(jax.ShapeDtypeStruct((feats, rows...  1.31 us
  transfers between devices with their start and end apart: 14, of which 6 were waited for; matrix products, arithmetic and copies ran while one was open for 0% of the time, Pallas kernels for 24%

profile of v9, /device:TPU:0, one launch (start us, length us, event | category | flops | bytes accessed | tf_op | source)
XLA Modules:
  0.0 46.8 jit_solution(6321318174390104296)
XLA Ops:
  0.7 3.1 %collective-permute-start.5 = (bf16[256,512]{1,0:T(8,128)(2,1)}, bf16[256,512]{1,0:T(8,128)(2,1)S(1)}, u32[]{:S(2)}, u32[]{:S(2)}) collective-permute-start(bf16[256,512]{1,0:T(8,128)(2,1)} %bitcast.11), channel_id=1, source_target_pairs={{0,4},{2,6},{4,0},{6,2},{8,12},{10,14},{12,8},{14,10},{1,5},{3,7},... | collective-permute-start | bytes 786440 | tf_op jit(solution)/shard_map/b2/ppermute | solution.py:399
  3.8 1.5 %collective-permute-start.6 = (bf16[256,512]{1,0:T(8,128)(2,1)}, bf16[256,512]{1,0:T(8,128)(2,1)S(1)}, u32[]{:S(2)}, u32[]{:S(2)}) collective-permute-start(bf16[256,512]{1,0:T(8,128)(2,1)} %bitcast.12), channel_id=1, source_target_pairs={{0,2},{2,0},{4,6},{6,4},{8,10},{10,8},{12,14},{14,12},{1,3},{3,1},... | collective-permute-start | bytes 786440 | tf_op jit(solution)/shard_map/b1/ppermute | solution.py:399
  5.3 2.6 %collective-permute-start = (bf16[256,512]{1,0:T(8,128)(2,1)}, bf16[256,512]{1,0:T(8,128)(2,1)S(1)}, u32[]{:S(2)}, u32[]{:S(2)}) collective-permute-start(bf16[256,512]{1,0:T(8,128)(2,1)} %bitcast.13), channel_id=1, source_target_pairs={{0,8},{2,10},{4,12},{6,14},{8,0},{10,2},{12,4},{14,6},{1,9},{3,11}... | collective-permute-start | bytes 786440 | tf_op jit(solution)/shard_map/b4/ppermute | solution.py:399
  7.9 0.5 %collective-permute-start.3 = (s32[16]{0:T(128)}, s32[16]{0:T(128)S(1)}, u32[]{:S(2)}, u32[]{:S(2)}) collective-permute-start(s32[16]{0:T(128)} %param.18), channel_id=1, source_target_pairs={{0,1},{1,0},{2,3},{3,2},{4,5},{5,4},{6,7},{7,6},{8,9},{9,8},{10,11... | collective-permute-start | bytes 200 | tf_op jit(solution)/shard_map/ppermute | solution.py:445
  8.4 0.0 copy-start.6
  8.4 0.0 copy-start.7
  8.4 0.0 copy-start.12
  8.5 0.5 %convert.1 = (bf16[1024,512]{1,0:T(8,128)(2,1)S(1)}, bf16[1024,144]{1,0:T(8,128)(2,1)S(1)}, bf16[144,1024]{1,0:T(8,128)(2,1)S(1)}) custom-call(f32[512,1024]{1,0:T(8,128)S(1)} %copy-done, f32[1024,128]{1,0:T(8,128)S(1)} %copy-done.1, f32[1,1024]{1,0:T(1,128)S(1)} %bitcast.9), custom_call_target="tpu_custom_call" | custom-call | flops 660000000 | tf_op jit(solution)/shard_map/convert/pallas_call | solution.py:131
  9.0 0.1 collective-permute-done.2
  9.1 0.2 collective-permute-done.3
  9.3 0.3 copy-done.4
  9.6 0.0 copy-done.6
  9.6 0.1 copy-done.7
  9.7 0.8 %side.1 = f32[8,256]{1,0:T(8,128)S(1)} custom-call(s32[1,16]{1,0:T(1,128)S(1)} %bitcast.17, s32[1,16]{1,0:T(1,128)S(1)} %bitcast.18, s32[1,16]{1,0:T(1,128)S(1)} %bitcast.19, s32[1,16]{1,0:T(1,128)S(1)} %bitcast.20, s32[16,16]{1,0:T(8,128)S(1)} %copy-done.9, f32[16,16]{1,0:T(8,128)S(1)} %copy-done.10, bf16[512,1024]{1,0:T(8,128)(2,1)S(1)} %copy-done.4, ...), custom_call_target="tpu_custom_call" | custom-call | flops 1430000000 | tf_op jit(solution)/shard_map/side/pallas_call | solution.py:101
  10.5 0.6 %collective-permute-start.4 = (f32[8,256]{1,0:T(8,128)S(1)}, f32[8,256]{1,0:T(8,128)S(1)}, u32[]{:S(2)}, u32[]{:S(2)}) collective-permute-start(f32[8,256]{1,0:T(8,128)S(1)} %side.1), channel_id=1, source_target_pairs={{0,2},{2,0},{4,6},{6,4},{8,10},{10,8},{12,14},{14,12},{1,3},{3,1},... | collective-permute-start | bytes 24584 | tf_op jit(solution)/shard_map/side_y/ppermute | solution.py:399
  11.1 3.5 %collective-permute-done.5.refs_2_ = bf16[256,512]{1,0:T(8,128)(2,1)S(1)} collective-permute-done((bf16[256,512]{1,0:T(8,128)(2,1)}, bf16[256,512]{1,0:T(8,128)(2,1)S(1)}, u32[]{:S(2)}, u32[]{:S(2)}) %collective-permute-start.5) | collective-permute-done | bytes 262176 | tf_op jit(solution)/shard_map/b2/ppermute | solution.py:399
  14.5 2.7 %collective-permute-start.10 = (bf16[256,512]{1,0:T(8,128)(2,1)S(1)}, bf16[256,512]{1,0:T(8,128)(2,1)S(1)}, u32[]{:S(2)}, u32[]{:S(2)}) collective-permute-start(bf16[256,512]{1,0:T(8,128)(2,1)S(1)} %collective-permute-done.5.refs_2_), channel_id=1, source_target_pairs={{0,2},{2,0},{4,6},{6,4},{8,10},{10,8},{12,14},{14,12},{1,3},{3,1},... | collective-permute-start | bytes 786440 | tf_op jit(solution)/shard_map/b3/ppermute | solution.py:399
  17.2 0.1 collective-permute-start.7
  17.3 3.0 %collective-permute-start.8 = (f32[16,256]{1,0:T(8,128)S(1)}, f32[16,256]{1,0:T(8,128)S(1)}, u32[]{:S(2)}, u32[]{:S(2)}) collective-permute-start(f32[16,256]{1,0:T(8,128)S(1)} %pad_maximum_fusion.refs_3_), channel_id=1, source_target_pairs={{0,8},{2,10},{4,12},{6,14},{8,0},{10,2},{12,4},{14,6},{1,9},{3,11}... | collective-permute-start | bytes 49160 | tf_op jit(solution)/shard_map/side_z/ppermute | solution.py:399
  20.3 1.3 %collective-permute-start.9 = (f32[16,256]{1,0:T(8,128)S(1)}, f32[16,256]{1,0:T(8,128)S(1)}, u32[]{:S(2)}, u32[]{:S(2)}) collective-permute-start(f32[16,256]{1,0:T(8,128)S(1)} %pad_maximum_fusion.refs_3_), channel_id=1, source_target_pairs={{0,12},{2,14},{4,8},{6,10},{8,4},{10,6},{12,0},{14,2},{1,13},{3,15... | collective-permute-start | bytes 49160 | tf_op jit(solution)/shard_map/side_z/ppermute | solution.py:399
  21.7 1.3 %ahead.1 = (bf16[512,768]{1,0:T(8,128)(2,1)S(1)}, bf16[1024,768]{1,0:T(8,128)(2,1)S(1)}, f32[144,768]{1,0:T(8,128)S(1)}) custom-call(bf16[256,512]{1,0:T(8,128)(2,1)S(1)} %bitcast.15, bf16[256,512]{1,0:T(8,128)(2,1)S(1)} %collective-permute-done.6.refs_1_, bf16[256,512]{1,0:T(8,128)(2,1)S(1)} %collective-permute-done.5.refs_2_, ...), custom_call_target="tpu_custom_call" | custom-call | flops 1760000000 | tf_op jit(solution)/shard_map/ahead/pallas_call | solution.py:252
  23.0 0.1 collective-permute-start.12
  23.1 3.0 %collective-permute-done.9.refs_6_ = f32[16,256]{1,0:T(8,128)S(1)} collective-permute-done((f32[16,256]{1,0:T(8,128)S(1)}, f32[16,256]{1,0:T(8,128)S(1)}, u32[]{:S(2)}, u32[]{:S(2)}) %collective-permute-start.9) | collective-permute-done | bytes 16416 | tf_op jit(solution)/shard_map/side_z/ppermute | solution.py:399
  26.1 2.6 %first.1 = (f32[656,1024]{1,0:T(8,128)S(1)}, f32[656,1024]{1,0:T(8,128)S(1)}, f32[16,128]{1,0:T(8,128)S(1)}, f32[64,256]{1,0:T(8,128)S(1)}) custom-call(bf16[512,768]{1,0:T(8,128)(2,1)S(1)} %get-tuple-element.52.refs_0_, bf16[1024,768]{1,0:T(8,128)(2,1)S(1)} %get-tuple-element.53.refs_1_, f32[144,768]{1,0:T(8,128)S(1)} %get-tuple-element.54.refs_2_, ...), custom_call_target="tpu_custom_call" | custom-call | flops 4400000000 | tf_op jit(solution)/shard_map/first/pallas_call | solution.py:342
  28.7 3.0 %second.1 = (f32[656,1024]{1,0:T(8,128)S(1)}, f32[656,1024]{1,0:T(8,128)S(1)}) custom-call(bf16[256,512]{1,0:T(8,128)(2,1)S(1)} %collective-permute-done.10.refs_0_, bf16[256,512]{1,0:T(8,128)(2,1)S(1)} %collective-permute-done.refs_1_, f32[64,256]{1,0:T(8,128)S(1)} %get-tuple-element.60.refs_2_.refs_1_, f32[16,128]{1,0:T(8,128)S(1)} %get-tuple-element.61.refs_3_.refs_2_, ...), custom_call_target="tpu_custom_call" | custom-call | flops 3080000000 | tf_op jit(solution)/shard_map/second/pallas_call | solution.py:342
  31.7 0.1 collective-permute-start.11
  31.8 2.9 %third.1 = (f32[656,1024]{1,0:T(8,128)S(1)}, f32[656,1024]{1,0:T(8,128)S(1)}) custom-call(bf16[256,512]{1,0:T(8,128)(2,1)S(1)} %collective-permute-done.12.refs_0_, bf16[256,512]{1,0:T(8,128)(2,1)S(1)} %collective-permute-done.1.refs_1_, f32[64,256]{1,0:T(8,128)S(1)} %get-tuple-element.60.refs_2_.refs_1_, f32[16,128]{1,0:T(8,128)S(1)} %get-tuple-element.61.refs_3_.refs_2_, ...), custom_call_target="tpu_custom_call" | custom-call | flops 3080000000 | tf_op jit(solution)/shard_map/third/pallas_call | solution.py:342
  34.7 3.4 %collective-permute-done.11.refs_0_ = bf16[256,512]{1,0:T(8,128)(2,1)S(1)} collective-permute-done((bf16[256,512]{1,0:T(8,128)(2,1)S(1)}, bf16[256,512]{1,0:T(8,128)(2,1)S(1)}, u32[]{:S(2)}, u32[]{:S(2)}) %collective-permute-start.11) | collective-permute-done | bytes 262176 | tf_op jit(solution)/shard_map/b7/ppermute | solution.py:399
  38.1 2.1 %fourth.1.mine = bf16[656,1024]{1,0:T(8,128)(2,1)S(1)} custom-call(bf16[256,512]{1,0:T(8,128)(2,1)S(1)} %collective-permute-done.11.refs_0_, f32[64,256]{1,0:T(8,128)S(1)} %get-tuple-element.60.refs_2_.refs_1_, f32[16,128]{1,0:T(8,128)S(1)} %get-tuple-element.61.refs_3_.refs_2_, f32[656,1024]{1,0:T(8,128)S(1)} %get-tuple-element.66.refs_3_, ...), custom_call_target="tpu_custom_call" | custom-call | flops 1760000000 | tf_op jit(solution)/shard_map/fourth/pallas_call | solution.py:342
  40.3 0.1 collective-permute-start.13
  40.3 3.1 %collective-permute-done.13.theirs = bf16[656,1024]{1,0:T(8,128)(2,1)S(1)} collective-permute-done((bf16[656,1024]{1,0:T(8,128)(2,1)S(1)}, bf16[656,1024]{1,0:T(8,128)(2,1)S(1)}, u32[]{:S(2)}, u32[]{:S(2)}) %collective-permute-start.13) | collective-permute-done | bytes 1343520 | tf_op jit(solution)/shard_map/ppermute | solution.py:455
  43.4 3.4 %update.1 = (bf16[256,128]{1,0:T(8,128)(2,1)}, f32[512,1024]{1,0:T(8,128)}, f32[1024,128]{1,0:T(8,128)}, f32[1,1024]{1,0:T(1,128)}, f32[512,1024]{1,0:T(8,128)}, /*index=5*/f32[1024,128]{1,0:T(8,128)}, f32[1,1024]{1,0:T(1,128)}) custom-call(bf16[656,1024]{1,0:T(8,128)(2,1)S(1)} %fourth.1.mine, bf16[656,1024]{1,0:T(8,128)(2,1)S(1)} %collective-permute-done.13.theirs, ...), custom_call_target="tpu_custom_call" | custom-call | flops 3740000000 | tf_op jit(solution)/shard_map/update/pallas_call | solution.py:385
  (34 shorter events, 0.1 us)
Async XLA Ops:
  0.6 7.8 %copy-start = (f32[512,1024]{1,0:T(8,128)S(1)}, f32[512,1024]{1,0:T(8,128)}, u32[]{:S(2)}) copy-start(f32[512,1024]{1,0:T(8,128)} %master_embed.3) | copy-start | bytes 6291460
  0.6 7.8 %copy-start.1 = (f32[1024,128]{1,0:T(8,128)S(1)}, f32[1024,128]{1,0:T(8,128)}, u32[]{:S(2)}) copy-start(f32[1024,128]{1,0:T(8,128)} %master_policy.3) | copy-start | bytes 1572868
  0.7 7.8 %copy-start.2 = (f32[1024]{0:T(1024)S(1)}, f32[1024]{0:T(1024)}, u32[]{:S(2)}) copy-start(f32[1024]{0:T(1024)} %param.23) | copy-start | bytes 12292
  0.7 13.9 %collective-permute-start.5 = (bf16[256,512]{1,0:T(8,128)(2,1)}, bf16[256,512]{1,0:T(8,128)(2,1)S(1)}, u32[]{:S(2)}, u32[]{:S(2)}) collective-permute-start(bf16[256,512]{1,0:T(8,128)(2,1)} %bitcast.11), channel_id=1, source_target_pairs={{0,4},{2,6},{4,0},{6,2},{8,12},{10,14},{12,8},{14,10},{1,5},{3,7},... | collective-permute-start | bytes 786440 | tf_op jit(solution)/shard_map/b2/ppermute | solution.py:399
  3.8 13.5 %collective-permute-start.6 = (bf16[256,512]{1,0:T(8,128)(2,1)}, bf16[256,512]{1,0:T(8,128)(2,1)S(1)}, u32[]{:S(2)}, u32[]{:S(2)}) collective-permute-start(bf16[256,512]{1,0:T(8,128)(2,1)} %bitcast.12), channel_id=1, source_target_pairs={{0,2},{2,0},{4,6},{6,4},{8,10},{10,8},{12,14},{14,12},{1,3},{3,1},... | collective-permute-start | bytes 786440 | tf_op jit(solution)/shard_map/b1/ppermute | solution.py:399
  5.3 16.4 %collective-permute-start = (bf16[256,512]{1,0:T(8,128)(2,1)}, bf16[256,512]{1,0:T(8,128)(2,1)S(1)}, u32[]{:S(2)}, u32[]{:S(2)}) collective-permute-start(bf16[256,512]{1,0:T(8,128)(2,1)} %bitcast.13), channel_id=1, source_target_pairs={{0,8},{2,10},{4,12},{6,14},{8,0},{10,2},{12,4},{14,6},{1,9},{3,11}... | collective-permute-start | bytes 786440 | tf_op jit(solution)/shard_map/b4/ppermute | solution.py:399
  7.9 1.3 %collective-permute-start.2 = (s32[16]{0:T(128)}, s32[16]{0:T(128)S(1)}, u32[]{:S(2)}, u32[]{:S(2)}) collective-permute-start(s32[16]{0:T(128)} %param.15), channel_id=1, source_target_pairs={{0,1},{1,0},{2,3},{3,2},{4,5},{5,4},{6,7},{7,6},{8,9},{9,8},{10,11... | collective-permute-start | bytes 200 | tf_op jit(solution)/shard_map/ppermute | solution.py:445
  7.9 1.5 %collective-permute-start.3 = (s32[16]{0:T(128)}, s32[16]{0:T(128)S(1)}, u32[]{:S(2)}, u32[]{:S(2)}) collective-permute-start(s32[16]{0:T(128)} %param.18), channel_id=1, source_target_pairs={{0,1},{1,0},{2,3},{3,2},{4,5},{5,4},{6,7},{7,6},{8,9},{9,8},{10,11... | collective-permute-start | bytes 200 | tf_op jit(solution)/shard_map/ppermute | solution.py:445
  8.4 1.2 %copy-start.4 = (bf16[512,1024]{1,0:T(8,128)(2,1)S(1)}, bf16[512,1024]{1,0:T(8,128)(2,1)}, u32[]{:S(2)}) copy-start(bf16[512,1024]{1,0:T(8,128)(2,1)} %actor_embed.1) | copy-start | bytes 3145732
  8.4 1.3 %copy-start.6 = (bf16[1024,128]{1,0:T(8,128)(2,1)S(1)}, bf16[1024,128]{1,0:T(8,128)(2,1)}, u32[]{:S(2)}) copy-start(bf16[1024,128]{1,0:T(8,128)(2,1)} %actor_policy.1) | copy-start | bytes 786436
  8.4 1.3 %copy-start.7 = (bf16[16,16,512]{2,1,0:T(8,128)(2,1)S(1)}, bf16[16,16,512]{2,1,0:T(8,128)(2,1)}, u32[]{:S(2)}) copy-start(bf16[16,16,512]{2,1,0:T(8,128)(2,1)} %param.14) | copy-start | bytes 786436
  8.4 1.3 %copy-start.9 = (s32[16,16]{1,0:T(8,128)S(1)}, s32[16,16]{1,0:T(8,128)}, u32[]{:S(2)}) copy-start(s32[16,16]{1,0:T(8,128)} %actions.1) | copy-start | bytes 3076
  8.4 1.3 %copy-start.10 = (f32[16,16]{1,0:T(8,128)S(1)}, f32[16,16]{1,0:T(8,128)}, u32[]{:S(2)}) copy-start(f32[16,16]{1,0:T(8,128)} %rewards.1) | copy-start | bytes 3076
  8.4 1.3 %copy-start.12 = (s32[16]{0:T(128)S(1)}, s32[16]{0:T(128)}, u32[]{:S(2)}) copy-start(s32[16]{0:T(128)} %param.15) | copy-start | bytes 196
  8.4 1.3 %copy-start.13 = (s32[16]{0:T(128)S(1)}, s32[16]{0:T(128)}, u32[]{:S(2)}) copy-start(s32[16]{0:T(128)} %param.18) | copy-start | bytes 196
  10.5 6.7 %collective-permute-start.4 = (f32[8,256]{1,0:T(8,128)S(1)}, f32[8,256]{1,0:T(8,128)S(1)}, u32[]{:S(2)}, u32[]{:S(2)}) collective-permute-start(f32[8,256]{1,0:T(8,128)S(1)} %side.1), channel_id=1, source_target_pairs={{0,2},{2,0},{4,6},{6,4},{8,10},{10,8},{12,14},{14,12},{1,3},{3,1},... | collective-permute-start | bytes 24584 | tf_op jit(solution)/shard_map/side_y/ppermute | solution.py:399
  14.5 11.6 %collective-permute-start.10 = (bf16[256,512]{1,0:T(8,128)(2,1)S(1)}, bf16[256,512]{1,0:T(8,128)(2,1)S(1)}, u32[]{:S(2)}, u32[]{:S(2)}) collective-permute-start(bf16[256,512]{1,0:T(8,128)(2,1)S(1)} %collective-permute-done.5.refs_2_), channel_id=1, source_target_pairs={{0,2},{2,0},{4,6},{6,4},{8,10},{10,8},{12,14},{14,12},{1,3},{3,1},... | collective-permute-start | bytes 786440 | tf_op jit(solution)/shard_map/b3/ppermute | solution.py:399
  17.2 5.8 %collective-permute-start.7 = (f32[16,256]{1,0:T(8,128)S(1)}, f32[16,256]{1,0:T(8,128)S(1)}, u32[]{:S(2)}, u32[]{:S(2)}) collective-permute-start(f32[16,256]{1,0:T(8,128)S(1)} %pad_maximum_fusion.refs_3_), channel_id=1, source_target_pairs={{0,4},{2,6},{4,0},{6,2},{8,12},{10,14},{12,8},{14,10},{1,5},{3,7},... | collective-permute-start | bytes 49160 | tf_op jit(solution)/shard_map/side_z/ppermute | solution.py:399
  17.3 5.8 %collective-permute-start.8 = (f32[16,256]{1,0:T(8,128)S(1)}, f32[16,256]{1,0:T(8,128)S(1)}, u32[]{:S(2)}, u32[]{:S(2)}) collective-permute-start(f32[16,256]{1,0:T(8,128)S(1)} %pad_maximum_fusion.refs_3_), channel_id=1, source_target_pairs={{0,8},{2,10},{4,12},{6,14},{8,0},{10,2},{12,4},{14,6},{1,9},{3,11}... | collective-permute-start | bytes 49160 | tf_op jit(solution)/shard_map/side_z/ppermute | solution.py:399
  20.3 5.8 %collective-permute-start.9 = (f32[16,256]{1,0:T(8,128)S(1)}, f32[16,256]{1,0:T(8,128)S(1)}, u32[]{:S(2)}, u32[]{:S(2)}) collective-permute-start(f32[16,256]{1,0:T(8,128)S(1)} %pad_maximum_fusion.refs_3_), channel_id=1, source_target_pairs={{0,12},{2,14},{4,8},{6,10},{8,4},{10,6},{12,0},{14,2},{1,13},{3,15... | collective-permute-start | bytes 49160 | tf_op jit(solution)/shard_map/side_z/ppermute | solution.py:399
  21.7 10.0 %collective-permute-start.1 = (bf16[256,512]{1,0:T(8,128)(2,1)S(1)}, bf16[256,512]{1,0:T(8,128)(2,1)S(1)}, u32[]{:S(2)}, u32[]{:S(2)}) collective-permute-start(bf16[256,512]{1,0:T(8,128)(2,1)S(1)} %collective-permute-done.refs_1_), channel_id=1, source_target_pairs={{0,4},{2,6},{4,0},{6,2},{8,12},{10,14},{12,8},{14,10},{1,5},{3,7},... | collective-permute-start | bytes 786440 | tf_op jit(solution)/shard_map/b6/ppermute | solution.py:399
  23.0 8.8 %collective-permute-start.12 = (bf16[256,512]{1,0:T(8,128)(2,1)S(1)}, bf16[256,512]{1,0:T(8,128)(2,1)S(1)}, u32[]{:S(2)}, u32[]{:S(2)}) collective-permute-start(bf16[256,512]{1,0:T(8,128)(2,1)S(1)} %collective-permute-done.refs_1_), channel_id=1, source_target_pairs={{0,2},{2,0},{4,6},{6,4},{8,10},{10,8},{12,14},{14,12},{1,3},{3,1},... | collective-permute-start | bytes 786440 | tf_op jit(solution)/shard_map/b5/ppermute | solution.py:399
  31.7 6.4 %collective-permute-start.11 = (bf16[256,512]{1,0:T(8,128)(2,1)S(1)}, bf16[256,512]{1,0:T(8,128)(2,1)S(1)}, u32[]{:S(2)}, u32[]{:S(2)}) collective-permute-start(bf16[256,512]{1,0:T(8,128)(2,1)S(1)} %collective-permute-done.1.refs_1_), channel_id=1, source_target_pairs={{0,2},{2,0},{4,6},{6,4},{8,10},{10,8},{12,14},{14,12},{1,3},{3,1},... | collective-permute-start | bytes 786440 | tf_op jit(solution)/shard_map/b7/ppermute | solution.py:399
  38.1 5.3 %copy-start.3 = (f32[512,1024]{1,0:T(8,128)S(1)}, f32[512,1024]{1,0:T(8,128)}, u32[]{:S(2)}) copy-start(f32[512,1024]{1,0:T(8,128)} %embed_moment.1) | copy-start | bytes 6291460
  38.1 5.3 %copy-start.5 = (f32[1024,128]{1,0:T(8,128)S(1)}, f32[1024,128]{1,0:T(8,128)}, u32[]{:S(2)}) copy-start(f32[1024,128]{1,0:T(8,128)} %policy_moment.1) | copy-start | bytes 1572868
  38.1 5.3 %copy-start.8 = (bf16[256,512]{1,0:T(8,128)(2,1)S(1)}, bf16[256,512]{1,0:T(8,128)(2,1)}, u32[]{:S(2)}) copy-start(bf16[256,512]{1,0:T(8,128)(2,1)} %next_obs.1) | copy-start | bytes 786436
  38.1 5.3 %copy-start.11 = (f32[1024]{0:T(1024)S(1)}, f32[1024]{0:T(1024)}, u32[]{:S(2)}) copy-start(f32[1024]{0:T(1024)} %param.26) | copy-start | bytes 12292
  40.3 3.1 %collective-permute-start.13 = (bf16[656,1024]{1,0:T(8,128)(2,1)S(1)}, bf16[656,1024]{1,0:T(8,128)(2,1)S(1)}, u32[]{:S(2)}, u32[]{:S(2)}) collective-permute-start(bf16[656,1024]{1,0:T(8,128)(2,1)S(1)} %fourth.1.mine), channel_id=1, source_target_pairs={{0,1},{1,0},{2,3},{3,2},{4,5},{5,4},{6,7},{7,6},{8,9},{9,8},{10,11... | collective-permute-start | bytes 4030472 | tf_op jit(solution)/shard_map/ppermute | solution.py:455

commit v10 on v9

--- a/solution.py
+++ b/solution.py
@@ -403,7 +403,8 @@
     pair = jnp.concatenate([side, exchange(side, 1, "side_y")], axis=0)
     pair, _, _ = lax.optimization_barrier((pair, b2, b1))
     pieces = [pair] + [exchange(pair, 2 * mask, "side_z") for mask in (1, 2, 3)]
-    b4 = exchange(own, 4, "b4")
+    again, _ = lax.optimization_barrier((own, side))
+    b4 = exchange(again, 4, "b4")
     b3 = exchange(b2, 1, "b3")
     b5 = exchange(b4, 1, "b5")
     b6 = exchange(b4, 2, "b6")
@@ -416,11 +417,12 @@
     sum_01, sum_2, weights, sides = call(
         first_kernel, "first", slots, 3, (*done, *pieces), mats, (grads, grads, weights, sides),
     )
+    b6, sum_2 = lax.optimization_barrier((b6, sum_2))
+    b3, _ = lax.optimization_barrier((b3, b6))
     sum_0123, sum_4 = call(
         second_kernel, "second", slots, 2, (b3, b4, sides, weights, sum_01, sum_2), mats,
         (grads, grads),
     )
-    b6, sum_4 = lax.optimization_barrier((b6, sum_4))
     b7 = exchange(b6, 1, "b7")
     sum_45, sum_6 = call(
         third_kernel, "third", slots, 2, (b5, b6, sides, weights, sum_4), mats, (grads, grads),
@@ -448,8 +450,8 @@
         spread, owner, own, *[array.reshape(1, -1) for array in (lengths, assign, *there)],
         actions, rewards, actor_embed, actor_policy,
     )
-    mats = convert(master_embed, master_policy, value_row)
-    side, mats = lax.optimization_barrier((side, mats))
+    late_row, _ = lax.optimization_barrier((value_row, side))
+    mats = convert(master_embed, master_policy, late_row)
     if gather:
         mine = gathered_grads(slots, own, side, mats)
         theirs = lax.ppermute(mine, "cores", flip)

time: 47 us -> 47.8 us (1.017)
  starting transfers between devices: 15.6 us -> 17.5 us
  waiting for transfers between devices: 13.3 us -> 12.7 us
    ppermute x11, starting transfers between devices: 15.1 us -> 16.9 us  [exchange(): return lax.ppermute(array, 'hst', [(at, at ^ mask) for at in range(8)])]
    ppermute x11, waiting for transfers between devices: 9.94 us -> 8.69 us  [exchange(): return lax.ppermute(array, 'hst', [(at, at ^ mask) for at in range(8)])]
    ppermute x2, waiting for transfers between devices: 0.34 us -> 0.95 us  [body(): there = [lax.ppermute(array, 'cores', flip) for array in (lengths, assign)]]
  transfers between devices with their start and end apart: 14 -> 14, of which waited for: 6 -> 5; matrix products, arithmetic and copies ran while one was open for 0% -> 0% of each run, Pallas kernels for 24% -> 23%
where the time goes in v10:
time: 47.8 us; the launch traced here: 47.6 us
  starting transfers between devices  17.5 us (37%)
  Pallas kernels  16.5 us (35%)
  waiting for transfers between devices  12.7 us (27%)
  between operations  0.85 us (2%)
    ppermute x11, starting transfers between devices, exchange(): return lax.ppermute(array, 'hst', [(at, at ^ mask) for at in range(8)])  16.9 us
    pallas_call x4, Pallas kernels, call(): pl.pallas_call(functools.partial(kernel, slots), out_shape=outs, in_specs...  10.5 us
    ppermute x11, waiting for transfers between devices, exchange(): return lax.ppermute(array, 'hst', [(at, at ^ mask) for at in range(8)])  8.69 us
    pallas_call x1, Pallas kernels, update(): pl.pallas_call(functools.partial(update_kernel, feats, nact), out_shape=(...  3.4 us
    ppermute x1, waiting for transfers between devices, body(): theirs = lax.ppermute(mine, 'cores', flip)  3.07 us
    pallas_call x1, Pallas kernels, ahead(): pl.pallas_call(ahead_kernel, out_shape=(jax.ShapeDtypeStruct((feats, rows...  1.3 us
  transfers between devices with their start and end apart: 14, of which 5 were waited for; matrix products, arithmetic and copies ran while one was open for 0% of the time, Pallas kernels for 23%

profile of v10, /device:TPU:0, one launch (start us, length us, event | category | flops | bytes accessed | tf_op | source)
XLA Modules:
  0.0 47.6 jit_solution(8587709321811418867)
XLA Ops:
  0.7 3.1 %collective-permute-start.5 = (bf16[256,512]{1,0:T(8,128)(2,1)}, bf16[256,512]{1,0:T(8,128)(2,1)S(1)}, u32[]{:S(2)}, u32[]{:S(2)}) collective-permute-start(bf16[256,512]{1,0:T(8,128)(2,1)} %bitcast.11), channel_id=1, source_target_pairs={{0,4},{2,6},{4,0},{6,2},{8,12},{10,14},{12,8},{14,10},{1,5},{3,7},... | collective-permute-start | bytes 786440 | tf_op jit(solution)/shard_map/b2/ppermute | solution.py:399
  3.8 1.5 %collective-permute-start.4 = (bf16[256,512]{1,0:T(8,128)(2,1)}, bf16[256,512]{1,0:T(8,128)(2,1)S(1)}, u32[]{:S(2)}, u32[]{:S(2)}) collective-permute-start(bf16[256,512]{1,0:T(8,128)(2,1)} %bitcast.12), channel_id=1, source_target_pairs={{0,2},{2,0},{4,6},{6,4},{8,10},{10,8},{12,14},{14,12},{1,3},{3,1},... | collective-permute-start | bytes 786440 | tf_op jit(solution)/shard_map/b1/ppermute | solution.py:399
  5.3 0.5 %collective-permute-start.1 = (s32[16]{0:T(128)}, s32[16]{0:T(128)S(1)}, u32[]{:S(2)}, u32[]{:S(2)}) collective-permute-start(s32[16]{0:T(128)} %param.18), channel_id=1, source_target_pairs={{0,1},{1,0},{2,3},{3,2},{4,5},{5,4},{6,7},{7,6},{8,9},{9,8},{10,11... | collective-permute-start | bytes 200 | tf_op jit(solution)/shard_map/ppermute | solution.py:447
  5.8 0.7 %collective-permute-done = s32[16]{0:T(128)S(1)} collective-permute-done((s32[16]{0:T(128)}, s32[16]{0:T(128)S(1)}, u32[]{:S(2)}, u32[]{:S(2)}) %collective-permute-start) | collective-permute-done | bytes 96 | tf_op jit(solution)/shard_map/ppermute | solution.py:447
  6.6 0.2 collective-permute-done.1
  6.8 0.0 copy-start
  6.8 0.0 copy-start.1
  6.8 0.0 copy-start.2
  6.9 0.8 %side.1 = f32[8,256]{1,0:T(8,128)S(1)} custom-call(s32[1,16]{1,0:T(1,128)S(1)} %bitcast.17, s32[1,16]{1,0:T(1,128)S(1)} %bitcast.18, s32[1,16]{1,0:T(1,128)S(1)} %bitcast.19, s32[1,16]{1,0:T(1,128)S(1)} %bitcast.20, s32[16,16]{1,0:T(8,128)S(1)} %copy-done.9, f32[16,16]{1,0:T(8,128)S(1)} %copy-done.10, bf16[512,1024]{1,0:T(8,128)(2,1)S(1)} %copy-done.4, ...), custom_call_target="tpu_custom_call" | custom-call | flops 1430000000 | tf_op jit(solution)/shard_map/side/pallas_call | solution.py:101
  7.6 0.6 %collective-permute-start.6 = (f32[8,256]{1,0:T(8,128)S(1)}, f32[8,256]{1,0:T(8,128)S(1)}, u32[]{:S(2)}, u32[]{:S(2)}) collective-permute-start(f32[8,256]{1,0:T(8,128)S(1)} %side.1), channel_id=1, source_target_pairs={{0,2},{2,0},{4,6},{6,4},{8,10},{10,8},{12,14},{14,12},{1,3},{3,1},... | collective-permute-start | bytes 24584 | tf_op jit(solution)/shard_map/side_y/ppermute | solution.py:399
  8.2 2.6 %collective-permute-start.2 = (bf16[256,512]{1,0:T(8,128)(2,1)S(1)}, bf16[256,512]{1,0:T(8,128)(2,1)S(1)}, u32[]{:S(2)}, u32[]{:S(2)}) collective-permute-start(bf16[256,512]{1,0:T(8,128)(2,1)S(1)} %bitcast.14), channel_id=1, source_target_pairs={{0,8},{2,10},{4,12},{6,14},{8,0},{10,2},{12,4},{14,6},{1,9},{3,11}... | collective-permute-start | bytes 786440 | tf_op jit(solution)/shard_map/b4/ppermute | solution.py:399
  10.8 0.5 %convert.1 = (bf16[1024,512]{1,0:T(8,128)(2,1)S(1)}, bf16[1024,144]{1,0:T(8,128)(2,1)S(1)}, bf16[144,1024]{1,0:T(8,128)(2,1)S(1)}) custom-call(f32[512,1024]{1,0:T(8,128)S(1)} %copy-done, f32[1024,128]{1,0:T(8,128)S(1)} %copy-done.1, f32[1,1024]{1,0:T(1,128)S(1)} %bitcast.9), custom_call_target="tpu_custom_call" | custom-call | flops 660000000 | tf_op jit(solution)/shard_map/convert/pallas_call | solution.py:131
  11.3 1.6 %collective-permute-start.10 = (bf16[256,512]{1,0:T(8,128)(2,1)S(1)}, bf16[256,512]{1,0:T(8,128)(2,1)S(1)}, u32[]{:S(2)}, u32[]{:S(2)}) collective-permute-start(bf16[256,512]{1,0:T(8,128)(2,1)S(1)} %collective-permute-done.5.refs_2_), channel_id=1, source_target_pairs={{0,2},{2,0},{4,6},{6,4},{8,10},{10,8},{12,14},{14,12},{1,3},{3,1},... | collective-permute-start | bytes 786440 | tf_op jit(solution)/shard_map/b3/ppermute | solution.py:399
  12.9 0.8 %collective-permute-start.7 = (f32[16,256]{1,0:T(8,128)S(1)}, f32[16,256]{1,0:T(8,128)S(1)}, u32[]{:S(2)}, u32[]{:S(2)}) collective-permute-start(f32[16,256]{1,0:T(8,128)S(1)} %pad_maximum_fusion.refs_3_), channel_id=1, source_target_pairs={{0,4},{2,6},{4,0},{6,2},{8,12},{10,14},{12,8},{14,10},{1,5},{3,7},... | collective-permute-start | bytes 49160 | tf_op jit(solution)/shard_map/side_z/ppermute | solution.py:399
  13.6 2.6 %collective-permute-start.8 = (f32[16,256]{1,0:T(8,128)S(1)}, f32[16,256]{1,0:T(8,128)S(1)}, u32[]{:S(2)}, u32[]{:S(2)}) collective-permute-start(f32[16,256]{1,0:T(8,128)S(1)} %pad_maximum_fusion.refs_3_), channel_id=1, source_target_pairs={{0,8},{2,10},{4,12},{6,14},{8,0},{10,2},{12,4},{14,6},{1,9},{3,11}... | collective-permute-start | bytes 49160 | tf_op jit(solution)/shard_map/side_z/ppermute | solution.py:399
  16.2 1.1 %collective-permute-start.9 = (f32[16,256]{1,0:T(8,128)S(1)}, f32[16,256]{1,0:T(8,128)S(1)}, u32[]{:S(2)}, u32[]{:S(2)}) collective-permute-start(f32[16,256]{1,0:T(8,128)S(1)} %pad_maximum_fusion.refs_3_), channel_id=1, source_target_pairs={{0,12},{2,14},{4,8},{6,10},{8,4},{10,6},{12,0},{14,2},{1,13},{3,15... | collective-permute-start | bytes 49160 | tf_op jit(solution)/shard_map/side_z/ppermute | solution.py:399
  17.3 1.3 %ahead.1 = (bf16[512,768]{1,0:T(8,128)(2,1)S(1)}, bf16[1024,768]{1,0:T(8,128)(2,1)S(1)}, f32[144,768]{1,0:T(8,128)S(1)}) custom-call(bf16[256,512]{1,0:T(8,128)(2,1)S(1)} %bitcast.15, bf16[256,512]{1,0:T(8,128)(2,1)S(1)} %collective-permute-done.4.refs_1_, bf16[256,512]{1,0:T(8,128)(2,1)S(1)} %collective-permute-done.5.refs_2_, ...), custom_call_target="tpu_custom_call" | custom-call | flops 1760000000 | tf_op jit(solution)/shard_map/ahead/pallas_call | solution.py:252
  18.6 5.3 %collective-permute-done.2.refs_1_ = bf16[256,512]{1,0:T(8,128)(2,1)S(1)} collective-permute-done((bf16[256,512]{1,0:T(8,128)(2,1)S(1)}, bf16[256,512]{1,0:T(8,128)(2,1)S(1)}, u32[]{:S(2)}, u32[]{:S(2)}) %collective-permute-start.2) | collective-permute-done | bytes 262176 | tf_op jit(solution)/shard_map/b4/ppermute | solution.py:399
  24.0 1.5 %collective-permute-start.12 = (bf16[256,512]{1,0:T(8,128)(2,1)S(1)}, bf16[256,512]{1,0:T(8,128)(2,1)S(1)}, u32[]{:S(2)}, u32[]{:S(2)}) collective-permute-start(bf16[256,512]{1,0:T(8,128)(2,1)S(1)} %collective-permute-done.2.refs_1_), channel_id=1, source_target_pairs={{0,2},{2,0},{4,6},{6,4},{8,10},{10,8},{12,14},{14,12},{1,3},{3,1},... | collective-permute-start | bytes 786440 | tf_op jit(solution)/shard_map/b5/ppermute | solution.py:399
  25.5 2.6 %first.1 = (f32[656,1024]{1,0:T(8,128)S(1)}, f32[656,1024]{1,0:T(8,128)S(1)}, f32[16,128]{1,0:T(8,128)S(1)}, f32[64,256]{1,0:T(8,128)S(1)}) custom-call(bf16[512,768]{1,0:T(8,128)(2,1)S(1)} %get-tuple-element.47.refs_0_, bf16[1024,768]{1,0:T(8,128)(2,1)S(1)} %get-tuple-element.48.refs_1_, f32[144,768]{1,0:T(8,128)S(1)} %get-tuple-element.49.refs_2_, ...), custom_call_target="tpu_custom_call" | custom-call | flops 4400000000 | tf_op jit(solution)/shard_map/first/pallas_call | solution.py:342
  28.1 3.4 %collective-permute-done.3.refs_1_ = bf16[256,512]{1,0:T(8,128)(2,1)S(1)} collective-permute-done((bf16[256,512]{1,0:T(8,128)(2,1)S(1)}, bf16[256,512]{1,0:T(8,128)(2,1)S(1)}, u32[]{:S(2)}, u32[]{:S(2)}) %collective-permute-start.3) | collective-permute-done | bytes 262176 | tf_op jit(solution)/shard_map/b6/ppermute | solution.py:399
  31.5 1.5 %collective-permute-start.11 = (bf16[256,512]{1,0:T(8,128)(2,1)S(1)}, bf16[256,512]{1,0:T(8,128)(2,1)S(1)}, u32[]{:S(2)}, u32[]{:S(2)}) collective-permute-start(bf16[256,512]{1,0:T(8,128)(2,1)S(1)} %collective-permute-done.3.refs_1_), channel_id=1, source_target_pairs={{0,2},{2,0},{4,6},{6,4},{8,10},{10,8},{12,14},{14,12},{1,3},{3,1},... | collective-permute-start | bytes 786440 | tf_op jit(solution)/shard_map/b7/ppermute | solution.py:399
  33.0 3.0 %second.1 = (f32[656,1024]{1,0:T(8,128)S(1)}, f32[656,1024]{1,0:T(8,128)S(1)}) custom-call(bf16[256,512]{1,0:T(8,128)(2,1)S(1)} %collective-permute-done.10.refs_0_, bf16[256,512]{1,0:T(8,128)(2,1)S(1)} %collective-permute-done.2.refs_1_, f32[64,256]{1,0:T(8,128)S(1)} %get-tuple-element.58.refs_2_.refs_1_, f32[16,128]{1,0:T(8,128)S(1)} %get-tuple-element.59.refs_3_.refs_2_, ...), custom_call_target="tpu_custom_call" | custom-call | flops 3080000000 | tf_op jit(solution)/shard_map/second/pallas_call | solution.py:342
  36.0 2.9 %third.1 = (f32[656,1024]{1,0:T(8,128)S(1)}, f32[656,1024]{1,0:T(8,128)S(1)}) custom-call(bf16[256,512]{1,0:T(8,128)(2,1)S(1)} %collective-permute-done.12.refs_0_, bf16[256,512]{1,0:T(8,128)(2,1)S(1)} %collective-permute-done.3.refs_1_, f32[64,256]{1,0:T(8,128)S(1)} %get-tuple-element.58.refs_2_.refs_1_, f32[16,128]{1,0:T(8,128)S(1)} %get-tuple-element.59.refs_3_.refs_2_, ...), custom_call_target="tpu_custom_call" | custom-call | flops 3080000000 | tf_op jit(solution)/shard_map/third/pallas_call | solution.py:342
  38.9 0.0 copy-start.3
  38.9 0.0 copy-start.5
  38.9 0.0 copy-start.8
  38.9 0.0 copy-start.11
  38.9 2.1 %fourth.1.mine = bf16[656,1024]{1,0:T(8,128)(2,1)S(1)} custom-call(bf16[256,512]{1,0:T(8,128)(2,1)S(1)} %collective-permute-done.11.refs_0_, f32[64,256]{1,0:T(8,128)S(1)} %get-tuple-element.58.refs_2_.refs_1_, f32[16,128]{1,0:T(8,128)S(1)} %get-tuple-element.59.refs_3_.refs_2_, f32[656,1024]{1,0:T(8,128)S(1)} %get-tuple-element.64.refs_3_, ...), custom_call_target="tpu_custom_call" | custom-call | flops 1760000000 | tf_op jit(solution)/shard_map/fourth/pallas_call | solution.py:342
  41.0 0.1 collective-permute-start.13
  41.1 3.1 %collective-permute-done.13.theirs = bf16[656,1024]{1,0:T(8,128)(2,1)S(1)} collective-permute-done((bf16[656,1024]{1,0:T(8,128)(2,1)S(1)}, bf16[656,1024]{1,0:T(8,128)(2,1)S(1)}, u32[]{:S(2)}, u32[]{:S(2)}) %collective-permute-start.13) | collective-permute-done | bytes 1343520 | tf_op jit(solution)/shard_map/ppermute | solution.py:457
  44.2 3.4 %update.1 = (bf16[256,128]{1,0:T(8,128)(2,1)}, f32[512,1024]{1,0:T(8,128)}, f32[1024,128]{1,0:T(8,128)}, f32[1,1024]{1,0:T(1,128)}, f32[512,1024]{1,0:T(8,128)}, /*index=5*/f32[1024,128]{1,0:T(8,128)}, f32[1,1024]{1,0:T(1,128)}) custom-call(bf16[656,1024]{1,0:T(8,128)(2,1)S(1)} %fourth.1.mine, bf16[656,1024]{1,0:T(8,128)(2,1)S(1)} %collective-permute-done.13.theirs, ...), custom_call_target="tpu_custom_call" | custom-call | flops 3740000000 | tf_op jit(solution)/shard_map/update/pallas_call | solution.py:385
  (34 shorter events, 0.1 us)
Async XLA Ops:
  0.6 6.1 %copy-start.4 = (bf16[512,1024]{1,0:T(8,128)(2,1)S(1)}, bf16[512,1024]{1,0:T(8,128)(2,1)}, u32[]{:S(2)}) copy-start(bf16[512,1024]{1,0:T(8,128)(2,1)} %actor_embed.1) | copy-start | bytes 3145732
  0.6 6.1 %copy-start.6 = (bf16[1024,128]{1,0:T(8,128)(2,1)S(1)}, bf16[1024,128]{1,0:T(8,128)(2,1)}, u32[]{:S(2)}) copy-start(bf16[1024,128]{1,0:T(8,128)(2,1)} %actor_policy.1) | copy-start | bytes 786436
  0.7 6.1 %copy-start.7 = (bf16[16,16,512]{2,1,0:T(8,128)(2,1)S(1)}, bf16[16,16,512]{2,1,0:T(8,128)(2,1)}, u32[]{:S(2)}) copy-start(bf16[16,16,512]{2,1,0:T(8,128)(2,1)} %param.14) | copy-start | bytes 786436
  0.7 6.1 %copy-start.9 = (s32[16,16]{1,0:T(8,128)S(1)}, s32[16,16]{1,0:T(8,128)}, u32[]{:S(2)}) copy-start(s32[16,16]{1,0:T(8,128)} %actions.1) | copy-start | bytes 3076
  0.7 6.1 %copy-start.10 = (f32[16,16]{1,0:T(8,128)S(1)}, f32[16,16]{1,0:T(8,128)}, u32[]{:S(2)}) copy-start(f32[16,16]{1,0:T(8,128)} %rewards.1) | copy-start | bytes 3076
  0.7 6.1 %copy-start.12 = (s32[16]{0:T(128)S(1)}, s32[16]{0:T(128)}, u32[]{:S(2)}) copy-start(s32[16]{0:T(128)} %param.15) | copy-start | bytes 196
  0.7 6.1 %copy-start.13 = (s32[16]{0:T(128)S(1)}, s32[16]{0:T(128)}, u32[]{:S(2)}) copy-start(s32[16]{0:T(128)} %param.18) | copy-start | bytes 196
  0.7 10.6 %collective-permute-start.5 = (bf16[256,512]{1,0:T(8,128)(2,1)}, bf16[256,512]{1,0:T(8,128)(2,1)S(1)}, u32[]{:S(2)}, u32[]{:S(2)}) collective-permute-start(bf16[256,512]{1,0:T(8,128)(2,1)} %bitcast.11), channel_id=1, source_target_pairs={{0,4},{2,6},{4,0},{6,2},{8,12},{10,14},{12,8},{14,10},{1,5},{3,7},... | collective-permute-start | bytes 786440 | tf_op jit(solution)/shard_map/b2/ppermute | solution.py:399
  3.8 9.1 %collective-permute-start.4 = (bf16[256,512]{1,0:T(8,128)(2,1)}, bf16[256,512]{1,0:T(8,128)(2,1)S(1)}, u32[]{:S(2)}, u32[]{:S(2)}) collective-permute-start(bf16[256,512]{1,0:T(8,128)(2,1)} %bitcast.12), channel_id=1, source_target_pairs={{0,2},{2,0},{4,6},{6,4},{8,10},{10,8},{12,14},{14,12},{1,3},{3,1},... | collective-permute-start | bytes 786440 | tf_op jit(solution)/shard_map/b1/ppermute | solution.py:399
  5.3 1.3 %collective-permute-start = (s32[16]{0:T(128)}, s32[16]{0:T(128)S(1)}, u32[]{:S(2)}, u32[]{:S(2)}) collective-permute-start(s32[16]{0:T(128)} %param.15), channel_id=1, source_target_pairs={{0,1},{1,0},{2,3},{3,2},{4,5},{5,4},{6,7},{7,6},{8,9},{9,8},{10,11... | collective-permute-start | bytes 200 | tf_op jit(solution)/shard_map/ppermute | solution.py:447
  5.3 1.5 %collective-permute-start.1 = (s32[16]{0:T(128)}, s32[16]{0:T(128)S(1)}, u32[]{:S(2)}, u32[]{:S(2)}) collective-permute-start(s32[16]{0:T(128)} %param.18), channel_id=1, source_target_pairs={{0,1},{1,0},{2,3},{3,2},{4,5},{5,4},{6,7},{7,6},{8,9},{9,8},{10,11... | collective-permute-start | bytes 200 | tf_op jit(solution)/shard_map/ppermute | solution.py:447
  6.8 4.0 %copy-start = (f32[512,1024]{1,0:T(8,128)S(1)}, f32[512,1024]{1,0:T(8,128)}, u32[]{:S(2)}) copy-start(f32[512,1024]{1,0:T(8,128)} %master_embed.3) | copy-start | bytes 6291460
  6.8 3.9 %copy-start.1 = (f32[1024,128]{1,0:T(8,128)S(1)}, f32[1024,128]{1,0:T(8,128)}, u32[]{:S(2)}) copy-start(f32[1024,128]{1,0:T(8,128)} %master_policy.3) | copy-start | bytes 1572868
  6.8 3.9 %copy-start.2 = (f32[1024]{0:T(1024)S(1)}, f32[1024]{0:T(1024)}, u32[]{:S(2)}) copy-start(f32[1024]{0:T(1024)} %param.23) | copy-start | bytes 12292
  7.6 5.3 %collective-permute-start.6 = (f32[8,256]{1,0:T(8,128)S(1)}, f32[8,256]{1,0:T(8,128)S(1)}, u32[]{:S(2)}, u32[]{:S(2)}) collective-permute-start(f32[8,256]{1,0:T(8,128)S(1)} %side.1), channel_id=1, source_target_pairs={{0,2},{2,0},{4,6},{6,4},{8,10},{10,8},{12,14},{14,12},{1,3},{3,1},... | collective-permute-start | bytes 24584 | tf_op jit(solution)/shard_map/side_y/ppermute | solution.py:399
  8.2 15.8 %collective-permute-start.2 = (bf16[256,512]{1,0:T(8,128)(2,1)S(1)}, bf16[256,512]{1,0:T(8,128)(2,1)S(1)}, u32[]{:S(2)}, u32[]{:S(2)}) collective-permute-start(bf16[256,512]{1,0:T(8,128)(2,1)S(1)} %bitcast.14), channel_id=1, source_target_pairs={{0,8},{2,10},{4,12},{6,14},{8,0},{10,2},{12,4},{14,6},{1,9},{3,11}... | collective-permute-start | bytes 786440 | tf_op jit(solution)/shard_map/b4/ppermute | solution.py:399
  11.3 14.2 %collective-permute-start.10 = (bf16[256,512]{1,0:T(8,128)(2,1)S(1)}, bf16[256,512]{1,0:T(8,128)(2,1)S(1)}, u32[]{:S(2)}, u32[]{:S(2)}) collective-permute-start(bf16[256,512]{1,0:T(8,128)(2,1)S(1)} %collective-permute-done.5.refs_2_), channel_id=1, source_target_pairs={{0,2},{2,0},{4,6},{6,4},{8,10},{10,8},{12,14},{14,12},{1,3},{3,1},... | collective-permute-start | bytes 786440 | tf_op jit(solution)/shard_map/b3/ppermute | solution.py:399
  12.9 11.1 %collective-permute-start.7 = (f32[16,256]{1,0:T(8,128)S(1)}, f32[16,256]{1,0:T(8,128)S(1)}, u32[]{:S(2)}, u32[]{:S(2)}) collective-permute-start(f32[16,256]{1,0:T(8,128)S(1)} %pad_maximum_fusion.refs_3_), channel_id=1, source_target_pairs={{0,4},{2,6},{4,0},{6,2},{8,12},{10,14},{12,8},{14,10},{1,5},{3,7},... | collective-permute-start | bytes 49160 | tf_op jit(solution)/shard_map/side_z/ppermute | solution.py:399
  13.6 11.9 %collective-permute-start.8 = (f32[16,256]{1,0:T(8,128)S(1)}, f32[16,256]{1,0:T(8,128)S(1)}, u32[]{:S(2)}, u32[]{:S(2)}) collective-permute-start(f32[16,256]{1,0:T(8,128)S(1)} %pad_maximum_fusion.refs_3_), channel_id=1, source_target_pairs={{0,8},{2,10},{4,12},{6,14},{8,0},{10,2},{12,4},{14,6},{1,9},{3,11}... | collective-permute-start | bytes 49160 | tf_op jit(solution)/shard_map/side_z/ppermute | solution.py:399
  16.2 9.3 %collective-permute-start.9 = (f32[16,256]{1,0:T(8,128)S(1)}, f32[16,256]{1,0:T(8,128)S(1)}, u32[]{:S(2)}, u32[]{:S(2)}) collective-permute-start(f32[16,256]{1,0:T(8,128)S(1)} %pad_maximum_fusion.refs_3_), channel_id=1, source_target_pairs={{0,12},{2,14},{4,8},{6,10},{8,4},{10,6},{12,0},{14,2},{1,13},{3,15... | collective-permute-start | bytes 49160 | tf_op jit(solution)/shard_map/side_z/ppermute | solution.py:399
  23.9 7.5 %collective-permute-start.3 = (bf16[256,512]{1,0:T(8,128)(2,1)S(1)}, bf16[256,512]{1,0:T(8,128)(2,1)S(1)}, u32[]{:S(2)}, u32[]{:S(2)}) collective-permute-start(bf16[256,512]{1,0:T(8,128)(2,1)S(1)} %collective-permute-done.2.refs_1_), channel_id=1, source_target_pairs={{0,4},{2,6},{4,0},{6,2},{8,12},{10,14},{12,8},{14,10},{1,5},{3,7},... | collective-permute-start | bytes 786440 | tf_op jit(solution)/shard_map/b6/ppermute | solution.py:399
  24.0 12.0 %collective-permute-start.12 = (bf16[256,512]{1,0:T(8,128)(2,1)S(1)}, bf16[256,512]{1,0:T(8,128)(2,1)S(1)}, u32[]{:S(2)}, u32[]{:S(2)}) collective-permute-start(bf16[256,512]{1,0:T(8,128)(2,1)S(1)} %collective-permute-done.2.refs_1_), channel_id=1, source_target_pairs={{0,2},{2,0},{4,6},{6,4},{8,10},{10,8},{12,14},{14,12},{1,3},{3,1},... | collective-permute-start | bytes 786440 | tf_op jit(solution)/shard_map/b5/ppermute | solution.py:399
  31.5 7.4 %collective-permute-start.11 = (bf16[256,512]{1,0:T(8,128)(2,1)S(1)}, bf16[256,512]{1,0:T(8,128)(2,1)S(1)}, u32[]{:S(2)}, u32[]{:S(2)}) collective-permute-start(bf16[256,512]{1,0:T(8,128)(2,1)S(1)} %collective-permute-done.3.refs_1_), channel_id=1, source_target_pairs={{0,2},{2,0},{4,6},{6,4},{8,10},{10,8},{12,14},{14,12},{1,3},{3,1},... | collective-permute-start | bytes 786440 | tf_op jit(solution)/shard_map/b7/ppermute | solution.py:399
  38.9 5.3 %copy-start.3 = (f32[512,1024]{1,0:T(8,128)S(1)}, f32[512,1024]{1,0:T(8,128)}, u32[]{:S(2)}) copy-start(f32[512,1024]{1,0:T(8,128)} %embed_moment.1) | copy-start | bytes 6291460
  38.9 5.3 %copy-start.5 = (f32[1024,128]{1,0:T(8,128)S(1)}, f32[1024,128]{1,0:T(8,128)}, u32[]{:S(2)}) copy-start(f32[1024,128]{1,0:T(8,128)} %policy_moment.1) | copy-start | bytes 1572868
  38.9 5.3 %copy-start.8 = (bf16[256,512]{1,0:T(8,128)(2,1)S(1)}, bf16[256,512]{1,0:T(8,128)(2,1)}, u32[]{:S(2)}) copy-start(bf16[256,512]{1,0:T(8,128)(2,1)} %next_obs.1) | copy-start | bytes 786436
  38.9 5.3 %copy-start.11 = (f32[1024]{0:T(1024)S(1)}, f32[1024]{0:T(1024)}, u32[]{:S(2)}) copy-start(f32[1024]{0:T(1024)} %param.26) | copy-start | bytes 12292
  41.0 3.1 %collective-permute-start.13 = (bf16[656,1024]{1,0:T(8,128)(2,1)S(1)}, bf16[656,1024]{1,0:T(8,128)(2,1)S(1)}, u32[]{:S(2)}, u32[]{:S(2)}) collective-permute-start(bf16[656,1024]{1,0:T(8,128)(2,1)S(1)} %fourth.1.mine), channel_id=1, source_target_pairs={{0,1},{1,0},{2,3},{3,2},{4,5},{5,4},{6,7},{7,6},{8,9},{9,8},{10,11... | collective-permute-start | bytes 4030472 | tf_op jit(solution)/shard_map/ppermute | solution.py:457

commit v11 on v6

--- a/solution.py
+++ b/solution.py
@@ -240,7 +240,7 @@
 def side_of(sides, back, flip):
     line = lax.div(lax.axis_index("hst"), 2)
     there = lax.bitwise_xor(line, lax.bitwise_and(line + 4 - back, 3))
-    return sides[pl.ds(pl.multiple_of(8 * (4 * flip + there), 8), 8), :]
+    return sides[pl.ds(pl.multiple_of(8 * (2 * there + flip), 8), 8), :]
 
 
 def ahead_kernel(*refs):
@@ -261,14 +261,14 @@
         in_specs=[VMEM] * (len(frames) + 2),
         out_specs=(VMEM,) * 3,
         compiler_params=params(20),
-        cost_estimate=cost(0.1),
+        cost_estimate=cost(1.6),
         name="ahead",
     )(*frames, embed_t, head_t)
 
 
 def first_kernel(slots, *refs):
     (frames_t, hidden_t, logits, *pieces), mats, (sum_0, sum_1, weights, sides), scratch = (
-        refs[0:5], refs[5:8], refs[8:12], refs[12:15])
+        refs[0:7], refs[7:10], refs[10:14], refs[14:17])
     start = 0
     for piece in pieces:
         sides[start : start + piece.shape[0], :] = piece[...]
@@ -396,37 +396,37 @@
 
 
 def gathered_grads(slots, own, side, mats):
-    def exchange(array, mask):
-        return lax.ppermute(array, "hst", [(at, at ^ mask) for at in range(8)])
-
-    def shift(array, by):
-        return lax.ppermute(array, "hst", [(at, (at + 2 * by) % 8) for at in range(8)])
-
-    one = shift(own, 1)
-    own_y = exchange(own, 1)
-    pieces = [side] + [exchange(side, 2 * mask) for mask in (1, 2, 3)]
-    line = jnp.concatenate(pieces, axis=0)
-    line, one, again = lax.optimization_barrier((line, one, own))
-    line_y = exchange(line, 1)
-    three = shift(again, -1)
-    one_y = exchange(one, 1)
-    two = shift(one, 1)
-    three_y = exchange(three, 1)
-    two_y = exchange(two, 1)
-
+    def exchange(array, mask, name):
+        with jax.named_scope(name):
+            return lax.ppermute(array, "hst", [(at, at ^ mask) for at in range(8)])
+
+    def shift(array, name):
+        with jax.named_scope(name):
+            return lax.ppermute(array, "hst", [(at, (at + 2) % 8) for at in range(8)])
+
+    one = shift(own, "one")
+    own_y = exchange(own, 1, "own_y")
+    pair = jnp.concatenate([side, exchange(side, 1, "side_y")], axis=0)
+    pair, _, _ = lax.optimization_barrier((pair, one, own_y))
+    pieces = [pair] + [exchange(pair, 2 * mask, "side_z") for mask in (1, 2, 3)]
+    two = shift(one, "two")
+    one_y = exchange(one, 1, "one_y")
     width, feats = mats[0].shape
     grads = jax.ShapeDtypeStruct((feats + mats[2].shape[0], width), F32)
     weights = jax.ShapeDtypeStruct((16, 128), F32)
     sides = jax.ShapeDtypeStruct((64, side.shape[1]), F32)
     done = ahead((own, own_y, one), mats[0], mats[2])
+    done, one_y, two = lax.optimization_barrier((done, one_y, two))
+    three = shift(two, "three")
+    two_y = exchange(two, 1, "two_y")
     sum_0, sum_1, weights, sides = call(
-        first_kernel, "first", slots, 3, (*done, line, line_y), mats,
-        (grads, grads, weights, sides),
+        first_kernel, "first", slots, 3, (*done, *pieces), mats, (grads, grads, weights, sides),
     )
     sum_1y, sum_2 = call(
         second_kernel, "second", slots, 2, (one_y, two, sides, weights, sum_1), mats,
         (grads, grads),
     )
+    three_y = exchange(three, 1, "three_y")
     even, sum_3 = call(
         third_kernel, "third", slots, 2, (two_y, three, sides, weights, sum_0, sum_2), mats,
         (grads, grads),
@@ -454,8 +454,8 @@
         spread, owner, own, *[array.reshape(1, -1) for array in (lengths, assign, *there)],
         actions, rewards, actor_embed, actor_policy,
     )
-    mats = convert(master_embed, master_policy, value_row)
-    side, mats = lax.optimization_barrier((side, mats))
+    late_row, _ = lax.optimization_barrier((value_row, side))
+    mats = convert(master_embed, master_policy, late_row)
     if gather:
         mine = gathered_grads(slots, own, side, mats)
         theirs = lax.ppermute(mine, "cores", flip)

time: 48.6 us -> 47.4 us (0.975)
  starting transfers between devices: 17.5 us -> 13.7 us
  waiting for transfers between devices: 13.2 us -> 15.8 us
    ppermute x3, waiting for transfers between devices: 2.43 us -> 9.45 us  [shift(): return lax.ppermute(array, 'hst', [(at, (at + 2) % 8) for at in range(8)])]
    ppermute x8, waiting for transfers between devices: 7.32 us -> 2.34 us  [exchange(): return lax.ppermute(array, 'hst', [(at, at ^ mask) for at in range(8)])]
    ppermute x3, starting transfers between devices: 6.91 us -> 3.08 us  [shift(): return lax.ppermute(array, 'hst', [(at, (at + 2) % 8) for at in range(8)])]
    ppermute x2, waiting for transfers between devices: 0.34 us -> 0.95 us  [body(): there = [lax.ppermute(array, 'cores', flip) for array in (lengths, assign)]]
  transfers between devices with their start and end apart: 14 -> 14, of which waited for: 10 -> 8; matrix products, arithmetic and copies ran while one was open for 0% -> 0% of each run, Pallas kernels for 23% -> 23%
where the time goes in v11:
time: 47.4 us; the launch traced here: 47.2 us
  Pallas kernels  16.5 us (35%)
  waiting for transfers between devices  15.8 us (33%)
  starting transfers between devices  13.7 us (29%)
  between operations  0.83 us (2%)
    pallas_call x4, Pallas kernels, call(): pl.pallas_call(functools.partial(kernel, slots), out_shape=outs, in_specs...  10.5 us
    ppermute x8, starting transfers between devices, exchange(): return lax.ppermute(array, 'hst', [(at, at ^ mask) for at in range(8)])  10.1 us
    ppermute x3, waiting for transfers between devices, shift(): return lax.ppermute(array, 'hst', [(at, (at + 2) % 8) for at in range(8)])  9.45 us
    pallas_call x1, Pallas kernels, update(): pl.pallas_call(functools.partial(update_kernel, feats, nact), out_shape=(...  3.42 us
    ppermute x3, starting transfers between devices, shift(): return lax.ppermute(array, 'hst', [(at, (at + 2) % 8) for at in range(8)])  3.08 us
    ppermute x1, waiting for transfers between devices, body(): theirs = lax.ppermute(mine, 'cores', flip)  3.07 us
    ppermute x8, waiting for transfers between devices, exchange(): return lax.ppermute(array, 'hst', [(at, at ^ mask) for at in range(8)])  2.34 us
    pallas_call x1, Pallas kernels, ahead(): pl.pallas_call(ahead_kernel, out_shape=(jax.ShapeDtypeStruct((feats, rows...  1.3 us
  transfers between devices with their start and end apart: 14, of which 8 were waited for; matrix products, arithmetic and copies ran while one was open for 0% of the time, Pallas kernels for 23%

profile of v11, /device:TPU:0, one launch (start us, length us, event | category | flops | bytes accessed | tf_op | source)
XLA Modules:
  0.0 47.2 jit_solution(6216140499606335474)
XLA Ops:
  0.7 3.1 %collective-permute-start.1 = (bf16[256,512]{1,0:T(8,128)(2,1)}, bf16[256,512]{1,0:T(8,128)(2,1)S(1)}, u32[]{:S(2)}, u32[]{:S(2)}) collective-permute-start(bf16[256,512]{1,0:T(8,128)(2,1)} %bitcast.11), channel_id=1, source_target_pairs={{0,4},{2,6},{4,8},{6,10},{8,12},{10,14},{12,0},{14,2},{1,5},{3,7},... | collective-permute-start | bytes 786440 | tf_op jit(solution)/shard_map/one/ppermute | solution.py:405
  3.8 1.5 %collective-permute-start = (bf16[256,512]{1,0:T(8,128)(2,1)}, bf16[256,512]{1,0:T(8,128)(2,1)S(1)}, u32[]{:S(2)}, u32[]{:S(2)}) collective-permute-start(bf16[256,512]{1,0:T(8,128)(2,1)} %bitcast.12), channel_id=1, source_target_pairs={{0,2},{2,0},{4,6},{6,4},{8,10},{10,8},{12,14},{14,12},{1,3},{3,1},... | collective-permute-start | bytes 786440 | tf_op jit(solution)/shard_map/own_y/ppermute | solution.py:401
  5.3 0.5 %collective-permute-start.3 = (s32[16]{0:T(128)}, s32[16]{0:T(128)S(1)}, u32[]{:S(2)}, u32[]{:S(2)}) collective-permute-start(s32[16]{0:T(128)} %param.18), channel_id=1, source_target_pairs={{0,1},{1,0},{2,3},{3,2},{4,5},{5,4},{6,7},{7,6},{8,9},{9,8},{10,11... | collective-permute-start | bytes 200 | tf_op jit(solution)/shard_map/ppermute | solution.py:451
  5.8 0.7 %collective-permute-done.2 = s32[16]{0:T(128)S(1)} collective-permute-done((s32[16]{0:T(128)}, s32[16]{0:T(128)S(1)}, u32[]{:S(2)}, u32[]{:S(2)}) %collective-permute-start.2) | collective-permute-done | bytes 96 | tf_op jit(solution)/shard_map/ppermute | solution.py:451
  6.6 0.2 collective-permute-done.3
  6.8 0.0 copy-start
  6.8 0.0 copy-start.1
  6.8 0.0 copy-start.2
  6.8 0.8 %side.1 = f32[8,256]{1,0:T(8,128)S(1)} custom-call(s32[1,16]{1,0:T(1,128)S(1)} %bitcast.16, s32[1,16]{1,0:T(1,128)S(1)} %bitcast.17, s32[1,16]{1,0:T(1,128)S(1)} %bitcast.18, s32[1,16]{1,0:T(1,128)S(1)} %bitcast.19, s32[16,16]{1,0:T(8,128)S(1)} %copy-done.9, f32[16,16]{1,0:T(8,128)S(1)} %copy-done.10, bf16[512,1024]{1,0:T(8,128)(2,1)S(1)} %copy-done.4, ...), custom_call_target="tpu_custom_call" | custom-call | flops 1430000000 | tf_op jit(solution)/shard_map/side/pallas_call | solution.py:101
  7.6 0.6 %collective-permute-start.8 = (f32[8,256]{1,0:T(8,128)S(1)}, f32[8,256]{1,0:T(8,128)S(1)}, u32[]{:S(2)}, u32[]{:S(2)}) collective-permute-start(f32[8,256]{1,0:T(8,128)S(1)} %side.1), channel_id=1, source_target_pairs={{0,2},{2,0},{4,6},{6,4},{8,10},{10,8},{12,14},{14,12},{1,3},{3,1},... | collective-permute-start | bytes 24584 | tf_op jit(solution)/shard_map/side_y/ppermute | solution.py:401
  8.2 0.2 copy-done
  8.4 0.1 copy-done.1
  8.5 0.5 %convert.1 = (bf16[1024,512]{1,0:T(8,128)(2,1)S(1)}, bf16[1024,144]{1,0:T(8,128)(2,1)S(1)}, bf16[144,1024]{1,0:T(8,128)(2,1)S(1)}) custom-call(f32[512,1024]{1,0:T(8,128)S(1)} %copy-done, f32[1024,128]{1,0:T(8,128)S(1)} %copy-done.1, f32[1,1024]{1,0:T(1,128)S(1)} %bitcast.9), custom_call_target="tpu_custom_call" | custom-call | flops 660000000 | tf_op jit(solution)/shard_map/convert/pallas_call | solution.py:131
  9.0 3.3 %collective-permute-done.1.refs_2_ = bf16[256,512]{1,0:T(8,128)(2,1)S(1)} collective-permute-done((bf16[256,512]{1,0:T(8,128)(2,1)}, bf16[256,512]{1,0:T(8,128)(2,1)S(1)}, u32[]{:S(2)}, u32[]{:S(2)}) %collective-permute-start.1) | collective-permute-done | bytes 262176 | tf_op jit(solution)/shard_map/one/ppermute | solution.py:405
  12.3 1.5 %collective-permute-start.4 = (bf16[256,512]{1,0:T(8,128)(2,1)S(1)}, bf16[256,512]{1,0:T(8,128)(2,1)S(1)}, u32[]{:S(2)}, u32[]{:S(2)}) collective-permute-start(bf16[256,512]{1,0:T(8,128)(2,1)S(1)} %collective-permute-done.1.refs_2_), channel_id=1, source_target_pairs={{0,2},{2,0},{4,6},{6,4},{8,10},{10,8},{12,14},{14,12},{1,3},{3,1},... | collective-permute-start | bytes 786440 | tf_op jit(solution)/shard_map/one_y/ppermute | solution.py:401
  13.9 2.4 %collective-permute-start.10 = (f32[16,256]{1,0:T(8,128)S(1)}, f32[16,256]{1,0:T(8,128)S(1)}, u32[]{:S(2)}, u32[]{:S(2)}) collective-permute-start(f32[16,256]{1,0:T(8,128)S(1)} %pad_maximum_fusion.refs_3_), channel_id=1, source_target_pairs={{0,8},{2,10},{4,12},{6,14},{8,0},{10,2},{12,4},{14,6},{1,9},{3,11}... | collective-permute-start | bytes 49160 | tf_op jit(solution)/shard_map/side_z/ppermute | solution.py:401
  16.2 1.6 %collective-permute-start.11 = (f32[16,256]{1,0:T(8,128)S(1)}, f32[16,256]{1,0:T(8,128)S(1)}, u32[]{:S(2)}, u32[]{:S(2)}) collective-permute-start(f32[16,256]{1,0:T(8,128)S(1)} %pad_maximum_fusion.refs_3_), channel_id=1, source_target_pairs={{0,12},{2,14},{4,8},{6,10},{8,4},{10,6},{12,0},{14,2},{1,13},{3,15... | collective-permute-start | bytes 49160 | tf_op jit(solution)/shard_map/side_z/ppermute | solution.py:401
  17.8 0.5 %collective-permute-start.9 = (f32[16,256]{1,0:T(8,128)S(1)}, f32[16,256]{1,0:T(8,128)S(1)}, u32[]{:S(2)}, u32[]{:S(2)}) collective-permute-start(f32[16,256]{1,0:T(8,128)S(1)} %pad_maximum_fusion.refs_3_), channel_id=1, source_target_pairs={{0,4},{2,6},{4,0},{6,2},{8,12},{10,14},{12,8},{14,10},{1,5},{3,7},... | collective-permute-start | bytes 49160 | tf_op jit(solution)/shard_map/side_z/ppermute | solution.py:401
  18.3 1.3 %ahead.1 = (bf16[512,768]{1,0:T(8,128)(2,1)S(1)}, bf16[1024,768]{1,0:T(8,128)(2,1)S(1)}, f32[144,768]{1,0:T(8,128)S(1)}) custom-call(bf16[256,512]{1,0:T(8,128)(2,1)S(1)} %bitcast.14, bf16[256,512]{1,0:T(8,128)(2,1)S(1)} %collective-permute-done.refs_1_, bf16[256,512]{1,0:T(8,128)(2,1)S(1)} %collective-permute-done.1.refs_2_, ...), custom_call_target="tpu_custom_call" | custom-call | flops 1760000000 | tf_op jit(solution)/shard_map/ahead/pallas_call | solution.py:254
  19.6 0.2 collective-permute-done.4.refs_0_
  19.8 3.4 %collective-permute-done.5.refs_1_ = bf16[256,512]{1,0:T(8,128)(2,1)S(1)} collective-permute-done((bf16[256,512]{1,0:T(8,128)(2,1)S(1)}, bf16[256,512]{1,0:T(8,128)(2,1)S(1)}, u32[]{:S(2)}, u32[]{:S(2)}) %collective-permute-start.5) | collective-permute-done | bytes 262176 | tf_op jit(solution)/shard_map/two/ppermute | solution.py:405
  23.2 0.8 %collective-permute-start.12 = (bf16[256,512]{1,0:T(8,128)(2,1)S(1)}, bf16[256,512]{1,0:T(8,128)(2,1)S(1)}, u32[]{:S(2)}, u32[]{:S(2)}) collective-permute-start(bf16[256,512]{1,0:T(8,128)(2,1)S(1)} %collective-permute-done.5.refs_1_), channel_id=1, source_target_pairs={{0,2},{2,0},{4,6},{6,4},{8,10},{10,8},{12,14},{14,12},{1,3},{3,1},... | collective-permute-start | bytes 786440 | tf_op jit(solution)/shard_map/two_y/ppermute | solution.py:401
  24.0 2.6 %first.1 = (f32[656,1024]{1,0:T(8,128)S(1)}, f32[656,1024]{1,0:T(8,128)S(1)}, f32[16,128]{1,0:T(8,128)S(1)}, f32[64,256]{1,0:T(8,128)S(1)}) custom-call(bf16[512,768]{1,0:T(8,128)(2,1)S(1)} %get-tuple-element.46.refs_0_, bf16[1024,768]{1,0:T(8,128)(2,1)S(1)} %get-tuple-element.47.refs_1_, f32[144,768]{1,0:T(8,128)S(1)} %get-tuple-element.48.refs_2_, ...), custom_call_target="tpu_custom_call" | custom-call | flops 4400000000 | tf_op jit(solution)/shard_map/first/pallas_call | solution.py:344
  26.6 2.9 %second.1 = (f32[656,1024]{1,0:T(8,128)S(1)}, f32[656,1024]{1,0:T(8,128)S(1)}) custom-call(bf16[256,512]{1,0:T(8,128)(2,1)S(1)} %collective-permute-done.4.refs_0_, bf16[256,512]{1,0:T(8,128)(2,1)S(1)} %collective-permute-done.5.refs_1_, f32[64,256]{1,0:T(8,128)S(1)} %get-tuple-element.51.refs_2_.refs_1_, f32[16,128]{1,0:T(8,128)S(1)} %get-tuple-element.52.refs_3_.refs_2_, ...), custom_call_target="tpu_custom_call" | custom-call | flops 3080000000 | tf_op jit(solution)/shard_map/second/pallas_call | solution.py:344
  29.5 2.7 %collective-permute-done.6.refs_1_ = bf16[256,512]{1,0:T(8,128)(2,1)S(1)} collective-permute-done((bf16[256,512]{1,0:T(8,128)(2,1)S(1)}, bf16[256,512]{1,0:T(8,128)(2,1)S(1)}, u32[]{:S(2)}, u32[]{:S(2)}) %collective-permute-start.6) | collective-permute-done | bytes 262176 | tf_op jit(solution)/shard_map/three/ppermute | solution.py:405
  32.2 1.3 %collective-permute-start.7 = (bf16[256,512]{1,0:T(8,128)(2,1)S(1)}, bf16[256,512]{1,0:T(8,128)(2,1)S(1)}, u32[]{:S(2)}, u32[]{:S(2)}) collective-permute-start(bf16[256,512]{1,0:T(8,128)(2,1)S(1)} %collective-permute-done.6.refs_1_), channel_id=1, source_target_pairs={{0,2},{2,0},{4,6},{6,4},{8,10},{10,8},{12,14},{14,12},{1,3},{3,1},... | collective-permute-start | bytes 786440 | tf_op jit(solution)/shard_map/three_y/ppermute | solution.py:401
  33.4 3.0 %third.1 = (f32[656,1024]{1,0:T(8,128)S(1)}, f32[656,1024]{1,0:T(8,128)S(1)}) custom-call(bf16[256,512]{1,0:T(8,128)(2,1)S(1)} %collective-permute-done.12.refs_0_, bf16[256,512]{1,0:T(8,128)(2,1)S(1)} %collective-permute-done.6.refs_1_, f32[64,256]{1,0:T(8,128)S(1)} %get-tuple-element.51.refs_2_.refs_1_, f32[16,128]{1,0:T(8,128)S(1)} %get-tuple-element.52.refs_3_.refs_2_, ...), custom_call_target="tpu_custom_call" | custom-call | flops 3080000000 | tf_op jit(solution)/shard_map/third/pallas_call | solution.py:344
  36.4 2.1 %collective-permute-done.7.refs_0_ = bf16[256,512]{1,0:T(8,128)(2,1)S(1)} collective-permute-done((bf16[256,512]{1,0:T(8,128)(2,1)S(1)}, bf16[256,512]{1,0:T(8,128)(2,1)S(1)}, u32[]{:S(2)}, u32[]{:S(2)}) %collective-permute-start.7) | collective-permute-done | bytes 262176 | tf_op jit(solution)/shard_map/three_y/ppermute | solution.py:401
  38.6 2.1 %fourth.1.mine = bf16[656,1024]{1,0:T(8,128)(2,1)S(1)} custom-call(bf16[256,512]{1,0:T(8,128)(2,1)S(1)} %collective-permute-done.7.refs_0_, f32[64,256]{1,0:T(8,128)S(1)} %get-tuple-element.51.refs_2_.refs_1_, f32[16,128]{1,0:T(8,128)S(1)} %get-tuple-element.52.refs_3_.refs_2_, f32[656,1024]{1,0:T(8,128)S(1)} %get-tuple-element.57.refs_3_, ...), custom_call_target="tpu_custom_call" | custom-call | flops 1760000000 | tf_op jit(solution)/shard_map/fourth/pallas_call | solution.py:344
  40.7 0.1 collective-permute-start.13
  40.7 3.1 %collective-permute-done.13.theirs = bf16[656,1024]{1,0:T(8,128)(2,1)S(1)} collective-permute-done((bf16[656,1024]{1,0:T(8,128)(2,1)S(1)}, bf16[656,1024]{1,0:T(8,128)(2,1)S(1)}, u32[]{:S(2)}, u32[]{:S(2)}) %collective-permute-start.13) | collective-permute-done | bytes 1343520 | tf_op jit(solution)/shard_map/ppermute | solution.py:461
  43.8 3.4 %update.1 = (bf16[256,128]{1,0:T(8,128)(2,1)}, f32[512,1024]{1,0:T(8,128)}, f32[1024,128]{1,0:T(8,128)}, f32[1,1024]{1,0:T(1,128)}, f32[512,1024]{1,0:T(8,128)}, /*index=5*/f32[1024,128]{1,0:T(8,128)}, f32[1,1024]{1,0:T(1,128)}) custom-call(bf16[656,1024]{1,0:T(8,128)(2,1)S(1)} %fourth.1.mine, bf16[656,1024]{1,0:T(8,128)(2,1)S(1)} %collective-permute-done.13.theirs, ...), custom_call_target="tpu_custom_call" | custom-call | flops 3740000000 | tf_op jit(solution)/shard_map/update/pallas_call | solution.py:387
  (34 shorter events, 0.1 us)
Async XLA Ops:
  0.6 6.1 %copy-start.4 = (bf16[512,1024]{1,0:T(8,128)(2,1)S(1)}, bf16[512,1024]{1,0:T(8,128)(2,1)}, u32[]{:S(2)}) copy-start(bf16[512,1024]{1,0:T(8,128)(2,1)} %actor_embed.1) | copy-start | bytes 3145732
  0.6 6.1 %copy-start.6 = (bf16[1024,128]{1,0:T(8,128)(2,1)S(1)}, bf16[1024,128]{1,0:T(8,128)(2,1)}, u32[]{:S(2)}) copy-start(bf16[1024,128]{1,0:T(8,128)(2,1)} %actor_policy.1) | copy-start | bytes 786436
  0.7 6.1 %copy-start.7 = (bf16[16,16,512]{2,1,0:T(8,128)(2,1)S(1)}, bf16[16,16,512]{2,1,0:T(8,128)(2,1)}, u32[]{:S(2)}) copy-start(bf16[16,16,512]{2,1,0:T(8,128)(2,1)} %param.14) | copy-start | bytes 786436
  0.7 6.1 %copy-start.9 = (s32[16,16]{1,0:T(8,128)S(1)}, s32[16,16]{1,0:T(8,128)}, u32[]{:S(2)}) copy-start(s32[16,16]{1,0:T(8,128)} %actions.1) | copy-start | bytes 3076
  0.7 6.1 %copy-start.10 = (f32[16,16]{1,0:T(8,128)S(1)}, f32[16,16]{1,0:T(8,128)}, u32[]{:S(2)}) copy-start(f32[16,16]{1,0:T(8,128)} %rewards.1) | copy-start | bytes 3076
  0.7 6.1 %copy-start.12 = (s32[16]{0:T(128)S(1)}, s32[16]{0:T(128)}, u32[]{:S(2)}) copy-start(s32[16]{0:T(128)} %param.15) | copy-start | bytes 196
  0.7 6.1 %copy-start.13 = (s32[16]{0:T(128)S(1)}, s32[16]{0:T(128)}, u32[]{:S(2)}) copy-start(s32[16]{0:T(128)} %param.18) | copy-start | bytes 196
  0.7 11.6 %collective-permute-start.1 = (bf16[256,512]{1,0:T(8,128)(2,1)}, bf16[256,512]{1,0:T(8,128)(2,1)S(1)}, u32[]{:S(2)}, u32[]{:S(2)}) collective-permute-start(bf16[256,512]{1,0:T(8,128)(2,1)} %bitcast.11), channel_id=1, source_target_pairs={{0,4},{2,6},{4,8},{6,10},{8,12},{10,14},{12,0},{14,2},{1,5},{3,7},... | collective-permute-start | bytes 786440 | tf_op jit(solution)/shard_map/one/ppermute | solution.py:405
  3.8 10.1 %collective-permute-start = (bf16[256,512]{1,0:T(8,128)(2,1)}, bf16[256,512]{1,0:T(8,128)(2,1)S(1)}, u32[]{:S(2)}, u32[]{:S(2)}) collective-permute-start(bf16[256,512]{1,0:T(8,128)(2,1)} %bitcast.12), channel_id=1, source_target_pairs={{0,2},{2,0},{4,6},{6,4},{8,10},{10,8},{12,14},{14,12},{1,3},{3,1},... | collective-permute-start | bytes 786440 | tf_op jit(solution)/shard_map/own_y/ppermute | solution.py:401
  5.3 1.3 %collective-permute-start.2 = (s32[16]{0:T(128)}, s32[16]{0:T(128)S(1)}, u32[]{:S(2)}, u32[]{:S(2)}) collective-permute-start(s32[16]{0:T(128)} %param.15), channel_id=1, source_target_pairs={{0,1},{1,0},{2,3},{3,2},{4,5},{5,4},{6,7},{7,6},{8,9},{9,8},{10,11... | collective-permute-start | bytes 200 | tf_op jit(solution)/shard_map/ppermute | solution.py:451
  5.3 1.5 %collective-permute-start.3 = (s32[16]{0:T(128)}, s32[16]{0:T(128)S(1)}, u32[]{:S(2)}, u32[]{:S(2)}) collective-permute-start(s32[16]{0:T(128)} %param.18), channel_id=1, source_target_pairs={{0,1},{1,0},{2,3},{3,2},{4,5},{5,4},{6,7},{7,6},{8,9},{9,8},{10,11... | collective-permute-start | bytes 200 | tf_op jit(solution)/shard_map/ppermute | solution.py:451
  6.8 1.6 %copy-start = (f32[512,1024]{1,0:T(8,128)S(1)}, f32[512,1024]{1,0:T(8,128)}, u32[]{:S(2)}) copy-start(f32[512,1024]{1,0:T(8,128)} %master_embed.3) | copy-start | bytes 6291460
  6.8 1.7 %copy-start.1 = (f32[1024,128]{1,0:T(8,128)S(1)}, f32[1024,128]{1,0:T(8,128)}, u32[]{:S(2)}) copy-start(f32[1024,128]{1,0:T(8,128)} %master_policy.3) | copy-start | bytes 1572868
  6.8 1.7 %copy-start.2 = (f32[1024]{0:T(1024)S(1)}, f32[1024]{0:T(1024)}, u32[]{:S(2)}) copy-start(f32[1024]{0:T(1024)} %param.23) | copy-start | bytes 12292
  7.6 6.2 %collective-permute-start.8 = (f32[8,256]{1,0:T(8,128)S(1)}, f32[8,256]{1,0:T(8,128)S(1)}, u32[]{:S(2)}, u32[]{:S(2)}) collective-permute-start(f32[8,256]{1,0:T(8,128)S(1)} %side.1), channel_id=1, source_target_pairs={{0,2},{2,0},{4,6},{6,4},{8,10},{10,8},{12,14},{14,12},{1,3},{3,1},... | collective-permute-start | bytes 24584 | tf_op jit(solution)/shard_map/side_y/ppermute | solution.py:401
  12.3 7.5 %collective-permute-start.4 = (bf16[256,512]{1,0:T(8,128)(2,1)S(1)}, bf16[256,512]{1,0:T(8,128)(2,1)S(1)}, u32[]{:S(2)}, u32[]{:S(2)}) collective-permute-start(bf16[256,512]{1,0:T(8,128)(2,1)S(1)} %collective-permute-done.1.refs_2_), channel_id=1, source_target_pairs={{0,2},{2,0},{4,6},{6,4},{8,10},{10,8},{12,14},{14,12},{1,3},{3,1},... | collective-permute-start | bytes 786440 | tf_op jit(solution)/shard_map/one_y/ppermute | solution.py:401
  13.8 9.4 %collective-permute-start.5 = (bf16[256,512]{1,0:T(8,128)(2,1)S(1)}, bf16[256,512]{1,0:T(8,128)(2,1)S(1)}, u32[]{:S(2)}, u32[]{:S(2)}) collective-permute-start(bf16[256,512]{1,0:T(8,128)(2,1)S(1)} %collective-permute-done.1.refs_2_), channel_id=1, source_target_pairs={{0,4},{2,6},{4,8},{6,10},{8,12},{10,14},{12,0},{14,2},{1,5},{3,7},... | collective-permute-start | bytes 786440 | tf_op jit(solution)/shard_map/two/ppermute | solution.py:405
  13.9 10.1 %collective-permute-start.10 = (f32[16,256]{1,0:T(8,128)S(1)}, f32[16,256]{1,0:T(8,128)S(1)}, u32[]{:S(2)}, u32[]{:S(2)}) collective-permute-start(f32[16,256]{1,0:T(8,128)S(1)} %pad_maximum_fusion.refs_3_), channel_id=1, source_target_pairs={{0,8},{2,10},{4,12},{6,14},{8,0},{10,2},{12,4},{14,6},{1,9},{3,11}... | collective-permute-start | bytes 49160 | tf_op jit(solution)/shard_map/side_z/ppermute | solution.py:401
  16.2 7.8 %collective-permute-start.11 = (f32[16,256]{1,0:T(8,128)S(1)}, f32[16,256]{1,0:T(8,128)S(1)}, u32[]{:S(2)}, u32[]{:S(2)}) collective-permute-start(f32[16,256]{1,0:T(8,128)S(1)} %pad_maximum_fusion.refs_3_), channel_id=1, source_target_pairs={{0,12},{2,14},{4,8},{6,10},{8,4},{10,6},{12,0},{14,2},{1,13},{3,15... | collective-permute-start | bytes 49160 | tf_op jit(solution)/shard_map/side_z/ppermute | solution.py:401
  17.8 6.2 %collective-permute-start.9 = (f32[16,256]{1,0:T(8,128)S(1)}, f32[16,256]{1,0:T(8,128)S(1)}, u32[]{:S(2)}, u32[]{:S(2)}) collective-permute-start(f32[16,256]{1,0:T(8,128)S(1)} %pad_maximum_fusion.refs_3_), channel_id=1, source_target_pairs={{0,4},{2,6},{4,0},{6,2},{8,12},{10,14},{12,8},{14,10},{1,5},{3,7},... | collective-permute-start | bytes 49160 | tf_op jit(solution)/shard_map/side_z/ppermute | solution.py:401
  23.2 10.2 %collective-permute-start.12 = (bf16[256,512]{1,0:T(8,128)(2,1)S(1)}, bf16[256,512]{1,0:T(8,128)(2,1)S(1)}, u32[]{:S(2)}, u32[]{:S(2)}) collective-permute-start(bf16[256,512]{1,0:T(8,128)(2,1)S(1)} %collective-permute-done.5.refs_1_), channel_id=1, source_target_pairs={{0,2},{2,0},{4,6},{6,4},{8,10},{10,8},{12,14},{14,12},{1,3},{3,1},... | collective-permute-start | bytes 786440 | tf_op jit(solution)/shard_map/two_y/ppermute | solution.py:401
  24.0 8.2 %collective-permute-start.6 = (bf16[256,512]{1,0:T(8,128)(2,1)S(1)}, bf16[256,512]{1,0:T(8,128)(2,1)S(1)}, u32[]{:S(2)}, u32[]{:S(2)}) collective-permute-start(bf16[256,512]{1,0:T(8,128)(2,1)S(1)} %collective-permute-done.5.refs_1_), channel_id=1, source_target_pairs={{0,4},{2,6},{4,8},{6,10},{8,12},{10,14},{12,0},{14,2},{1,5},{3,7},... | collective-permute-start | bytes 786440 | tf_op jit(solution)/shard_map/three/ppermute | solution.py:405
  32.2 6.4 %collective-permute-start.7 = (bf16[256,512]{1,0:T(8,128)(2,1)S(1)}, bf16[256,512]{1,0:T(8,128)(2,1)S(1)}, u32[]{:S(2)}, u32[]{:S(2)}) collective-permute-start(bf16[256,512]{1,0:T(8,128)(2,1)S(1)} %collective-permute-done.6.refs_1_), channel_id=1, source_target_pairs={{0,2},{2,0},{4,6},{6,4},{8,10},{10,8},{12,14},{14,12},{1,3},{3,1},... | collective-permute-start | bytes 786440 | tf_op jit(solution)/shard_map/three_y/ppermute | solution.py:401
  38.5 5.3 %copy-start.3 = (f32[512,1024]{1,0:T(8,128)S(1)}, f32[512,1024]{1,0:T(8,128)}, u32[]{:S(2)}) copy-start(f32[512,1024]{1,0:T(8,128)} %embed_moment.1) | copy-start | bytes 6291460
  38.5 5.3 %copy-start.5 = (f32[1024,128]{1,0:T(8,128)S(1)}, f32[1024,128]{1,0:T(8,128)}, u32[]{:S(2)}) copy-start(f32[1024,128]{1,0:T(8,128)} %policy_moment.1) | copy-start | bytes 1572868
  38.5 5.3 %copy-start.8 = (bf16[256,512]{1,0:T(8,128)(2,1)S(1)}, bf16[256,512]{1,0:T(8,128)(2,1)}, u32[]{:S(2)}) copy-start(bf16[256,512]{1,0:T(8,128)(2,1)} %next_obs.1) | copy-start | bytes 786436
  38.5 5.3 %copy-start.11 = (f32[1024]{0:T(1024)S(1)}, f32[1024]{0:T(1024)}, u32[]{:S(2)}) copy-start(f32[1024]{0:T(1024)} %param.26) | copy-start | bytes 12292
  40.7 3.1 %collective-permute-start.13 = (bf16[656,1024]{1,0:T(8,128)(2,1)S(1)}, bf16[656,1024]{1,0:T(8,128)(2,1)S(1)}, u32[]{:S(2)}, u32[]{:S(2)}) collective-permute-start(bf16[656,1024]{1,0:T(8,128)(2,1)S(1)} %fourth.1.mine), channel_id=1, source_target_pairs={{0,1},{1,0},{2,3},{3,2},{4,5},{5,4},{6,7},{7,6},{8,9},{9,8},{10,11... | collective-permute-start | bytes 4030472 | tf_op jit(solution)/shard_map/ppermute | solution.py:461

commit v12 on v10

--- a/solution.py
+++ b/solution.py
@@ -237,7 +237,15 @@
     backward(slots, logits, side, weights, head, frames_t, hidden_t, preact_t, add)
 
 
+def on_mid():
+    line = lax.div(lax.axis_index("hst"), 2)
+    return jnp.logical_or(line == 1, line == 2)
+
+
 def side_of(sides, mask):
+    if mask >= 4:
+        mask = lax.bitwise_xor(mask, jnp.where(on_mid(), 2, 0))
+        return sides[pl.ds(pl.multiple_of(8 * mask, 8), 8), :]
     return sides[8 * mask : 8 * mask + 8, :]
 
 
@@ -266,7 +274,7 @@
 
 def first_kernel(slots, *refs):
     (frames_t, hidden_t, logits, *pieces), mats, (sum_01, sum_2, weights, sides), scratch = (
-        refs[0:7], refs[7:10], refs[10:14], refs[14:17])
+        refs[0:6], refs[6:9], refs[9:13], refs[13:16])
     start = 0
     for piece in pieces:
         sides[start : start + piece.shape[0], :] = piece[...]
@@ -398,31 +406,39 @@
         with jax.named_scope(name):
             return lax.ppermute(array, "hst", [(at, at ^ mask) for at in range(8)])
 
+    def middle(array, name):
+        with jax.named_scope(name):
+            pairs = [(at, at ^ 6 if at in (2, 3, 4, 5) else at) for at in range(8)]
+            return lax.ppermute(array, "hst", pairs)
+
     b2 = exchange(own, 2, "b2")
+    over = middle(own, "over")
     b1 = exchange(own, 1, "b1")
     pair = jnp.concatenate([side, exchange(side, 1, "side_y")], axis=0)
     pair, _, _ = lax.optimization_barrier((pair, b2, b1))
-    pieces = [pair] + [exchange(pair, 2 * mask, "side_z") for mask in (1, 2, 3)]
-    again, _ = lax.optimization_barrier((own, side))
-    b4 = exchange(again, 4, "b4")
+    pieces = [pair, exchange(pair, 2, "side_z")]
+    four = jnp.concatenate(pieces, axis=0)
+    pieces.append(exchange(four, 4, "side_zz"))
     b3 = exchange(b2, 1, "b3")
-    b5 = exchange(b4, 1, "b5")
-    b6 = exchange(b4, 2, "b6")
-    pieces, b3 = lax.optimization_barrier((pieces, b3))
+    end_4 = exchange(over, 2, "end_4")
+    mid_6 = middle(b2, "mid_6")
     width, feats = mats[0].shape
     grads = jax.ShapeDtypeStruct((feats + mats[2].shape[0], width), F32)
     weights = jax.ShapeDtypeStruct((16, 128), F32)
     sides = jax.ShapeDtypeStruct((64, side.shape[1]), F32)
     done = ahead((own, b1, b2), mats[0], mats[2])
+    end_6 = exchange(mid_6, 2, "end_6")
+    b4 = jnp.where(on_mid(), over, end_4)
+    b5 = exchange(b4, 1, "b5")
+    done, b3, b4 = lax.optimization_barrier((done, b3, b4))
     sum_01, sum_2, weights, sides = call(
         first_kernel, "first", slots, 3, (*done, *pieces), mats, (grads, grads, weights, sides),
     )
-    b6, sum_2 = lax.optimization_barrier((b6, sum_2))
-    b3, _ = lax.optimization_barrier((b3, b6))
     sum_0123, sum_4 = call(
         second_kernel, "second", slots, 2, (b3, b4, sides, weights, sum_01, sum_2), mats,
         (grads, grads),
     )
+    b6 = jnp.where(on_mid(), mid_6, end_6)
     b7 = exchange(b6, 1, "b7")
     sum_45, sum_6 = call(
         third_kernel, "third", slots, 2, (b5, b6, sides, weights, sum_4), mats, (grads, grads),

time: 47.8 us -> 49.7 us (1.040)
  starting transfers between devices: 17.5 us -> 20.2 us
  waiting for transfers between devices: 12.7 us -> 11.2 us
  local copies, waits for them, and re-layouts: 0.07 us -> 0.75 us
    ppermute x0 -> x2, starting transfers between devices: none -> 2.27 us  [middle(): return lax.ppermute(array, 'hst', pairs)]
    ppermute x11 -> x10, waiting for transfers between devices: 8.69 us -> 7.21 us  [exchange(): return lax.ppermute(array, 'hst', [(at, at ^ mask) for at in range(8)])]
    unnamed x28, local copies, waits for them, and re-layouts: 0.07 us -> 0.75 us
    ppermute x11 -> x10, starting transfers between devices: 16.9 us -> 17.3 us  [exchange(): return lax.ppermute(array, 'hst', [(at, at ^ mask) for at in range(8)])]
  transfers between devices with their start and end apart: 14 -> 15, of which waited for: 5 -> 6; matrix products, arithmetic and copies ran while one was open for 0% -> 0% of each run, Pallas kernels for 23% -> 22%
where the time goes in v12:
time: 49.7 us; the launch traced here: 49.5 us
  starting transfers between devices  20.2 us (41%)
  Pallas kernels  16.5 us (33%)
  waiting for transfers between devices  11.2 us (23%)
  between operations  0.82 us (2%)
  local copies, waits for them, and re-layouts  0.75 us (2%)
    ppermute x10, starting transfers between devices, exchange(): return lax.ppermute(array, 'hst', [(at, at ^ mask) for at in range(8)])  17.3 us
    pallas_call x4, Pallas kernels, call(): pl.pallas_call(functools.partial(kernel, slots), out_shape=outs, in_specs...  10.6 us
    ppermute x10, waiting for transfers between devices, exchange(): return lax.ppermute(array, 'hst', [(at, at ^ mask) for at in range(8)])  7.21 us
    pallas_call x1, Pallas kernels, update(): pl.pallas_call(functools.partial(update_kernel, feats, nact), out_shape=(...  3.4 us
    ppermute x1, waiting for transfers between devices, body(): theirs = lax.ppermute(mine, 'cores', flip)  3.07 us
    ppermute x2, starting transfers between devices, middle(): return lax.ppermute(array, 'hst', pairs)  2.27 us
    pallas_call x1, Pallas kernels, ahead(): pl.pallas_call(ahead_kernel, out_shape=(jax.ShapeDtypeStruct((feats, rows...  1.3 us
  transfers between devices with their start and end apart: 15, of which 6 were waited for; matrix products, arithmetic and copies ran while one was open for 0% of the time, Pallas kernels for 22%

profile of v12, /device:TPU:0, one launch (start us, length us, event | category | flops | bytes accessed | tf_op | source)
XLA Modules:
  0.0 49.5 jit_solution(7337213842272150675)
XLA Ops:
  0.6 1.6 %collective-permute-start.8 = (bf16[256,512]{1,0:T(8,128)(2,1)}, bf16[256,512]{1,0:T(8,128)(2,1)S(1)}, u32[]{:S(2)}, u32[]{:S(2)}) collective-permute-start(bf16[256,512]{1,0:T(8,128)(2,1)} %bitcast.11), channel_id=1, source_target_pairs={{0,0},{2,2},{4,8},{6,10},{8,4},{10,6},{12,12},{14,14},{1,1},{3,3},... | collective-permute-start | bytes 786440 | tf_op jit(solution)/shard_map/over/ppermute | solution.py:412
  2.2 5.0 %collective-permute-start = (bf16[256,512]{1,0:T(8,128)(2,1)}, bf16[256,512]{1,0:T(8,128)(2,1)S(1)}, u32[]{:S(2)}, u32[]{:S(2)}) collective-permute-start(bf16[256,512]{1,0:T(8,128)(2,1)} %bitcast.12), channel_id=1, source_target_pairs={{0,4},{2,6},{4,0},{6,2},{8,12},{10,14},{12,8},{14,10},{1,5},{3,7},... | collective-permute-start | bytes 786440 | tf_op jit(solution)/shard_map/b2/ppermute | solution.py:407
  7.2 1.5 %collective-permute-start.4 = (bf16[256,512]{1,0:T(8,128)(2,1)}, bf16[256,512]{1,0:T(8,128)(2,1)S(1)}, u32[]{:S(2)}, u32[]{:S(2)}) collective-permute-start(bf16[256,512]{1,0:T(8,128)(2,1)} %bitcast.13), channel_id=1, source_target_pairs={{0,2},{2,0},{4,6},{6,4},{8,10},{10,8},{12,14},{14,12},{1,3},{3,1},... | collective-permute-start | bytes 786440 | tf_op jit(solution)/shard_map/b1/ppermute | solution.py:407
  8.7 0.5 %collective-permute-start.6 = (s32[16]{0:T(128)}, s32[16]{0:T(128)S(1)}, u32[]{:S(2)}, u32[]{:S(2)}) collective-permute-start(s32[16]{0:T(128)} %param.18), channel_id=1, source_target_pairs={{0,1},{1,0},{2,3},{3,2},{4,5},{5,4},{6,7},{7,6},{8,9},{9,8},{10,11... | collective-permute-start | bytes 200 | tf_op jit(solution)/shard_map/ppermute | solution.py:463
  9.3 0.7 %collective-permute-done.5 = s32[16]{0:T(128)S(1)} collective-permute-done((s32[16]{0:T(128)}, s32[16]{0:T(128)S(1)}, u32[]{:S(2)}, u32[]{:S(2)}) %collective-permute-start.5) | collective-permute-done | bytes 96 | tf_op jit(solution)/shard_map/ppermute | solution.py:463
  10.0 0.2 collective-permute-done.6
  10.2 0.3 copy-done.4
  10.5 0.1 copy-done.7
  10.6 0.8 %side.1 = f32[8,256]{1,0:T(8,128)S(1)} custom-call(s32[1,16]{1,0:T(1,128)S(1)} %bitcast.17, s32[1,16]{1,0:T(1,128)S(1)} %bitcast.18, s32[1,16]{1,0:T(1,128)S(1)} %bitcast.19, s32[1,16]{1,0:T(1,128)S(1)} %bitcast.20, s32[16,16]{1,0:T(8,128)S(1)} %copy-done.9, f32[16,16]{1,0:T(8,128)S(1)} %copy-done.10, bf16[512,1024]{1,0:T(8,128)(2,1)S(1)} %copy-done.4, ...), custom_call_target="tpu_custom_call" | custom-call | flops 1430000000 | tf_op jit(solution)/shard_map/side/pallas_call | solution.py:101
  11.4 0.6 %collective-permute-start.10 = (f32[8,256]{1,0:T(8,128)S(1)}, f32[8,256]{1,0:T(8,128)S(1)}, u32[]{:S(2)}, u32[]{:S(2)}) collective-permute-start(f32[8,256]{1,0:T(8,128)S(1)} %side.1), channel_id=1, source_target_pairs={{0,2},{2,0},{4,6},{6,4},{8,10},{10,8},{12,14},{14,12},{1,3},{3,1},... | collective-permute-start | bytes 24584 | tf_op jit(solution)/shard_map/side_y/ppermute | solution.py:407
  12.0 0.2 copy-done
  12.2 0.1 copy-done.1
  12.3 0.5 convert.1
  12.8 2.3 %collective-permute-done.10 = f32[8,256]{1,0:T(8,128)S(1)} collective-permute-done((f32[8,256]{1,0:T(8,128)S(1)}, f32[8,256]{1,0:T(8,128)S(1)}, u32[]{:S(2)}, u32[]{:S(2)}) %collective-permute-start.10) | collective-permute-done | bytes 8224 | tf_op jit(solution)/shard_map/side_y/ppermute | solution.py:407
  15.1 0.4 collective-permute-start.11
  15.5 1.5 %collective-permute-start.7 = (bf16[256,512]{1,0:T(8,128)(2,1)S(1)}, bf16[256,512]{1,0:T(8,128)(2,1)S(1)}, u32[]{:S(2)}, u32[]{:S(2)}) collective-permute-start(bf16[256,512]{1,0:T(8,128)(2,1)S(1)} %collective-permute-done.refs_2_), channel_id=1, source_target_pairs={{0,2},{2,0},{4,6},{6,4},{8,10},{10,8},{12,14},{14,12},{1,3},{3,1},... | collective-permute-start | bytes 786440 | tf_op jit(solution)/shard_map/b3/ppermute | solution.py:407
  17.0 0.7 %collective-permute-start.1 = (bf16[256,512]{1,0:T(8,128)(2,1)S(1)}, bf16[256,512]{1,0:T(8,128)(2,1)S(1)}, u32[]{:S(2)}, u32[]{:S(2)}) collective-permute-start(bf16[256,512]{1,0:T(8,128)(2,1)S(1)} %collective-permute-done.refs_2_), channel_id=1, source_target_pairs={{0,0},{2,2},{4,8},{6,10},{8,4},{10,6},{12,12},{14,14},{1,1},{3,3},... | collective-permute-start | bytes 786440 | tf_op jit(solution)/shard_map/mid_6/ppermute | solution.py:412
  17.7 3.4 %collective-permute-start.9 = (bf16[256,512]{1,0:T(8,128)(2,1)S(1)}, bf16[256,512]{1,0:T(8,128)(2,1)S(1)}, u32[]{:S(2)}, u32[]{:S(2)}) collective-permute-start(bf16[256,512]{1,0:T(8,128)(2,1)S(1)} %collective-permute-done.8), channel_id=1, source_target_pairs={{0,4},{2,6},{4,0},{6,2},{8,12},{10,14},{12,8},{14,10},{1,5},{3,7},... | collective-permute-start | bytes 786440 | tf_op jit(solution)/shard_map/end_4/ppermute | solution.py:407
  21.1 1.3 %ahead.1 = (bf16[512,768]{1,0:T(8,128)(2,1)S(1)}, bf16[1024,768]{1,0:T(8,128)(2,1)S(1)}, f32[144,768]{1,0:T(8,128)S(1)}) custom-call(bf16[256,512]{1,0:T(8,128)(2,1)S(1)} %bitcast.15, bf16[256,512]{1,0:T(8,128)(2,1)S(1)} %collective-permute-done.4.refs_1_, bf16[256,512]{1,0:T(8,128)(2,1)S(1)} %collective-permute-done.refs_2_, ...), custom_call_target="tpu_custom_call" | custom-call | flops 1760000000 | tf_op jit(solution)/shard_map/ahead/pallas_call | solution.py:260
  22.5 1.1 %collective-permute-start.12 = (f32[32,256]{1,0:T(8,128)S(1)}, f32[32,256]{1,0:T(8,128)S(1)}, u32[]{:S(2)}, u32[]{:S(2)}) collective-permute-start(f32[32,256]{1,0:T(8,128)S(1)} %pad_maximum_fusion), channel_id=1, source_target_pairs={{0,8},{2,10},{4,12},{6,14},{8,0},{10,2},{12,4},{14,6},{1,9},{3,11}... | collective-permute-start | bytes 98312 | tf_op jit(solution)/shard_map/side_zz/ppermute | solution.py:407
  23.6 2.3 %collective-permute-done.9 = bf16[256,512]{1,0:T(8,128)(2,1)S(1)} collective-permute-done((bf16[256,512]{1,0:T(8,128)(2,1)S(1)}, bf16[256,512]{1,0:T(8,128)(2,1)S(1)}, u32[]{:S(2)}, u32[]{:S(2)}) %collective-permute-start.9) | collective-permute-done | bytes 262176 | tf_op jit(solution)/shard_map/end_4/ppermute | solution.py:407
  25.9 1.2 %collective-permute-start.13 = (bf16[256,512]{1,0:T(8,128)(2,1)S(1)}, bf16[256,512]{1,0:T(8,128)(2,1)S(1)}, u32[]{:S(2)}, u32[]{:S(2)}) collective-permute-start(bf16[256,512]{1,0:T(8,128)(2,1)S(1)} %broadcast_select_fusion.refs_1_), channel_id=1, source_target_pairs={{0,2},{2,0},{4,6},{6,4},{8,10},{10,8},{12,14},{14,12},{1,3},{3,1},... | collective-permute-start | bytes 786440 | tf_op jit(solution)/shard_map/b5/ppermute | solution.py:407
  27.1 1.7 %collective-permute-start.2 = (bf16[256,512]{1,0:T(8,128)(2,1)S(1)}, bf16[256,512]{1,0:T(8,128)(2,1)S(1)}, u32[]{:S(2)}, u32[]{:S(2)}) collective-permute-start(bf16[256,512]{1,0:T(8,128)(2,1)S(1)} %collective-permute-done.1), channel_id=1, source_target_pairs={{0,4},{2,6},{4,0},{6,2},{8,12},{10,14},{12,8},{14,10},{1,5},{3,7},... | collective-permute-start | bytes 786440 | tf_op jit(solution)/shard_map/end_6/ppermute | solution.py:407
  28.8 2.6 %first.1 = (f32[656,1024]{1,0:T(8,128)S(1)}, f32[656,1024]{1,0:T(8,128)S(1)}, f32[16,128]{1,0:T(8,128)S(1)}, f32[64,256]{1,0:T(8,128)S(1)}) custom-call(bf16[512,768]{1,0:T(8,128)(2,1)S(1)} %get-tuple-element.45.refs_0_, bf16[1024,768]{1,0:T(8,128)(2,1)S(1)} %get-tuple-element.46.refs_1_, f32[144,768]{1,0:T(8,128)S(1)} %get-tuple-element.47.refs_2_, ...), custom_call_target="tpu_custom_call" | custom-call | flops 4400000000 | tf_op jit(solution)/shard_map/first/pallas_call | solution.py:350
  31.4 3.0 %second.1 = (f32[656,1024]{1,0:T(8,128)S(1)}, f32[656,1024]{1,0:T(8,128)S(1)}) custom-call(bf16[256,512]{1,0:T(8,128)(2,1)S(1)} %collective-permute-done.7.refs_0_, bf16[256,512]{1,0:T(8,128)(2,1)S(1)} %broadcast_select_fusion.refs_1_, f32[64,256]{1,0:T(8,128)S(1)} %get-tuple-element.50.refs_2_.refs_1_, f32[16,128]{1,0:T(8,128)S(1)} %get-tuple-element.51.refs_3_.refs_2_, ...), custom_call_target="tpu_custom_call" | custom-call | flops 3080000000 | tf_op jit(solution)/shard_map/second/pallas_call | solution.py:350
  34.4 0.9 %collective-permute-start.3 = (bf16[256,512]{1,0:T(8,128)(2,1)S(1)}, bf16[256,512]{1,0:T(8,128)(2,1)S(1)}, u32[]{:S(2)}, u32[]{:S(2)}) collective-permute-start(bf16[256,512]{1,0:T(8,128)(2,1)S(1)} %broadcast_select_fusion.1.refs_1_), channel_id=1, source_target_pairs={{0,2},{2,0},{4,6},{6,4},{8,10},{10,8},{12,14},{14,12},{1,3},{3,1},... | collective-permute-start | bytes 786440 | tf_op jit(solution)/shard_map/b7/ppermute | solution.py:407
  35.3 2.9 %third.1 = (f32[656,1024]{1,0:T(8,128)S(1)}, f32[656,1024]{1,0:T(8,128)S(1)}) custom-call(bf16[256,512]{1,0:T(8,128)(2,1)S(1)} %collective-permute-done.13.refs_0_, bf16[256,512]{1,0:T(8,128)(2,1)S(1)} %broadcast_select_fusion.1.refs_1_, f32[64,256]{1,0:T(8,128)S(1)} %get-tuple-element.50.refs_2_.refs_1_, f32[16,128]{1,0:T(8,128)S(1)} %get-tuple-element.51.refs_3_.refs_2_, ...), custom_call_target="tpu_custom_call" | custom-call | flops 3080000000 | tf_op jit(solution)/shard_map/third/pallas_call | solution.py:350
  38.2 2.6 %collective-permute-done.3.refs_0_ = bf16[256,512]{1,0:T(8,128)(2,1)S(1)} collective-permute-done((bf16[256,512]{1,0:T(8,128)(2,1)S(1)}, bf16[256,512]{1,0:T(8,128)(2,1)S(1)}, u32[]{:S(2)}, u32[]{:S(2)}) %collective-permute-start.3) | collective-permute-done | bytes 262176 | tf_op jit(solution)/shard_map/b7/ppermute | solution.py:407
  40.8 2.1 %fourth.1.mine = bf16[656,1024]{1,0:T(8,128)(2,1)S(1)} custom-call(bf16[256,512]{1,0:T(8,128)(2,1)S(1)} %collective-permute-done.3.refs_0_, f32[64,256]{1,0:T(8,128)S(1)} %get-tuple-element.50.refs_2_.refs_1_, f32[16,128]{1,0:T(8,128)S(1)} %get-tuple-element.51.refs_3_.refs_2_, f32[656,1024]{1,0:T(8,128)S(1)} %get-tuple-element.56.refs_3_, ...), custom_call_target="tpu_custom_call" | custom-call | flops 1760000000 | tf_op jit(solution)/shard_map/fourth/pallas_call | solution.py:350
  42.9 0.1 collective-permute-start.14
  43.0 3.1 %collective-permute-done.14.theirs = bf16[656,1024]{1,0:T(8,128)(2,1)S(1)} collective-permute-done((bf16[656,1024]{1,0:T(8,128)(2,1)S(1)}, bf16[656,1024]{1,0:T(8,128)(2,1)S(1)}, u32[]{:S(2)}, u32[]{:S(2)}) %collective-permute-start.14) | collective-permute-done | bytes 1343520 | tf_op jit(solution)/shard_map/ppermute | solution.py:473
  46.1 3.4 %update.1 = (bf16[256,128]{1,0:T(8,128)(2,1)}, f32[512,1024]{1,0:T(8,128)}, f32[1024,128]{1,0:T(8,128)}, f32[1,1024]{1,0:T(1,128)}, f32[512,1024]{1,0:T(8,128)}, /*index=5*/f32[1024,128]{1,0:T(8,128)}, f32[1,1024]{1,0:T(1,128)}) custom-call(bf16[656,1024]{1,0:T(8,128)(2,1)S(1)} %fourth.1.mine, bf16[656,1024]{1,0:T(8,128)(2,1)S(1)} %collective-permute-done.14.theirs, ...), custom_call_target="tpu_custom_call" | custom-call | flops 3740000000 | tf_op jit(solution)/shard_map/update/pallas_call | solution.py:393
  (39 shorter events, 0.2 us)
Async XLA Ops:
  0.6 17.1 %collective-permute-start.8 = (bf16[256,512]{1,0:T(8,128)(2,1)}, bf16[256,512]{1,0:T(8,128)(2,1)S(1)}, u32[]{:S(2)}, u32[]{:S(2)}) collective-permute-start(bf16[256,512]{1,0:T(8,128)(2,1)} %bitcast.11), channel_id=1, source_target_pairs={{0,0},{2,2},{4,8},{6,10},{8,4},{10,6},{12,12},{14,14},{1,1},{3,3},... | collective-permute-start | bytes 786440 | tf_op jit(solution)/shard_map/over/ppermute | solution.py:412
  2.2 12.9 %collective-permute-start = (bf16[256,512]{1,0:T(8,128)(2,1)}, bf16[256,512]{1,0:T(8,128)(2,1)S(1)}, u32[]{:S(2)}, u32[]{:S(2)}) collective-permute-start(bf16[256,512]{1,0:T(8,128)(2,1)} %bitcast.12), channel_id=1, source_target_pairs={{0,4},{2,6},{4,0},{6,2},{8,12},{10,14},{12,8},{14,10},{1,5},{3,7},... | collective-permute-start | bytes 786440 | tf_op jit(solution)/shard_map/b2/ppermute | solution.py:407
  7.2 7.9 %collective-permute-start.4 = (bf16[256,512]{1,0:T(8,128)(2,1)}, bf16[256,512]{1,0:T(8,128)(2,1)S(1)}, u32[]{:S(2)}, u32[]{:S(2)}) collective-permute-start(bf16[256,512]{1,0:T(8,128)(2,1)} %bitcast.13), channel_id=1, source_target_pairs={{0,2},{2,0},{4,6},{6,4},{8,10},{10,8},{12,14},{14,12},{1,3},{3,1},... | collective-permute-start | bytes 786440 | tf_op jit(solution)/shard_map/b1/ppermute | solution.py:407
  8.7 1.3 %collective-permute-start.5 = (s32[16]{0:T(128)}, s32[16]{0:T(128)S(1)}, u32[]{:S(2)}, u32[]{:S(2)}) collective-permute-start(s32[16]{0:T(128)} %param.15), channel_id=1, source_target_pairs={{0,1},{1,0},{2,3},{3,2},{4,5},{5,4},{6,7},{7,6},{8,9},{9,8},{10,11... | collective-permute-start | bytes 200 | tf_op jit(solution)/shard_map/ppermute | solution.py:463
  8.7 1.5 %collective-permute-start.6 = (s32[16]{0:T(128)}, s32[16]{0:T(128)S(1)}, u32[]{:S(2)}, u32[]{:S(2)}) collective-permute-start(s32[16]{0:T(128)} %param.18), channel_id=1, source_target_pairs={{0,1},{1,0},{2,3},{3,2},{4,5},{5,4},{6,7},{7,6},{8,9},{9,8},{10,11... | collective-permute-start | bytes 200 | tf_op jit(solution)/shard_map/ppermute | solution.py:463
  9.2 1.2 %copy-start.4 = (bf16[512,1024]{1,0:T(8,128)(2,1)S(1)}, bf16[512,1024]{1,0:T(8,128)(2,1)}, u32[]{:S(2)}) copy-start(bf16[512,1024]{1,0:T(8,128)(2,1)} %actor_embed.1) | copy-start | bytes 3145732
  9.2 1.3 %copy-start.6 = (bf16[1024,128]{1,0:T(8,128)(2,1)S(1)}, bf16[1024,128]{1,0:T(8,128)(2,1)}, u32[]{:S(2)}) copy-start(bf16[1024,128]{1,0:T(8,128)(2,1)} %actor_policy.1) | copy-start | bytes 786436
  9.3 1.3 %copy-start.7 = (bf16[16,16,512]{2,1,0:T(8,128)(2,1)S(1)}, bf16[16,16,512]{2,1,0:T(8,128)(2,1)}, u32[]{:S(2)}) copy-start(bf16[16,16,512]{2,1,0:T(8,128)(2,1)} %param.14) | copy-start | bytes 786436
  9.3 1.3 %copy-start.9 = (s32[16,16]{1,0:T(8,128)S(1)}, s32[16,16]{1,0:T(8,128)}, u32[]{:S(2)}) copy-start(s32[16,16]{1,0:T(8,128)} %actions.1) | copy-start | bytes 3076
  9.3 1.3 %copy-start.10 = (f32[16,16]{1,0:T(8,128)S(1)}, f32[16,16]{1,0:T(8,128)}, u32[]{:S(2)}) copy-start(f32[16,16]{1,0:T(8,128)} %rewards.1) | copy-start | bytes 3076
  9.3 1.3 %copy-start.12 = (s32[16]{0:T(128)S(1)}, s32[16]{0:T(128)}, u32[]{:S(2)}) copy-start(s32[16]{0:T(128)} %param.15) | copy-start | bytes 196
  9.3 1.3 %copy-start.13 = (s32[16]{0:T(128)S(1)}, s32[16]{0:T(128)}, u32[]{:S(2)}) copy-start(s32[16]{0:T(128)} %param.18) | copy-start | bytes 196
  10.6 1.6 %copy-start = (f32[512,1024]{1,0:T(8,128)S(1)}, f32[512,1024]{1,0:T(8,128)}, u32[]{:S(2)}) copy-start(f32[512,1024]{1,0:T(8,128)} %master_embed.3) | copy-start | bytes 6291460
  10.6 1.7 %copy-start.1 = (f32[1024,128]{1,0:T(8,128)S(1)}, f32[1024,128]{1,0:T(8,128)}, u32[]{:S(2)}) copy-start(f32[1024,128]{1,0:T(8,128)} %master_policy.3) | copy-start | bytes 1572868
  10.6 1.7 %copy-start.2 = (f32[1024]{0:T(1024)S(1)}, f32[1024]{0:T(1024)}, u32[]{:S(2)}) copy-start(f32[1024]{0:T(1024)} %param.23) | copy-start | bytes 12292
  11.4 3.7 %collective-permute-start.10 = (f32[8,256]{1,0:T(8,128)S(1)}, f32[8,256]{1,0:T(8,128)S(1)}, u32[]{:S(2)}, u32[]{:S(2)}) collective-permute-start(f32[8,256]{1,0:T(8,128)S(1)} %side.1), channel_id=1, source_target_pairs={{0,2},{2,0},{4,6},{6,4},{8,10},{10,8},{12,14},{14,12},{1,3},{3,1},... | collective-permute-start | bytes 24584 | tf_op jit(solution)/shard_map/side_y/ppermute | solution.py:407
  15.1 7.3 %collective-permute-start.11 = (f32[16,256]{1,0:T(8,128)S(1)}, f32[16,256]{1,0:T(8,128)S(1)}, u32[]{:S(2)}, u32[]{:S(2)}) collective-permute-start(f32[16,256]{1,0:T(8,128)S(1)} %pad_maximum_fusion.1.refs_3_), channel_id=1, source_target_pairs={{0,4},{2,6},{4,0},{6,2},{8,12},{10,14},{12,8},{14,10},{1,5},{3,7},... | collective-permute-start | bytes 49160 | tf_op jit(solution)/shard_map/side_z/ppermute | solution.py:407
  15.5 11.5 %collective-permute-start.7 = (bf16[256,512]{1,0:T(8,128)(2,1)S(1)}, bf16[256,512]{1,0:T(8,128)(2,1)S(1)}, u32[]{:S(2)}, u32[]{:S(2)}) collective-permute-start(bf16[256,512]{1,0:T(8,128)(2,1)S(1)} %collective-permute-done.refs_2_), channel_id=1, source_target_pairs={{0,2},{2,0},{4,6},{6,4},{8,10},{10,8},{12,14},{14,12},{1,3},{3,1},... | collective-permute-start | bytes 786440 | tf_op jit(solution)/shard_map/b3/ppermute | solution.py:407
  17.0 10.0 %collective-permute-start.1 = (bf16[256,512]{1,0:T(8,128)(2,1)S(1)}, bf16[256,512]{1,0:T(8,128)(2,1)S(1)}, u32[]{:S(2)}, u32[]{:S(2)}) collective-permute-start(bf16[256,512]{1,0:T(8,128)(2,1)S(1)} %collective-permute-done.refs_2_), channel_id=1, source_target_pairs={{0,0},{2,2},{4,8},{6,10},{8,4},{10,6},{12,12},{14,14},{1,1},{3,3},... | collective-permute-start | bytes 786440 | tf_op jit(solution)/shard_map/mid_6/ppermute | solution.py:412
  17.7 8.1 %collective-permute-start.9 = (bf16[256,512]{1,0:T(8,128)(2,1)S(1)}, bf16[256,512]{1,0:T(8,128)(2,1)S(1)}, u32[]{:S(2)}, u32[]{:S(2)}) collective-permute-start(bf16[256,512]{1,0:T(8,128)(2,1)S(1)} %collective-permute-done.8), channel_id=1, source_target_pairs={{0,4},{2,6},{4,0},{6,2},{8,12},{10,14},{12,8},{14,10},{1,5},{3,7},... | collective-permute-start | bytes 786440 | tf_op jit(solution)/shard_map/end_4/ppermute | solution.py:407
  22.5 6.3 %collective-permute-start.12 = (f32[32,256]{1,0:T(8,128)S(1)}, f32[32,256]{1,0:T(8,128)S(1)}, u32[]{:S(2)}, u32[]{:S(2)}) collective-permute-start(f32[32,256]{1,0:T(8,128)S(1)} %pad_maximum_fusion), channel_id=1, source_target_pairs={{0,8},{2,10},{4,12},{6,14},{8,0},{10,2},{12,4},{14,6},{1,9},{3,11}... | collective-permute-start | bytes 98312 | tf_op jit(solution)/shard_map/side_zz/ppermute | solution.py:407
  25.9 9.5 %collective-permute-start.13 = (bf16[256,512]{1,0:T(8,128)(2,1)S(1)}, bf16[256,512]{1,0:T(8,128)(2,1)S(1)}, u32[]{:S(2)}, u32[]{:S(2)}) collective-permute-start(bf16[256,512]{1,0:T(8,128)(2,1)S(1)} %broadcast_select_fusion.refs_1_), channel_id=1, source_target_pairs={{0,2},{2,0},{4,6},{6,4},{8,10},{10,8},{12,14},{14,12},{1,3},{3,1},... | collective-permute-start | bytes 786440 | tf_op jit(solution)/shard_map/b5/ppermute | solution.py:407
  27.1 7.3 %collective-permute-start.2 = (bf16[256,512]{1,0:T(8,128)(2,1)S(1)}, bf16[256,512]{1,0:T(8,128)(2,1)S(1)}, u32[]{:S(2)}, u32[]{:S(2)}) collective-permute-start(bf16[256,512]{1,0:T(8,128)(2,1)S(1)} %collective-permute-done.1), channel_id=1, source_target_pairs={{0,4},{2,6},{4,0},{6,2},{8,12},{10,14},{12,8},{14,10},{1,5},{3,7},... | collective-permute-start | bytes 786440 | tf_op jit(solution)/shard_map/end_6/ppermute | solution.py:407
  34.4 6.4 %collective-permute-start.3 = (bf16[256,512]{1,0:T(8,128)(2,1)S(1)}, bf16[256,512]{1,0:T(8,128)(2,1)S(1)}, u32[]{:S(2)}, u32[]{:S(2)}) collective-permute-start(bf16[256,512]{1,0:T(8,128)(2,1)S(1)} %broadcast_select_fusion.1.refs_1_), channel_id=1, source_target_pairs={{0,2},{2,0},{4,6},{6,4},{8,10},{10,8},{12,14},{14,12},{1,3},{3,1},... | collective-permute-start | bytes 786440 | tf_op jit(solution)/shard_map/b7/ppermute | solution.py:407
  40.8 5.3 %copy-start.3 = (f32[512,1024]{1,0:T(8,128)S(1)}, f32[512,1024]{1,0:T(8,128)}, u32[]{:S(2)}) copy-start(f32[512,1024]{1,0:T(8,128)} %embed_moment.1) | copy-start | bytes 6291460
  40.8 5.3 %copy-start.5 = (f32[1024,128]{1,0:T(8,128)S(1)}, f32[1024,128]{1,0:T(8,128)}, u32[]{:S(2)}) copy-start(f32[1024,128]{1,0:T(8,128)} %policy_moment.1) | copy-start | bytes 1572868
  40.8 5.3 %copy-start.8 = (bf16[256,512]{1,0:T(8,128)(2,1)S(1)}, bf16[256,512]{1,0:T(8,128)(2,1)}, u32[]{:S(2)}) copy-start(bf16[256,512]{1,0:T(8,128)(2,1)} %next_obs.1) | copy-start | bytes 786436
  40.8 5.3 %copy-start.11 = (f32[1024]{0:T(1024)S(1)}, f32[1024]{0:T(1024)}, u32[]{:S(2)}) copy-start(f32[1024]{0:T(1024)} %param.26) | copy-start | bytes 12292
  42.9 3.1 %collective-permute-start.14 = (bf16[656,1024]{1,0:T(8,128)(2,1)S(1)}, bf16[656,1024]{1,0:T(8,128)(2,1)S(1)}, u32[]{:S(2)}, u32[]{:S(2)}) collective-permute-start(bf16[656,1024]{1,0:T(8,128)(2,1)S(1)} %fourth.1.mine), channel_id=1, source_target_pairs={{0,1},{1,0},{2,3},{3,2},{4,5},{5,4},{6,7},{7,6},{8,9},{9,8},{10,11... | collective-permute-start | bytes 4030472 | tf_op jit(solution)/shard_map/ppermute | solution.py:473

commit v13 on v11

--- a/solution.py
+++ b/solution.py
@@ -240,7 +240,7 @@
 def side_of(sides, back, flip):
     line = lax.div(lax.axis_index("hst"), 2)
     there = lax.bitwise_xor(line, lax.bitwise_and(line + 4 - back, 3))
-    return sides[pl.ds(pl.multiple_of(8 * (2 * there + flip), 8), 8), :]
+    return sides[pl.ds(pl.multiple_of(8 * (4 * flip + there), 8), 8), :]
 
 
 def ahead_kernel(*refs):
@@ -268,7 +268,7 @@
 
 def first_kernel(slots, *refs):
     (frames_t, hidden_t, logits, *pieces), mats, (sum_0, sum_1, weights, sides), scratch = (
-        refs[0:7], refs[7:10], refs[10:14], refs[14:17])
+        refs[0:5], refs[5:8], refs[8:12], refs[12:15])
     start = 0
     for piece in pieces:
         sides[start : start + piece.shape[0], :] = piece[...]
@@ -288,43 +288,43 @@
 
 
 def second_kernel(slots, *refs):
-    frames, (sides, weights, sum_1), mats, (sum_1y, sum_2), scratch = (
+    frames, (sides, weights, sum_1), mats, (sum_1y, sum_3), scratch = (
         refs[0:2], refs[2:5], refs[5:8], refs[8:10], refs[10:13])
 
     def add(index, rows, value):
         if index == 0:
             sum_1y[rows, :] = sum_1[rows, :] + value
         else:
-            sum_2[rows, :] = value
-
-    side = jnp.concatenate([side_of(sides, 1, 1), side_of(sides, 2, 0)], axis=1)
+            sum_3[rows, :] = value
+
+    side = jnp.concatenate([side_of(sides, 1, 1), side_of(sides, 3, 0)], axis=1)
     work(slots, frames, side, weights, *mats, *scratch, add)
 
 
 def third_kernel(slots, *refs):
-    frames, (sides, weights, sum_0, sum_2), mats, (even, sum_3), scratch = (
+    frames, (sides, weights, sum_1y, sum_3), mats, (odd, sum_2), scratch = (
         refs[0:2], refs[2:6], refs[6:9], refs[9:11], refs[11:14])
 
     def add(index, rows, value):
         if index == 0:
-            even[rows, :] = sum_0[rows, :] + (sum_2[rows, :] + value)
+            odd[rows, :] = sum_1y[rows, :] + (sum_3[rows, :] + value)
         else:
-            sum_3[rows, :] = value
-
-    side = jnp.concatenate([side_of(sides, 2, 1), side_of(sides, 3, 0)], axis=1)
+            sum_2[rows, :] = value
+
+    side = jnp.concatenate([side_of(sides, 3, 1), side_of(sides, 2, 0)], axis=1)
     work(slots, frames, side, weights, *mats, *scratch, add)
 
 
 def fourth_kernel(slots, *refs):
-    frames, (sides, weights, even, sum_1y, sum_3), mats, out, scratch = (
+    frames, (sides, weights, odd, sum_0, sum_2), mats, out, scratch = (
         refs[0:1], refs[1:6], refs[6:9], refs[9], refs[10:13])
 
     def add(index, rows, value):
         out[rows, :] = (
-            even[rows, :] + (sum_1y[rows, :] + (sum_3[rows, :] + value))
+            odd[rows, :] + (sum_0[rows, :] + (sum_2[rows, :] + value))
         ).astype(BF16)
 
-    work(slots, frames, side_of(sides, 3, 1), weights, *mats, *scratch, add)
+    work(slots, frames, side_of(sides, 2, 1), weights, *mats, *scratch, add)
 
 
 def local_kernel(slots, frames, side, weights, embed_t, head, head_t, out, *scratch):
@@ -400,39 +400,44 @@
         with jax.named_scope(name):
             return lax.ppermute(array, "hst", [(at, at ^ mask) for at in range(8)])
 
-    def shift(array, name):
+    def shift(array, by, name):
         with jax.named_scope(name):
-            return lax.ppermute(array, "hst", [(at, (at + 2) % 8) for at in range(8)])
-
-    one = shift(own, "one")
+            return lax.ppermute(array, "hst", [(at, (at + 2 * by) % 8) for at in range(8)])
+
+    one = shift(own, 1, "one")
     own_y = exchange(own, 1, "own_y")
-    pair = jnp.concatenate([side, exchange(side, 1, "side_y")], axis=0)
-    pair, _, _ = lax.optimization_barrier((pair, one, own_y))
-    pieces = [pair] + [exchange(pair, 2 * mask, "side_z") for mask in (1, 2, 3)]
-    two = shift(one, "two")
+    pieces = [side] + [exchange(side, 2 * mask, "side_z") for mask in (1, 2, 3)]
+    line = jnp.concatenate(pieces, axis=0)
+    line, _ = lax.optimization_barrier((line, side))
+    one, _ = lax.optimization_barrier((one, pieces[1]))
+    again, _ = lax.optimization_barrier((own, pieces[1]))
+    line_y = exchange(line, 1, "side_y")
+    three = shift(again, -1, "three")
     one_y = exchange(one, 1, "one_y")
+    two = shift(one, 1, "two")
+    three_y = exchange(three, 1, "three_y")
+
     width, feats = mats[0].shape
     grads = jax.ShapeDtypeStruct((feats + mats[2].shape[0], width), F32)
     weights = jax.ShapeDtypeStruct((16, 128), F32)
     sides = jax.ShapeDtypeStruct((64, side.shape[1]), F32)
     done = ahead((own, own_y, one), mats[0], mats[2])
-    done, one_y, two = lax.optimization_barrier((done, one_y, two))
-    three = shift(two, "three")
+    sum_0, sum_1, weights, sides = call(
+        first_kernel, "first", slots, 3, (*done, line, line_y), mats,
+        (grads, grads, weights, sides),
+    )
+    sum_1y, sum_3 = call(
+        second_kernel, "second", slots, 2, (one_y, three, sides, weights, sum_1), mats,
+        (grads, grads),
+    )
+    two, sum_3 = lax.optimization_barrier((two, sum_3))
     two_y = exchange(two, 1, "two_y")
-    sum_0, sum_1, weights, sides = call(
-        first_kernel, "first", slots, 3, (*done, *pieces), mats, (grads, grads, weights, sides),
-    )
-    sum_1y, sum_2 = call(
-        second_kernel, "second", slots, 2, (one_y, two, sides, weights, sum_1), mats,
+    odd, sum_2 = call(
+        third_kernel, "third", slots, 2, (three_y, two, sides, weights, sum_1y, sum_3), mats,
         (grads, grads),
     )
-    three_y = exchange(three, 1, "three_y")
-    even, sum_3 = call(
-        third_kernel, "third", slots, 2, (two_y, three, sides, weights, sum_0, sum_2), mats,
-        (grads, grads),
-    )
     return call(
-        fourth_kernel, "fourth", slots, 1, (three_y, sides, weights, even, sum_1y, sum_3), mats,
+        fourth_kernel, "fourth", slots, 1, (two_y, sides, weights, odd, sum_0, sum_2), mats,
         jax.ShapeDtypeStruct(grads.shape, BF16),
     )
 

time: 47.4 us -> 45 us (0.949)
  waiting for transfers between devices: 15.8 us -> 10.2 us
  starting transfers between devices: 13.7 us -> 17.3 us
    ppermute x3, waiting for transfers between devices: 9.45 us -> 1.5 us  [shift(): lax.ppermute(array, 'hst', [(at, (at + 2 * by) % 8) for at in range(8)])]
    ppermute x8, starting transfers between devices: 10.1 us -> 12.7 us  [exchange(): return lax.ppermute(array, 'hst', [(at, at ^ mask) for at in range(8)])]
    ppermute x8, waiting for transfers between devices: 2.34 us -> 4.66 us  [exchange(): return lax.ppermute(array, 'hst', [(at, at ^ mask) for at in range(8)])]
    ppermute x3, starting transfers between devices: 3.08 us -> 4.05 us  [shift(): lax.ppermute(array, 'hst', [(at, (at + 2 * by) % 8) for at in range(8)])]
  transfers between devices with their start and end apart: 14 -> 14, of which waited for: 8 -> 9; matrix products, arithmetic and copies ran while one was open for 0% -> 0% of each run, Pallas kernels for 23% -> 25%
where the time goes in v13:
time: 45 us; the launch traced here: 44.9 us
  starting transfers between devices  17.3 us (38%)
  Pallas kernels  16.5 us (37%)
  waiting for transfers between devices  10.2 us (23%)
  between operations  0.81 us (2%)
    ppermute x8, starting transfers between devices, exchange(): return lax.ppermute(array, 'hst', [(at, at ^ mask) for at in range(8)])  12.7 us
    pallas_call x4, Pallas kernels, call(): pl.pallas_call(functools.partial(kernel, slots), out_shape=outs, in_specs...  10.5 us
    ppermute x8, waiting for transfers between devices, exchange(): return lax.ppermute(array, 'hst', [(at, at ^ mask) for at in range(8)])  4.66 us
    ppermute x3, starting transfers between devices, shift(): lax.ppermute(array, 'hst', [(at, (at + 2 * by) % 8) for at in range(8)])  4.05 us
    pallas_call x1, Pallas kernels, update(): pl.pallas_call(functools.partial(update_kernel, feats, nact), out_shape=(...  3.42 us
    ppermute x1, waiting for transfers between devices, body(): theirs = lax.ppermute(mine, 'cores', flip)  3.07 us
    ppermute x3, waiting for transfers between devices, shift(): lax.ppermute(array, 'hst', [(at, (at + 2 * by) % 8) for at in range(8)])  1.5 us
    pallas_call x1, Pallas kernels, ahead(): pl.pallas_call(ahead_kernel, out_shape=(jax.ShapeDtypeStruct((feats, rows...  1.31 us
  transfers between devices with their start and end apart: 14, of which 9 were waited for; matrix products, arithmetic and copies ran while one was open for 0% of the time, Pallas kernels for 25%

profile of v13, /device:TPU:0, one launch (start us, length us, event | category | flops | bytes accessed | tf_op | source)
XLA Modules:
  0.0 44.9 jit_solution(16628520836010221871)
XLA Ops:
  0.7 3.0 %collective-permute-start.7 = (bf16[256,512]{1,0:T(8,128)(2,1)}, bf16[256,512]{1,0:T(8,128)(2,1)S(1)}, u32[]{:S(2)}, u32[]{:S(2)}) collective-permute-start(bf16[256,512]{1,0:T(8,128)(2,1)} %bitcast.11), channel_id=1, source_target_pairs={{0,2},{2,0},{4,6},{6,4},{8,10},{10,8},{12,14},{14,12},{1,3},{3,1},... | collective-permute-start | bytes 786440 | tf_op jit(solution)/shard_map/own_y/ppermute | solution.py:401
  3.7 1.6 %collective-permute-start = (bf16[256,512]{1,0:T(8,128)(2,1)}, bf16[256,512]{1,0:T(8,128)(2,1)S(1)}, u32[]{:S(2)}, u32[]{:S(2)}) collective-permute-start(bf16[256,512]{1,0:T(8,128)(2,1)} %bitcast.12), channel_id=1, source_target_pairs={{0,4},{2,6},{4,8},{6,10},{8,12},{10,14},{12,0},{14,2},{1,5},{3,7},... | collective-permute-start | bytes 786440 | tf_op jit(solution)/shard_map/one/ppermute | solution.py:405
  5.3 0.5 %collective-permute-start.2 = (s32[16]{0:T(128)}, s32[16]{0:T(128)S(1)}, u32[]{:S(2)}, u32[]{:S(2)}) collective-permute-start(s32[16]{0:T(128)} %param.18), channel_id=1, source_target_pairs={{0,1},{1,0},{2,3},{3,2},{4,5},{5,4},{6,7},{7,6},{8,9},{9,8},{10,11... | collective-permute-start | bytes 200 | tf_op jit(solution)/shard_map/ppermute | solution.py:456
  5.8 0.7 %collective-permute-done.1 = s32[16]{0:T(128)S(1)} collective-permute-done((s32[16]{0:T(128)}, s32[16]{0:T(128)S(1)}, u32[]{:S(2)}, u32[]{:S(2)}) %collective-permute-start.1) | collective-permute-done | bytes 96 | tf_op jit(solution)/shard_map/ppermute | solution.py:456
  6.6 0.2 collective-permute-done.2
  6.8 0.0 copy-start
  6.8 0.0 copy-start.1
  6.8 0.0 copy-start.2
  6.9 0.8 %side.1 = f32[8,256]{1,0:T(8,128)S(1)} custom-call(s32[1,16]{1,0:T(1,128)S(1)} %bitcast.17, s32[1,16]{1,0:T(1,128)S(1)} %bitcast.18, s32[1,16]{1,0:T(1,128)S(1)} %bitcast.19, s32[1,16]{1,0:T(1,128)S(1)} %bitcast.20, s32[16,16]{1,0:T(8,128)S(1)} %copy-done.9, f32[16,16]{1,0:T(8,128)S(1)} %copy-done.10, bf16[512,1024]{1,0:T(8,128)(2,1)S(1)} %copy-done.4, ...), custom_call_target="tpu_custom_call" | custom-call | flops 1430000000 | tf_op jit(solution)/shard_map/side/pallas_call | solution.py:101
  7.6 2.3 %collective-permute-start.9 = (f32[8,256]{1,0:T(8,128)S(1)}, f32[8,256]{1,0:T(8,128)S(1)}, u32[]{:S(2)}, u32[]{:S(2)}) collective-permute-start(f32[8,256]{1,0:T(8,128)S(1)} %side.1), channel_id=1, source_target_pairs={{0,12},{2,14},{4,8},{6,10},{8,4},{10,6},{12,0},{14,2},{1,13},{3,15... | collective-permute-start | bytes 24584 | tf_op jit(solution)/shard_map/side_z/ppermute | solution.py:401
  9.9 0.8 %collective-permute-start.8 = (f32[8,256]{1,0:T(8,128)S(1)}, f32[8,256]{1,0:T(8,128)S(1)}, u32[]{:S(2)}, u32[]{:S(2)}) collective-permute-start(f32[8,256]{1,0:T(8,128)S(1)} %side.1), channel_id=1, source_target_pairs={{0,8},{2,10},{4,12},{6,14},{8,0},{10,2},{12,4},{14,6},{1,9},{3,11}... | collective-permute-start | bytes 24584 | tf_op jit(solution)/shard_map/side_z/ppermute | solution.py:401
  10.7 1.3 %collective-permute-start.3 = (f32[8,256]{1,0:T(8,128)S(1)}, f32[8,256]{1,0:T(8,128)S(1)}, u32[]{:S(2)}, u32[]{:S(2)}) collective-permute-start(f32[8,256]{1,0:T(8,128)S(1)} %side.1), channel_id=1, source_target_pairs={{0,4},{2,6},{4,0},{6,2},{8,12},{10,14},{12,8},{14,10},{1,5},{3,7},... | collective-permute-start | bytes 24584 | tf_op jit(solution)/shard_map/side_z/ppermute | solution.py:401
  12.1 0.5 %convert.1 = (bf16[1024,512]{1,0:T(8,128)(2,1)S(1)}, bf16[1024,144]{1,0:T(8,128)(2,1)S(1)}, bf16[144,1024]{1,0:T(8,128)(2,1)S(1)}) custom-call(f32[512,1024]{1,0:T(8,128)S(1)} %copy-done, f32[1024,128]{1,0:T(8,128)S(1)} %copy-done.1, f32[1,1024]{1,0:T(1,128)S(1)} %bitcast.9), custom_call_target="tpu_custom_call" | custom-call | flops 660000000 | tf_op jit(solution)/shard_map/convert/pallas_call | solution.py:131
  12.6 1.8 %collective-permute-done.3 = f32[8,256]{1,0:T(8,128)S(1)} collective-permute-done((f32[8,256]{1,0:T(8,128)S(1)}, f32[8,256]{1,0:T(8,128)S(1)}, u32[]{:S(2)}, u32[]{:S(2)}) %collective-permute-start.3) | collective-permute-done | bytes 8224 | tf_op jit(solution)/shard_map/side_z/ppermute | solution.py:401
  14.4 0.1 collective-permute-done.8
  14.5 0.5 %collective-permute-start.10 = (f32[32,256]{1,0:T(8,128)S(1)}, f32[32,256]{1,0:T(8,128)S(1)}, u32[]{:S(2)}, u32[]{:S(2)}) collective-permute-start(f32[32,256]{1,0:T(8,128)S(1)} %pad_maximum_fusion.refs_3_), channel_id=1, source_target_pairs={{0,2},{2,0},{4,6},{6,4},{8,10},{10,8},{12,14},{14,12},{1,3},{3,1},... | collective-permute-start | bytes 98312 | tf_op jit(solution)/shard_map/side_y/ppermute | solution.py:401
  15.0 2.5 %collective-permute-start.6 = (bf16[256,512]{1,0:T(8,128)(2,1)S(1)}, bf16[256,512]{1,0:T(8,128)(2,1)S(1)}, u32[]{:S(2)}, u32[]{:S(2)}) collective-permute-start(bf16[256,512]{1,0:T(8,128)(2,1)S(1)} %bitcast.14), channel_id=1, source_target_pairs={{0,12},{2,14},{4,0},{6,2},{8,4},{10,6},{12,8},{14,10},{1,13},{3,15... | collective-permute-start | bytes 786440 | tf_op jit(solution)/shard_map/three/ppermute | solution.py:405
  17.4 1.5 %collective-permute-start.5 = (bf16[256,512]{1,0:T(8,128)(2,1)S(1)}, bf16[256,512]{1,0:T(8,128)(2,1)S(1)}, u32[]{:S(2)}, u32[]{:S(2)}) collective-permute-start(bf16[256,512]{1,0:T(8,128)(2,1)S(1)} %collective-permute-done.refs_2_), channel_id=1, source_target_pairs={{0,2},{2,0},{4,6},{6,4},{8,10},{10,8},{12,14},{14,12},{1,3},{3,1},... | collective-permute-start | bytes 786440 | tf_op jit(solution)/shard_map/one_y/ppermute | solution.py:401
  19.0 1.3 %ahead.1 = (bf16[512,768]{1,0:T(8,128)(2,1)S(1)}, bf16[1024,768]{1,0:T(8,128)(2,1)S(1)}, f32[144,768]{1,0:T(8,128)S(1)}) custom-call(bf16[256,512]{1,0:T(8,128)(2,1)S(1)} %bitcast.15, bf16[256,512]{1,0:T(8,128)(2,1)S(1)} %collective-permute-done.7.refs_1_, bf16[256,512]{1,0:T(8,128)(2,1)S(1)} %collective-permute-done.refs_2_, ...), custom_call_target="tpu_custom_call" | custom-call | flops 1760000000 | tf_op jit(solution)/shard_map/ahead/pallas_call | solution.py:254
  20.3 2.6 %first.1 = (f32[656,1024]{1,0:T(8,128)S(1)}, f32[656,1024]{1,0:T(8,128)S(1)}, f32[16,128]{1,0:T(8,128)S(1)}, f32[64,256]{1,0:T(8,128)S(1)}) custom-call(bf16[512,768]{1,0:T(8,128)(2,1)S(1)} %get-tuple-element.43.refs_0_, bf16[1024,768]{1,0:T(8,128)(2,1)S(1)} %get-tuple-element.44.refs_1_, f32[144,768]{1,0:T(8,128)S(1)} %get-tuple-element.45.refs_2_, ...), custom_call_target="tpu_custom_call" | custom-call | flops 4400000000 | tf_op jit(solution)/shard_map/first/pallas_call | solution.py:344
  22.9 1.3 %collective-permute-done.6.refs_1_ = bf16[256,512]{1,0:T(8,128)(2,1)S(1)} collective-permute-done((bf16[256,512]{1,0:T(8,128)(2,1)S(1)}, bf16[256,512]{1,0:T(8,128)(2,1)S(1)}, u32[]{:S(2)}, u32[]{:S(2)}) %collective-permute-start.6) | collective-permute-done | bytes 262176 | tf_op jit(solution)/shard_map/three/ppermute | solution.py:405
  24.2 1.5 %collective-permute-start.12 = (bf16[256,512]{1,0:T(8,128)(2,1)S(1)}, bf16[256,512]{1,0:T(8,128)(2,1)S(1)}, u32[]{:S(2)}, u32[]{:S(2)}) collective-permute-start(bf16[256,512]{1,0:T(8,128)(2,1)S(1)} %collective-permute-done.6.refs_1_), channel_id=1, source_target_pairs={{0,2},{2,0},{4,6},{6,4},{8,10},{10,8},{12,14},{14,12},{1,3},{3,1},... | collective-permute-start | bytes 786440 | tf_op jit(solution)/shard_map/three_y/ppermute | solution.py:401
  25.7 2.9 %second.1 = (f32[656,1024]{1,0:T(8,128)S(1)}, f32[656,1024]{1,0:T(8,128)S(1)}) custom-call(bf16[256,512]{1,0:T(8,128)(2,1)S(1)} %collective-permute-done.5.refs_0_, bf16[256,512]{1,0:T(8,128)(2,1)S(1)} %collective-permute-done.6.refs_1_, f32[64,256]{1,0:T(8,128)S(1)} %get-tuple-element.48.refs_2_.refs_1_, f32[16,128]{1,0:T(8,128)S(1)} %get-tuple-element.49.refs_3_.refs_2_, ...), custom_call_target="tpu_custom_call" | custom-call | flops 3080000000 | tf_op jit(solution)/shard_map/second/pallas_call | solution.py:344
  28.6 0.2 collective-permute-done.4.refs_1_
  28.8 1.7 %collective-permute-start.11 = (bf16[256,512]{1,0:T(8,128)(2,1)S(1)}, bf16[256,512]{1,0:T(8,128)(2,1)S(1)}, u32[]{:S(2)}, u32[]{:S(2)}) collective-permute-start(bf16[256,512]{1,0:T(8,128)(2,1)S(1)} %collective-permute-done.4.refs_1_), channel_id=1, source_target_pairs={{0,2},{2,0},{4,6},{6,4},{8,10},{10,8},{12,14},{14,12},{1,3},{3,1},... | collective-permute-start | bytes 786440 | tf_op jit(solution)/shard_map/two_y/ppermute | solution.py:401
  30.5 0.8 %collective-permute-done.12.refs_0_ = bf16[256,512]{1,0:T(8,128)(2,1)S(1)} collective-permute-done((bf16[256,512]{1,0:T(8,128)(2,1)S(1)}, bf16[256,512]{1,0:T(8,128)(2,1)S(1)}, u32[]{:S(2)}, u32[]{:S(2)}) %collective-permute-start.12) | collective-permute-done | bytes 262176 | tf_op jit(solution)/shard_map/three_y/ppermute | solution.py:401
  31.2 3.0 %third.1 = (f32[656,1024]{1,0:T(8,128)S(1)}, f32[656,1024]{1,0:T(8,128)S(1)}) custom-call(bf16[256,512]{1,0:T(8,128)(2,1)S(1)} %collective-permute-done.12.refs_0_, bf16[256,512]{1,0:T(8,128)(2,1)S(1)} %collective-permute-done.4.refs_1_, f32[64,256]{1,0:T(8,128)S(1)} %get-tuple-element.48.refs_2_.refs_1_, f32[16,128]{1,0:T(8,128)S(1)} %get-tuple-element.49.refs_3_.refs_2_, ...), custom_call_target="tpu_custom_call" | custom-call | flops 3080000000 | tf_op jit(solution)/shard_map/third/pallas_call | solution.py:344
  34.2 2.0 %collective-permute-done.11.refs_0_ = bf16[256,512]{1,0:T(8,128)(2,1)S(1)} collective-permute-done((bf16[256,512]{1,0:T(8,128)(2,1)S(1)}, bf16[256,512]{1,0:T(8,128)(2,1)S(1)}, u32[]{:S(2)}, u32[]{:S(2)}) %collective-permute-start.11) | collective-permute-done | bytes 262176 | tf_op jit(solution)/shard_map/two_y/ppermute | solution.py:401
  36.2 2.1 %fourth.1.mine = bf16[656,1024]{1,0:T(8,128)(2,1)S(1)} custom-call(bf16[256,512]{1,0:T(8,128)(2,1)S(1)} %collective-permute-done.11.refs_0_, f32[64,256]{1,0:T(8,128)S(1)} %get-tuple-element.48.refs_2_.refs_1_, f32[16,128]{1,0:T(8,128)S(1)} %get-tuple-element.49.refs_3_.refs_2_, f32[656,1024]{1,0:T(8,128)S(1)} %get-tuple-element.55.refs_3_, ...), custom_call_target="tpu_custom_call" | custom-call | flops 1760000000 | tf_op jit(solution)/shard_map/fourth/pallas_call | solution.py:344
  38.3 0.1 collective-permute-start.13
  38.4 3.1 %collective-permute-done.13.theirs = bf16[656,1024]{1,0:T(8,128)(2,1)S(1)} collective-permute-done((bf16[656,1024]{1,0:T(8,128)(2,1)S(1)}, bf16[656,1024]{1,0:T(8,128)(2,1)S(1)}, u32[]{:S(2)}, u32[]{:S(2)}) %collective-permute-start.13) | collective-permute-done | bytes 1343520 | tf_op jit(solution)/shard_map/ppermute | solution.py:466
  41.5 3.4 %update.1 = (bf16[256,128]{1,0:T(8,128)(2,1)}, f32[512,1024]{1,0:T(8,128)}, f32[1024,128]{1,0:T(8,128)}, f32[1,1024]{1,0:T(1,128)}, f32[512,1024]{1,0:T(8,128)}, /*index=5*/f32[1024,128]{1,0:T(8,128)}, f32[1,1024]{1,0:T(1,128)}) custom-call(bf16[656,1024]{1,0:T(8,128)(2,1)S(1)} %fourth.1.mine, bf16[656,1024]{1,0:T(8,128)(2,1)S(1)} %collective-permute-done.13.theirs, ...), custom_call_target="tpu_custom_call" | custom-call | flops 3740000000 | tf_op jit(solution)/shard_map/update/pallas_call | solution.py:387
  (34 shorter events, 0.1 us)
Async XLA Ops:
  0.6 6.1 %copy-start.4 = (bf16[512,1024]{1,0:T(8,128)(2,1)S(1)}, bf16[512,1024]{1,0:T(8,128)(2,1)}, u32[]{:S(2)}) copy-start(bf16[512,1024]{1,0:T(8,128)(2,1)} %actor_embed.1) | copy-start | bytes 3145732
  0.6 6.1 %copy-start.6 = (bf16[1024,128]{1,0:T(8,128)(2,1)S(1)}, bf16[1024,128]{1,0:T(8,128)(2,1)}, u32[]{:S(2)}) copy-start(bf16[1024,128]{1,0:T(8,128)(2,1)} %actor_policy.1) | copy-start | bytes 786436
  0.7 6.1 %copy-start.7 = (bf16[16,16,512]{2,1,0:T(8,128)(2,1)S(1)}, bf16[16,16,512]{2,1,0:T(8,128)(2,1)}, u32[]{:S(2)}) copy-start(bf16[16,16,512]{2,1,0:T(8,128)(2,1)} %param.14) | copy-start | bytes 786436
  0.7 6.1 %copy-start.9 = (s32[16,16]{1,0:T(8,128)S(1)}, s32[16,16]{1,0:T(8,128)}, u32[]{:S(2)}) copy-start(s32[16,16]{1,0:T(8,128)} %actions.1) | copy-start | bytes 3076
  0.7 6.1 %copy-start.10 = (f32[16,16]{1,0:T(8,128)S(1)}, f32[16,16]{1,0:T(8,128)}, u32[]{:S(2)}) copy-start(f32[16,16]{1,0:T(8,128)} %rewards.1) | copy-start | bytes 3076
  0.7 6.1 %copy-start.12 = (s32[16]{0:T(128)S(1)}, s32[16]{0:T(128)}, u32[]{:S(2)}) copy-start(s32[16]{0:T(128)} %param.15) | copy-start | bytes 196
  0.7 6.1 %copy-start.13 = (s32[16]{0:T(128)S(1)}, s32[16]{0:T(128)}, u32[]{:S(2)}) copy-start(s32[16]{0:T(128)} %param.18) | copy-start | bytes 196
  0.7 18.3 %collective-permute-start.7 = (bf16[256,512]{1,0:T(8,128)(2,1)}, bf16[256,512]{1,0:T(8,128)(2,1)S(1)}, u32[]{:S(2)}, u32[]{:S(2)}) collective-permute-start(bf16[256,512]{1,0:T(8,128)(2,1)} %bitcast.11), channel_id=1, source_target_pairs={{0,2},{2,0},{4,6},{6,4},{8,10},{10,8},{12,14},{14,12},{1,3},{3,1},... | collective-permute-start | bytes 786440 | tf_op jit(solution)/shard_map/own_y/ppermute | solution.py:401
  3.7 13.7 %collective-permute-start = (bf16[256,512]{1,0:T(8,128)(2,1)}, bf16[256,512]{1,0:T(8,128)(2,1)S(1)}, u32[]{:S(2)}, u32[]{:S(2)}) collective-permute-start(bf16[256,512]{1,0:T(8,128)(2,1)} %bitcast.12), channel_id=1, source_target_pairs={{0,4},{2,6},{4,8},{6,10},{8,12},{10,14},{12,0},{14,2},{1,5},{3,7},... | collective-permute-start | bytes 786440 | tf_op jit(solution)/shard_map/one/ppermute | solution.py:405
  5.3 1.3 %collective-permute-start.1 = (s32[16]{0:T(128)}, s32[16]{0:T(128)S(1)}, u32[]{:S(2)}, u32[]{:S(2)}) collective-permute-start(s32[16]{0:T(128)} %param.15), channel_id=1, source_target_pairs={{0,1},{1,0},{2,3},{3,2},{4,5},{5,4},{6,7},{7,6},{8,9},{9,8},{10,11... | collective-permute-start | bytes 200 | tf_op jit(solution)/shard_map/ppermute | solution.py:456
  5.3 1.5 %collective-permute-start.2 = (s32[16]{0:T(128)}, s32[16]{0:T(128)S(1)}, u32[]{:S(2)}, u32[]{:S(2)}) collective-permute-start(s32[16]{0:T(128)} %param.18), channel_id=1, source_target_pairs={{0,1},{1,0},{2,3},{3,2},{4,5},{5,4},{6,7},{7,6},{8,9},{9,8},{10,11... | collective-permute-start | bytes 200 | tf_op jit(solution)/shard_map/ppermute | solution.py:456
  6.8 5.2 %copy-start = (f32[512,1024]{1,0:T(8,128)S(1)}, f32[512,1024]{1,0:T(8,128)}, u32[]{:S(2)}) copy-start(f32[512,1024]{1,0:T(8,128)} %master_embed.3) | copy-start | bytes 6291460
  6.8 5.2 %copy-start.1 = (f32[1024,128]{1,0:T(8,128)S(1)}, f32[1024,128]{1,0:T(8,128)}, u32[]{:S(2)}) copy-start(f32[1024,128]{1,0:T(8,128)} %master_policy.3) | copy-start | bytes 1572868
  6.8 5.2 %copy-start.2 = (f32[1024]{0:T(1024)S(1)}, f32[1024]{0:T(1024)}, u32[]{:S(2)}) copy-start(f32[1024]{0:T(1024)} %param.23) | copy-start | bytes 12292
  7.6 6.8 %collective-permute-start.9 = (f32[8,256]{1,0:T(8,128)S(1)}, f32[8,256]{1,0:T(8,128)S(1)}, u32[]{:S(2)}, u32[]{:S(2)}) collective-permute-start(f32[8,256]{1,0:T(8,128)S(1)} %side.1), channel_id=1, source_target_pairs={{0,12},{2,14},{4,8},{6,10},{8,4},{10,6},{12,0},{14,2},{1,13},{3,15... | collective-permute-start | bytes 24584 | tf_op jit(solution)/shard_map/side_z/ppermute | solution.py:401
  9.9 4.5 %collective-permute-start.8 = (f32[8,256]{1,0:T(8,128)S(1)}, f32[8,256]{1,0:T(8,128)S(1)}, u32[]{:S(2)}, u32[]{:S(2)}) collective-permute-start(f32[8,256]{1,0:T(8,128)S(1)} %side.1), channel_id=1, source_target_pairs={{0,8},{2,10},{4,12},{6,14},{8,0},{10,2},{12,4},{14,6},{1,9},{3,11}... | collective-permute-start | bytes 24584 | tf_op jit(solution)/shard_map/side_z/ppermute | solution.py:401
  10.7 3.7 %collective-permute-start.3 = (f32[8,256]{1,0:T(8,128)S(1)}, f32[8,256]{1,0:T(8,128)S(1)}, u32[]{:S(2)}, u32[]{:S(2)}) collective-permute-start(f32[8,256]{1,0:T(8,128)S(1)} %side.1), channel_id=1, source_target_pairs={{0,4},{2,6},{4,0},{6,2},{8,12},{10,14},{12,8},{14,10},{1,5},{3,7},... | collective-permute-start | bytes 24584 | tf_op jit(solution)/shard_map/side_z/ppermute | solution.py:401
  14.5 5.8 %collective-permute-start.10 = (f32[32,256]{1,0:T(8,128)S(1)}, f32[32,256]{1,0:T(8,128)S(1)}, u32[]{:S(2)}, u32[]{:S(2)}) collective-permute-start(f32[32,256]{1,0:T(8,128)S(1)} %pad_maximum_fusion.refs_3_), channel_id=1, source_target_pairs={{0,2},{2,0},{4,6},{6,4},{8,10},{10,8},{12,14},{14,12},{1,3},{3,1},... | collective-permute-start | bytes 98312 | tf_op jit(solution)/shard_map/side_y/ppermute | solution.py:401
  15.0 9.2 %collective-permute-start.6 = (bf16[256,512]{1,0:T(8,128)(2,1)S(1)}, bf16[256,512]{1,0:T(8,128)(2,1)S(1)}, u32[]{:S(2)}, u32[]{:S(2)}) collective-permute-start(bf16[256,512]{1,0:T(8,128)(2,1)S(1)} %bitcast.14), channel_id=1, source_target_pairs={{0,12},{2,14},{4,0},{6,2},{8,4},{10,6},{12,8},{14,10},{1,13},{3,15... | collective-permute-start | bytes 786440 | tf_op jit(solution)/shard_map/three/ppermute | solution.py:405
  17.4 8.3 %collective-permute-start.5 = (bf16[256,512]{1,0:T(8,128)(2,1)S(1)}, bf16[256,512]{1,0:T(8,128)(2,1)S(1)}, u32[]{:S(2)}, u32[]{:S(2)}) collective-permute-start(bf16[256,512]{1,0:T(8,128)(2,1)S(1)} %collective-permute-done.refs_2_), channel_id=1, source_target_pairs={{0,2},{2,0},{4,6},{6,4},{8,10},{10,8},{12,14},{14,12},{1,3},{3,1},... | collective-permute-start | bytes 786440 | tf_op jit(solution)/shard_map/one_y/ppermute | solution.py:401
  19.0 9.8 %collective-permute-start.4 = (bf16[256,512]{1,0:T(8,128)(2,1)S(1)}, bf16[256,512]{1,0:T(8,128)(2,1)S(1)}, u32[]{:S(2)}, u32[]{:S(2)}) collective-permute-start(bf16[256,512]{1,0:T(8,128)(2,1)S(1)} %collective-permute-done.refs_2_), channel_id=1, source_target_pairs={{0,4},{2,6},{4,8},{6,10},{8,12},{10,14},{12,0},{14,2},{1,5},{3,7},... | collective-permute-start | bytes 786440 | tf_op jit(solution)/shard_map/two/ppermute | solution.py:405
  24.2 7.0 %collective-permute-start.12 = (bf16[256,512]{1,0:T(8,128)(2,1)S(1)}, bf16[256,512]{1,0:T(8,128)(2,1)S(1)}, u32[]{:S(2)}, u32[]{:S(2)}) collective-permute-start(bf16[256,512]{1,0:T(8,128)(2,1)S(1)} %collective-permute-done.6.refs_1_), channel_id=1, source_target_pairs={{0,2},{2,0},{4,6},{6,4},{8,10},{10,8},{12,14},{14,12},{1,3},{3,1},... | collective-permute-start | bytes 786440 | tf_op jit(solution)/shard_map/three_y/ppermute | solution.py:401
  28.8 7.4 %collective-permute-start.11 = (bf16[256,512]{1,0:T(8,128)(2,1)S(1)}, bf16[256,512]{1,0:T(8,128)(2,1)S(1)}, u32[]{:S(2)}, u32[]{:S(2)}) collective-permute-start(bf16[256,512]{1,0:T(8,128)(2,1)S(1)} %collective-permute-done.4.refs_1_), channel_id=1, source_target_pairs={{0,2},{2,0},{4,6},{6,4},{8,10},{10,8},{12,14},{14,12},{1,3},{3,1},... | collective-permute-start | bytes 786440 | tf_op jit(solution)/shard_map/two_y/ppermute | solution.py:401
  36.2 5.3 %copy-start.3 = (f32[512,1024]{1,0:T(8,128)S(1)}, f32[512,1024]{1,0:T(8,128)}, u32[]{:S(2)}) copy-start(f32[512,1024]{1,0:T(8,128)} %embed_moment.1) | copy-start | bytes 6291460
  36.2 5.3 %copy-start.5 = (f32[1024,128]{1,0:T(8,128)S(1)}, f32[1024,128]{1,0:T(8,128)}, u32[]{:S(2)}) copy-start(f32[1024,128]{1,0:T(8,128)} %policy_moment.1) | copy-start | bytes 1572868
  36.2 5.3 %copy-start.8 = (bf16[256,512]{1,0:T(8,128)(2,1)S(1)}, bf16[256,512]{1,0:T(8,128)(2,1)}, u32[]{:S(2)}) copy-start(bf16[256,512]{1,0:T(8,128)(2,1)} %next_obs.1) | copy-start | bytes 786436
  36.2 5.3 %copy-start.11 = (f32[1024]{0:T(1024)S(1)}, f32[1024]{0:T(1024)}, u32[]{:S(2)}) copy-start(f32[1024]{0:T(1024)} %param.26) | copy-start | bytes 12292
  38.3 3.1 %collective-permute-start.13 = (bf16[656,1024]{1,0:T(8,128)(2,1)S(1)}, bf16[656,1024]{1,0:T(8,128)(2,1)S(1)}, u32[]{:S(2)}, u32[]{:S(2)}) collective-permute-start(bf16[656,1024]{1,0:T(8,128)(2,1)S(1)} %fourth.1.mine), channel_id=1, source_target_pairs={{0,1},{1,0},{2,3},{3,2},{4,5},{5,4},{6,7},{7,6},{8,9},{9,8},{10,11... | collective-permute-start | bytes 4030472 | tf_op jit(solution)/shard_map/ppermute | solution.py:466

commit v14 on v13

--- a/solution.py
+++ b/solution.py
@@ -352,7 +352,7 @@
             pltpu.VMEM((width, rows), BF16),
         ],
         compiler_params=params(32),
-        cost_estimate=cost(1.2 * blocks + 0.4),
+        cost_estimate=cost(0.3 * blocks),
         name=name,
     )(*args, *mats)
 
@@ -409,8 +409,7 @@
     pieces = [side] + [exchange(side, 2 * mask, "side_z") for mask in (1, 2, 3)]
     line = jnp.concatenate(pieces, axis=0)
     line, _ = lax.optimization_barrier((line, side))
-    one, _ = lax.optimization_barrier((one, pieces[1]))
-    again, _ = lax.optimization_barrier((own, pieces[1]))
+    again, _ = lax.optimization_barrier((own, one))
     line_y = exchange(line, 1, "side_y")
     three = shift(again, -1, "three")
     one_y = exchange(one, 1, "one_y")

time: 45 us -> 46.2 us (1.027)
  waiting for transfers between devices: 10.2 us -> 12.8 us
  starting transfers between devices: 17.3 us -> 15.9 us
    ppermute x8, waiting for transfers between devices: 4.66 us -> 7.47 us  [exchange(): return lax.ppermute(array, 'hst', [(at, at ^ mask) for at in range(8)])]
    ppermute x8, starting transfers between devices: 12.7 us -> 11.7 us  [exchange(): return lax.ppermute(array, 'hst', [(at, at ^ mask) for at in range(8)])]
  transfers between devices with their start and end apart: 14 -> 14, of which waited for: 9 -> 6; matrix products, arithmetic and copies ran while one was open for 0% -> 0% of each run, Pallas kernels for 25% -> 24%
where the time goes in v14:
time: 46.2 us; the launch traced here: 46.1 us
  Pallas kernels  16.5 us (36%)
  starting transfers between devices  15.9 us (34%)
  waiting for transfers between devices  12.8 us (28%)
  between operations  0.85 us (2%)
    ppermute x8, starting transfers between devices, exchange(): return lax.ppermute(array, 'hst', [(at, at ^ mask) for at in range(8)])  11.7 us
    pallas_call x4, Pallas kernels, call(): pl.pallas_call(functools.partial(kernel, slots), out_shape=outs, in_specs...  10.5 us
    ppermute x8, waiting for transfers between devices, exchange(): return lax.ppermute(array, 'hst', [(at, at ^ mask) for at in range(8)])  7.47 us
    ppermute x3, starting transfers between devices, shift(): lax.ppermute(array, 'hst', [(at, (at + 2 * by) % 8) for at in range(8)])  3.6 us
    pallas_call x1, Pallas kernels, update(): pl.pallas_call(functools.partial(update_kernel, feats, nact), out_shape=(...  3.4 us
    ppermute x1, waiting for transfers between devices, body(): theirs = lax.ppermute(mine, 'cores', flip)  3.07 us
    pallas_call x1, Pallas kernels, ahead(): pl.pallas_call(ahead_kernel, out_shape=(jax.ShapeDtypeStruct((feats, rows...  1.31 us
    ppermute x3, waiting for transfers between devices, shift(): lax.ppermute(array, 'hst', [(at, (at + 2 * by) % 8) for at in range(8)])  1.3 us
  transfers between devices with their start and end apart: 14, of which 6 were waited for; matrix products, arithmetic and copies ran while one was open for 0% of the time, Pallas kernels for 24%

profile of v14, /device:TPU:0, one launch (start us, length us, event | category | flops | bytes accessed | tf_op | source)
XLA Modules:
  0.0 46.1 jit_solution(13415041833899742770)
XLA Ops:
  0.7 3.0 %collective-permute-start.4 = (bf16[256,512]{1,0:T(8,128)(2,1)}, bf16[256,512]{1,0:T(8,128)(2,1)S(1)}, u32[]{:S(2)}, u32[]{:S(2)}) collective-permute-start(bf16[256,512]{1,0:T(8,128)(2,1)} %bitcast.11), channel_id=1, source_target_pairs={{0,2},{2,0},{4,6},{6,4},{8,10},{10,8},{12,14},{14,12},{1,3},{3,1},... | collective-permute-start | bytes 786440 | tf_op jit(solution)/shard_map/own_y/ppermute | solution.py:401
  3.7 1.6 %collective-permute-start = (bf16[256,512]{1,0:T(8,128)(2,1)}, bf16[256,512]{1,0:T(8,128)(2,1)S(1)}, u32[]{:S(2)}, u32[]{:S(2)}) collective-permute-start(bf16[256,512]{1,0:T(8,128)(2,1)} %bitcast.12), channel_id=1, source_target_pairs={{0,4},{2,6},{4,8},{6,10},{8,12},{10,14},{12,0},{14,2},{1,5},{3,7},... | collective-permute-start | bytes 786440 | tf_op jit(solution)/shard_map/one/ppermute | solution.py:405
  5.3 0.5 %collective-permute-start.6 = (s32[16]{0:T(128)}, s32[16]{0:T(128)S(1)}, u32[]{:S(2)}, u32[]{:S(2)}) collective-permute-start(s32[16]{0:T(128)} %param.18), channel_id=1, source_target_pairs={{0,1},{1,0},{2,3},{3,2},{4,5},{5,4},{6,7},{7,6},{8,9},{9,8},{10,11... | collective-permute-start | bytes 200 | tf_op jit(solution)/shard_map/ppermute | solution.py:455
  5.8 0.7 %collective-permute-done.5 = s32[16]{0:T(128)S(1)} collective-permute-done((s32[16]{0:T(128)}, s32[16]{0:T(128)S(1)}, u32[]{:S(2)}, u32[]{:S(2)}) %collective-permute-start.5) | collective-permute-done | bytes 96 | tf_op jit(solution)/shard_map/ppermute | solution.py:455
  6.6 0.2 collective-permute-done.6
  6.8 0.0 copy-start
  6.8 0.0 copy-start.1
  6.8 0.0 copy-start.2
  6.9 0.8 %side.1 = f32[8,256]{1,0:T(8,128)S(1)} custom-call(s32[1,16]{1,0:T(1,128)S(1)} %bitcast.17, s32[1,16]{1,0:T(1,128)S(1)} %bitcast.18, s32[1,16]{1,0:T(1,128)S(1)} %bitcast.19, s32[1,16]{1,0:T(1,128)S(1)} %bitcast.20, s32[16,16]{1,0:T(8,128)S(1)} %copy-done.9, f32[16,16]{1,0:T(8,128)S(1)} %copy-done.10, bf16[512,1024]{1,0:T(8,128)(2,1)S(1)} %copy-done.4, ...), custom_call_target="tpu_custom_call" | custom-call | flops 1430000000 | tf_op jit(solution)/shard_map/side/pallas_call | solution.py:101
  7.6 2.3 %collective-permute-start.9 = (f32[8,256]{1,0:T(8,128)S(1)}, f32[8,256]{1,0:T(8,128)S(1)}, u32[]{:S(2)}, u32[]{:S(2)}) collective-permute-start(f32[8,256]{1,0:T(8,128)S(1)} %side.1), channel_id=1, source_target_pairs={{0,12},{2,14},{4,8},{6,10},{8,4},{10,6},{12,0},{14,2},{1,13},{3,15... | collective-permute-start | bytes 24584 | tf_op jit(solution)/shard_map/side_z/ppermute | solution.py:401
  9.9 0.8 %collective-permute-start.8 = (f32[8,256]{1,0:T(8,128)S(1)}, f32[8,256]{1,0:T(8,128)S(1)}, u32[]{:S(2)}, u32[]{:S(2)}) collective-permute-start(f32[8,256]{1,0:T(8,128)S(1)} %side.1), channel_id=1, source_target_pairs={{0,8},{2,10},{4,12},{6,14},{8,0},{10,2},{12,4},{14,6},{1,9},{3,11}... | collective-permute-start | bytes 24584 | tf_op jit(solution)/shard_map/side_z/ppermute | solution.py:401
  10.7 1.3 %collective-permute-start.7 = (f32[8,256]{1,0:T(8,128)S(1)}, f32[8,256]{1,0:T(8,128)S(1)}, u32[]{:S(2)}, u32[]{:S(2)}) collective-permute-start(f32[8,256]{1,0:T(8,128)S(1)} %side.1), channel_id=1, source_target_pairs={{0,4},{2,6},{4,0},{6,2},{8,12},{10,14},{12,8},{14,10},{1,5},{3,7},... | collective-permute-start | bytes 24584 | tf_op jit(solution)/shard_map/side_z/ppermute | solution.py:401
  12.1 0.5 %convert.1 = (bf16[1024,512]{1,0:T(8,128)(2,1)S(1)}, bf16[1024,144]{1,0:T(8,128)(2,1)S(1)}, bf16[144,1024]{1,0:T(8,128)(2,1)S(1)}) custom-call(f32[512,1024]{1,0:T(8,128)S(1)} %copy-done, f32[1024,128]{1,0:T(8,128)S(1)} %copy-done.1, f32[1,1024]{1,0:T(1,128)S(1)} %bitcast.9), custom_call_target="tpu_custom_call" | custom-call | flops 660000000 | tf_op jit(solution)/shard_map/convert/pallas_call | solution.py:131
  12.6 1.3 %collective-permute-done.refs_2_ = bf16[256,512]{1,0:T(8,128)(2,1)S(1)} collective-permute-done((bf16[256,512]{1,0:T(8,128)(2,1)}, bf16[256,512]{1,0:T(8,128)(2,1)S(1)}, u32[]{:S(2)}, u32[]{:S(2)}) %collective-permute-start) | collective-permute-done | bytes 262176 | tf_op jit(solution)/shard_map/one/ppermute | solution.py:405
  13.9 1.7 %collective-permute-start.3 = (bf16[256,512]{1,0:T(8,128)(2,1)S(1)}, bf16[256,512]{1,0:T(8,128)(2,1)S(1)}, u32[]{:S(2)}, u32[]{:S(2)}) collective-permute-start(bf16[256,512]{1,0:T(8,128)(2,1)S(1)} %bitcast.14), channel_id=1, source_target_pairs={{0,12},{2,14},{4,0},{6,2},{8,4},{10,6},{12,8},{14,10},{1,13},{3,15... | collective-permute-start | bytes 786440 | tf_op jit(solution)/shard_map/three/ppermute | solution.py:405
  15.6 0.5 %collective-permute-start.2 = (bf16[256,512]{1,0:T(8,128)(2,1)S(1)}, bf16[256,512]{1,0:T(8,128)(2,1)S(1)}, u32[]{:S(2)}, u32[]{:S(2)}) collective-permute-start(bf16[256,512]{1,0:T(8,128)(2,1)S(1)} %collective-permute-done.refs_2_), channel_id=1, source_target_pairs={{0,2},{2,0},{4,6},{6,4},{8,10},{10,8},{12,14},{14,12},{1,3},{3,1},... | collective-permute-start | bytes 786440 | tf_op jit(solution)/shard_map/one_y/ppermute | solution.py:401
  16.1 1.6 %collective-permute-start.10 = (f32[32,256]{1,0:T(8,128)S(1)}, f32[32,256]{1,0:T(8,128)S(1)}, u32[]{:S(2)}, u32[]{:S(2)}) collective-permute-start(f32[32,256]{1,0:T(8,128)S(1)} %pad_maximum_fusion.refs_3_), channel_id=1, source_target_pairs={{0,2},{2,0},{4,6},{6,4},{8,10},{10,8},{12,14},{14,12},{1,3},{3,1},... | collective-permute-start | bytes 98312 | tf_op jit(solution)/shard_map/side_y/ppermute | solution.py:401
  17.7 0.3 collective-permute-start.1
  18.0 1.3 %ahead.1 = (bf16[512,768]{1,0:T(8,128)(2,1)S(1)}, bf16[1024,768]{1,0:T(8,128)(2,1)S(1)}, f32[144,768]{1,0:T(8,128)S(1)}) custom-call(bf16[256,512]{1,0:T(8,128)(2,1)S(1)} %bitcast.15, bf16[256,512]{1,0:T(8,128)(2,1)S(1)} %collective-permute-done.4.refs_1_, bf16[256,512]{1,0:T(8,128)(2,1)S(1)} %collective-permute-done.refs_2_, ...), custom_call_target="tpu_custom_call" | custom-call | flops 1760000000 | tf_op jit(solution)/shard_map/ahead/pallas_call | solution.py:254
  19.3 3.7 %collective-permute-done.10.refs_4_ = f32[32,256]{1,0:T(8,128)S(1)} collective-permute-done((f32[32,256]{1,0:T(8,128)S(1)}, f32[32,256]{1,0:T(8,128)S(1)}, u32[]{:S(2)}, u32[]{:S(2)}) %collective-permute-start.10) | collective-permute-done | bytes 32800 | tf_op jit(solution)/shard_map/side_y/ppermute | solution.py:401
  23.0 2.6 %first.1 = (f32[656,1024]{1,0:T(8,128)S(1)}, f32[656,1024]{1,0:T(8,128)S(1)}, f32[16,128]{1,0:T(8,128)S(1)}, f32[64,256]{1,0:T(8,128)S(1)}) custom-call(bf16[512,768]{1,0:T(8,128)(2,1)S(1)} %get-tuple-element.41.refs_0_, bf16[1024,768]{1,0:T(8,128)(2,1)S(1)} %get-tuple-element.42.refs_1_, f32[144,768]{1,0:T(8,128)S(1)} %get-tuple-element.43.refs_2_, ...), custom_call_target="tpu_custom_call" | custom-call | flops 990000000 | tf_op jit(solution)/shard_map/first/pallas_call | solution.py:344
  25.6 0.4 collective-permute-start.12
  25.9 2.9 %second.1 = (f32[656,1024]{1,0:T(8,128)S(1)}, f32[656,1024]{1,0:T(8,128)S(1)}) custom-call(bf16[256,512]{1,0:T(8,128)(2,1)S(1)} %collective-permute-done.2.refs_0_, bf16[256,512]{1,0:T(8,128)(2,1)S(1)} %collective-permute-done.3.refs_1_, f32[64,256]{1,0:T(8,128)S(1)} %get-tuple-element.46.refs_2_.refs_1_, f32[16,128]{1,0:T(8,128)S(1)} %get-tuple-element.47.refs_3_.refs_2_, ...), custom_call_target="tpu_custom_call" | custom-call | flops 660000000 | tf_op jit(solution)/shard_map/second/pallas_call | solution.py:344
  28.8 1.8 %collective-permute-start.11 = (bf16[256,512]{1,0:T(8,128)(2,1)S(1)}, bf16[256,512]{1,0:T(8,128)(2,1)S(1)}, u32[]{:S(2)}, u32[]{:S(2)}) collective-permute-start(bf16[256,512]{1,0:T(8,128)(2,1)S(1)} %collective-permute-done.1.refs_1_), channel_id=1, source_target_pairs={{0,2},{2,0},{4,6},{6,4},{8,10},{10,8},{12,14},{14,12},{1,3},{3,1},... | collective-permute-start | bytes 786440 | tf_op jit(solution)/shard_map/two_y/ppermute | solution.py:401
  30.6 3.8 %collective-permute-done.12.refs_0_ = bf16[256,512]{1,0:T(8,128)(2,1)S(1)} collective-permute-done((bf16[256,512]{1,0:T(8,128)(2,1)S(1)}, bf16[256,512]{1,0:T(8,128)(2,1)S(1)}, u32[]{:S(2)}, u32[]{:S(2)}) %collective-permute-start.12) | collective-permute-done | bytes 262176 | tf_op jit(solution)/shard_map/three_y/ppermute | solution.py:401
  34.4 3.0 %third.1 = (f32[656,1024]{1,0:T(8,128)S(1)}, f32[656,1024]{1,0:T(8,128)S(1)}) custom-call(bf16[256,512]{1,0:T(8,128)(2,1)S(1)} %collective-permute-done.12.refs_0_, bf16[256,512]{1,0:T(8,128)(2,1)S(1)} %collective-permute-done.1.refs_1_, f32[64,256]{1,0:T(8,128)S(1)} %get-tuple-element.46.refs_2_.refs_1_, f32[16,128]{1,0:T(8,128)S(1)} %get-tuple-element.47.refs_3_.refs_2_, ...), custom_call_target="tpu_custom_call" | custom-call | flops 660000000 | tf_op jit(solution)/shard_map/third/pallas_call | solution.py:344
  37.4 0.0 copy-start.3
  37.4 0.0 copy-start.5
  37.4 2.1 %fourth.1.mine = bf16[656,1024]{1,0:T(8,128)(2,1)S(1)} custom-call(bf16[256,512]{1,0:T(8,128)(2,1)S(1)} %collective-permute-done.11.refs_0_, f32[64,256]{1,0:T(8,128)S(1)} %get-tuple-element.46.refs_2_.refs_1_, f32[16,128]{1,0:T(8,128)S(1)} %get-tuple-element.47.refs_3_.refs_2_, f32[656,1024]{1,0:T(8,128)S(1)} %get-tuple-element.53.refs_3_, ...), custom_call_target="tpu_custom_call" | custom-call | flops 330000000 | tf_op jit(solution)/shard_map/fourth/pallas_call | solution.py:344
  39.5 0.1 collective-permute-start.13
  39.6 3.1 %collective-permute-done.13.theirs = bf16[656,1024]{1,0:T(8,128)(2,1)S(1)} collective-permute-done((bf16[656,1024]{1,0:T(8,128)(2,1)S(1)}, bf16[656,1024]{1,0:T(8,128)(2,1)S(1)}, u32[]{:S(2)}, u32[]{:S(2)}) %collective-permute-start.13) | collective-permute-done | bytes 1343520 | tf_op jit(solution)/shard_map/ppermute | solution.py:465
  42.7 3.4 %update.1 = (bf16[256,128]{1,0:T(8,128)(2,1)}, f32[512,1024]{1,0:T(8,128)}, f32[1024,128]{1,0:T(8,128)}, f32[1,1024]{1,0:T(1,128)}, f32[512,1024]{1,0:T(8,128)}, /*index=5*/f32[1024,128]{1,0:T(8,128)}, f32[1,1024]{1,0:T(1,128)}) custom-call(bf16[656,1024]{1,0:T(8,128)(2,1)S(1)} %fourth.1.mine, bf16[656,1024]{1,0:T(8,128)(2,1)S(1)} %collective-permute-done.13.theirs, ...), custom_call_target="tpu_custom_call" | custom-call | flops 3740000000 | tf_op jit(solution)/shard_map/update/pallas_call | solution.py:387
  (34 shorter events, 0.1 us)
Async XLA Ops:
  0.6 6.1 %copy-start.4 = (bf16[512,1024]{1,0:T(8,128)(2,1)S(1)}, bf16[512,1024]{1,0:T(8,128)(2,1)}, u32[]{:S(2)}) copy-start(bf16[512,1024]{1,0:T(8,128)(2,1)} %actor_embed.1) | copy-start | bytes 3145732
  0.6 6.1 %copy-start.6 = (bf16[1024,128]{1,0:T(8,128)(2,1)S(1)}, bf16[1024,128]{1,0:T(8,128)(2,1)}, u32[]{:S(2)}) copy-start(bf16[1024,128]{1,0:T(8,128)(2,1)} %actor_policy.1) | copy-start | bytes 786436
  0.7 6.1 %copy-start.7 = (bf16[16,16,512]{2,1,0:T(8,128)(2,1)S(1)}, bf16[16,16,512]{2,1,0:T(8,128)(2,1)}, u32[]{:S(2)}) copy-start(bf16[16,16,512]{2,1,0:T(8,128)(2,1)} %param.14) | copy-start | bytes 786436
  0.7 6.1 %copy-start.9 = (s32[16,16]{1,0:T(8,128)S(1)}, s32[16,16]{1,0:T(8,128)}, u32[]{:S(2)}) copy-start(s32[16,16]{1,0:T(8,128)} %actions.1) | copy-start | bytes 3076
  0.7 6.1 %copy-start.10 = (f32[16,16]{1,0:T(8,128)S(1)}, f32[16,16]{1,0:T(8,128)}, u32[]{:S(2)}) copy-start(f32[16,16]{1,0:T(8,128)} %rewards.1) | copy-start | bytes 3076
  0.7 6.1 %copy-start.12 = (s32[16]{0:T(128)S(1)}, s32[16]{0:T(128)}, u32[]{:S(2)}) copy-start(s32[16]{0:T(128)} %param.15) | copy-start | bytes 196
  0.7 6.1 %copy-start.13 = (s32[16]{0:T(128)S(1)}, s32[16]{0:T(128)}, u32[]{:S(2)}) copy-start(s32[16]{0:T(128)} %param.18) | copy-start | bytes 196
  0.7 17.3 %collective-permute-start.4 = (bf16[256,512]{1,0:T(8,128)(2,1)}, bf16[256,512]{1,0:T(8,128)(2,1)S(1)}, u32[]{:S(2)}, u32[]{:S(2)}) collective-permute-start(bf16[256,512]{1,0:T(8,128)(2,1)} %bitcast.11), channel_id=1, source_target_pairs={{0,2},{2,0},{4,6},{6,4},{8,10},{10,8},{12,14},{14,12},{1,3},{3,1},... | collective-permute-start | bytes 786440 | tf_op jit(solution)/shard_map/own_y/ppermute | solution.py:401
  3.7 10.1 %collective-permute-start = (bf16[256,512]{1,0:T(8,128)(2,1)}, bf16[256,512]{1,0:T(8,128)(2,1)S(1)}, u32[]{:S(2)}, u32[]{:S(2)}) collective-permute-start(bf16[256,512]{1,0:T(8,128)(2,1)} %bitcast.12), channel_id=1, source_target_pairs={{0,4},{2,6},{4,8},{6,10},{8,12},{10,14},{12,0},{14,2},{1,5},{3,7},... | collective-permute-start | bytes 786440 | tf_op jit(solution)/shard_map/one/ppermute | solution.py:405
  5.3 1.3 %collective-permute-start.5 = (s32[16]{0:T(128)}, s32[16]{0:T(128)S(1)}, u32[]{:S(2)}, u32[]{:S(2)}) collective-permute-start(s32[16]{0:T(128)} %param.15), channel_id=1, source_target_pairs={{0,1},{1,0},{2,3},{3,2},{4,5},{5,4},{6,7},{7,6},{8,9},{9,8},{10,11... | collective-permute-start | bytes 200 | tf_op jit(solution)/shard_map/ppermute | solution.py:455
  5.3 1.5 %collective-permute-start.6 = (s32[16]{0:T(128)}, s32[16]{0:T(128)S(1)}, u32[]{:S(2)}, u32[]{:S(2)}) collective-permute-start(s32[16]{0:T(128)} %param.18), channel_id=1, source_target_pairs={{0,1},{1,0},{2,3},{3,2},{4,5},{5,4},{6,7},{7,6},{8,9},{9,8},{10,11... | collective-permute-start | bytes 200 | tf_op jit(solution)/shard_map/ppermute | solution.py:455
  6.8 5.2 %copy-start = (f32[512,1024]{1,0:T(8,128)S(1)}, f32[512,1024]{1,0:T(8,128)}, u32[]{:S(2)}) copy-start(f32[512,1024]{1,0:T(8,128)} %master_embed.3) | copy-start | bytes 6291460
  6.8 5.2 %copy-start.1 = (f32[1024,128]{1,0:T(8,128)S(1)}, f32[1024,128]{1,0:T(8,128)}, u32[]{:S(2)}) copy-start(f32[1024,128]{1,0:T(8,128)} %master_policy.3) | copy-start | bytes 1572868
  6.8 5.2 %copy-start.2 = (f32[1024]{0:T(1024)S(1)}, f32[1024]{0:T(1024)}, u32[]{:S(2)}) copy-start(f32[1024]{0:T(1024)} %param.23) | copy-start | bytes 12292
  7.6 8.0 %collective-permute-start.9 = (f32[8,256]{1,0:T(8,128)S(1)}, f32[8,256]{1,0:T(8,128)S(1)}, u32[]{:S(2)}, u32[]{:S(2)}) collective-permute-start(f32[8,256]{1,0:T(8,128)S(1)} %side.1), channel_id=1, source_target_pairs={{0,12},{2,14},{4,8},{6,10},{8,4},{10,6},{12,0},{14,2},{1,13},{3,15... | collective-permute-start | bytes 24584 | tf_op jit(solution)/shard_map/side_z/ppermute | solution.py:401
  9.9 6.2 %collective-permute-start.8 = (f32[8,256]{1,0:T(8,128)S(1)}, f32[8,256]{1,0:T(8,128)S(1)}, u32[]{:S(2)}, u32[]{:S(2)}) collective-permute-start(f32[8,256]{1,0:T(8,128)S(1)} %side.1), channel_id=1, source_target_pairs={{0,8},{2,10},{4,12},{6,14},{8,0},{10,2},{12,4},{14,6},{1,9},{3,11}... | collective-permute-start | bytes 24584 | tf_op jit(solution)/shard_map/side_z/ppermute | solution.py:401
  10.7 5.4 %collective-permute-start.7 = (f32[8,256]{1,0:T(8,128)S(1)}, f32[8,256]{1,0:T(8,128)S(1)}, u32[]{:S(2)}, u32[]{:S(2)}) collective-permute-start(f32[8,256]{1,0:T(8,128)S(1)} %side.1), channel_id=1, source_target_pairs={{0,4},{2,6},{4,0},{6,2},{8,12},{10,14},{12,8},{14,10},{1,5},{3,7},... | collective-permute-start | bytes 24584 | tf_op jit(solution)/shard_map/side_z/ppermute | solution.py:401
  13.9 11.7 %collective-permute-start.3 = (bf16[256,512]{1,0:T(8,128)(2,1)S(1)}, bf16[256,512]{1,0:T(8,128)(2,1)S(1)}, u32[]{:S(2)}, u32[]{:S(2)}) collective-permute-start(bf16[256,512]{1,0:T(8,128)(2,1)S(1)} %bitcast.14), channel_id=1, source_target_pairs={{0,12},{2,14},{4,0},{6,2},{8,4},{10,6},{12,8},{14,10},{1,13},{3,15... | collective-permute-start | bytes 786440 | tf_op jit(solution)/shard_map/three/ppermute | solution.py:405
  15.6 10.4 %collective-permute-start.2 = (bf16[256,512]{1,0:T(8,128)(2,1)S(1)}, bf16[256,512]{1,0:T(8,128)(2,1)S(1)}, u32[]{:S(2)}, u32[]{:S(2)}) collective-permute-start(bf16[256,512]{1,0:T(8,128)(2,1)S(1)} %collective-permute-done.refs_2_), channel_id=1, source_target_pairs={{0,2},{2,0},{4,6},{6,4},{8,10},{10,8},{12,14},{14,12},{1,3},{3,1},... | collective-permute-start | bytes 786440 | tf_op jit(solution)/shard_map/one_y/ppermute | solution.py:401
  16.1 6.9 %collective-permute-start.10 = (f32[32,256]{1,0:T(8,128)S(1)}, f32[32,256]{1,0:T(8,128)S(1)}, u32[]{:S(2)}, u32[]{:S(2)}) collective-permute-start(f32[32,256]{1,0:T(8,128)S(1)} %pad_maximum_fusion.refs_3_), channel_id=1, source_target_pairs={{0,2},{2,0},{4,6},{6,4},{8,10},{10,8},{12,14},{14,12},{1,3},{3,1},... | collective-permute-start | bytes 98312 | tf_op jit(solution)/shard_map/side_y/ppermute | solution.py:401
  17.7 11.1 %collective-permute-start.1 = (bf16[256,512]{1,0:T(8,128)(2,1)S(1)}, bf16[256,512]{1,0:T(8,128)(2,1)S(1)}, u32[]{:S(2)}, u32[]{:S(2)}) collective-permute-start(bf16[256,512]{1,0:T(8,128)(2,1)S(1)} %collective-permute-done.refs_2_), channel_id=1, source_target_pairs={{0,4},{2,6},{4,8},{6,10},{8,12},{10,14},{12,0},{14,2},{1,5},{3,7},... | collective-permute-start | bytes 786440 | tf_op jit(solution)/shard_map/two/ppermute | solution.py:405
  25.6 8.8 %collective-permute-start.12 = (bf16[256,512]{1,0:T(8,128)(2,1)S(1)}, bf16[256,512]{1,0:T(8,128)(2,1)S(1)}, u32[]{:S(2)}, u32[]{:S(2)}) collective-permute-start(bf16[256,512]{1,0:T(8,128)(2,1)S(1)} %collective-permute-done.3.refs_1_), channel_id=1, source_target_pairs={{0,2},{2,0},{4,6},{6,4},{8,10},{10,8},{12,14},{14,12},{1,3},{3,1},... | collective-permute-start | bytes 786440 | tf_op jit(solution)/shard_map/three_y/ppermute | solution.py:401
  28.8 8.5 %collective-permute-start.11 = (bf16[256,512]{1,0:T(8,128)(2,1)S(1)}, bf16[256,512]{1,0:T(8,128)(2,1)S(1)}, u32[]{:S(2)}, u32[]{:S(2)}) collective-permute-start(bf16[256,512]{1,0:T(8,128)(2,1)S(1)} %collective-permute-done.1.refs_1_), channel_id=1, source_target_pairs={{0,2},{2,0},{4,6},{6,4},{8,10},{10,8},{12,14},{14,12},{1,3},{3,1},... | collective-permute-start | bytes 786440 | tf_op jit(solution)/shard_map/two_y/ppermute | solution.py:401
  37.4 5.3 %copy-start.3 = (f32[512,1024]{1,0:T(8,128)S(1)}, f32[512,1024]{1,0:T(8,128)}, u32[]{:S(2)}) copy-start(f32[512,1024]{1,0:T(8,128)} %embed_moment.1) | copy-start | bytes 6291460
  37.4 5.3 %copy-start.5 = (f32[1024,128]{1,0:T(8,128)S(1)}, f32[1024,128]{1,0:T(8,128)}, u32[]{:S(2)}) copy-start(f32[1024,128]{1,0:T(8,128)} %policy_moment.1) | copy-start | bytes 1572868
  37.4 5.3 %copy-start.8 = (bf16[256,512]{1,0:T(8,128)(2,1)S(1)}, bf16[256,512]{1,0:T(8,128)(2,1)}, u32[]{:S(2)}) copy-start(bf16[256,512]{1,0:T(8,128)(2,1)} %next_obs.1) | copy-start | bytes 786436
  37.4 5.3 %copy-start.11 = (f32[1024]{0:T(1024)S(1)}, f32[1024]{0:T(1024)}, u32[]{:S(2)}) copy-start(f32[1024]{0:T(1024)} %param.26) | copy-start | bytes 12292
  39.5 3.1 %collective-permute-start.13 = (bf16[656,1024]{1,0:T(8,128)(2,1)S(1)}, bf16[656,1024]{1,0:T(8,128)(2,1)S(1)}, u32[]{:S(2)}, u32[]{:S(2)}) collective-permute-start(bf16[656,1024]{1,0:T(8,128)(2,1)S(1)} %fourth.1.mine), channel_id=1, source_target_pairs={{0,1},{1,0},{2,3},{3,2},{4,5},{5,4},{6,7},{7,6},{8,9},{9,8},{10,11... | collective-permute-start | bytes 4030472 | tf_op jit(solution)/shard_map/ppermute | solution.py:465

commit v15 on v14

--- a/solution.py
+++ b/solution.py
@@ -352,7 +352,7 @@
             pltpu.VMEM((width, rows), BF16),
         ],
         compiler_params=params(32),
-        cost_estimate=cost(0.3 * blocks),
+        cost_estimate=cost(0.6 * blocks),
         name=name,
     )(*args, *mats)
 
@@ -409,7 +409,7 @@
     pieces = [side] + [exchange(side, 2 * mask, "side_z") for mask in (1, 2, 3)]
     line = jnp.concatenate(pieces, axis=0)
     line, _ = lax.optimization_barrier((line, side))
-    again, _ = lax.optimization_barrier((own, one))
+    again, _ = lax.optimization_barrier((own, side))
     line_y = exchange(line, 1, "side_y")
     three = shift(again, -1, "three")
     one_y = exchange(one, 1, "one_y")

time: 46.2 us -> 44.8 us (0.970)
  the two profiles are of different devices: /device:TPU:0 before, /device:TPU:9 now
where the time goes in v15:
time: 44.8 us; the launch traced here: 44.6 us
  Pallas kernels  16.5 us (37%)
  starting transfers between devices  15.5 us (35%)
  waiting for transfers between devices  11.8 us (26%)
  between operations  0.82 us (2%)
    pallas_call x4, Pallas kernels, call(): pl.pallas_call(functools.partial(kernel, slots), out_shape=outs, in_specs...  10.5 us
    ppermute x8, starting transfers between devices, exchange(): return lax.ppermute(array, 'hst', [(at, at ^ mask) for at in range(8)])  5.94 us
    ppermute x1, starting transfers between devices, body(): theirs = lax.ppermute(mine, 'cores', flip)  5.54 us
    ppermute x8, waiting for transfers between devices, exchange(): return lax.ppermute(array, 'hst', [(at, at ^ mask) for at in range(8)])  5.23 us
    pallas_call x1, Pallas kernels, update(): pl.pallas_call(functools.partial(update_kernel, feats, nact), out_shape=(...  3.4 us
    ppermute x3, starting transfers between devices, shift(): lax.ppermute(array, 'hst', [(at, (at + 2 * by) % 8) for at in range(8)])  2.75 us
    ppermute x1, waiting for transfers between devices, body(): theirs = lax.ppermute(mine, 'cores', flip)  2.71 us
    ppermute x3, waiting for transfers between devices, shift(): lax.ppermute(array, 'hst', [(at, (at + 2 * by) % 8) for at in range(8)])  2.61 us
  transfers between devices with their start and end apart: 14, of which 8 were waited for; matrix products, arithmetic and copies ran while one was open for 0% of the time, Pallas kernels for 25%

profile of v15, /device:TPU:9, one launch (start us, length us, event | category | flops | bytes accessed | tf_op | source)
XLA Modules:
  0.0 44.6 jit_solution(11231486859464612298)
XLA Ops:
  0.7 1.3 %collective-permute-start.6 = (bf16[256,512]{1,0:T(8,128)(2,1)}, bf16[256,512]{1,0:T(8,128)(2,1)S(1)}, u32[]{:S(2)}, u32[]{:S(2)}) collective-permute-start(bf16[256,512]{1,0:T(8,128)(2,1)} %bitcast.11), channel_id=1, source_target_pairs={{0,2},{2,0},{4,6},{6,4},{8,10},{10,8},{12,14},{14,12},{1,3},{3,1},... | collective-permute-start | bytes 786440 | tf_op jit(solution)/shard_map/own_y/ppermute | solution.py:401
  2.0 1.3 %collective-permute-start = (bf16[256,512]{1,0:T(8,128)(2,1)}, bf16[256,512]{1,0:T(8,128)(2,1)S(1)}, u32[]{:S(2)}, u32[]{:S(2)}) collective-permute-start(bf16[256,512]{1,0:T(8,128)(2,1)} %bitcast.12), channel_id=1, source_target_pairs={{0,4},{2,6},{4,8},{6,10},{8,12},{10,14},{12,0},{14,2},{1,5},{3,7},... | collective-permute-start | bytes 786440 | tf_op jit(solution)/shard_map/one/ppermute | solution.py:405
  3.3 1.2 %collective-permute-start.3 = (s32[16]{0:T(128)}, s32[16]{0:T(128)S(1)}, u32[]{:S(2)}, u32[]{:S(2)}) collective-permute-start(s32[16]{0:T(128)} %param.15), channel_id=1, source_target_pairs={{0,1},{1,0},{2,3},{3,2},{4,5},{5,4},{6,7},{7,6},{8,9},{9,8},{10,11... | collective-permute-start | bytes 200 | tf_op jit(solution)/shard_map/ppermute | solution.py:455
  4.6 0.9 %collective-permute-done.3 = s32[16]{0:T(128)S(1)} collective-permute-done((s32[16]{0:T(128)}, s32[16]{0:T(128)S(1)}, u32[]{:S(2)}, u32[]{:S(2)}) %collective-permute-start.3) | collective-permute-done | bytes 96 | tf_op jit(solution)/shard_map/ppermute | solution.py:455
  5.5 0.3 collective-permute-done.4
  5.8 0.0 copy-start
  5.9 0.0 copy-start.1
  5.9 0.0 copy-start.2
  5.9 0.8 %side.1 = f32[8,256]{1,0:T(8,128)S(1)} custom-call(s32[1,16]{1,0:T(1,128)S(1)} %bitcast.17, s32[1,16]{1,0:T(1,128)S(1)} %bitcast.18, s32[1,16]{1,0:T(1,128)S(1)} %bitcast.19, s32[1,16]{1,0:T(1,128)S(1)} %bitcast.20, s32[16,16]{1,0:T(8,128)S(1)} %copy-done.9, f32[16,16]{1,0:T(8,128)S(1)} %copy-done.10, bf16[512,1024]{1,0:T(8,128)(2,1)S(1)} %copy-done.4, ...), custom_call_target="tpu_custom_call" | custom-call | flops 1430000000 | tf_op jit(solution)/shard_map/side/pallas_call | solution.py:101
  6.6 1.4 %collective-permute-start.9 = (f32[8,256]{1,0:T(8,128)S(1)}, f32[8,256]{1,0:T(8,128)S(1)}, u32[]{:S(2)}, u32[]{:S(2)}) collective-permute-start(f32[8,256]{1,0:T(8,128)S(1)} %side.1), channel_id=1, source_target_pairs={{0,12},{2,14},{4,8},{6,10},{8,4},{10,6},{12,0},{14,2},{1,13},{3,15... | collective-permute-start | bytes 24584 | tf_op jit(solution)/shard_map/side_z/ppermute | solution.py:401
  8.0 1.0 %collective-permute-start.8 = (f32[8,256]{1,0:T(8,128)S(1)}, f32[8,256]{1,0:T(8,128)S(1)}, u32[]{:S(2)}, u32[]{:S(2)}) collective-permute-start(f32[8,256]{1,0:T(8,128)S(1)} %side.1), channel_id=1, source_target_pairs={{0,8},{2,10},{4,12},{6,14},{8,0},{10,2},{12,4},{14,6},{1,9},{3,11}... | collective-permute-start | bytes 24584 | tf_op jit(solution)/shard_map/side_z/ppermute | solution.py:401
  9.0 0.4 collective-permute-start.7
  9.4 0.5 %convert.1 = (bf16[1024,512]{1,0:T(8,128)(2,1)S(1)}, bf16[1024,144]{1,0:T(8,128)(2,1)S(1)}, bf16[144,1024]{1,0:T(8,128)(2,1)S(1)}) custom-call(f32[512,1024]{1,0:T(8,128)S(1)} %copy-done, f32[1024,128]{1,0:T(8,128)S(1)} %copy-done.1, f32[1,1024]{1,0:T(1,128)S(1)} %bitcast.9), custom_call_target="tpu_custom_call" | custom-call | flops 660000000 | tf_op jit(solution)/shard_map/convert/pallas_call | solution.py:131
  9.9 1.9 %collective-permute-done.9 = f32[8,256]{1,0:T(8,128)S(1)} collective-permute-done((f32[8,256]{1,0:T(8,128)S(1)}, f32[8,256]{1,0:T(8,128)S(1)}, u32[]{:S(2)}, u32[]{:S(2)}) %collective-permute-start.9) | collective-permute-done | bytes 8224 | tf_op jit(solution)/shard_map/side_z/ppermute | solution.py:401
  11.8 0.3 collective-permute-start.10
  12.1 1.2 %collective-permute-start.2 = (bf16[256,512]{1,0:T(8,128)(2,1)S(1)}, bf16[256,512]{1,0:T(8,128)(2,1)S(1)}, u32[]{:S(2)}, u32[]{:S(2)}) collective-permute-start(bf16[256,512]{1,0:T(8,128)(2,1)S(1)} %collective-permute-done.refs_2_), channel_id=1, source_target_pairs={{0,2},{2,0},{4,6},{6,4},{8,10},{10,8},{12,14},{14,12},{1,3},{3,1},... | collective-permute-start | bytes 786440 | tf_op jit(solution)/shard_map/one_y/ppermute | solution.py:401
  13.4 1.5 %collective-permute-start.1 = (bf16[256,512]{1,0:T(8,128)(2,1)S(1)}, bf16[256,512]{1,0:T(8,128)(2,1)S(1)}, u32[]{:S(2)}, u32[]{:S(2)}) collective-permute-start(bf16[256,512]{1,0:T(8,128)(2,1)S(1)} %collective-permute-done.refs_2_), channel_id=1, source_target_pairs={{0,4},{2,6},{4,8},{6,10},{8,12},{10,14},{12,0},{14,2},{1,5},{3,7},... | collective-permute-start | bytes 786440 | tf_op jit(solution)/shard_map/two/ppermute | solution.py:405
  14.8 0.0 collective-permute-done.6.refs_1_
  14.8 1.3 %ahead.1 = (bf16[512,768]{1,0:T(8,128)(2,1)S(1)}, bf16[1024,768]{1,0:T(8,128)(2,1)S(1)}, f32[144,768]{1,0:T(8,128)S(1)}) custom-call(bf16[256,512]{1,0:T(8,128)(2,1)S(1)} %bitcast.15, bf16[256,512]{1,0:T(8,128)(2,1)S(1)} %collective-permute-done.6.refs_1_, bf16[256,512]{1,0:T(8,128)(2,1)S(1)} %collective-permute-done.refs_2_, ...), custom_call_target="tpu_custom_call" | custom-call | flops 1760000000 | tf_op jit(solution)/shard_map/ahead/pallas_call | solution.py:254
  16.1 2.6 %first.1 = (f32[656,1024]{1,0:T(8,128)S(1)}, f32[656,1024]{1,0:T(8,128)S(1)}, f32[16,128]{1,0:T(8,128)S(1)}, f32[64,256]{1,0:T(8,128)S(1)}) custom-call(bf16[512,768]{1,0:T(8,128)(2,1)S(1)} %get-tuple-element.41.refs_0_, bf16[1024,768]{1,0:T(8,128)(2,1)S(1)} %get-tuple-element.42.refs_1_, f32[144,768]{1,0:T(8,128)S(1)} %get-tuple-element.43.refs_2_, ...), custom_call_target="tpu_custom_call" | custom-call | flops 1980000000 | tf_op jit(solution)/shard_map/first/pallas_call | solution.py:344
  18.7 1.4 %collective-permute-done.5.refs_1_ = bf16[256,512]{1,0:T(8,128)(2,1)S(1)} collective-permute-done((bf16[256,512]{1,0:T(8,128)(2,1)S(1)}, bf16[256,512]{1,0:T(8,128)(2,1)S(1)}, u32[]{:S(2)}, u32[]{:S(2)}) %collective-permute-start.5) | collective-permute-done | bytes 262176 | tf_op jit(solution)/shard_map/three/ppermute | solution.py:405
  20.1 0.4 collective-permute-start.12
  20.5 2.9 %second.1 = (f32[656,1024]{1,0:T(8,128)S(1)}, f32[656,1024]{1,0:T(8,128)S(1)}) custom-call(bf16[256,512]{1,0:T(8,128)(2,1)S(1)} %collective-permute-done.2.refs_0_, bf16[256,512]{1,0:T(8,128)(2,1)S(1)} %collective-permute-done.5.refs_1_, f32[64,256]{1,0:T(8,128)S(1)} %get-tuple-element.46.refs_2_.refs_1_, f32[16,128]{1,0:T(8,128)S(1)} %get-tuple-element.47.refs_3_.refs_2_, ...), custom_call_target="tpu_custom_call" | custom-call | flops 1320000000 | tf_op jit(solution)/shard_map/second/pallas_call | solution.py:344
  23.3 1.2 %collective-permute-done.1.refs_1_ = bf16[256,512]{1,0:T(8,128)(2,1)S(1)} collective-permute-done((bf16[256,512]{1,0:T(8,128)(2,1)S(1)}, bf16[256,512]{1,0:T(8,128)(2,1)S(1)}, u32[]{:S(2)}, u32[]{:S(2)}) %collective-permute-start.1) | collective-permute-done | bytes 262176 | tf_op jit(solution)/shard_map/two/ppermute | solution.py:405
  24.6 0.0 collective-permute-start.11
  24.6 1.0 %collective-permute-done.12.refs_0_ = bf16[256,512]{1,0:T(8,128)(2,1)S(1)} collective-permute-done((bf16[256,512]{1,0:T(8,128)(2,1)S(1)}, bf16[256,512]{1,0:T(8,128)(2,1)S(1)}, u32[]{:S(2)}, u32[]{:S(2)}) %collective-permute-start.12) | collective-permute-done | bytes 262176 | tf_op jit(solution)/shard_map/three_y/ppermute | solution.py:401
  25.6 3.0 %third.1 = (f32[656,1024]{1,0:T(8,128)S(1)}, f32[656,1024]{1,0:T(8,128)S(1)}) custom-call(bf16[256,512]{1,0:T(8,128)(2,1)S(1)} %collective-permute-done.12.refs_0_, bf16[256,512]{1,0:T(8,128)(2,1)S(1)} %collective-permute-done.1.refs_1_, f32[64,256]{1,0:T(8,128)S(1)} %get-tuple-element.46.refs_2_.refs_1_, f32[16,128]{1,0:T(8,128)S(1)} %get-tuple-element.47.refs_3_.refs_2_, ...), custom_call_target="tpu_custom_call" | custom-call | flops 1320000000 | tf_op jit(solution)/shard_map/third/pallas_call | solution.py:344
  28.6 2.3 %collective-permute-done.11.refs_0_ = bf16[256,512]{1,0:T(8,128)(2,1)S(1)} collective-permute-done((bf16[256,512]{1,0:T(8,128)(2,1)S(1)}, bf16[256,512]{1,0:T(8,128)(2,1)S(1)}, u32[]{:S(2)}, u32[]{:S(2)}) %collective-permute-start.11) | collective-permute-done | bytes 262176 | tf_op jit(solution)/shard_map/two_y/ppermute | solution.py:401
  30.9 2.1 %fourth.1.mine = bf16[656,1024]{1,0:T(8,128)(2,1)S(1)} custom-call(bf16[256,512]{1,0:T(8,128)(2,1)S(1)} %collective-permute-done.11.refs_0_, f32[64,256]{1,0:T(8,128)S(1)} %get-tuple-element.46.refs_2_.refs_1_, f32[16,128]{1,0:T(8,128)S(1)} %get-tuple-element.47.refs_3_.refs_2_, f32[656,1024]{1,0:T(8,128)S(1)} %get-tuple-element.53.refs_3_, ...), custom_call_target="tpu_custom_call" | custom-call | flops 660000000 | tf_op jit(solution)/shard_map/fourth/pallas_call | solution.py:344
  33.0 5.5 %collective-permute-start.13 = (bf16[656,1024]{1,0:T(8,128)(2,1)S(1)}, bf16[656,1024]{1,0:T(8,128)(2,1)S(1)}, u32[]{:S(2)}, u32[]{:S(2)}) collective-permute-start(bf16[656,1024]{1,0:T(8,128)(2,1)S(1)} %fourth.1.mine), channel_id=1, source_target_pairs={{0,1},{1,0},{2,3},{3,2},{4,5},{5,4},{6,7},{7,6},{8,9},{9,8},{10,11... | collective-permute-start | bytes 4030472 | tf_op jit(solution)/shard_map/ppermute | solution.py:465
  38.5 2.7 %collective-permute-done.13.theirs = bf16[656,1024]{1,0:T(8,128)(2,1)S(1)} collective-permute-done((bf16[656,1024]{1,0:T(8,128)(2,1)S(1)}, bf16[656,1024]{1,0:T(8,128)(2,1)S(1)}, u32[]{:S(2)}, u32[]{:S(2)}) %collective-permute-start.13) | collective-permute-done | bytes 1343520 | tf_op jit(solution)/shard_map/ppermute | solution.py:465
  41.2 3.4 %update.1 = (bf16[256,128]{1,0:T(8,128)(2,1)}, f32[512,1024]{1,0:T(8,128)}, f32[1024,128]{1,0:T(8,128)}, f32[1,1024]{1,0:T(1,128)}, f32[512,1024]{1,0:T(8,128)}, /*index=5*/f32[1024,128]{1,0:T(8,128)}, f32[1,1024]{1,0:T(1,128)}) custom-call(bf16[656,1024]{1,0:T(8,128)(2,1)S(1)} %fourth.1.mine, bf16[656,1024]{1,0:T(8,128)(2,1)S(1)} %collective-permute-done.13.theirs, ...), custom_call_target="tpu_custom_call" | custom-call | flops 3740000000 | tf_op jit(solution)/shard_map/update/pallas_call | solution.py:387
  (34 shorter events, 0.1 us)
Async XLA Ops:
  0.6 5.2 %copy-start.4 = (bf16[512,1024]{1,0:T(8,128)(2,1)S(1)}, bf16[512,1024]{1,0:T(8,128)(2,1)}, u32[]{:S(2)}) copy-start(bf16[512,1024]{1,0:T(8,128)(2,1)} %actor_embed.1) | copy-start | bytes 3145732
  0.6 5.2 %copy-start.6 = (bf16[1024,128]{1,0:T(8,128)(2,1)S(1)}, bf16[1024,128]{1,0:T(8,128)(2,1)}, u32[]{:S(2)}) copy-start(bf16[1024,128]{1,0:T(8,128)(2,1)} %actor_policy.1) | copy-start | bytes 786436
  0.7 5.2 %copy-start.7 = (bf16[16,16,512]{2,1,0:T(8,128)(2,1)S(1)}, bf16[16,16,512]{2,1,0:T(8,128)(2,1)}, u32[]{:S(2)}) copy-start(bf16[16,16,512]{2,1,0:T(8,128)(2,1)} %param.14) | copy-start | bytes 786436
  0.7 5.1 %copy-start.9 = (s32[16,16]{1,0:T(8,128)S(1)}, s32[16,16]{1,0:T(8,128)}, u32[]{:S(2)}) copy-start(s32[16,16]{1,0:T(8,128)} %actions.1) | copy-start | bytes 3076
  0.7 5.1 %copy-start.10 = (f32[16,16]{1,0:T(8,128)S(1)}, f32[16,16]{1,0:T(8,128)}, u32[]{:S(2)}) copy-start(f32[16,16]{1,0:T(8,128)} %rewards.1) | copy-start | bytes 3076
  0.7 5.1 %copy-start.12 = (s32[16]{0:T(128)S(1)}, s32[16]{0:T(128)}, u32[]{:S(2)}) copy-start(s32[16]{0:T(128)} %param.15) | copy-start | bytes 196
  0.7 5.1 %copy-start.13 = (s32[16]{0:T(128)S(1)}, s32[16]{0:T(128)}, u32[]{:S(2)}) copy-start(s32[16]{0:T(128)} %param.18) | copy-start | bytes 196
  0.7 14.1 %collective-permute-start.6 = (bf16[256,512]{1,0:T(8,128)(2,1)}, bf16[256,512]{1,0:T(8,128)(2,1)S(1)}, u32[]{:S(2)}, u32[]{:S(2)}) collective-permute-start(bf16[256,512]{1,0:T(8,128)(2,1)} %bitcast.11), channel_id=1, source_target_pairs={{0,2},{2,0},{4,6},{6,4},{8,10},{10,8},{12,14},{14,12},{1,3},{3,1},... | collective-permute-start | bytes 786440 | tf_op jit(solution)/shard_map/own_y/ppermute | solution.py:401
  2.0 10.1 %collective-permute-start = (bf16[256,512]{1,0:T(8,128)(2,1)}, bf16[256,512]{1,0:T(8,128)(2,1)S(1)}, u32[]{:S(2)}, u32[]{:S(2)}) collective-permute-start(bf16[256,512]{1,0:T(8,128)(2,1)} %bitcast.12), channel_id=1, source_target_pairs={{0,4},{2,6},{4,8},{6,10},{8,12},{10,14},{12,0},{14,2},{1,5},{3,7},... | collective-permute-start | bytes 786440 | tf_op jit(solution)/shard_map/one/ppermute | solution.py:405
  3.3 2.2 %collective-permute-start.3 = (s32[16]{0:T(128)}, s32[16]{0:T(128)S(1)}, u32[]{:S(2)}, u32[]{:S(2)}) collective-permute-start(s32[16]{0:T(128)} %param.15), channel_id=1, source_target_pairs={{0,1},{1,0},{2,3},{3,2},{4,5},{5,4},{6,7},{7,6},{8,9},{9,8},{10,11... | collective-permute-start | bytes 200 | tf_op jit(solution)/shard_map/ppermute | solution.py:455
  4.5 1.3 %collective-permute-start.4 = (s32[16]{0:T(128)}, s32[16]{0:T(128)S(1)}, u32[]{:S(2)}, u32[]{:S(2)}) collective-permute-start(s32[16]{0:T(128)} %param.18), channel_id=1, source_target_pairs={{0,1},{1,0},{2,3},{3,2},{4,5},{5,4},{6,7},{7,6},{8,9},{9,8},{10,11... | collective-permute-start | bytes 200 | tf_op jit(solution)/shard_map/ppermute | solution.py:455
  5.8 3.5 %copy-start = (f32[512,1024]{1,0:T(8,128)S(1)}, f32[512,1024]{1,0:T(8,128)}, u32[]{:S(2)}) copy-start(f32[512,1024]{1,0:T(8,128)} %master_embed.3) | copy-start | bytes 6291460
  5.9 3.5 %copy-start.1 = (f32[1024,128]{1,0:T(8,128)S(1)}, f32[1024,128]{1,0:T(8,128)}, u32[]{:S(2)}) copy-start(f32[1024,128]{1,0:T(8,128)} %master_policy.3) | copy-start | bytes 1572868
  5.9 3.5 %copy-start.2 = (f32[1024]{0:T(1024)S(1)}, f32[1024]{0:T(1024)}, u32[]{:S(2)}) copy-start(f32[1024]{0:T(1024)} %param.23) | copy-start | bytes 12292
  6.6 5.2 %collective-permute-start.9 = (f32[8,256]{1,0:T(8,128)S(1)}, f32[8,256]{1,0:T(8,128)S(1)}, u32[]{:S(2)}, u32[]{:S(2)}) collective-permute-start(f32[8,256]{1,0:T(8,128)S(1)} %side.1), channel_id=1, source_target_pairs={{0,12},{2,14},{4,8},{6,10},{8,4},{10,6},{12,0},{14,2},{1,13},{3,15... | collective-permute-start | bytes 24584 | tf_op jit(solution)/shard_map/side_z/ppermute | solution.py:401
  8.0 3.8 %collective-permute-start.8 = (f32[8,256]{1,0:T(8,128)S(1)}, f32[8,256]{1,0:T(8,128)S(1)}, u32[]{:S(2)}, u32[]{:S(2)}) collective-permute-start(f32[8,256]{1,0:T(8,128)S(1)} %side.1), channel_id=1, source_target_pairs={{0,8},{2,10},{4,12},{6,14},{8,0},{10,2},{12,4},{14,6},{1,9},{3,11}... | collective-permute-start | bytes 24584 | tf_op jit(solution)/shard_map/side_z/ppermute | solution.py:401
  9.0 2.9 %collective-permute-start.7 = (f32[8,256]{1,0:T(8,128)S(1)}, f32[8,256]{1,0:T(8,128)S(1)}, u32[]{:S(2)}, u32[]{:S(2)}) collective-permute-start(f32[8,256]{1,0:T(8,128)S(1)} %side.1), channel_id=1, source_target_pairs={{0,4},{2,6},{4,0},{6,2},{8,12},{10,14},{12,8},{14,10},{1,5},{3,7},... | collective-permute-start | bytes 24584 | tf_op jit(solution)/shard_map/side_z/ppermute | solution.py:401
  11.8 8.3 %collective-permute-start.5 = (bf16[256,512]{1,0:T(8,128)(2,1)S(1)}, bf16[256,512]{1,0:T(8,128)(2,1)S(1)}, u32[]{:S(2)}, u32[]{:S(2)}) collective-permute-start(bf16[256,512]{1,0:T(8,128)(2,1)S(1)} %bitcast.14), channel_id=1, source_target_pairs={{0,12},{2,14},{4,0},{6,2},{8,4},{10,6},{12,8},{14,10},{1,13},{3,15... | collective-permute-start | bytes 786440 | tf_op jit(solution)/shard_map/three/ppermute | solution.py:405
  11.8 4.3 %collective-permute-start.10 = (f32[32,256]{1,0:T(8,128)S(1)}, f32[32,256]{1,0:T(8,128)S(1)}, u32[]{:S(2)}, u32[]{:S(2)}) collective-permute-start(f32[32,256]{1,0:T(8,128)S(1)} %pad_maximum_fusion.refs_3_), channel_id=1, source_target_pairs={{0,2},{2,0},{4,6},{6,4},{8,10},{10,8},{12,14},{14,12},{1,3},{3,1},... | collective-permute-start | bytes 98312 | tf_op jit(solution)/shard_map/side_y/ppermute | solution.py:401
  12.1 8.3 %collective-permute-start.2 = (bf16[256,512]{1,0:T(8,128)(2,1)S(1)}, bf16[256,512]{1,0:T(8,128)(2,1)S(1)}, u32[]{:S(2)}, u32[]{:S(2)}) collective-permute-start(bf16[256,512]{1,0:T(8,128)(2,1)S(1)} %collective-permute-done.refs_2_), channel_id=1, source_target_pairs={{0,2},{2,0},{4,6},{6,4},{8,10},{10,8},{12,14},{14,12},{1,3},{3,1},... | collective-permute-start | bytes 786440 | tf_op jit(solution)/shard_map/one_y/ppermute | solution.py:401
  13.4 11.2 %collective-permute-start.1 = (bf16[256,512]{1,0:T(8,128)(2,1)S(1)}, bf16[256,512]{1,0:T(8,128)(2,1)S(1)}, u32[]{:S(2)}, u32[]{:S(2)}) collective-permute-start(bf16[256,512]{1,0:T(8,128)(2,1)S(1)} %collective-permute-done.refs_2_), channel_id=1, source_target_pairs={{0,4},{2,6},{4,8},{6,10},{8,12},{10,14},{12,0},{14,2},{1,5},{3,7},... | collective-permute-start | bytes 786440 | tf_op jit(solution)/shard_map/two/ppermute | solution.py:405
  20.1 5.5 %collective-permute-start.12 = (bf16[256,512]{1,0:T(8,128)(2,1)S(1)}, bf16[256,512]{1,0:T(8,128)(2,1)S(1)}, u32[]{:S(2)}, u32[]{:S(2)}) collective-permute-start(bf16[256,512]{1,0:T(8,128)(2,1)S(1)} %collective-permute-done.5.refs_1_), channel_id=1, source_target_pairs={{0,2},{2,0},{4,6},{6,4},{8,10},{10,8},{12,14},{14,12},{1,3},{3,1},... | collective-permute-start | bytes 786440 | tf_op jit(solution)/shard_map/three_y/ppermute | solution.py:401
  24.6 6.3 %collective-permute-start.11 = (bf16[256,512]{1,0:T(8,128)(2,1)S(1)}, bf16[256,512]{1,0:T(8,128)(2,1)S(1)}, u32[]{:S(2)}, u32[]{:S(2)}) collective-permute-start(bf16[256,512]{1,0:T(8,128)(2,1)S(1)} %collective-permute-done.1.refs_1_), channel_id=1, source_target_pairs={{0,2},{2,0},{4,6},{6,4},{8,10},{10,8},{12,14},{14,12},{1,3},{3,1},... | collective-permute-start | bytes 786440 | tf_op jit(solution)/shard_map/two_y/ppermute | solution.py:401
  30.8 10.4 %copy-start.3 = (f32[512,1024]{1,0:T(8,128)S(1)}, f32[512,1024]{1,0:T(8,128)}, u32[]{:S(2)}) copy-start(f32[512,1024]{1,0:T(8,128)} %embed_moment.1) | copy-start | bytes 6291460
  30.9 10.4 %copy-start.5 = (f32[1024,128]{1,0:T(8,128)S(1)}, f32[1024,128]{1,0:T(8,128)}, u32[]{:S(2)}) copy-start(f32[1024,128]{1,0:T(8,128)} %policy_moment.1) | copy-start | bytes 1572868
  30.9 10.4 %copy-start.8 = (bf16[256,512]{1,0:T(8,128)(2,1)S(1)}, bf16[256,512]{1,0:T(8,128)(2,1)}, u32[]{:S(2)}) copy-start(bf16[256,512]{1,0:T(8,128)(2,1)} %next_obs.1) | copy-start | bytes 786436
  30.9 10.4 %copy-start.11 = (f32[1024]{0:T(1024)S(1)}, f32[1024]{0:T(1024)}, u32[]{:S(2)}) copy-start(f32[1024]{0:T(1024)} %param.26) | copy-start | bytes 12292
  33.0 8.2 %collective-permute-start.13 = (bf16[656,1024]{1,0:T(8,128)(2,1)S(1)}, bf16[656,1024]{1,0:T(8,128)(2,1)S(1)}, u32[]{:S(2)}, u32[]{:S(2)}) collective-permute-start(bf16[656,1024]{1,0:T(8,128)(2,1)S(1)} %fourth.1.mine), channel_id=1, source_target_pairs={{0,1},{1,0},{2,3},{3,2},{4,5},{5,4},{6,7},{7,6},{8,9},{9,8},{10,11... | collective-permute-start | bytes 4030472 | tf_op jit(solution)/shard_map/ppermute | solution.py:465
